TPU v7x, 32 devices: a whole 2x2x4 slice. The times are simulated.
32 devices in a mesh: groups: 2 (over y), row: 4 (over z), col: 4 (over x, core).
Axes of the slice: x: 2, y: 2, z: 4, core: 2. Of those that a mesh axis runs over, the one named last changes fastest.
Arguments:
- alignment_embedding: bfloat16 [16, 512, 64], P(None, ('groups', 'row', 'col')), parts along dimension 1, may hold values from -6 to 6
- alignment_cell_exists: int32 [16, 512], P(None, ('groups', 'row', 'col')), parts along dimension 1, may hold values 0 or 1
- alignment_lines_exist: int32 [32], P('groups'), parts along dimension 0, may hold values 0 or 1
- sitewise_factors: bfloat16 [64, 64], replicated, may hold values from -0.75 to 0.75
- pairing_matrix: bfloat16 [1024, 128], replicated, may hold values from -0.1875 to 0.1875
- offset_vector: float32 [128], replicated, may hold values from -3 to 3
- upstream_adjoint: bfloat16 [512, 256, 128], P(('groups', 'row'), 'col'), parts along dimension 0, may hold values from -6 to 6
Outputs:
- coupling_update: bfloat16 [512, 256, 128], P(('groups', 'row'), 'col'), parts along dimension 0
- alignment_embedding_adjoint: float32 [16, 512, 64], P(None, ('groups', 'row', 'col')), parts along dimension 1
- sitewise_factors_adjoint: float32 [128, 64], P('groups'), parts along dimension 0
- pairing_matrix_adjoint: float32 [2048, 128], P('groups'), parts along dimension 0
- offset_vector_slope: float32 [256], P('groups'), parts along dimension 0
There are 2 independent parts, one for each index of `groups`. A program takes and returns all parts, laid end to end along the dimension named above; an argument that names none is the same for every part. Nothing has to cross between parts.
All inputs are finite; a program needn't handle non-finite values. No bound on the sum of `alignment_cell_exists` on one device may be relied on, other than what follows from the above.
Results may differ from a plain program's by a relative error of at most 0.0095.
Values may be sent and summed in bfloat16 or wider, within the bound.
No kernel may reach another device: no remote copies, remote signals or barrier semaphores. Data moves between devices by JAX's collectives and lax.ppermute only.
A program may use at most 64 MiB of HBM per device.

v0:
```python
import jax
import jax.numpy as jnp
from jax import lax
from jax.sharding import PartitionSpec as P


def spread_2(block, axis, owner):
    block = jnp.where(lax.axis_index(axis) == owner, block, jnp.zeros_like(block))
    return lax.psum(block, axis)


def layer_norm(forward_results):
    center = forward_results - jnp.mean(forward_results, axis=-1, keepdims=True)
    spread = jnp.mean(center * center, axis=-1, keepdims=True)
    return center * lax.rsqrt(spread + 1e-05)


def per_device(
    alignment_embedding,
    alignment_cell_exists,
    alignment_lines_exist,
    sitewise_factors,
    pairing_matrix,
    offset_vector,
    upstream_adjoint,
):
    highest = lax.Precision.HIGHEST
    width = sitewise_factors.shape[1] // 2
    block = upstream_adjoint.shape[0]
    pair_width = upstream_adjoint.shape[2]
    owned_positions = alignment_embedding.shape[1]
    forward_results = alignment_embedding.astype(jnp.float32)
    normed = layer_norm(forward_results).astype(jnp.bfloat16)
    weight = (alignment_cell_exists * alignment_lines_exist[:, None]).astype(jnp.float32)
    proj = jnp.einsum("stk,kn->tsn", normed, sitewise_factors, preferred_element_type=jnp.float32)
    proj = (proj * weight.T[:, :, None]).astype(jnp.bfloat16)
    weight_tokens = weight.T.astype(jnp.bfloat16)
    all_proj, all_weight = (
        lax.all_gather(proj, ("row", "col"), axis=0, tiled=True),
        lax.all_gather(weight_tokens, ("row", "col"), axis=0, tiled=True),
    )
    row_start = lax.axis_index("row") * block
    col_start = lax.axis_index("col") * block
    rows_proj = lax.dynamic_slice_in_dim(all_proj, row_start, block, 0)
    rows_weight = lax.dynamic_slice_in_dim(all_weight, row_start, block, 0)
    cols_proj = lax.dynamic_slice_in_dim(all_proj, col_start, block, 0)
    cols_weight = lax.dynamic_slice_in_dim(all_weight, col_start, block, 0)
    left_rows = rows_proj[:, :, :width]
    right_cols = cols_proj[:, :, width:]
    count = jnp.dot(rows_weight, cols_weight.T, preferred_element_type=jnp.float32)
    inner = 16
    steps_count = block // inner
    seq_rows = left_rows.shape[1]

    def one_block(carry, inputs):
        d_right, d_wout = carry
        left_part, count_part, cot_part = inputs
        outer = jnp.einsum(
            "isc,jse->ijce", left_part, right_cols, preferred_element_type=jnp.float32
        )
        outer = outer.reshape(inner, block, width * width)
        outer = (outer / (count_part + 0.001)[:, :, None]).astype(jnp.bfloat16)
        flat = outer.reshape(inner * block, width * width)
        cot_flat = cot_part.reshape(inner * block, pair_width)
        pair_part = (
            jnp.dot(flat, pairing_matrix, preferred_element_type=jnp.float32) + offset_vector
        ).astype(jnp.bfloat16)
        d_wout = d_wout + jnp.dot(flat.T, cot_flat, preferred_element_type=jnp.float32)
        d_outer = jnp.dot(cot_flat, pairing_matrix.T, preferred_element_type=jnp.float32).reshape(
            inner, block, width * width
        )
        d_outer = (d_outer / (count_part + 0.001)[:, :, None]).astype(jnp.bfloat16)
        d_outer = d_outer.reshape(inner, block, width, width)
        adjoint_leftside = jnp.einsum(
            "ijce,jse->isc", d_outer, right_cols, preferred_element_type=jnp.float32
        )
        d_right = d_right + jnp.einsum(
            "ijce,isc->jse", d_outer, left_part, preferred_element_type=jnp.float32
        )
        return ((d_right, d_wout), (pair_part.reshape(inner, block, pair_width), adjoint_leftside))

    inputs = (
        left_rows.reshape(steps_count, inner, seq_rows, width),
        count.reshape(steps_count, inner, block),
        upstream_adjoint.reshape(steps_count, inner, block, pair_width),
    )
    initial_accumulator = (
        jnp.zeros((block, seq_rows, width), jnp.float32),
        jnp.zeros((width * width, pair_width), jnp.float32),
    )
    (d_right, d_wout_part), (pair_blocks, adjoint_leftside_pieces) = lax.scan(
        one_block, initial_accumulator, inputs
    )
    coupling_update = pair_blocks.reshape(block, block, pair_width)
    adjoint_leftside = adjoint_leftside_pieces.reshape(block, seq_rows, width)
    d_right_sum = lax.psum(d_right.astype(jnp.bfloat16), "row").astype(jnp.float32)
    d_left_own = lax.psum_scatter(
        adjoint_leftside.astype(jnp.bfloat16), "col", scatter_dimension=0, tiled=True
    ).astype(jnp.float32)
    d_right_rows = spread_2(d_right_sum.astype(jnp.bfloat16), "col", lax.axis_index("row")).astype(
        d_right_sum.dtype
    )
    d_right_own = lax.dynamic_slice_in_dim(
        d_right_rows, lax.axis_index("col") * owned_positions, owned_positions, 0
    )
    d_proj = jnp.concatenate([d_left_own, d_right_own], axis=-1)
    d_proj = jnp.transpose(d_proj * weight.T[:, :, None], (1, 0, 2))
    d_wab_part = jnp.einsum("stk,stn->kn", normed.astype(jnp.float32), d_proj, precision=highest)
    standardized_adjoint = jnp.einsum(
        "stn,kn->stk", d_proj, sitewise_factors.astype(jnp.float32), precision=highest
    )
    unused, reverse_pass_rule = jax.vjp(layer_norm, forward_results)
    alignment_embedding_adjoint = reverse_pass_rule(standardized_adjoint)[0]
    d_bias_part = jnp.sum(upstream_adjoint.astype(jnp.float32), axis=(0, 1))
    sitewise_factors_adjoint, pairing_matrix_adjoint, offset_vector_slope = lax.psum(
        (d_wab_part, d_wout_part, d_bias_part), ("row", "col")
    )
    return (
        coupling_update,
        alignment_embedding_adjoint,
        sitewise_factors_adjoint,
        pairing_matrix_adjoint,
        offset_vector_slope,
    )


def solution(mesh):
    placed = (
        P(None, ("groups", "row", "col"), None),
        P(None, ("groups", "row", "col")),
        P("groups"),
        P(),
        P(),
        P(),
        P(("groups", "row"), "col", None),
    )
    return jax.shard_map(
        per_device,
        mesh=mesh,
        in_specs=placed,
        out_specs=(
            P(("groups", "row"), "col", None),
            P(None, ("groups", "row", "col"), None),
            P("groups", None),
            P("groups", None),
            P("groups"),
        ),
        check_vma=False,
    )
```

profile of v0, /device:TPU:0, one launch (start us, length us, event | category | flops | bytes accessed | tf_op | source)
XLA Modules:
  0.0 437.9 jit_solution(12482326080878711298)
XLA Ops:
  12.2 26.2 %all_gather.6 = bf16[256,16,64]{2,1,0:T(8,128)(2,1)S(1)} all-gather(bf16[16,16,64]{2,1,0:T(8,128)(2,1)S(1)} %copy.86), channel_id=1, replica_groups=mesh['groups'=2,'row'=4,'col'=4] {'row','col'}, dimensions={0}, use_global_device_ids=true | all-gather | bytes 557056 | tf_op jit(solution)/shard_map/all_gather | solution.py:39
  38.9 17.6 %all_gather.7 = bf16[256,16]{1,0:T(8,128)(2,1)S(1)} all-gather(bf16[16,16]{1,0:T(8,128)(2,1)S(1)} %get-tuple-element.206), channel_id=1, replica_groups=mesh['groups'=2,'row'=4,'col'=4] {'row','col'}, dimensions={0}, use_global_device_ids=true | all-gather | bytes 8704 | tf_op jit(solution)/shard_map/all_gather | solution.py:40
  56.7 188.0 %while.17 = (s32[]{:T(128)}, f32[64,16,32]{0,1,2:T(8,128)S(1)}, f32[1024,128]{1,0:T(8,128)S(1)}, bf16[4,16,64,128]{3,2,1,0:T(8,128)(2,1)}, bf16[4,16,16,32]{3,2,...) while((s32[]{:T(128)}, f32[64,16,32]{0,1,2:T(8,128)S(1)}, ...), condition=%wide.region_3.4_spmd.clone, body=%wide.region_2.3_spmd.clone.sunk | while | flops 912852992 | bytes 73575800 | solution.py:91
  56.7 3.2 divide_convert_fusion.12
  59.9 8.1 %copy.119 = f32[16,64,32,32]{1,0,3,2:T(8,128)} copy(f32[16,64,32,32]{1,2,3,0:T(8,128)S(1)} %get-tuple-element.287) | data formatting | bytes 8388608 | tf_op jit(solution)/shard_map/while/body/eval_jaxpr/isc,jse->ijce/transpose | solution.py:58
  68.0 7.7 %reshape.101 = f32[1024,1024]{0,1:T(8,128)} reshape(f32[16,64,32,32]{1,0,3,2:T(8,128)} %copy.119) | data formatting | bytes 8388608 | tf_op jit(solution)/shard_map/while/body/eval_jaxpr/reshape | solution.py:61
  75.8 3.1 fusion.84
  78.9 1.7 constant_dynamic-update-slice_fusion.2
  80.6 4.6 %copy.121 = bf16[16,64,32,32]{1,0,3,2:T(8,128)(2,1)} copy(bf16[16,64,32,32]{1,2,3,0:T(8,128)(2,1)S(1)} %copy-done.1) | data formatting | bytes 4194304 | tf_op jit(solution)/shard_map/while/body/eval_jaxpr/convert_element_type | solution.py:62
  85.2 5.5 %convert_element_type.120 = bf16[1024,1024]{0,1:T(8,128)(2,1)S(1)} reshape(bf16[16,64,32,32]{1,0,3,2:T(8,128)(2,1)} %copy.121) | data formatting | bytes 4194304 | tf_op jit(solution)/shard_map/while/body/eval_jaxpr/convert_element_type | solution.py:62
  93.2 3.2 copy.120
  96.4 3.7 fusion.85
  100.1 2.9 fusion.86
  103.7 3.2 divide_convert_fusion.12
  106.9 8.1 %copy.119 = f32[16,64,32,32]{1,0,3,2:T(8,128)} copy(f32[16,64,32,32]{1,2,3,0:T(8,128)S(1)} %get-tuple-element.287) | data formatting | bytes 8388608 | tf_op jit(solution)/shard_map/while/body/eval_jaxpr/isc,jse->ijce/transpose | solution.py:58
  115.0 7.7 %reshape.101 = f32[1024,1024]{0,1:T(8,128)} reshape(f32[16,64,32,32]{1,0,3,2:T(8,128)} %copy.119) | data formatting | bytes 8388608 | tf_op jit(solution)/shard_map/while/body/eval_jaxpr/reshape | solution.py:61
  122.8 3.1 fusion.84
  127.6 4.6 %copy.121 = bf16[16,64,32,32]{1,0,3,2:T(8,128)(2,1)} copy(bf16[16,64,32,32]{1,2,3,0:T(8,128)(2,1)S(1)} %copy-done.1) | data formatting | bytes 4194304 | tf_op jit(solution)/shard_map/while/body/eval_jaxpr/convert_element_type | solution.py:62
  132.2 5.5 %convert_element_type.120 = bf16[1024,1024]{0,1:T(8,128)(2,1)S(1)} reshape(bf16[16,64,32,32]{1,0,3,2:T(8,128)(2,1)} %copy.121) | data formatting | bytes 4194304 | tf_op jit(solution)/shard_map/while/body/eval_jaxpr/convert_element_type | solution.py:62
  140.2 3.2 copy.120
  143.3 3.7 fusion.85
  147.1 2.9 fusion.86
  150.7 3.2 divide_convert_fusion.12
  153.9 8.1 %copy.119 = f32[16,64,32,32]{1,0,3,2:T(8,128)} copy(f32[16,64,32,32]{1,2,3,0:T(8,128)S(1)} %get-tuple-element.287) | data formatting | bytes 8388608 | tf_op jit(solution)/shard_map/while/body/eval_jaxpr/isc,jse->ijce/transpose | solution.py:58
  162.0 7.7 %reshape.101 = f32[1024,1024]{0,1:T(8,128)} reshape(f32[16,64,32,32]{1,0,3,2:T(8,128)} %copy.119) | data formatting | bytes 8388608 | tf_op jit(solution)/shard_map/while/body/eval_jaxpr/reshape | solution.py:61
  169.8 3.1 fusion.84
  174.6 4.6 %copy.121 = bf16[16,64,32,32]{1,0,3,2:T(8,128)(2,1)} copy(bf16[16,64,32,32]{1,2,3,0:T(8,128)(2,1)S(1)} %copy-done.1) | data formatting | bytes 4194304 | tf_op jit(solution)/shard_map/while/body/eval_jaxpr/convert_element_type | solution.py:62
  179.2 5.5 %convert_element_type.120 = bf16[1024,1024]{0,1:T(8,128)(2,1)S(1)} reshape(bf16[16,64,32,32]{1,0,3,2:T(8,128)(2,1)} %copy.121) | data formatting | bytes 4194304 | tf_op jit(solution)/shard_map/while/body/eval_jaxpr/convert_element_type | solution.py:62
  187.2 3.2 copy.120
  190.3 3.7 fusion.85
  194.1 2.9 fusion.86
  197.7 3.2 divide_convert_fusion.12
  200.9 8.1 %copy.119 = f32[16,64,32,32]{1,0,3,2:T(8,128)} copy(f32[16,64,32,32]{1,2,3,0:T(8,128)S(1)} %get-tuple-element.287) | data formatting | bytes 8388608 | tf_op jit(solution)/shard_map/while/body/eval_jaxpr/isc,jse->ijce/transpose | solution.py:58
  209.0 7.7 %reshape.101 = f32[1024,1024]{0,1:T(8,128)} reshape(f32[16,64,32,32]{1,0,3,2:T(8,128)} %copy.119) | data formatting | bytes 8388608 | tf_op jit(solution)/shard_map/while/body/eval_jaxpr/reshape | solution.py:61
  216.7 3.1 fusion.84
  219.8 1.7 constant_dynamic-update-slice_fusion.2
  221.5 4.6 %copy.121 = bf16[16,64,32,32]{1,0,3,2:T(8,128)(2,1)} copy(bf16[16,64,32,32]{1,2,3,0:T(8,128)(2,1)S(1)} %copy-done.1) | data formatting | bytes 4194304 | tf_op jit(solution)/shard_map/while/body/eval_jaxpr/convert_element_type | solution.py:62
  226.2 5.5 %convert_element_type.120 = bf16[1024,1024]{0,1:T(8,128)(2,1)S(1)} reshape(bf16[16,64,32,32]{1,0,3,2:T(8,128)(2,1)} %copy.121) | data formatting | bytes 4194304 | tf_op jit(solution)/shard_map/while/body/eval_jaxpr/convert_element_type | solution.py:62
  234.1 3.2 copy.120
  237.3 3.7 fusion.85
  241.1 2.9 fusion.86
  245.6 33.0 %all-reduce.5.cloned.1.call-done = bf16[64,16,32]{0,2,1:T(8,128)(2,1)} async-done(((bf16[64,16,32]{0,2,1:T(8,128)(2,1)}), bf16[64,16,32]{0,2,1:T(8,128)(2,1)}) %all-reduce.5.cloned.1.call-update) | async-done | bytes 65552 | tf_op jit(solution)/shard_map/psum | solution.py:96
  281.4 1.8 convert_reduce_fusion
  283.2 29.4 %all-reduce.7.cloned.1.call-done = bf16[64,16,32]{0,2,1:T(8,128)(2,1)} async-done(((bf16[64,16,32]{0,2,1:T(8,128)(2,1)}), bf16[64,16,32]{0,2,1:T(8,128)(2,1)}) %all-reduce.7.cloned.1.call-update) | async-done | bytes 65552 | tf_op jit(solution)/shard_map/psum | solution.py:9
  313.6 21.5 %reduce-scatter.2.cloned.1.call-done = bf16[16,16,32]{2,1,0:T(8,128)(2,1)} async-done(((bf16[64,16,32]{2,1,0:T(8,128)(2,1)}), bf16[16,16,32]{2,1,0:T(8,128)(2,1)}) %reduce-scatter.2.cloned.1.call-update) | async-done | bytes 16400 | tf_op jit(solution)/shard_map/reduce_scatter | solution.py:97
  337.8 61.0 %all-reduce = (f32[64,64]{1,0:T(8,128)}, f32[128]{0:T(128)}) all-reduce(f32[64,64]{1,0:T(8,128)S(1)} %convolution_bitcast_fusion.2, f32[128]{0:T(128)S(1)} %convert_reduce_fusion), channel_id=1, replica_groups=mesh['groups'=2,'row'=4,'col'=4] {'row','col'}, use_global_device_ids=true, to_apply=%region_9.10 | all-reduce | flops 4224 | bytes 33792 | tf_op jit(solution)/shard_map/psum | solution.py:115
  399.7 29.8 %all-reduce.9.cloned.1.call-done = f32[1024,128]{1,0:T(8,128)} async-done(((f32[1024,128]{1,0:T(8,128)}), f32[1024,128]{1,0:T(8,128)}) %all-reduce.9.cloned.1.call-update) | async-done | bytes 524304 | tf_op jit(solution)/shard_map/psum | solution.py:115
  429.5 1.9 copy.142
  (143 shorter events, 30.2 us)
Async XLA Ops:
  7.2 3.7 copy-start
  7.2 271.3 %all-reduce.5.cloned.1.call-start = ((), (), s32[]{:S(2)}) async-start(), calls=%async_computation.2 | async-start | bytes 262144 | tf_op jit(solution)/shard_map/psum | solution.py:96
  8.2 3.8 copy-start.5
  9.3 1.5 copy-start.15
  9.3 29.6 %copy-start.11 = (f32[16,16]{1,0:T(8,128)}, f32[16,16]{1,0:T(8,128)S(1)}, u32[]{:S(2)}) copy-start(f32[16,16]{1,0:T(8,128)S(1)} %fusion.52) | copy-start | bytes 3076
  10.8 28.1 %copy-start.13 = (f32[16,16]{0,1:T(8,128)}, f32[16,16]{0,1:T(8,128)S(1)}, u32[]{:S(2)}) copy-start(f32[16,16]{0,1:T(8,128)S(1)} %copy.85) | copy-start | bytes 3076
  56.6 279.5 %copy-start.4 = (bf16[16,16,64]{2,1,0:T(8,128)(2,1)S(1)}, bf16[16,16,64]{2,1,0:T(8,128)(2,1)}, u32[]{:S(2)}) copy-start(bf16[16,16,64]{2,1,0:T(8,128)(2,1)} %param.9) | copy-start | bytes 98308
  56.6 279.5 %copy-start.6 = (f32[16,16]{1,0:T(8,128)S(1)}, f32[16,16]{1,0:T(8,128)}, u32[]{:S(2)}) copy-start(f32[16,16]{1,0:T(8,128)} %copy-done.5) | copy-start | bytes 3076
  56.6 279.5 %copy-start.14 = (f32[16,16]{0,1:T(8,128)S(1)}, f32[16,16]{0,1:T(8,128)}, u32[]{:S(2)}) copy-start(f32[16,16]{0,1:T(8,128)} %copy-done.13) | copy-start | bytes 3076
  56.7 3.3 copy-start.9
  68.0 7.7 %copy-start.17 = (bf16[1024,128]{1,0:T(8,128)(2,1)S(1)}, bf16[1024,128]{1,0:T(8,128)(2,1)}, u32[]{:S(2)}) copy-start(bf16[1024,128]{1,0:T(8,128)(2,1)} %get-tuple-element.324) | copy-start | bytes 786436 | tf_op jit(solution)/shard_map/while
  68.0 7.7 %copy-start.18 = (f32[128]{0:T(128)S(1)}, f32[128]{0:T(128)}, u32[]{:S(2)}) copy-start(f32[128]{0:T(128)} %get-tuple-element.327) | copy-start | bytes 1540 | tf_op jit(solution)/shard_map/while
  75.8 4.8 %copy-start.1 = (bf16[16,64,32,32]{1,2,3,0:T(8,128)(2,1)S(1)}, bf16[16,64,32,32]{1,2,3,0:T(8,128)(2,1)}, u32[]{:S(2)}) copy-start(bf16[16,64,32,32]{1,2,3,0:T(8,128)(2,1)} %get-tuple-element.289) | copy-start | bytes 6291460 | tf_op jit(solution)/shard_map/while
  93.2 6.9 %copy-start.7 = (bf16[4,16,16,32]{3,2,1,0:T(8,128)(2,1)S(1)}, bf16[4,16,16,32]{3,2,1,0:T(8,128)(2,1)}, u32[]{:S(2)}) copy-start(bf16[4,16,16,32]{3,2,1,0:T(8,128)(2,1)} %get-tuple-element.308) | copy-start | bytes 196612 | tf_op jit(solution)/shard_map/while
  96.3 3.7 copy-start.2
  96.3 3.7 copy-start.10
  103.0 0.7 copy-start.8
  103.7 3.2 copy-start.9
  115.0 7.7 %copy-start.17 = (bf16[1024,128]{1,0:T(8,128)(2,1)S(1)}, bf16[1024,128]{1,0:T(8,128)(2,1)}, u32[]{:S(2)}) copy-start(bf16[1024,128]{1,0:T(8,128)(2,1)} %get-tuple-element.324) | copy-start | bytes 786436 | tf_op jit(solution)/shard_map/while
  115.0 7.7 %copy-start.18 = (f32[128]{0:T(128)S(1)}, f32[128]{0:T(128)}, u32[]{:S(2)}) copy-start(f32[128]{0:T(128)} %get-tuple-element.327) | copy-start | bytes 1540 | tf_op jit(solution)/shard_map/while
  122.8 4.8 %copy-start.1 = (bf16[16,64,32,32]{1,2,3,0:T(8,128)(2,1)S(1)}, bf16[16,64,32,32]{1,2,3,0:T(8,128)(2,1)}, u32[]{:S(2)}) copy-start(bf16[16,64,32,32]{1,2,3,0:T(8,128)(2,1)} %get-tuple-element.289) | copy-start | bytes 6291460 | tf_op jit(solution)/shard_map/while
  140.2 6.9 %copy-start.7 = (bf16[4,16,16,32]{3,2,1,0:T(8,128)(2,1)S(1)}, bf16[4,16,16,32]{3,2,1,0:T(8,128)(2,1)}, u32[]{:S(2)}) copy-start(bf16[4,16,16,32]{3,2,1,0:T(8,128)(2,1)} %get-tuple-element.308) | copy-start | bytes 196612 | tf_op jit(solution)/shard_map/while
  143.3 3.7 copy-start.2
  143.3 3.7 copy-start.10
  150.0 0.7 copy-start.8
  150.7 3.2 copy-start.9
  162.0 7.7 %copy-start.17 = (bf16[1024,128]{1,0:T(8,128)(2,1)S(1)}, bf16[1024,128]{1,0:T(8,128)(2,1)}, u32[]{:S(2)}) copy-start(bf16[1024,128]{1,0:T(8,128)(2,1)} %get-tuple-element.324) | copy-start | bytes 786436 | tf_op jit(solution)/shard_map/while
  162.0 7.7 %copy-start.18 = (f32[128]{0:T(128)S(1)}, f32[128]{0:T(128)}, u32[]{:S(2)}) copy-start(f32[128]{0:T(128)} %get-tuple-element.327) | copy-start | bytes 1540 | tf_op jit(solution)/shard_map/while
  169.8 4.8 %copy-start.1 = (bf16[16,64,32,32]{1,2,3,0:T(8,128)(2,1)S(1)}, bf16[16,64,32,32]{1,2,3,0:T(8,128)(2,1)}, u32[]{:S(2)}) copy-start(bf16[16,64,32,32]{1,2,3,0:T(8,128)(2,1)} %get-tuple-element.289) | copy-start | bytes 6291460 | tf_op jit(solution)/shard_map/while
  187.1 6.9 %copy-start.7 = (bf16[4,16,16,32]{3,2,1,0:T(8,128)(2,1)S(1)}, bf16[4,16,16,32]{3,2,1,0:T(8,128)(2,1)}, u32[]{:S(2)}) copy-start(bf16[4,16,16,32]{3,2,1,0:T(8,128)(2,1)} %get-tuple-element.308) | copy-start | bytes 196612 | tf_op jit(solution)/shard_map/while
  190.3 3.7 copy-start.2
  190.3 3.7 copy-start.10
  197.0 0.7 copy-start.8
  197.7 3.2 copy-start.9
  209.0 7.7 %copy-start.17 = (bf16[1024,128]{1,0:T(8,128)(2,1)S(1)}, bf16[1024,128]{1,0:T(8,128)(2,1)}, u32[]{:S(2)}) copy-start(bf16[1024,128]{1,0:T(8,128)(2,1)} %get-tuple-element.324) | copy-start | bytes 786436 | tf_op jit(solution)/shard_map/while
  209.0 7.7 %copy-start.18 = (f32[128]{0:T(128)S(1)}, f32[128]{0:T(128)}, u32[]{:S(2)}) copy-start(f32[128]{0:T(128)} %get-tuple-element.327) | copy-start | bytes 1540 | tf_op jit(solution)/shard_map/while
  216.7 4.8 %copy-start.1 = (bf16[16,64,32,32]{1,2,3,0:T(8,128)(2,1)S(1)}, bf16[16,64,32,32]{1,2,3,0:T(8,128)(2,1)}, u32[]{:S(2)}) copy-start(bf16[16,64,32,32]{1,2,3,0:T(8,128)(2,1)} %get-tuple-element.289) | copy-start | bytes 6291460 | tf_op jit(solution)/shard_map/while
  234.1 6.9 %copy-start.7 = (bf16[4,16,16,32]{3,2,1,0:T(8,128)(2,1)S(1)}, bf16[4,16,16,32]{3,2,1,0:T(8,128)(2,1)}, u32[]{:S(2)}) copy-start(bf16[4,16,16,32]{3,2,1,0:T(8,128)(2,1)} %get-tuple-element.308) | copy-start | bytes 196612 | tf_op jit(solution)/shard_map/while
  237.3 3.7 copy-start.2
  237.3 3.7 copy-start.10
  244.0 0.7 copy-start.8
  244.7 36.2 %copy-start.3 = (f32[1024,128]{1,0:T(8,128)}, f32[1024,128]{1,0:T(8,128)S(1)}, u32[]{:S(2)}) copy-start(f32[1024,128]{1,0:T(8,128)S(1)} %get-tuple-element.68) | copy-start | bytes 1572868
  244.7 92.2 %copy-start.16 = (f32[16,16]{1,0:T(8,128)S(1)}, f32[16,16]{1,0:T(8,128)}, u32[]{:S(2)}) copy-start(f32[16,16]{1,0:T(8,128)} %copy-done.15) | copy-start | bytes 3076
  244.7 92.2 %copy-start.12 = (f32[16,16]{1,0:T(8,128)S(1)}, f32[16,16]{1,0:T(8,128)}, u32[]{:S(2)}) copy-start(f32[16,16]{1,0:T(8,128)} %copy-done.11) | copy-start | bytes 3076
  245.5 67.1 %all-reduce.7.cloned.1.call-start = ((), (), s32[]{:S(2)}) async-start(), calls=%async_computation.3 | async-start | bytes 262144 | tf_op jit(solution)/shard_map/psum | solution.py:9
  280.1 55.0 %reduce-scatter.2.cloned.1.call-start = ((), (), s32[]{:S(2)}) async-start(), calls=%async_computation.1 | async-start | bytes 327680 | tf_op jit(solution)/shard_map/reduce_scatter | solution.py:97
  280.9 148.6 %all-reduce.9.cloned.1.call-start = ((), (), s32[]{:S(2)}) async-start(), calls=%async_computation.4 | async-start | bytes 1048576 | tf_op jit(solution)/shard_map/psum | solution.py:115
Sparse Core Ops, SparseCore 0:
  245.6 32.8 all-reduce.4
  281.5 31.0 all-reduce.6
  315.0 20.0 reduce-scatter.1
  339.3 90.1 all-reduce.8
where the time goes:
time: 439 us; the launch traced here: 438 us
  local copies, waits for them, and re-layouts  131 us (30%)
  waiting for transfers between devices  115 us (26%)
  blocking collectives  105 us (24%)
  matrix products  64.3 us (15%)
  between operations  14 us (3%)
  other arithmetic  8.18 us (2%)
    psum x1, blocking collectives, per_device(): lax.psum((d_wab_part, d_wout_part, d_bias_part), ('row', 'col'))  61 us
    convert_element_type x8, local copies, waits for them, and re-layouts, one_block(): outer = (outer / (count_part + 0.001)[:, :, None]).astype(jnp.bfloat16)  40.4 us
    psum x1, waiting for transfers between devices, per_device(): lax.psum(d_right.astype(jnp.bfloat16), 'row').astype(jnp.float32)  33 us
    transpose x4, local copies, waits for them, and re-layouts, one_block(): jnp.einsum('isc,jse->ijce', left_part, right_cols, preferred_element_type...  32.3 us
    reshape x4, local copies, waits for them, and re-layouts, one_block(): outer = outer.reshape(inner, block, width * width)  30.6 us
    psum x1, waiting for transfers between devices, per_device(): lax.psum((d_wab_part, d_wout_part, d_bias_part), ('row', 'col'))  29.8 us
    psum x1, waiting for transfers between devices, spread_2(): return lax.psum(block, axis)  29.4 us
    all_gather x1, blocking collectives, per_device(): lax.all_gather(proj, ('row', 'col'), axis=0, tiled=True)  26.2 us
  transfers between devices with their start and end apart: 4, of which 4 were waited for; matrix products, arithmetic and copies ran while one was open for 1% of the time, Pallas kernels for 0%

commit v1 on v0

v1 whole, which is shorter than its diff:
```python
import functools

import jax
import jax.numpy as jnp
from jax import lax
from jax.experimental import pallas as pl
from jax.experimental.pallas import tpu as pltpu
from jax.sharding import PartitionSpec as P

F32 = jnp.float32
BF16 = jnp.bfloat16
LANES = 128
VMEM_LIMIT = 40 * 1024 * 1024
NT = (((1,), (1,)), ((), ()))


def dot(left, right):
    return jnp.dot(left, right, preferred_element_type=F32)


def dot_nt(left, right):
    return lax.dot_general(left, right, NT, preferred_element_type=F32)


def iota(shape, axis):
    return lax.broadcasted_iota(jnp.int32, shape, axis)


def one_hot(mask):
    return jnp.where(mask, 1.0, 0.0).astype(BF16)


def full(shape):
    return pl.BlockSpec(shape, lambda *g: (0,) * len(shape))


def cost(flops, nbytes):
    return pl.CostEstimate(flops=int(flops), bytes_accessed=int(nbytes), transcendentals=0)


def call(kernel, grid, in_specs, out_specs, out_shape, scratch=(), estimate=None):
    return pl.pallas_call(
        kernel,
        grid=grid,
        in_specs=in_specs,
        out_specs=out_specs,
        out_shape=out_shape,
        scratch_shapes=list(scratch),
        compiler_params=pltpu.CompilerParams(vmem_limit_bytes=VMEM_LIMIT),
        cost_estimate=estimate,
    )


def stats(x):
    center = x - jnp.mean(x, axis=-1, keepdims=True)
    scale = lax.rsqrt(jnp.mean(center * center, axis=-1, keepdims=True) + 1e-05)
    return center * scale, scale


def prep_kernel(depth, own, x_ref, cell_ref, line_ref, by_token_ref, by_row_ref):
    rows = depth * own
    normed, _ = stats(x_ref[...].astype(F32))
    features = normed.shape[1]
    cell = cell_ref[...].astype(F32).astype(BF16)
    pick = one_hot(iota((rows, depth), 0) // own == iota((rows, depth), 1))
    line = line_ref[...].astype(F32)
    line_column = jnp.sum(pick.astype(F32) * line, axis=1, keepdims=True)
    cells = dot(pick, cell)
    here = iota((rows, own), 0) % own == iota((rows, own), 1)
    weight = jnp.sum(jnp.where(here, cells, 0.0), axis=1, keepdims=True) * line_column
    masked = normed.astype(BF16).astype(F32) * weight
    wide = jnp.concatenate([masked, jnp.zeros((rows, LANES - features), F32)], axis=1)
    lane = iota((rows, LANES), 1)
    at = lane == features + iota((rows, LANES), 0) // own
    wide = (wide + jnp.where(at, weight, 0.0)).astype(BF16)
    by_row_ref[...] = wide
    p, q = iota((rows, rows), 0), iota((rows, rows), 1)
    swap = one_hot(q == (p % depth) * own + p // depth)
    by_token_ref[...] = dot(swap, wide).astype(BF16)


def scaled_pair(up_ref, inv, at):
    parts = [up_ref[i].astype(F32) * inv[:, i : i + 1] for i in (at, at + 1)]
    return jnp.concatenate(parts, axis=1).astype(BF16)


def fill_v(up_ref, inv, bt, v_ref, depth):
    chunk, _, pair = up_ref.shape
    width = v_ref.shape[0]
    for at in range(0, chunk, 2):
        v = dot(bt, scaled_pair(up_ref, inv, at)).astype(BF16)
        for k in range(2):
            part = v[:, k * pair : (k + 1) * pair].reshape(width, depth, pair)
            v_ref[:, (at + k) * depth : (at + k + 1) * depth, :] = part


def fill_t(a_chunk, wc_ref, t_ref, depth):
    chunk, rows, pair = t_ref.shape
    width = rows // depth
    for e in range(0, width, 2):
        t = dot(a_chunk, wc_ref[:, e * pair : (e + 2) * pair]).astype(BF16)
        for k in range(2):
            part = t[:, k * pair : (k + 1) * pair].reshape(chunk, depth, pair)
            t_ref[:, (e + k) * depth : (e + k + 1) * depth, :] = part


def two(ref, at):
    return jnp.concatenate([ref[at], ref[at + 1]], axis=1)


def weight_kernel(depth, n, pieces, *refs):
    a_refs, b_refs = refs[:pieces], refs[pieces : 2 * pieces]
    up_ref, w_ref, wt_ref, perm_ref = refs[2 * pieces : 2 * pieces + 4]
    outs = refs[2 * pieces + 4 :]
    mi_ref, mj_ref, a_ref, b_ref, bt_ref, inv_ref, bias_ref = outs[:7]
    send_refs = outs[7 : 7 + n]
    at_ref, v_ref, acc_ref = outs[7 + n :]
    g, last = pl.program_id(0), pl.num_programs(0) - 1
    chunk, block, pair = up_ref.shape
    features = w_ref.shape[0]
    width = w_ref.shape[1] // 2
    r, c = lax.axis_index("row"), lax.axis_index("col")

    @pl.when(g == 0)
    def _():
        if pieces == 1:
            mi_ref[...] = a_refs[0][...]
            mj_ref[...] = b_refs[0][...]
        else:
            own = block // pieces
            for k in range(pieces):
                src = lax.rem(c - k + n, n)
                rows = pl.ds(pl.multiple_of(src * own * depth, own * depth), own * depth)
                mi_ref[rows, :] = a_refs[k][...]
                src = lax.rem(r - k + n, n)
                rows = pl.ds(pl.multiple_of(src * own, own), own)
                for s in range(depth):
                    mj_ref[s, rows, :] = b_refs[k][s * own : (s + 1) * own, :]
        pad = jnp.zeros((LANES - features, 2 * width), BF16)
        w = jnp.concatenate([w_ref[...], pad], axis=0)
        pad = jnp.zeros((2 * width, LANES - features), BF16)
        wt = jnp.concatenate([wt_ref[...], pad], axis=1)
        mi = mi_ref[...]
        a_ref[...] = dot(mi, w[:, :width]).astype(BF16)
        at_ref[...] = dot_nt(wt[:width, :], mi).astype(BF16)
        b = jnp.zeros((block, width * depth), F32)
        seen = jnp.zeros((block, LANES), F32)
        for s in range(depth):
            mj = mj_ref[s]
            seen = seen + mj.astype(F32)
            part = dot(mj, w[:, width:]).astype(BF16)
            b = b + dot(part, perm_ref[s * width : (s + 1) * width, :])
        b_ref[...] = b.astype(BF16)
        bt_ref[...] = b.T.astype(BF16)
        keep = iota((block, LANES), 1) >= features
        seen_j = jnp.where(keep, seen, 0.0).astype(BF16)
        rows = block * depth
        gather = one_hot(iota((block, rows), 0) == iota((block, rows), 1) // depth)
        seen_i = dot(gather, mi).astype(BF16)
        for k in range(block // chunk):
            count = dot_nt(seen_j, seen_i[k * chunk : (k + 1) * chunk, :])
            inv_ref[k] = 1.0 / (count + 0.001)
        acc_ref[...] = jnp.zeros_like(acc_ref)
        bias_ref[...] = jnp.zeros_like(bias_ref)

    bias_ref[0:1, :] += jnp.sum(
        jnp.sum(up_ref[...].astype(F32), axis=0), axis=0, keepdims=True
    )
    fill_v(up_ref, inv_ref[g], bt_ref[...], v_ref, depth)
    span = chunk * depth
    a_t = at_ref[:, pl.ds(pl.multiple_of(g * span, span), span)]
    for e in range(0, width, 2):
        part = dot(a_t, two(v_ref, e))
        for k in range(2):
            acc_ref[(e + k) * width : (e + k + 1) * width, :] += part[:, k * pair : (k + 1) * pair]

    @pl.when(g == last)
    def _():
        rows = acc_ref.shape[0] // n
        for k in range(n):
            at = pl.multiple_of(lax.rem(c + k, n) * rows, rows)
            send_refs[k][...] = acc_ref[pl.ds(at, rows), :].astype(BF16)


def token_kernel(depth, n, split, *refs):
    up_ref, inv_ref, a_ref, bt_ref, wc_ref, mi_ref, mj_ref, perm_ref, bias_ref = refs[:9]
    outs = refs[9:]
    small_ref = outs[0]
    count = n if split else 1
    da_refs, db_refs = outs[1 : 1 + count], outs[1 + count : 1 + 2 * count]
    v_ref, t_ref, da_ref, db_ref = outs[1 + 2 * count :]
    g, last = pl.program_id(0), pl.num_programs(0) - 1
    chunk, block, pair = up_ref.shape
    width = wc_ref.shape[0]
    span = chunk * depth
    r, c = lax.axis_index("row"), lax.axis_index("col")
    inv = inv_ref[g]

    @pl.when(g == 0)
    def _():
        db_ref[...] = jnp.zeros_like(db_ref)

    fill_v(up_ref, inv, bt_ref[...], v_ref, depth)
    d_a = jnp.zeros((width, span), F32)
    for e in range(0, width, 2):
        d_a = d_a + dot_nt(wc_ref[:, e * pair : (e + 2) * pair], two(v_ref, e))
    da_ref[:, pl.ds(pl.multiple_of(g * span, span), span)] = d_a.astype(BF16)
    a_chunk = a_ref[pl.ds(pl.multiple_of(g * span, span), span), :]
    fill_t(a_chunk, wc_ref, t_ref, depth)
    d_b = db_ref[...]
    for at in range(0, chunk, 2):
        d_b = d_b + dot_nt(scaled_pair(up_ref, inv, at), two(t_ref, at))
    db_ref[...] = d_b

    @pl.when(g == last)
    def _():
        d_b = db_ref[...].astype(BF16)
        turned = dot_nt(perm_ref[...], d_b).astype(BF16)
        left = dot(da_ref[...], mi_ref[...])
        right = jnp.zeros((width, LANES), F32)
        for s in range(depth):
            right = right + dot(turned[s * width : (s + 1) * width, :], mj_ref[s])
        small_ref[0:width, :] = left
        small_ref[width : 2 * width, :] = right
        small_ref[2 * width :, :] = jnp.zeros_like(small_ref[2 * width :, :])
        small_ref[2 * width : 2 * width + 1, :] = bias_ref[0:1, :]
        if split:
            own = block // n
            for k in range(n):
                lanes = own * depth
                at = pl.multiple_of(lax.rem(c + k, n) * lanes, lanes)
                da_refs[k][...] = da_ref[:, pl.ds(at, lanes)]
                at = pl.multiple_of(lax.rem(r + k, n) * own, own)
                db_refs[k][...] = db_ref[pl.ds(at, own), :].astype(BF16)
        else:
            da_refs[0][...] = da_ref[...]
            db_refs[0][...] = d_b


def update_kernel(depth, inv_ref, a_ref, b_ref, wc_ref, offset_ref, out_ref, t_ref):
    g = pl.program_id(0)
    chunk, block, pair = out_ref.shape
    span = chunk * depth
    inv = inv_ref[g]
    fill_t(a_ref[pl.ds(pl.multiple_of(g * span, span), span), :], wc_ref, t_ref, depth)
    b = b_ref[...]
    offset = offset_ref[...]
    for at in range(0, chunk, 2):
        part = dot(b, two(t_ref, at))
        for k in range(2):
            value = part[:, k * pair : (k + 1) * pair] * inv[:, at + k : at + k + 1] + offset
            out_ref[at + k] = value.astype(BF16)


def sum_kernel(axis, n, *refs):
    ins, outs = refs[:n], refs[n:]
    me = lax.axis_index(axis)
    for k in range(n):
        at = lax.rem(me + k, n)
        total = ins[0][at].astype(F32)
        for ref in ins[1:]:
            total = total + ref[at].astype(F32)
        outs[k][...] = total.astype(BF16)


def owner_kernel(depth, own, n, *refs):
    da_refs, db_refs = refs[:n], refs[n : 2 * n]
    x_ref, message_ref, wt_ref, perm_ref, out_ref = refs[2 * n :]
    rows = depth * own
    width = wt_ref.shape[0] // 2
    features = x_ref.shape[1]
    p, q = iota((rows, rows), 0), iota((rows, rows), 1)
    swap = one_hot(q == (p % own) * depth + p // own)
    d_a = jnp.zeros((rows, width), F32)
    d_b = jnp.zeros((own, width * depth), F32)
    for k in range(n):
        d_a = d_a + dot_nt(swap, da_refs[k][...])
        d_b = d_b + dot_nt(db_refs[k][...], perm_ref[...])
    d_b = jnp.concatenate([d_b[:, s * width : (s + 1) * width] for s in range(depth)], axis=0)
    highest = lax.Precision.HIGHEST
    wt = wt_ref[...].astype(F32)
    d_normed = jnp.dot(d_a, wt[:width, :], precision=highest, preferred_element_type=F32)
    d_normed = d_normed + jnp.dot(d_b, wt[width:, :], precision=highest, preferred_element_type=F32)
    message = message_ref[...].astype(F32)
    mask = iota((rows, LANES), 1) >= features
    d_normed = d_normed * jnp.sum(jnp.where(mask, message, 0.0), axis=1, keepdims=True)
    normed, scale = stats(x_ref[...].astype(F32))
    mean = jnp.mean(d_normed, axis=-1, keepdims=True)
    along = jnp.mean(d_normed * normed, axis=-1, keepdims=True)
    out_ref[...] = scale * (d_normed - mean - normed * along)


def place_kernel(n, *refs):
    ins, out_ref, full_ref = refs[:n], refs[n], refs[n + 1]
    r, c = lax.axis_index("row"), lax.axis_index("col")
    width = out_ref.shape[0]
    each = width // (n * n)
    for k in range(n):
        col = lax.rem(c - k + n, n)
        for m in range(n):
            row = lax.rem(r - m + n, n)
            value = ins[k][m].astype(F32).reshape(each, width, LANES)
            full_ref[pl.ds((col * n + row) * each, each)] = value
    for e in range(width):
        out_ref[:, e, :] = full_ref[e]


def per_device(
    n,
    alignment_embedding,
    alignment_cell_exists,
    alignment_lines_exist,
    sitewise_factors,
    pairing_matrix,
    offset_vector,
    upstream_adjoint,
):
    depth, own, features = alignment_embedding.shape
    width = sitewise_factors.shape[1] // 2
    block, pair = upstream_adjoint.shape[0], upstream_adjoint.shape[2]
    rows, chunk = depth * own, 16
    steps = block // chunk
    split = own % 16 == 0
    axes = ("row", "col")
    sds = jax.ShapeDtypeStruct

    def along_col(x, k):
        return lax.ppermute(x, "col", [(i, (i + k) % n) for i in range(n)])

    def along_row(x, k):
        return lax.ppermute(x, "row", [(i, (i + k) % n) for i in range(n)])

    def to_column(x, k):
        pairs = [(i * n + j, (j + k) % n * n + i) for i in range(n) for j in range(n)]
        return lax.ppermute(x, axes, pairs)

    def to_owner(x, k):
        pairs = [(i * n + j, j * n + (i + k) % n) for i in range(n) for j in range(n)]
        return lax.ppermute(x, axes, pairs)

    r, c = lax.axis_index("row"), lax.axis_index("col")

    def cut(x, axis, at):
        size = x.shape[axis] // n
        return lax.dynamic_slice_in_dim(x, at % n * size, size, axis)

    x = alignment_embedding.reshape(rows, features)
    by_token, by_row = call(
        functools.partial(prep_kernel, depth, own),
        (),
        [full(x.shape), full(alignment_cell_exists.shape), full((1, depth))],
        [full((rows, LANES))] * 2,
        [sds((rows, LANES), BF16)] * 2,
    )(x, alignment_cell_exists, alignment_lines_exist.reshape(1, depth))
    a_pieces = [by_token] + [along_col(by_token, k) for k in range(1, n)]
    b_pieces = [to_column(by_row, k) for k in range(n)]
    if not split:
        order = (c - jnp.arange(n)) % n
        held = jnp.zeros((n, rows, LANES), BF16).at[order].set(jnp.stack(a_pieces))
        a_pieces = [held.reshape(block * depth, LANES)]
        order = (r - jnp.arange(n)) % n
        held = jnp.zeros((n, depth, own, LANES), BF16)
        held = held.at[order].set(jnp.stack(b_pieces).reshape(n, depth, own, LANES))
        b_pieces = [held.transpose(1, 0, 2, 3).reshape(depth, block, LANES)]
    pieces = len(a_pieces)

    wide = width * depth
    source = jnp.arange(wide)
    perm = (jnp.arange(wide)[None, :] == (source % width * depth + source // width)[:, None]).astype(BF16)
    factors_t = sitewise_factors.T
    pairing_wide = pairing_matrix.reshape(width, width * pair)
    up_spec = pl.BlockSpec((chunk, block, pair), lambda g: (g, 0, 0))
    tokens = block * depth
    out_shapes = [
        sds((tokens, LANES), BF16),
        sds((depth, block, LANES), BF16),
        sds((tokens, width), BF16),
        sds((block, wide), BF16),
        sds((wide, block), BF16),
        sds((steps, block, chunk), F32),
        sds((8, pair), F32),
    ] + [sds((width * width // n, pair), BF16)] * n
    outs = call(
        functools.partial(weight_kernel, depth, n, pieces),
        (steps,),
        [full(p.shape) for p in a_pieces]
        + [full(p.shape) for p in b_pieces]
        + [up_spec, full(sitewise_factors.shape), full(factors_t.shape), full(perm.shape)],
        [full(o.shape) for o in out_shapes],
        out_shapes,
        [
            pltpu.VMEM((width, tokens), BF16),
            pltpu.VMEM((width, chunk * depth, pair), BF16),
            pltpu.VMEM((width * width, pair), F32),
        ],
        cost(5e9, 8e6),
    )(*a_pieces, *b_pieces, upstream_adjoint, sitewise_factors, factors_t, perm)
    mi, mj, a, b, b_t, inv, bias = outs[:7]
    sends = list(outs[7:])

    shard = width * width // (n * n)
    parts = [sends[0]] + [along_col(sends[k], k) for k in range(1, n)]
    parts = [part.reshape(n, shard, pair) for part in parts]

    count = n if split else 1
    piece = block // count
    out_shapes = (
        [sds((2 * width + 16, LANES), F32)]
        + [sds((width, piece * depth), BF16)] * count
        + [sds((piece, wide), BF16)] * count
    )
    outs = call(
        functools.partial(token_kernel, depth, n, split),
        (steps,),
        [up_spec]
        + [full(v.shape) for v in (inv, a, b_t, pairing_wide, mi, mj, perm, bias)],
        [full(o.shape) for o in out_shapes],
        out_shapes,
        [
            pltpu.VMEM((width, chunk * depth, pair), BF16),
            pltpu.VMEM((chunk, wide, pair), BF16),
            pltpu.VMEM((width, tokens), BF16),
            pltpu.VMEM((block, wide), F32),
        ],
        cost(8e9, 8e6),
    )(upstream_adjoint, inv, a, b_t, pairing_wide, mi, mj, perm, bias)
    small = outs[0]
    d_a, d_b = list(outs[1 : 1 + count]), list(outs[1 + count :])
    if not split:
        d_a = [cut(d_a[0], 1, c + k) for k in range(n)]
        d_b = [cut(d_b[0], 0, r + k) for k in range(n)]
    d_a = [d_a[0]] + [along_col(d_a[k], k) for k in range(1, n)]
    d_b = [to_owner(d_b[k], k) for k in range(n)]
    small = small + sum(along_col(small, k) for k in range(1, n))
    small = small + sum(along_row(small, k) for k in range(1, n))

    shards = call(
        functools.partial(sum_kernel, "row", n),
        (),
        [full(part.shape) for part in parts],
        [full((shard, pair))] * n,
        [sds((shard, pair), BF16)] * n,
    )(*parts)
    mine = [shards[0].astype(F32)] + [along_row(shards[k], k).astype(F32) for k in range(1, n)]
    mine = sum(mine).astype(BF16)
    gathered = jnp.stack([mine] + [along_row(mine, k) for k in range(1, n)])
    gathered = [gathered] + [along_col(gathered, k) for k in range(1, n)]

    coupling_update = call(
        functools.partial(update_kernel, depth),
        (steps,),
        [full(v.shape) for v in (inv, a, b, pairing_wide)] + [full((1, pair))],
        up_spec,
        sds((block, block, pair), BF16),
        [pltpu.VMEM((chunk, wide, pair), BF16)],
        cost(5e9, 8e6),
    )(inv, a, b, pairing_wide, offset_vector.reshape(1, pair))

    embedding_adjoint = call(
        functools.partial(owner_kernel, depth, own, n),
        (),
        [full(v.shape) for v in d_a + d_b]
        + [full(v.shape) for v in (x, by_row, factors_t, perm)],
        full((rows, features)),
        sds((rows, features), F32),
    )(*d_a, *d_b, x, by_row, factors_t, perm)

    if width % (n * n) == 0:
        placed = call(
            functools.partial(place_kernel, n),
            (),
            [full(part.shape) for part in gathered],
            full((width, width, pair)),
            sds((width, width, pair), F32),
            [pltpu.VMEM((width, width, pair), F32)],
        )(*gathered)
    else:
        held = jnp.stack(gathered)
        held = held[(c - jnp.arange(n)) % n][:, (r - jnp.arange(n)) % n]
        placed = held.astype(F32).reshape(width, width, pair).transpose(1, 0, 2)
    factors = jnp.concatenate([small[:width], small[width : 2 * width]], axis=0)
    return (
        coupling_update,
        embedding_adjoint.reshape(depth, own, features),
        factors[:, :features].T,
        placed.reshape(width * width, pair),
        small[2 * width],
    )


def solution(mesh):
    n = mesh.shape["col"]
    placed = (
        P(None, ("groups", "row", "col"), None),
        P(None, ("groups", "row", "col")),
        P("groups"),
        P(),
        P(),
        P(),
        P(("groups", "row"), "col", None),
    )
    return jax.shard_map(
        functools.partial(per_device, n),
        mesh=mesh,
        in_specs=placed,
        out_specs=(
            P(("groups", "row"), "col", None),
            P(None, ("groups", "row", "col"), None),
            P("groups", None),
            P("groups", None),
            P("groups"),
        ),
        check_vma=False,
    )
```

time: 439 us -> 83.8 us (0.19)
  local copies, waits for them, and re-layouts: 131 us -> 5.23 us
  waiting for transfers between devices: 115 us -> 6.83 us
  blocking collectives: 105 us -> 0 us
  matrix products: 64.3 us -> 0 us
  starting transfers between devices: 0.16 us -> 44.1 us
  Pallas kernels: 0 us -> 26.3 us
  between operations: 14 us -> 0.81 us
  other arithmetic: 8.18 us -> 0.21 us
    psum x3 -> x0, waiting for transfers between devices: 92.1 us -> none  [the longest x1 33 us: per_device(): lax.psum(d_right.astype(jnp.bfloat16), 'row').astype(jnp.float32)]
    dot_general x28 -> x0, matrix products: 64.3 us -> none  [the longest x4 14.9 us: one_block(): jnp.einsum('ijce,isc->jse', d_outer, left_part, preferred_element_type=jn...]
    psum x1 -> x0, blocking collectives: 61 us -> none  [per_device(): lax.psum((d_wab_part, d_wout_part, d_bias_part), ('row', 'col'))]
    convert_element_type x13 -> x0, local copies, waits for them, and re-layouts: 53.3 us -> none  [the longest x8 40.4 us: one_block(): outer = (outer / (count_part + 0.001)[:, :, None]).astype(jnp.bfloat16)]
    ppermute x0 -> x32, starting transfers between devices: none -> 44.1 us  [the longest x9 12.7 us: along_row(): return lax.ppermute(x, 'row', [(i, (i + k) % n) for i in range(n)])]
    all_gather x2 -> x0, blocking collectives: 43.8 us -> none  [the longest x1 26.2 us: per_device(): lax.all_gather(proj, ('row', 'col'), axis=0, tiled=True)]
    transpose x5 -> x1, local copies, waits for them, and re-layouts: 32.4 us -> 0.01 us  [per_device(): factors[:, :features]]
    reshape x4 -> x1, local copies, waits for them, and re-layouts: 30.6 us -> 1.08 us  [per_device(): pairing_wide = pairing_matrix.reshape(width, width * pair)]
  transfers between devices with their start and end apart: 4 -> 32, of which waited for: 4 -> 8; matrix products, arithmetic and copies ran while one was open for 1% -> 3% of each run, Pallas kernels for 0% -> 21%
where the time goes in v1:
time: 83.8 us; the launch traced here: 83.4 us
  starting transfers between devices  44.1 us (53%)
  Pallas kernels  26.3 us (31%)
  waiting for transfers between devices  6.83 us (8%)
  local copies, waits for them, and re-layouts  5.23 us (6%)
    ppermute x9, starting transfers between devices, along_row(): return lax.ppermute(x, 'row', [(i, (i + k) % n) for i in range(n)])  12.7 us
    ppermute x15, starting transfers between devices, along_col(): return lax.ppermute(x, 'col', [(i, (i + k) % n) for i in range(n)])  12.2 us
    ppermute x4, starting transfers between devices, to_column(): return lax.ppermute(x, axes, pairs)  11 us
    pallas_call x1, Pallas kernels, per_device(): call(functools.partial(token_kernel, depth, n, split), (steps,), [up_spec...  10.3 us
    ppermute x4, starting transfers between devices, to_owner(): return lax.ppermute(x, axes, pairs)  8.07 us
    pallas_call x1, Pallas kernels, per_device(): call(functools.partial(weight_kernel, depth, n, pieces), (steps,), [full(...  7.07 us
    pallas_call x1, Pallas kernels, per_device(): call(functools.partial(update_kernel, depth), (steps,), [full(v.shape) fo...  4.87 us
    unnamed x16, local copies, waits for them, and re-layouts  3.64 us
  transfers between devices with their start and end apart: 32, of which 8 were waited for; matrix products, arithmetic and copies ran while one was open for 3% of the time, Pallas kernels for 21%

profile of v1, /device:TPU:0, one launch (start us, length us, event | category | flops | bytes accessed | tf_op | source)
XLA Modules:
  0.0 83.4 jit_solution(13454502344522824712)
XLA Ops:
  0.6 0.6 copy-done.4
  1.3 0.8 %copy-done = bf16[16,16,64]{2,1,0:T(8,128)(2,1)S(1)} copy-done((bf16[16,16,64]{2,1,0:T(8,128)(2,1)S(1)}, bf16[16,16,64]{2,1,0:T(8,128)(2,1)}, u32[]{:S(2)}) %copy-start) | copy-done | bytes 32792
  2.1 0.7 copy-done.3
  2.8 0.4 shard_map.110
  3.3 0.7 collective-permute-start.3
  3.9 4.3 %collective-permute-start.4 = (bf16[256,128]{1,0:T(8,128)(2,1)S(1)}, bf16[256,128]{1,0:T(8,128)(2,1)S(1)}, u32[]{:S(2)}, u32[]{:S(2)}) collective-permute-start(bf16[256,128]{1,0:T(8,128)(2,1)S(1)} %get-tuple-element.32.refs_9_), channel_id=1, source_target_pairs={{0,4},{1,8},{2,12},{3,0},{4,5},{5,9},{6,13},{7,1},{8,6},{9,10},{10... | collective-permute-start | bytes 196616 | tf_op jit(solution)/shard_map/ppermute | solution.py:335
  8.3 3.4 %collective-permute-start.5 = (bf16[256,128]{1,0:T(8,128)(2,1)S(1)}, bf16[256,128]{1,0:T(8,128)(2,1)S(1)}, u32[]{:S(2)}, u32[]{:S(2)}) collective-permute-start(bf16[256,128]{1,0:T(8,128)(2,1)S(1)} %get-tuple-element.32.refs_9_), channel_id=1, source_target_pairs={{0,8},{1,12},{2,0},{3,4},{4,9},{5,13},{6,1},{7,5},{8,10},{9,14},{1... | collective-permute-start | bytes 196616 | tf_op jit(solution)/shard_map/ppermute | solution.py:335
  11.6 2.6 %collective-permute-start.6 = (bf16[256,128]{1,0:T(8,128)(2,1)S(1)}, bf16[256,128]{1,0:T(8,128)(2,1)S(1)}, u32[]{:S(2)}, u32[]{:S(2)}) collective-permute-start(bf16[256,128]{1,0:T(8,128)(2,1)S(1)} %get-tuple-element.32.refs_9_), channel_id=1, source_target_pairs={{0,12},{1,0},{2,4},{3,8},{4,13},{5,1},{6,5},{7,9},{8,14},{9,2},{10... | collective-permute-start | bytes 196616 | tf_op jit(solution)/shard_map/ppermute | solution.py:335
  14.3 1.5 %collective-permute-start.1 = (bf16[256,128]{1,0:T(8,128)(2,1)S(1)}, bf16[256,128]{1,0:T(8,128)(2,1)S(1)}, u32[]{:S(2)}, u32[]{:S(2)}) collective-permute-start(bf16[256,128]{1,0:T(8,128)(2,1)S(1)} %get-tuple-element.31.refs_0_), channel_id=1, source_target_pairs={{0,2},{1,3},{2,0},{3,1},{4,6},{5,7},{6,4},{7,5},{8,10},{9,11},{10,... | collective-permute-start | bytes 196616 | tf_op jit(solution)/shard_map/ppermute | solution.py:328
  15.8 0.7 collective-permute-start.2
  16.5 0.1 fusion.refs_11_.refs_7_
  16.8 1.1 %reshape.64.wc_ref.refs_4_ = bf16[32,4096]{1,0:T(8,128)(2,1)S(1)} reshape(bf16[1024,128]{1,0:T(8,128)(2,1)} %param.11) | data formatting | bytes 524288 | tf_op jit(solution)/shard_map/reshape | solution.py:371
  17.9 0.2 collective-permute-done.refs_1_
  18.1 1.2 %collective-permute-done.1.refs_2_ = bf16[256,128]{1,0:T(8,128)(2,1)S(1)} collective-permute-done((bf16[256,128]{1,0:T(8,128)(2,1)S(1)}, bf16[256,128]{1,0:T(8,128)(2,1)S(1)}, u32[]{:S(2)}, u32[]{:S(2)}) %collective-permute-start.1) | collective-permute-done | bytes 65568 | tf_op jit(solution)/shard_map/ppermute | solution.py:328
  19.3 7.1 %shard_map.111 = (bf16[1024,128]{1,0:T(8,128)(2,1)S(1)}, bf16[16,64,128]{2,1,0:T(8,128)(2,1)S(1)}, bf16[1024,32]{1,0:T(8,128)(2,1)S(1)}, bf16[64,512]{1,0:T(8,12...) custom-call(bf16[256,128]{1,0:T(8,128)(2,1)S(1)} %get-tuple-element., ...), custom_call_target="tpu_custom_call" | custom-call | flops 5000000000 | bytes 8000000 | tf_op jit(solution)/shard_map/pallas_call | solution.py:383
  26.4 0.7 collective-permute-start.20
  27.0 10.3 %shard_map.113 = (f32[80,128]{1,0:T(8,128)S(1)}, bf16[32,256]{1,0:T(8,128)(2,1)S(1)}, bf16[32,256]{1,0:T(8,128)(2,1)S(1)}, bf16[32,256]{1,0:T(8,128)(2,1)S(1)}, ...) custom-call(bf16[64,64,128]{2,1,0:T(8,128)(2,1)S(1)} %copy-done.5, ...), custom_call_target="tpu_custom_call" | custom-call | flops 8000000000 | bytes 8000000 | tf_op jit(solution)/shard_map/pallas_call | solution.py:412
  37.4 0.7 collective-permute-start.10
  38.0 2.4 %collective-permute-start.11 = (bf16[16,512]{1,0:T(8,128)(2,1)S(1)}, bf16[16,512]{1,0:T(8,128)(2,1)S(1)}, u32[]{:S(2)}, u32[]{:S(2)}) collective-permute-start(bf16[16,512]{1,0:T(8,128)(2,1)S(1)} %get-tuple-element.45), channel_id=1, source_target_pairs={{0,1},{1,5},{2,9},{3,13},{4,2},{5,6},{6,10},{7,14},{8,3},{9,7},{10... | collective-permute-start | bytes 49160 | tf_op jit(solution)/shard_map/ppermute | solution.py:339
  40.5 2.5 %collective-permute-start.12 = (bf16[16,512]{1,0:T(8,128)(2,1)S(1)}, bf16[16,512]{1,0:T(8,128)(2,1)S(1)}, u32[]{:S(2)}, u32[]{:S(2)}) collective-permute-start(bf16[16,512]{1,0:T(8,128)(2,1)S(1)} %get-tuple-element.46), channel_id=1, source_target_pairs={{0,2},{1,6},{2,10},{3,14},{4,3},{5,7},{6,11},{7,15},{8,0},{9,4},{1... | collective-permute-start | bytes 49160 | tf_op jit(solution)/shard_map/ppermute | solution.py:339
  43.0 2.5 %collective-permute-start.13 = (bf16[16,512]{1,0:T(8,128)(2,1)S(1)}, bf16[16,512]{1,0:T(8,128)(2,1)S(1)}, u32[]{:S(2)}, u32[]{:S(2)}) collective-permute-start(bf16[16,512]{1,0:T(8,128)(2,1)S(1)} %get-tuple-element.47), channel_id=1, source_target_pairs={{0,3},{1,7},{2,11},{3,15},{4,0},{5,4},{6,8},{7,12},{8,1},{9,5},{10... | collective-permute-start | bytes 49160 | tf_op jit(solution)/shard_map/ppermute | solution.py:339
  45.4 0.2 collective-permute-done.11.refs_5_
  45.7 1.4 %collective-permute-start.8 = (bf16[32,256]{1,0:T(8,128)(2,1)S(1)}, bf16[32,256]{1,0:T(8,128)(2,1)S(1)}, u32[]{:S(2)}, u32[]{:S(2)}) collective-permute-start(bf16[32,256]{1,0:T(8,128)(2,1)S(1)} %get-tuple-element.42), channel_id=1, source_target_pairs={{0,2},{1,3},{2,0},{3,1},{4,6},{5,7},{6,4},{7,5},{8,10},{9,11},{10,... | collective-permute-start | bytes 49160 | tf_op jit(solution)/shard_map/ppermute | solution.py:328
  47.1 0.9 %collective-permute-done.12.refs_6_ = bf16[16,512]{1,0:T(8,128)(2,1)S(1)} collective-permute-done((bf16[16,512]{1,0:T(8,128)(2,1)S(1)}, bf16[16,512]{1,0:T(8,128)(2,1)S(1)}, u32[]{:S(2)}, u32[]{:S(2)}) %collective-permute-start.12) | collective-permute-done | bytes 16416 | tf_op jit(solution)/shard_map/ppermute | solution.py:339
  48.0 1.0 %collective-permute-start.9 = (bf16[32,256]{1,0:T(8,128)(2,1)S(1)}, bf16[32,256]{1,0:T(8,128)(2,1)S(1)}, u32[]{:S(2)}, u32[]{:S(2)}) collective-permute-start(bf16[32,256]{1,0:T(8,128)(2,1)S(1)} %get-tuple-element.43), channel_id=1, source_target_pairs={{0,3},{1,0},{2,1},{3,2},{4,7},{5,4},{6,5},{7,6},{8,11},{9,8},{10,9... | collective-permute-start | bytes 49160 | tf_op jit(solution)/shard_map/ppermute | solution.py:328
  49.2 1.6 %collective-permute-start.15 = (f32[80,128]{1,0:T(8,128)S(1)}, f32[80,128]{1,0:T(8,128)S(1)}, u32[]{:S(2)}, u32[]{:S(2)}) collective-permute-start(f32[80,128]{1,0:T(8,128)S(1)} %get-tuple-element.48), channel_id=1, source_target_pairs={{0,2},{1,3},{2,0},{3,1},{4,6},{5,7},{6,4},{7,5},{8,10},{9,11},{10,... | collective-permute-start | bytes 122888 | tf_op jit(solution)/shard_map/ppermute | solution.py:328
  50.8 1.4 %collective-permute-start.16 = (f32[80,128]{1,0:T(8,128)S(1)}, f32[80,128]{1,0:T(8,128)S(1)}, u32[]{:S(2)}, u32[]{:S(2)}) collective-permute-start(f32[80,128]{1,0:T(8,128)S(1)} %get-tuple-element.48), channel_id=1, source_target_pairs={{0,3},{1,0},{2,1},{3,2},{4,7},{5,4},{6,5},{7,6},{8,11},{9,8},{10,9... | collective-permute-start | bytes 122888 | tf_op jit(solution)/shard_map/ppermute | solution.py:328
  52.2 0.3 collective-permute-start.21
  52.6 1.5 %collective-permute-start.22 = (bf16[256,128]{1,0:T(8,128)(2,1)S(1)}, bf16[256,128]{1,0:T(8,128)(2,1)S(1)}, u32[]{:S(2)}, u32[]{:S(2)}) collective-permute-start(bf16[256,128]{1,0:T(8,128)(2,1)S(1)} %get-tuple-element.52), channel_id=1, source_target_pairs={{0,3},{1,0},{2,1},{3,2},{4,7},{5,4},{6,5},{7,6},{8,11},{9,8},{10,9... | collective-permute-start | bytes 196616 | tf_op jit(solution)/shard_map/ppermute | solution.py:328
  54.1 0.7 copy-done.6
  54.8 4.9 %shard_map.112 = bf16[64,64,128]{2,1,0:T(8,128)(2,1)} custom-call(f32[4,64,16]{2,1,0:T(8,128)S(1)} %get-tuple-element.33.inv_ref.refs_1_, bf16[1024,32]{1,0:T(8,128)(2,1)S(1)} %get-tuple-element.34.a_ref.refs_2_, bf16[64,512]{1,0:T(8,128)(2,1)S(1)} %get-tuple-element.35.b_ref, bf16[32,4096]{1,0:T(8,128)(2,1)S(1)} %reshape.64.wc_ref.refs_4_, ...), custom_call_target="tpu_custom_call" | custom-call | flops 5000000000 | bytes 8000000 | tf_op jit(solution)/shard_map/pallas_call | solution.py:449
  59.6 2.2 %shard_map.114 = f32[256,64]{1,0:T(8,128)} custom-call(bf16[32,256]{1,0:T(8,128)(2,1)S(1)} %get-tuple-element.40.refs_0_, bf16[32,256]{1,0:T(8,128)(2,1)S(1)} %collective-permute-done.7.refs_1_, bf16[32,256]{1,0:T(8,128)(2,1)S(1)} %collective-permute-done.8.refs_2_, bf16[32,256]{1,0:T(8,128)(2,1)S(1)} %collective-permute-done.9.refs_3_, ...), custom_call_target="tpu_custom_call" | custom-call | tf_op jit(solution)/shard_map/pallas_call | solution.py:459
  62.0 1.2 %collective-permute-start.24 = (bf16[64,128]{1,0:T(8,128)(2,1)S(1)}, bf16[64,128]{1,0:T(8,128)(2,1)S(1)}, u32[]{:S(2)}, u32[]{:S(2)}) collective-permute-start(bf16[64,128]{1,0:T(8,128)(2,1)S(1)} %get-tuple-element.55), channel_id=1, source_target_pairs={{0,8},{4,12},{8,0},{12,4},{1,9},{5,13},{9,1},{13,5},{2,10},{6,14},... | collective-permute-start | bytes 49160 | tf_op jit(solution)/shard_map/ppermute | solution.py:331
  63.2 2.6 %collective-permute-start.25 = (bf16[64,128]{1,0:T(8,128)(2,1)S(1)}, bf16[64,128]{1,0:T(8,128)(2,1)S(1)}, u32[]{:S(2)}, u32[]{:S(2)}) collective-permute-start(bf16[64,128]{1,0:T(8,128)(2,1)S(1)} %get-tuple-element.56), channel_id=1, source_target_pairs={{0,12},{4,0},{8,4},{12,8},{1,13},{5,1},{9,5},{13,9},{2,14},{6,2},{... | collective-permute-start | bytes 49160 | tf_op jit(solution)/shard_map/ppermute | solution.py:331
  65.8 0.6 collective-permute-start.17
  66.5 1.5 %collective-permute-start.18 = (f32[80,128]{1,0:T(8,128)S(1)}, f32[80,128]{1,0:T(8,128)S(1)}, u32[]{:S(2)}, u32[]{:S(2)}) collective-permute-start(f32[80,128]{1,0:T(8,128)S(1)} %add_add_fusion.1), channel_id=1, source_target_pairs={{0,8},{4,12},{8,0},{12,4},{1,9},{5,13},{9,1},{13,5},{2,10},{6,14},... | collective-permute-start | bytes 122888 | tf_op jit(solution)/shard_map/ppermute | solution.py:331
  68.0 2.8 %collective-permute-start.19 = (f32[80,128]{1,0:T(8,128)S(1)}, f32[80,128]{1,0:T(8,128)S(1)}, u32[]{:S(2)}, u32[]{:S(2)}) collective-permute-start(f32[80,128]{1,0:T(8,128)S(1)} %add_add_fusion.1), channel_id=1, source_target_pairs={{0,12},{4,0},{8,4},{12,8},{1,13},{5,1},{9,5},{13,9},{2,14},{6,2},{... | collective-permute-start | bytes 122888 | tf_op jit(solution)/shard_map/ppermute | solution.py:331
  70.9 1.2 %collective-permute-start.27 = (bf16[64,128]{1,0:T(8,128)(2,1)S(1)}, bf16[64,128]{1,0:T(8,128)(2,1)S(1)}, u32[]{:S(2)}, u32[]{:S(2)}) collective-permute-start(bf16[64,128]{1,0:T(8,128)(2,1)S(1)} %add_convert_fusion), channel_id=1, source_target_pairs={{0,8},{4,12},{8,0},{12,4},{1,9},{5,13},{9,1},{13,5},{2,10},{6,14},... | collective-permute-start | bytes 49160 | tf_op jit(solution)/shard_map/ppermute | solution.py:331
  72.1 2.7 %collective-permute-start.28 = (bf16[64,128]{1,0:T(8,128)(2,1)S(1)}, bf16[64,128]{1,0:T(8,128)(2,1)S(1)}, u32[]{:S(2)}, u32[]{:S(2)}) collective-permute-start(bf16[64,128]{1,0:T(8,128)(2,1)S(1)} %add_convert_fusion), channel_id=1, source_target_pairs={{0,12},{4,0},{8,4},{12,8},{1,13},{5,1},{9,5},{13,9},{2,14},{6,2},{... | collective-permute-start | bytes 49160 | tf_op jit(solution)/shard_map/ppermute | solution.py:331
  74.8 1.7 %collective-permute-done.26 = bf16[64,128]{1,0:T(8,128)(2,1)S(1)} collective-permute-done((bf16[64,128]{1,0:T(8,128)(2,1)S(1)}, bf16[64,128]{1,0:T(8,128)(2,1)S(1)}, u32[]{:S(2)}, u32[]{:S(2)}) %collective-permute-start.26) | collective-permute-done | bytes 16416 | tf_op jit(solution)/shard_map/ppermute | solution.py:331
  76.5 0.6 collective-permute-done.28
  77.1 0.4 collective-permute-start.30
  77.5 1.4 %collective-permute-start.31 = (bf16[4,64,128]{2,1,0:T(8,128)(2,1)S(1)}, bf16[4,64,128]{2,1,0:T(8,128)(2,1)S(1)}, u32[]{:S(2)}, u32[]{:S(2)}) collective-permute-start(bf16[4,64,128]{2,1,0:T(8,128)(2,1)S(1)} %pad_maximum_fusion.refs_0_), channel_id=1, source_target_pairs={{0,3},{1,0},{2,1},{3,2},{4,7},{5,4},{6,5},{7,6},{8,11},{9,8},{10,9... | collective-permute-start | bytes 196616 | tf_op jit(solution)/shard_map/ppermute | solution.py:328
  78.9 0.5 slice_bitcast_fusion.1
  79.4 0.7 copy.13
  80.1 0.8 collective-permute-done.29.refs_1_
  80.9 1.2 %collective-permute-done.30.refs_2_ = bf16[4,64,128]{2,1,0:T(8,128)(2,1)S(1)} collective-permute-done((bf16[4,64,128]{2,1,0:T(8,128)(2,1)S(1)}, bf16[4,64,128]{2,1,0:T(8,128)(2,1)S(1)}, u32[]{:S(2)}, u32[]{:S(2)}) %collective-permute-start.30) | collective-permute-done | bytes 65568 | tf_op jit(solution)/shard_map/ppermute | solution.py:328
  82.1 1.3 %shard_map.116 = f32[32,32,128]{2,1,0:T(8,128)} custom-call(bf16[4,64,128]{2,1,0:T(8,128)(2,1)S(1)} %pad_maximum_fusion.refs_0_, bf16[4,64,128]{2,1,0:T(8,128)(2,1)S(1)} %collective-permute-done.29.refs_1_, bf16[4,64,128]{2,1,0:T(8,128)(2,1)S(1)} %collective-permute-done.30.refs_2_, bf16[4,64,128]{2,1,0:T(8,128)(2,1)S(1)} %collective-permute-done.31.refs_3_), custom_call_target="tpu_custom_call" | custom-call | tf_op jit(solution)/shard_map/pallas_call | solution.py:469
  (48 shorter events, 0.6 us)
Async XLA Ops:
  0.6 0.7 copy-start.4
  1.3 0.8 %copy-start = (bf16[16,16,64]{2,1,0:T(8,128)(2,1)S(1)}, bf16[16,16,64]{2,1,0:T(8,128)(2,1)}, u32[]{:S(2)}) copy-start(bf16[16,16,64]{2,1,0:T(8,128)(2,1)} %param.7) | copy-start | bytes 98308
  2.1 0.7 copy-start.3
  3.3 11.0 %collective-permute-start.3 = (bf16[256,128]{1,0:T(8,128)(2,1)S(1)}, bf16[256,128]{1,0:T(8,128)(2,1)S(1)}, u32[]{:S(2)}, u32[]{:S(2)}) collective-permute-start(bf16[256,128]{1,0:T(8,128)(2,1)S(1)} %get-tuple-element.32.refs_9_), channel_id=1, source_target_pairs={{0,0},{1,4},{2,8},{3,12},{4,1},{5,5},{6,9},{7,13},{8,2},{9,6},{10,... | collective-permute-start | bytes 196616 | tf_op jit(solution)/shard_map/ppermute | solution.py:335
  3.9 11.9 %collective-permute-start.4 = (bf16[256,128]{1,0:T(8,128)(2,1)S(1)}, bf16[256,128]{1,0:T(8,128)(2,1)S(1)}, u32[]{:S(2)}, u32[]{:S(2)}) collective-permute-start(bf16[256,128]{1,0:T(8,128)(2,1)S(1)} %get-tuple-element.32.refs_9_), channel_id=1, source_target_pairs={{0,4},{1,8},{2,12},{3,0},{4,5},{5,9},{6,13},{7,1},{8,6},{9,10},{10... | collective-permute-start | bytes 196616 | tf_op jit(solution)/shard_map/ppermute | solution.py:335
  8.3 9.6 %collective-permute-start.5 = (bf16[256,128]{1,0:T(8,128)(2,1)S(1)}, bf16[256,128]{1,0:T(8,128)(2,1)S(1)}, u32[]{:S(2)}, u32[]{:S(2)}) collective-permute-start(bf16[256,128]{1,0:T(8,128)(2,1)S(1)} %get-tuple-element.32.refs_9_), channel_id=1, source_target_pairs={{0,8},{1,12},{2,0},{3,4},{4,9},{5,13},{6,1},{7,5},{8,10},{9,14},{1... | collective-permute-start | bytes 196616 | tf_op jit(solution)/shard_map/ppermute | solution.py:335
  11.6 6.2 %collective-permute-start.6 = (bf16[256,128]{1,0:T(8,128)(2,1)S(1)}, bf16[256,128]{1,0:T(8,128)(2,1)S(1)}, u32[]{:S(2)}, u32[]{:S(2)}) collective-permute-start(bf16[256,128]{1,0:T(8,128)(2,1)S(1)} %get-tuple-element.32.refs_9_), channel_id=1, source_target_pairs={{0,12},{1,0},{2,4},{3,8},{4,13},{5,1},{6,5},{7,9},{8,14},{9,2},{10... | collective-permute-start | bytes 196616 | tf_op jit(solution)/shard_map/ppermute | solution.py:335
  14.3 3.8 %collective-permute-start = (bf16[256,128]{1,0:T(8,128)(2,1)S(1)}, bf16[256,128]{1,0:T(8,128)(2,1)S(1)}, u32[]{:S(2)}, u32[]{:S(2)}) collective-permute-start(bf16[256,128]{1,0:T(8,128)(2,1)S(1)} %get-tuple-element.31.refs_0_), channel_id=1, source_target_pairs={{0,1},{1,2},{2,3},{3,0},{4,5},{5,6},{6,7},{7,4},{8,9},{9,10},{10,1... | collective-permute-start | bytes 196616 | tf_op jit(solution)/shard_map/ppermute | solution.py:328
  14.3 2.4 %copy-start.2 = (bf16[64,64]{1,0:T(8,128)(2,1)S(1)}, bf16[64,64]{1,0:T(8,128)(2,1)}, u32[]{:S(2)}) copy-start(bf16[64,64]{1,0:T(8,128)(2,1)} %refs_9_.1) | copy-start | bytes 24580
  14.3 5.0 %copy-start.5 = (bf16[64,64,128]{2,1,0:T(8,128)(2,1)S(1)}, bf16[64,64,128]{2,1,0:T(8,128)(2,1)}, u32[]{:S(2)}) copy-start(bf16[64,64,128]{2,1,0:T(8,128)(2,1)} %refs_0_.1) | copy-start | bytes 3145732
  14.3 5.0 %collective-permute-start.1 = (bf16[256,128]{1,0:T(8,128)(2,1)S(1)}, bf16[256,128]{1,0:T(8,128)(2,1)S(1)}, u32[]{:S(2)}, u32[]{:S(2)}) collective-permute-start(bf16[256,128]{1,0:T(8,128)(2,1)S(1)} %get-tuple-element.31.refs_0_), channel_id=1, source_target_pairs={{0,2},{1,3},{2,0},{3,1},{4,6},{5,7},{6,4},{7,5},{8,10},{9,11},{10,... | collective-permute-start | bytes 196616 | tf_op jit(solution)/shard_map/ppermute | solution.py:328
  15.8 3.5 %collective-permute-start.2 = (bf16[256,128]{1,0:T(8,128)(2,1)S(1)}, bf16[256,128]{1,0:T(8,128)(2,1)S(1)}, u32[]{:S(2)}, u32[]{:S(2)}) collective-permute-start(bf16[256,128]{1,0:T(8,128)(2,1)S(1)} %get-tuple-element.31.refs_0_), channel_id=1, source_target_pairs={{0,3},{1,0},{2,1},{3,2},{4,7},{5,4},{6,5},{7,6},{8,11},{9,8},{10,9... | collective-permute-start | bytes 196616 | tf_op jit(solution)/shard_map/ppermute | solution.py:328
  26.4 26.2 %collective-permute-start.20 = (bf16[256,128]{1,0:T(8,128)(2,1)S(1)}, bf16[256,128]{1,0:T(8,128)(2,1)S(1)}, u32[]{:S(2)}, u32[]{:S(2)}) collective-permute-start(bf16[256,128]{1,0:T(8,128)(2,1)S(1)} %get-tuple-element.50), channel_id=1, source_target_pairs={{0,1},{1,2},{2,3},{3,0},{4,5},{5,6},{6,7},{7,4},{8,9},{9,10},{10,1... | collective-permute-start | bytes 196616 | tf_op jit(solution)/shard_map/ppermute | solution.py:328
  37.4 8.1 %collective-permute-start.10 = (bf16[16,512]{1,0:T(8,128)(2,1)S(1)}, bf16[16,512]{1,0:T(8,128)(2,1)S(1)}, u32[]{:S(2)}, u32[]{:S(2)}) collective-permute-start(bf16[16,512]{1,0:T(8,128)(2,1)S(1)} %get-tuple-element.44), channel_id=1, source_target_pairs={{0,0},{1,4},{2,8},{3,12},{4,1},{5,5},{6,9},{7,13},{8,2},{9,6},{10,... | collective-permute-start | bytes 49160 | tf_op jit(solution)/shard_map/ppermute | solution.py:339
  38.0 7.6 %collective-permute-start.11 = (bf16[16,512]{1,0:T(8,128)(2,1)S(1)}, bf16[16,512]{1,0:T(8,128)(2,1)S(1)}, u32[]{:S(2)}, u32[]{:S(2)}) collective-permute-start(bf16[16,512]{1,0:T(8,128)(2,1)S(1)} %get-tuple-element.45), channel_id=1, source_target_pairs={{0,1},{1,5},{2,9},{3,13},{4,2},{5,6},{6,10},{7,14},{8,3},{9,7},{10... | collective-permute-start | bytes 49160 | tf_op jit(solution)/shard_map/ppermute | solution.py:339
  40.5 7.5 %collective-permute-start.12 = (bf16[16,512]{1,0:T(8,128)(2,1)S(1)}, bf16[16,512]{1,0:T(8,128)(2,1)S(1)}, u32[]{:S(2)}, u32[]{:S(2)}) collective-permute-start(bf16[16,512]{1,0:T(8,128)(2,1)S(1)} %get-tuple-element.46), channel_id=1, source_target_pairs={{0,2},{1,6},{2,10},{3,14},{4,3},{5,7},{6,11},{7,15},{8,0},{9,4},{1... | collective-permute-start | bytes 49160 | tf_op jit(solution)/shard_map/ppermute | solution.py:339
  43.0 6.0 %collective-permute-start.13 = (bf16[16,512]{1,0:T(8,128)(2,1)S(1)}, bf16[16,512]{1,0:T(8,128)(2,1)S(1)}, u32[]{:S(2)}, u32[]{:S(2)}) collective-permute-start(bf16[16,512]{1,0:T(8,128)(2,1)S(1)} %get-tuple-element.47), channel_id=1, source_target_pairs={{0,3},{1,7},{2,11},{3,15},{4,0},{5,4},{6,8},{7,12},{8,1},{9,5},{10... | collective-permute-start | bytes 49160 | tf_op jit(solution)/shard_map/ppermute | solution.py:339
  45.4 3.7 %collective-permute-start.7 = (bf16[32,256]{1,0:T(8,128)(2,1)S(1)}, bf16[32,256]{1,0:T(8,128)(2,1)S(1)}, u32[]{:S(2)}, u32[]{:S(2)}) collective-permute-start(bf16[32,256]{1,0:T(8,128)(2,1)S(1)} %get-tuple-element.41), channel_id=1, source_target_pairs={{0,1},{1,2},{2,3},{3,0},{4,5},{5,6},{6,7},{7,4},{8,9},{9,10},{10,1... | collective-permute-start | bytes 49160 | tf_op jit(solution)/shard_map/ppermute | solution.py:328
  45.7 5.2 %collective-permute-start.8 = (bf16[32,256]{1,0:T(8,128)(2,1)S(1)}, bf16[32,256]{1,0:T(8,128)(2,1)S(1)}, u32[]{:S(2)}, u32[]{:S(2)}) collective-permute-start(bf16[32,256]{1,0:T(8,128)(2,1)S(1)} %get-tuple-element.42), channel_id=1, source_target_pairs={{0,2},{1,3},{2,0},{3,1},{4,6},{5,7},{6,4},{7,5},{8,10},{9,11},{10,... | collective-permute-start | bytes 49160 | tf_op jit(solution)/shard_map/ppermute | solution.py:328
  48.0 4.2 %collective-permute-start.9 = (bf16[32,256]{1,0:T(8,128)(2,1)S(1)}, bf16[32,256]{1,0:T(8,128)(2,1)S(1)}, u32[]{:S(2)}, u32[]{:S(2)}) collective-permute-start(bf16[32,256]{1,0:T(8,128)(2,1)S(1)} %get-tuple-element.43), channel_id=1, source_target_pairs={{0,3},{1,0},{2,1},{3,2},{4,7},{5,4},{6,5},{7,6},{8,11},{9,8},{10,9... | collective-permute-start | bytes 49160 | tf_op jit(solution)/shard_map/ppermute | solution.py:328
  49.0 14.2 %collective-permute-start.14 = (f32[80,128]{1,0:T(8,128)S(1)}, f32[80,128]{1,0:T(8,128)S(1)}, u32[]{:S(2)}, u32[]{:S(2)}) collective-permute-start(f32[80,128]{1,0:T(8,128)S(1)} %get-tuple-element.48), channel_id=1, source_target_pairs={{0,1},{1,2},{2,3},{3,0},{4,5},{5,6},{6,7},{7,4},{8,9},{9,10},{10,1... | collective-permute-start | bytes 122888 | tf_op jit(solution)/shard_map/ppermute | solution.py:328
  49.2 16.6 %collective-permute-start.15 = (f32[80,128]{1,0:T(8,128)S(1)}, f32[80,128]{1,0:T(8,128)S(1)}, u32[]{:S(2)}, u32[]{:S(2)}) collective-permute-start(f32[80,128]{1,0:T(8,128)S(1)} %get-tuple-element.48), channel_id=1, source_target_pairs={{0,2},{1,3},{2,0},{3,1},{4,6},{5,7},{6,4},{7,5},{8,10},{9,11},{10,... | collective-permute-start | bytes 122888 | tf_op jit(solution)/shard_map/ppermute | solution.py:328
  50.8 15.0 %collective-permute-start.16 = (f32[80,128]{1,0:T(8,128)S(1)}, f32[80,128]{1,0:T(8,128)S(1)}, u32[]{:S(2)}, u32[]{:S(2)}) collective-permute-start(f32[80,128]{1,0:T(8,128)S(1)} %get-tuple-element.48), channel_id=1, source_target_pairs={{0,3},{1,0},{2,1},{3,2},{4,7},{5,4},{6,5},{7,6},{8,11},{9,8},{10,9... | collective-permute-start | bytes 122888 | tf_op jit(solution)/shard_map/ppermute | solution.py:328
  52.2 9.7 %collective-permute-start.21 = (bf16[256,128]{1,0:T(8,128)(2,1)S(1)}, bf16[256,128]{1,0:T(8,128)(2,1)S(1)}, u32[]{:S(2)}, u32[]{:S(2)}) collective-permute-start(bf16[256,128]{1,0:T(8,128)(2,1)S(1)} %get-tuple-element.51), channel_id=1, source_target_pairs={{0,2},{1,3},{2,0},{3,1},{4,6},{5,7},{6,4},{7,5},{8,10},{9,11},{10,... | collective-permute-start | bytes 196616 | tf_op jit(solution)/shard_map/ppermute | solution.py:328
  52.6 9.3 %collective-permute-start.22 = (bf16[256,128]{1,0:T(8,128)(2,1)S(1)}, bf16[256,128]{1,0:T(8,128)(2,1)S(1)}, u32[]{:S(2)}, u32[]{:S(2)}) collective-permute-start(bf16[256,128]{1,0:T(8,128)(2,1)S(1)} %get-tuple-element.52), channel_id=1, source_target_pairs={{0,3},{1,0},{2,1},{3,2},{4,7},{5,4},{6,5},{7,6},{8,11},{9,8},{10,9... | collective-permute-start | bytes 196616 | tf_op jit(solution)/shard_map/ppermute | solution.py:328
  54.1 0.7 copy-start.6
  54.8 4.9 %copy-start.1 = (bf16[16,16,64]{2,1,0:T(8,128)(2,1)S(1)}, bf16[16,16,64]{2,1,0:T(8,128)(2,1)}, u32[]{:S(2)}) copy-start(bf16[16,16,64]{2,1,0:T(8,128)(2,1)} %param.7) | copy-start | bytes 98308
  61.9 6.1 %collective-permute-start.23 = (bf16[64,128]{1,0:T(8,128)(2,1)S(1)}, bf16[64,128]{1,0:T(8,128)(2,1)S(1)}, u32[]{:S(2)}, u32[]{:S(2)}) collective-permute-start(bf16[64,128]{1,0:T(8,128)(2,1)S(1)} %get-tuple-element.54), channel_id=1, source_target_pairs={{0,4},{4,8},{8,12},{12,0},{1,5},{5,9},{9,13},{13,1},{2,6},{6,10},{... | collective-permute-start | bytes 49160 | tf_op jit(solution)/shard_map/ppermute | solution.py:331
  62.0 8.8 %collective-permute-start.24 = (bf16[64,128]{1,0:T(8,128)(2,1)S(1)}, bf16[64,128]{1,0:T(8,128)(2,1)S(1)}, u32[]{:S(2)}, u32[]{:S(2)}) collective-permute-start(bf16[64,128]{1,0:T(8,128)(2,1)S(1)} %get-tuple-element.55), channel_id=1, source_target_pairs={{0,8},{4,12},{8,0},{12,4},{1,9},{5,13},{9,1},{13,5},{2,10},{6,14},... | collective-permute-start | bytes 49160 | tf_op jit(solution)/shard_map/ppermute | solution.py:331
  63.2 7.6 %collective-permute-start.25 = (bf16[64,128]{1,0:T(8,128)(2,1)S(1)}, bf16[64,128]{1,0:T(8,128)(2,1)S(1)}, u32[]{:S(2)}, u32[]{:S(2)}) collective-permute-start(bf16[64,128]{1,0:T(8,128)(2,1)S(1)} %get-tuple-element.56), channel_id=1, source_target_pairs={{0,12},{4,0},{8,4},{12,8},{1,13},{5,1},{9,5},{13,9},{2,14},{6,2},{... | collective-permute-start | bytes 49160 | tf_op jit(solution)/shard_map/ppermute | solution.py:331
  65.8 6.3 %collective-permute-start.17 = (f32[80,128]{1,0:T(8,128)S(1)}, f32[80,128]{1,0:T(8,128)S(1)}, u32[]{:S(2)}, u32[]{:S(2)}) collective-permute-start(f32[80,128]{1,0:T(8,128)S(1)} %add_add_fusion.1), channel_id=1, source_target_pairs={{0,4},{4,8},{8,12},{12,0},{1,5},{5,9},{9,13},{13,1},{2,6},{6,10},{... | collective-permute-start | bytes 122888 | tf_op jit(solution)/shard_map/ppermute | solution.py:331
  66.5 8.3 %collective-permute-start.18 = (f32[80,128]{1,0:T(8,128)S(1)}, f32[80,128]{1,0:T(8,128)S(1)}, u32[]{:S(2)}, u32[]{:S(2)}) collective-permute-start(f32[80,128]{1,0:T(8,128)S(1)} %add_add_fusion.1), channel_id=1, source_target_pairs={{0,8},{4,12},{8,0},{12,4},{1,9},{5,13},{9,1},{13,5},{2,10},{6,14},... | collective-permute-start | bytes 122888 | tf_op jit(solution)/shard_map/ppermute | solution.py:331
  68.0 6.8 %collective-permute-start.19 = (f32[80,128]{1,0:T(8,128)S(1)}, f32[80,128]{1,0:T(8,128)S(1)}, u32[]{:S(2)}, u32[]{:S(2)}) collective-permute-start(f32[80,128]{1,0:T(8,128)S(1)} %add_add_fusion.1), channel_id=1, source_target_pairs={{0,12},{4,0},{8,4},{12,8},{1,13},{5,1},{9,5},{13,9},{2,14},{6,2},{... | collective-permute-start | bytes 122888 | tf_op jit(solution)/shard_map/ppermute | solution.py:331
  70.9 5.6 %collective-permute-start.26 = (bf16[64,128]{1,0:T(8,128)(2,1)S(1)}, bf16[64,128]{1,0:T(8,128)(2,1)S(1)}, u32[]{:S(2)}, u32[]{:S(2)}) collective-permute-start(bf16[64,128]{1,0:T(8,128)(2,1)S(1)} %add_convert_fusion), channel_id=1, source_target_pairs={{0,4},{4,8},{8,12},{12,0},{1,5},{5,9},{9,13},{13,1},{2,6},{6,10},{... | collective-permute-start | bytes 49160 | tf_op jit(solution)/shard_map/ppermute | solution.py:331
  70.9 5.5 %collective-permute-start.27 = (bf16[64,128]{1,0:T(8,128)(2,1)S(1)}, bf16[64,128]{1,0:T(8,128)(2,1)S(1)}, u32[]{:S(2)}, u32[]{:S(2)}) collective-permute-start(bf16[64,128]{1,0:T(8,128)(2,1)S(1)} %add_convert_fusion), channel_id=1, source_target_pairs={{0,8},{4,12},{8,0},{12,4},{1,9},{5,13},{9,1},{13,5},{2,10},{6,14},... | collective-permute-start | bytes 49160 | tf_op jit(solution)/shard_map/ppermute | solution.py:331
  72.1 4.9 %collective-permute-start.28 = (bf16[64,128]{1,0:T(8,128)(2,1)S(1)}, bf16[64,128]{1,0:T(8,128)(2,1)S(1)}, u32[]{:S(2)}, u32[]{:S(2)}) collective-permute-start(bf16[64,128]{1,0:T(8,128)(2,1)S(1)} %add_convert_fusion), channel_id=1, source_target_pairs={{0,12},{4,0},{8,4},{12,8},{1,13},{5,1},{9,5},{13,9},{2,14},{6,2},{... | collective-permute-start | bytes 49160 | tf_op jit(solution)/shard_map/ppermute | solution.py:331
  77.0 3.8 %collective-permute-start.29 = (bf16[4,64,128]{2,1,0:T(8,128)(2,1)S(1)}, bf16[4,64,128]{2,1,0:T(8,128)(2,1)S(1)}, u32[]{:S(2)}, u32[]{:S(2)}) collective-permute-start(bf16[4,64,128]{2,1,0:T(8,128)(2,1)S(1)} %pad_maximum_fusion.refs_0_), channel_id=1, source_target_pairs={{0,1},{1,2},{2,3},{3,0},{4,5},{5,6},{6,7},{7,4},{8,9},{9,10},{10,1... | collective-permute-start | bytes 196616 | tf_op jit(solution)/shard_map/ppermute | solution.py:328
  77.1 5.0 %collective-permute-start.30 = (bf16[4,64,128]{2,1,0:T(8,128)(2,1)S(1)}, bf16[4,64,128]{2,1,0:T(8,128)(2,1)S(1)}, u32[]{:S(2)}, u32[]{:S(2)}) collective-permute-start(bf16[4,64,128]{2,1,0:T(8,128)(2,1)S(1)} %pad_maximum_fusion.refs_0_), channel_id=1, source_target_pairs={{0,2},{1,3},{2,0},{3,1},{4,6},{5,7},{6,4},{7,5},{8,10},{9,11},{10,... | collective-permute-start | bytes 196616 | tf_op jit(solution)/shard_map/ppermute | solution.py:328
  77.5 4.6 %collective-permute-start.31 = (bf16[4,64,128]{2,1,0:T(8,128)(2,1)S(1)}, bf16[4,64,128]{2,1,0:T(8,128)(2,1)S(1)}, u32[]{:S(2)}, u32[]{:S(2)}) collective-permute-start(bf16[4,64,128]{2,1,0:T(8,128)(2,1)S(1)} %pad_maximum_fusion.refs_0_), channel_id=1, source_target_pairs={{0,3},{1,0},{2,1},{3,2},{4,7},{5,4},{6,5},{7,6},{8,11},{9,8},{10,9... | collective-permute-start | bytes 196616 | tf_op jit(solution)/shard_map/ppermute | solution.py:328

commit v2 on v1

--- a/solution.py
+++ b/solution.py
@@ -110,11 +110,10 @@
 
 def weight_kernel(depth, n, pieces, *refs):
     a_refs, b_refs = refs[:pieces], refs[pieces : 2 * pieces]
-    up_ref, w_ref, wt_ref, perm_ref = refs[2 * pieces : 2 * pieces + 4]
-    outs = refs[2 * pieces + 4 :]
-    mi_ref, mj_ref, a_ref, b_ref, bt_ref, inv_ref, bias_ref = outs[:7]
-    send_refs = outs[7 : 7 + n]
-    at_ref, v_ref, acc_ref = outs[7 + n :]
+    up_ref, w_ref, wt_ref, perm_ref, wc_ref = refs[2 * pieces : 2 * pieces + 5]
+    outs = refs[2 * pieces + 5 :]
+    mi_ref, mj_ref, a_ref, b_ref, inv_ref, bias_ref, dw_ref, da_ref = outs[:8]
+    bt_ref, at_ref, v_ref, acc_ref = outs[8:]
     g, last = pl.program_id(0), pl.num_programs(0) - 1
     chunk, block, pair = up_ref.shape
     features = w_ref.shape[0]
@@ -169,42 +168,33 @@
     fill_v(up_ref, inv_ref[g], bt_ref[...], v_ref, depth)
     span = chunk * depth
     a_t = at_ref[:, pl.ds(pl.multiple_of(g * span, span), span)]
+    d_a = jnp.zeros((width, span), F32)
     for e in range(0, width, 2):
-        part = dot(a_t, two(v_ref, e))
+        v = two(v_ref, e)
+        part = dot(a_t, v)
         for k in range(2):
             acc_ref[(e + k) * width : (e + k + 1) * width, :] += part[:, k * pair : (k + 1) * pair]
+        d_a = d_a + dot_nt(wc_ref[:, e * pair : (e + 2) * pair], v)
+    da_ref[:, pl.ds(pl.multiple_of(g * span, span), span)] = d_a.astype(BF16)
 
     @pl.when(g == last)
     def _():
-        rows = acc_ref.shape[0] // n
-        for k in range(n):
-            at = pl.multiple_of(lax.rem(c + k, n) * rows, rows)
-            send_refs[k][...] = acc_ref[pl.ds(at, rows), :].astype(BF16)
-
-
-def token_kernel(depth, n, split, *refs):
-    up_ref, inv_ref, a_ref, bt_ref, wc_ref, mi_ref, mj_ref, perm_ref, bias_ref = refs[:9]
-    outs = refs[9:]
-    small_ref = outs[0]
-    count = n if split else 1
-    da_refs, db_refs = outs[1 : 1 + count], outs[1 + count : 1 + 2 * count]
-    v_ref, t_ref, da_ref, db_ref = outs[1 + 2 * count :]
+        dw_ref[...] = acc_ref[...].astype(BF16)
+
+
+def token_kernel(depth, *refs):
+    up_ref, inv_ref, a_ref, wc_ref, mi_ref, mj_ref, perm_ref, bias_ref, da_ref = refs[:9]
+    small_ref, out_ref, t_ref, db_ref = refs[9:]
     g, last = pl.program_id(0), pl.num_programs(0) - 1
-    chunk, block, pair = up_ref.shape
+    chunk = up_ref.shape[0]
     width = wc_ref.shape[0]
     span = chunk * depth
-    r, c = lax.axis_index("row"), lax.axis_index("col")
     inv = inv_ref[g]
 
     @pl.when(g == 0)
     def _():
         db_ref[...] = jnp.zeros_like(db_ref)
 
-    fill_v(up_ref, inv, bt_ref[...], v_ref, depth)
-    d_a = jnp.zeros((width, span), F32)
-    for e in range(0, width, 2):
-        d_a = d_a + dot_nt(wc_ref[:, e * pair : (e + 2) * pair], two(v_ref, e))
-    da_ref[:, pl.ds(pl.multiple_of(g * span, span), span)] = d_a.astype(BF16)
     a_chunk = a_ref[pl.ds(pl.multiple_of(g * span, span), span), :]
     fill_t(a_chunk, wc_ref, t_ref, depth)
     d_b = db_ref[...]
@@ -215,26 +205,15 @@
     @pl.when(g == last)
     def _():
         d_b = db_ref[...].astype(BF16)
+        out_ref[...] = d_b
         turned = dot_nt(perm_ref[...], d_b).astype(BF16)
-        left = dot(da_ref[...], mi_ref[...])
         right = jnp.zeros((width, LANES), F32)
         for s in range(depth):
             right = right + dot(turned[s * width : (s + 1) * width, :], mj_ref[s])
-        small_ref[0:width, :] = left
-        small_ref[width : 2 * width, :] = right
-        small_ref[2 * width :, :] = jnp.zeros_like(small_ref[2 * width :, :])
-        small_ref[2 * width : 2 * width + 1, :] = bias_ref[0:1, :]
-        if split:
-            own = block // n
-            for k in range(n):
-                lanes = own * depth
-                at = pl.multiple_of(lax.rem(c + k, n) * lanes, lanes)
-                da_refs[k][...] = da_ref[:, pl.ds(at, lanes)]
-                at = pl.multiple_of(lax.rem(r + k, n) * own, own)
-                db_refs[k][...] = db_ref[pl.ds(at, own), :].astype(BF16)
-        else:
-            da_refs[0][...] = da_ref[...]
-            db_refs[0][...] = d_b
+        small_ref[0:width, :] = dot(da_ref[...], mi_ref[...]).astype(BF16)
+        small_ref[width : 2 * width, :] = right.astype(BF16)
+        tail = jnp.broadcast_to(bias_ref[0:1, :], (16, LANES))
+        small_ref[2 * width :, :] = tail.astype(BF16)
 
 
 def update_kernel(depth, inv_ref, a_ref, b_ref, wc_ref, offset_ref, out_ref, t_ref):
@@ -252,20 +231,9 @@
             out_ref[at + k] = value.astype(BF16)
 
 
-def sum_kernel(axis, n, *refs):
-    ins, outs = refs[:n], refs[n:]
-    me = lax.axis_index(axis)
-    for k in range(n):
-        at = lax.rem(me + k, n)
-        total = ins[0][at].astype(F32)
-        for ref in ins[1:]:
-            total = total + ref[at].astype(F32)
-        outs[k][...] = total.astype(BF16)
-
-
-def owner_kernel(depth, own, n, *refs):
-    da_refs, db_refs = refs[:n], refs[n : 2 * n]
-    x_ref, message_ref, wt_ref, perm_ref, out_ref = refs[2 * n :]
+def owner_kernel(depth, own, *refs):
+    da_refs, db_refs = refs[:2], refs[2:4]
+    x_ref, message_ref, wt_ref, perm_ref, out_ref = refs[4:]
     rows = depth * own
     width = wt_ref.shape[0] // 2
     features = x_ref.shape[1]
@@ -273,7 +241,7 @@
     swap = one_hot(q == (p % own) * depth + p // own)
     d_a = jnp.zeros((rows, width), F32)
     d_b = jnp.zeros((own, width * depth), F32)
-    for k in range(n):
+    for k in range(2):
         d_a = d_a + dot_nt(swap, da_refs[k][...])
         d_b = d_b + dot_nt(db_refs[k][...], perm_ref[...])
     d_b = jnp.concatenate([d_b[:, s * width : (s + 1) * width] for s in range(depth)], axis=0)
@@ -290,19 +258,55 @@
     out_ref[...] = scale * (d_normed - mean - normed * along)
 
 
-def place_kernel(n, *refs):
-    ins, out_ref, full_ref = refs[:n], refs[n], refs[n + 1]
-    r, c = lax.axis_index("row"), lax.axis_index("col")
-    width = out_ref.shape[0]
-    each = width // (n * n)
-    for k in range(n):
-        col = lax.rem(c - k + n, n)
-        for m in range(n):
-            row = lax.rem(r - m + n, n)
-            value = ins[k][m].astype(F32).reshape(each, width, LANES)
-            full_ref[pl.ds((col * n + row) * each, each)] = value
-    for e in range(width):
-        out_ref[:, e, :] = full_ref[e]
+def place_kernel(in_ref, out_ref):
+    for e in range(in_ref.shape[0]):
+        out_ref[:, e, :] = in_ref[e].astype(F32)
+
+
+def lay_out(x):
+    rows, lanes = x.shape
+    if lanes % LANES:
+        return x.reshape(-1, LANES)
+    return x.reshape(rows, lanes // LANES, LANES).transpose(1, 0, 2).reshape(-1, LANES)
+
+
+def lay_back(x, rows, lanes):
+    if lanes % LANES:
+        return x.reshape(rows, lanes)
+    return x.reshape(lanes // LANES, rows, LANES).transpose(1, 0, 2).reshape(rows, lanes)
+
+
+def bit_of(axis, bit):
+    return (lax.axis_index(axis) >> bit) & 1
+
+
+def swap_parts(parts, axis, bit, n):
+    parts = [part.reshape(-1, LANES) for part in parts]
+    message = jnp.concatenate(parts, axis=0) if len(parts) > 1 else parts[0]
+    message = lax.ppermute(message, axis, [(i, i ^ (1 << bit)) for i in range(n)])
+    got, at = [], 0
+    for part in parts:
+        got.append(message[at : at + part.shape[0]])
+        at += part.shape[0]
+    return got
+
+
+def halves(x, axis, bit):
+    x = x.reshape((x.shape[0] // 2, 2) + x.shape[1:])
+    here = bit_of(axis, bit)
+    keep = lax.dynamic_index_in_dim(x, here, 1, keepdims=False)
+    return keep, lax.dynamic_index_in_dim(x, 1 - here, 1, keepdims=False)
+
+
+def in_order(mine, other, axis, bit, at):
+    first = bit_of(axis, bit) == 0
+    low = jnp.where(first, mine, other)
+    return jnp.stack([low, jnp.where(first, other, mine)], axis=at)
+
+
+def add(mine, other):
+    other = other.reshape(mine.shape)
+    return lax.optimization_barrier((mine.astype(F32) + other.astype(F32)).astype(BF16))
 
 
 def per_device(
@@ -334,16 +338,7 @@
         pairs = [(i * n + j, (j + k) % n * n + i) for i in range(n) for j in range(n)]
         return lax.ppermute(x, axes, pairs)
 
-    def to_owner(x, k):
-        pairs = [(i * n + j, j * n + (i + k) % n) for i in range(n) for j in range(n)]
-        return lax.ppermute(x, axes, pairs)
-
     r, c = lax.axis_index("row"), lax.axis_index("col")
-
-    def cut(x, axis, at):
-        size = x.shape[axis] // n
-        return lax.dynamic_slice_in_dim(x, at % n * size, size, axis)
-
     x = alignment_embedding.reshape(rows, features)
     by_token, by_row = call(
         functools.partial(prep_kernel, depth, own),
@@ -376,75 +371,79 @@
         sds((depth, block, LANES), BF16),
         sds((tokens, width), BF16),
         sds((block, wide), BF16),
-        sds((wide, block), BF16),
         sds((steps, block, chunk), F32),
         sds((8, pair), F32),
-    ] + [sds((width * width // n, pair), BF16)] * n
+        sds((width * width, pair), BF16),
+        sds((width, tokens), BF16),
+    ]
     outs = call(
         functools.partial(weight_kernel, depth, n, pieces),
         (steps,),
         [full(p.shape) for p in a_pieces]
         + [full(p.shape) for p in b_pieces]
-        + [up_spec, full(sitewise_factors.shape), full(factors_t.shape), full(perm.shape)],
+        + [up_spec]
+        + [full(v.shape) for v in (sitewise_factors, factors_t, perm, pairing_wide)],
         [full(o.shape) for o in out_shapes],
         out_shapes,
         [
+            pltpu.VMEM((wide, block), BF16),
             pltpu.VMEM((width, tokens), BF16),
             pltpu.VMEM((width, chunk * depth, pair), BF16),
             pltpu.VMEM((width * width, pair), F32),
         ],
         cost(5e9, 8e6),
-    )(*a_pieces, *b_pieces, upstream_adjoint, sitewise_factors, factors_t, perm)
-    mi, mj, a, b, b_t, inv, bias = outs[:7]
-    sends = list(outs[7:])
-
-    shard = width * width // (n * n)
-    parts = [sends[0]] + [along_col(sends[k], k) for k in range(1, n)]
-    parts = [part.reshape(n, shard, pair) for part in parts]
-
-    count = n if split else 1
-    piece = block // count
-    out_shapes = (
-        [sds((2 * width + 16, LANES), F32)]
-        + [sds((width, piece * depth), BF16)] * count
-        + [sds((piece, wide), BF16)] * count
-    )
-    outs = call(
-        functools.partial(token_kernel, depth, n, split),
+    )(*a_pieces, *b_pieces, upstream_adjoint, sitewise_factors, factors_t, perm, pairing_wide)
+    mi, mj, a, b, inv, bias, d_pairing, d_a = outs
+
+    bits = n.bit_length() - 1
+    d_pairing = d_pairing.reshape(n, -1, LANES)
+    d_a = jnp.stack([lay_out(d_a[:, k * rows : (k + 1) * rows]) for k in range(n)])
+    da_parts = [d_a]
+    for bit in range(bits):
+        keep, go = halves(d_pairing, "col", bit)
+        if bit:
+            d_a = add(*da_parts)
+        da_keep, da_go = halves(d_a, "col", bit)
+        got, da_got = swap_parts([go, da_go], "col", bit, n)
+        d_pairing = add(keep, got)
+        da_parts = [da_keep, da_got.reshape(da_keep.shape)]
+
+    out_shapes = [sds((2 * width + 16, LANES), BF16), sds((block, wide), BF16)]
+    small, d_b = call(
+        functools.partial(token_kernel, depth),
         (steps,),
         [up_spec]
-        + [full(v.shape) for v in (inv, a, b_t, pairing_wide, mi, mj, perm, bias)],
+        + [full(v.shape) for v in (inv, a, pairing_wide, mi, mj, perm, bias)]
+        + [full((width, tokens))],
         [full(o.shape) for o in out_shapes],
         out_shapes,
-        [
-            pltpu.VMEM((width, chunk * depth, pair), BF16),
-            pltpu.VMEM((chunk, wide, pair), BF16),
-            pltpu.VMEM((width, tokens), BF16),
-            pltpu.VMEM((block, wide), F32),
-        ],
-        cost(8e9, 8e6),
-    )(upstream_adjoint, inv, a, b_t, pairing_wide, mi, mj, perm, bias)
-    small = outs[0]
-    d_a, d_b = list(outs[1 : 1 + count]), list(outs[1 + count :])
-    if not split:
-        d_a = [cut(d_a[0], 1, c + k) for k in range(n)]
-        d_b = [cut(d_b[0], 0, r + k) for k in range(n)]
-    d_a = [d_a[0]] + [along_col(d_a[k], k) for k in range(1, n)]
-    d_b = [to_owner(d_b[k], k) for k in range(n)]
-    small = small + sum(along_col(small, k) for k in range(1, n))
-    small = small + sum(along_row(small, k) for k in range(1, n))
-
-    shards = call(
-        functools.partial(sum_kernel, "row", n),
-        (),
-        [full(part.shape) for part in parts],
-        [full((shard, pair))] * n,
-        [sds((shard, pair), BF16)] * n,
-    )(*parts)
-    mine = [shards[0].astype(F32)] + [along_row(shards[k], k).astype(F32) for k in range(1, n)]
-    mine = sum(mine).astype(BF16)
-    gathered = jnp.stack([mine] + [along_row(mine, k) for k in range(1, n)])
-    gathered = [gathered] + [along_col(gathered, k) for k in range(1, n)]
+        [pltpu.VMEM((chunk, wide, pair), BF16), pltpu.VMEM((block, wide), F32)],
+        cost(5e9, 8e6),
+    )(upstream_adjoint, inv, a, pairing_wide, mi, mj, perm, bias, outs[7])
+
+    d_b = jnp.stack([lay_out(d_b[k * own : (k + 1) * own]) for k in range(n)])[:, None]
+    for bit in range(bits):
+        keep, go = halves(d_b, "col", bit)
+        got, small_got = swap_parts([go, small], "col", bit, n)
+        small = add(small, small_got)
+        d_b = in_order(keep, got.reshape(keep.shape), "col", bit, 1)
+        d_b = d_b.reshape((keep.shape[0], -1) + keep.shape[2:])
+    db_parts = [d_b[0]]
+    for bit in range(bits):
+        if bit:
+            db_parts = [add(*db_parts)]
+        db_keep, db_go = halves(db_parts[0], "row", bit)
+        got, db_got, small_got = swap_parts([d_pairing, db_go, small], "row", bit, n)
+        d_pairing = add(d_pairing, got)
+        small = add(small, small_got)
+        db_parts = [db_keep, db_got.reshape(db_keep.shape)]
+    d_pairing = d_pairing.reshape(1, -1, LANES)
+    for bit in reversed(range(bits)):
+        (got,) = swap_parts([d_pairing], "col", bit, n)
+        d_pairing = in_order(d_pairing, got.reshape(d_pairing.shape), "col", bit, 1)
+        d_pairing = d_pairing.reshape((-1,) + d_pairing.shape[2:])
+    d_a = [lay_back(part[0], width, rows) for part in da_parts]
+    d_b = [lay_back(part[0], own, wide) for part in db_parts]
 
     coupling_update = call(
         functools.partial(update_kernel, depth),
@@ -457,7 +456,7 @@
     )(inv, a, b, pairing_wide, offset_vector.reshape(1, pair))
 
     embedding_adjoint = call(
-        functools.partial(owner_kernel, depth, own, n),
+        functools.partial(owner_kernel, depth, own),
         (),
         [full(v.shape) for v in d_a + d_b]
         + [full(v.shape) for v in (x, by_row, factors_t, perm)],
@@ -465,19 +464,15 @@
         sds((rows, features), F32),
     )(*d_a, *d_b, x, by_row, factors_t, perm)
 
-    if width % (n * n) == 0:
-        placed = call(
-            functools.partial(place_kernel, n),
-            (),
-            [full(part.shape) for part in gathered],
-            full((width, width, pair)),
-            sds((width, width, pair), F32),
-            [pltpu.VMEM((width, width, pair), F32)],
-        )(*gathered)
-    else:
-        held = jnp.stack(gathered)
-        held = held[(c - jnp.arange(n)) % n][:, (r - jnp.arange(n)) % n]
-        placed = held.astype(F32).reshape(width, width, pair).transpose(1, 0, 2)
+    d_pairing = d_pairing.reshape(width, width, pair)
+    placed = call(
+        place_kernel,
+        (),
+        [full(d_pairing.shape)],
+        full((width, width, pair)),
+        sds((width, width, pair), F32),
+    )(d_pairing)
+    small = small.astype(F32)
     factors = jnp.concatenate([small[:width], small[width : 2 * width]], axis=0)
     return (
         coupling_update,

time: 83.8 us -> 67.4 us (0.80)
  starting transfers between devices: 44.1 us -> 19.7 us
  waiting for transfers between devices: 6.83 us -> 13.6 us
  local copies, waits for them, and re-layouts: 5.23 us -> 6.26 us
    ppermute x13 -> x8, starting transfers between devices: 20.8 us -> 6.44 us  [swap_parts(): message = lax.ppermute(message, axis, [(i, i ^ 1 << bit) for i in range(n)])]
    ppermute x15 -> x3, starting transfers between devices: 12.2 us -> 2.23 us  [along_col(): return lax.ppermute(x, 'col', [(i, (i + k) % n) for i in range(n)])]
    ppermute x13 -> x8, waiting for transfers between devices: 3.39 us -> 12.2 us  [swap_parts(): message = lax.ppermute(message, axis, [(i, i ^ 1 << bit) for i in range(n)])]
    pallas_call x4 -> x3, Pallas kernels: 13.9 us -> 9.11 us  [the longest x1 5.89 us: per_device(): call(functools.partial(token_kernel, depth), (steps,), [up_spec] + [full(...]
    pallas_call x1, Pallas kernels: 7.07 us -> 11.5 us  [per_device(): call(functools.partial(weight_kernel, depth, n, pieces), (steps,), [full(...]
    ppermute x15 -> x3, waiting for transfers between devices: 3.43 us -> 1.37 us  [along_col(): return lax.ppermute(x, 'col', [(i, (i + k) % n) for i in range(n)])]
    unnamed x16 -> x20, local copies, waits for them, and re-layouts: 3.64 us -> 4.48 us
  transfers between devices with their start and end apart: 32 -> 15, of which waited for: 8 -> 8; matrix products, arithmetic and copies ran while one was open for 3% -> 4% of each run, Pallas kernels for 21% -> 10%
where the time goes in v2:
time: 67.4 us; the launch traced here: 67.1 us
  Pallas kernels  25.9 us (38%)
  starting transfers between devices  19.7 us (29%)
  waiting for transfers between devices  13.6 us (20%)
  local copies, waits for them, and re-layouts  6.26 us (9%)
  between operations  1.11 us (2%)
    ppermute x8, waiting for transfers between devices, swap_parts(): message = lax.ppermute(message, axis, [(i, i ^ 1 << bit) for i in range(n)])  12.2 us
    pallas_call x1, Pallas kernels, per_device(): call(functools.partial(weight_kernel, depth, n, pieces), (steps,), [full(...  11.5 us
    ppermute x4, starting transfers between devices, to_column(): return lax.ppermute(x, axes, pairs)  11 us
    ppermute x8, starting transfers between devices, swap_parts(): message = lax.ppermute(message, axis, [(i, i ^ 1 << bit) for i in range(n)])  6.44 us
    pallas_call x1, Pallas kernels, per_device(): call(functools.partial(token_kernel, depth), (steps,), [up_spec] + [full(...  5.89 us
    pallas_call x1, Pallas kernels, per_device(): call(functools.partial(update_kernel, depth), (steps,), [full(v.shape) fo...  4.86 us
    unnamed x20, local copies, waits for them, and re-layouts  4.48 us
    ppermute x3, starting transfers between devices, along_col(): return lax.ppermute(x, 'col', [(i, (i + k) % n) for i in range(n)])  2.23 us
  transfers between devices with their start and end apart: 15, of which 8 were waited for; matrix products, arithmetic and copies ran while one was open for 4% of the time, Pallas kernels for 10%

profile of v2, /device:TPU:0, one launch (start us, length us, event | category | flops | bytes accessed | tf_op | source)
XLA Modules:
  0.0 67.1 jit_solution(1223494334952960833)
XLA Ops:
  0.6 0.0 copy-start.4
  0.6 0.6 copy-done.4
  1.3 0.8 %copy-done = bf16[16,16,64]{2,1,0:T(8,128)(2,1)S(1)} copy-done((bf16[16,16,64]{2,1,0:T(8,128)(2,1)S(1)}, bf16[16,16,64]{2,1,0:T(8,128)(2,1)}, u32[]{:S(2)}) %copy-start) | copy-done | bytes 32792
  2.1 0.7 %copy-done.3 = s32[16,16]{1,0:T(8,128)S(1)} copy-done((s32[16,16]{1,0:T(8,128)S(1)}, s32[16,16]{1,0:T(8,128)}, u32[]{:S(2)}) %copy-start.3) | copy-done | bytes 1048
  2.8 0.4 shard_map.110
  3.3 0.7 collective-permute-start.3
  3.9 4.3 %collective-permute-start.4 = (bf16[256,128]{1,0:T(8,128)(2,1)S(1)}, bf16[256,128]{1,0:T(8,128)(2,1)S(1)}, u32[]{:S(2)}, u32[]{:S(2)}) collective-permute-start(bf16[256,128]{1,0:T(8,128)(2,1)S(1)} %get-tuple-element.18.refs_5_), channel_id=1, source_target_pairs={{0,4},{1,8},{2,12},{3,0},{4,5},{5,9},{6,13},{7,1},{8,6},{9,10},{10... | collective-permute-start | bytes 196616 | tf_op jit(solution)/shard_map/ppermute | solution.py:339
  8.3 3.4 %collective-permute-start.5 = (bf16[256,128]{1,0:T(8,128)(2,1)S(1)}, bf16[256,128]{1,0:T(8,128)(2,1)S(1)}, u32[]{:S(2)}, u32[]{:S(2)}) collective-permute-start(bf16[256,128]{1,0:T(8,128)(2,1)S(1)} %get-tuple-element.18.refs_5_), channel_id=1, source_target_pairs={{0,8},{1,12},{2,0},{3,4},{4,9},{5,13},{6,1},{7,5},{8,10},{9,14},{1... | collective-permute-start | bytes 196616 | tf_op jit(solution)/shard_map/ppermute | solution.py:339
  11.6 2.6 %collective-permute-start.6 = (bf16[256,128]{1,0:T(8,128)(2,1)S(1)}, bf16[256,128]{1,0:T(8,128)(2,1)S(1)}, u32[]{:S(2)}, u32[]{:S(2)}) collective-permute-start(bf16[256,128]{1,0:T(8,128)(2,1)S(1)} %get-tuple-element.18.refs_5_), channel_id=1, source_target_pairs={{0,12},{1,0},{2,4},{3,8},{4,13},{5,1},{6,5},{7,9},{8,14},{9,2},{10... | collective-permute-start | bytes 196616 | tf_op jit(solution)/shard_map/ppermute | solution.py:339
  14.3 0.0 collective-permute-start
  14.3 0.0 collective-permute-done.3.refs_4_
  14.3 1.5 %collective-permute-start.1 = (bf16[256,128]{1,0:T(8,128)(2,1)S(1)}, bf16[256,128]{1,0:T(8,128)(2,1)S(1)}, u32[]{:S(2)}, u32[]{:S(2)}) collective-permute-start(bf16[256,128]{1,0:T(8,128)(2,1)S(1)} %get-tuple-element.17.refs_0_), channel_id=1, source_target_pairs={{0,2},{1,3},{2,0},{3,1},{4,6},{5,7},{6,4},{7,5},{8,10},{9,11},{10,... | collective-permute-start | bytes 196616 | tf_op jit(solution)/shard_map/ppermute | solution.py:332
  15.8 0.0 collective-permute-done.4.refs_5_
  15.8 0.7 %collective-permute-start.2 = (bf16[256,128]{1,0:T(8,128)(2,1)S(1)}, bf16[256,128]{1,0:T(8,128)(2,1)S(1)}, u32[]{:S(2)}, u32[]{:S(2)}) collective-permute-start(bf16[256,128]{1,0:T(8,128)(2,1)S(1)} %get-tuple-element.17.refs_0_), channel_id=1, source_target_pairs={{0,3},{1,0},{2,1},{3,2},{4,7},{5,4},{6,5},{7,6},{8,11},{9,8},{10,9... | collective-permute-start | bytes 196616 | tf_op jit(solution)/shard_map/ppermute | solution.py:332
  16.5 0.1 fusion.refs_11_.refs_6_.refs_7_
  16.7 0.0 copy-start.2
  16.7 1.1 %reshape.291.refs_12_.wc_ref.refs_3_ = bf16[32,4096]{1,0:T(8,128)(2,1)S(1)} reshape(bf16[1024,128]{1,0:T(8,128)(2,1)} %param.11) | data formatting | bytes 524288 | tf_op jit(solution)/shard_map/reshape | solution.py:366
  17.8 0.1 copy.21
  17.9 0.0 collective-permute-done.5.refs_6_
  17.9 0.0 collective-permute-done.6.refs_7_
  17.9 0.2 collective-permute-done.refs_1_
  18.1 1.2 %collective-permute-done.1.refs_2_ = bf16[256,128]{1,0:T(8,128)(2,1)S(1)} collective-permute-done((bf16[256,128]{1,0:T(8,128)(2,1)S(1)}, bf16[256,128]{1,0:T(8,128)(2,1)S(1)}, u32[]{:S(2)}, u32[]{:S(2)}) %collective-permute-start.1) | collective-permute-done | bytes 65568 | tf_op jit(solution)/shard_map/ppermute | solution.py:332
  19.3 0.0 collective-permute-done.2.refs_3_
  19.3 11.5 %shard_map.111 = (bf16[1024,128]{1,0:T(8,128)(2,1)S(1)}, bf16[16,64,128]{2,1,0:T(8,128)(2,1)S(1)}, bf16[1024,32]{1,0:T(8,128)(2,1)S(1)}, bf16[64,512]{1,0:T(8,12...) custom-call(bf16[256,128]{1,0:T(8,128)(2,1)S(1)} %get-tuple-element., ...), custom_call_target="tpu_custom_call" | custom-call | flops 5000000000 | bytes 8000000 | tf_op jit(solution)/shard_map/pallas_call | solution.py:379
  30.8 5.9 %shard_map.113 = (bf16[80,128]{1,0:T(8,128)(2,1)S(1)}, bf16[64,512]{1,0:T(8,128)(2,1)S(1)}) custom-call(bf16[64,64,128]{2,1,0:T(8,128)(2,1)S(1)} %copy-done.5, f32[4,64,16]{2,1,0:T(8,128)S(1)} %get-tuple-element.19.inv_ref.refs_1_, bf16[1024,32]{1,0:T(8,128)(2,1)S(1)} %get-tuple-element.20.a_ref.refs_2_, ...), custom_call_target="tpu_custom_call" | custom-call | flops 5000000000 | bytes 8000000 | tf_op jit(solution)/shard_map/pallas_call | solution.py:412
  36.9 0.7 %collective-permute-start.9 = (bf16[208,128]{1,0:T(8,128)(2,1)S(1)}, bf16[208,128]{1,0:T(8,128)(2,1)S(1)}, u32[]{:S(2)}, u32[]{:S(2)}) collective-permute-start(bf16[208,128]{1,0:T(8,128)(2,1)S(1)} %pad_maximum_fusion.8), channel_id=1, source_target_pairs={{0,1},{1,0},{2,3},{3,2},{4,5},{5,4},{6,7},{7,6},{8,9},{9,8},{10,11... | collective-permute-start | bytes 159752 | tf_op jit(solution)/shard_map/ppermute | solution.py:286
  37.6 0.8 %collective-permute-done.9 = bf16[208,128]{1,0:T(8,128)(2,1)S(1)} collective-permute-done((bf16[208,128]{1,0:T(8,128)(2,1)S(1)}, bf16[208,128]{1,0:T(8,128)(2,1)S(1)}, u32[]{:S(2)}, u32[]{:S(2)}) %collective-permute-start.9) | collective-permute-done | bytes 53280 | tf_op jit(solution)/shard_map/ppermute | solution.py:286
  38.5 1.1 %collective-permute-start.10 = (bf16[208,128]{1,0:T(8,128)(2,1)S(1)}, bf16[208,128]{1,0:T(8,128)(2,1)S(1)}, u32[]{:S(2)}, u32[]{:S(2)}) collective-permute-start(bf16[208,128]{1,0:T(8,128)(2,1)S(1)} %pad_maximum_fusion.9), channel_id=1, source_target_pairs={{0,2},{1,3},{2,0},{3,1},{4,6},{5,7},{6,4},{7,5},{8,10},{9,11},{10,... | collective-permute-start | bytes 159752 | tf_op jit(solution)/shard_map/ppermute | solution.py:286
  39.7 0.1 collective-permute-start.7
  39.8 2.9 %collective-permute-done.10 = bf16[208,128]{1,0:T(8,128)(2,1)S(1)} collective-permute-done((bf16[208,128]{1,0:T(8,128)(2,1)S(1)}, bf16[208,128]{1,0:T(8,128)(2,1)S(1)}, u32[]{:S(2)}, u32[]{:S(2)}) %collective-permute-start.10) | collective-permute-done | bytes 53280 | tf_op jit(solution)/shard_map/ppermute | solution.py:286
  42.8 0.0 collective-permute-done.7
  43.0 1.1 %collective-permute-start.8 = (bf16[320,128]{1,0:T(8,128)(2,1)S(1)}, bf16[320,128]{1,0:T(8,128)(2,1)S(1)}, u32[]{:S(2)}, u32[]{:S(2)}) collective-permute-start(bf16[320,128]{1,0:T(8,128)(2,1)S(1)} %pad_maximum_fusion.5), channel_id=1, source_target_pairs={{0,2},{1,3},{2,0},{3,1},{4,6},{5,7},{6,4},{7,5},{8,10},{9,11},{10,... | collective-permute-start | bytes 245768 | tf_op jit(solution)/shard_map/ppermute | solution.py:286
  44.1 3.4 %collective-permute-done.8 = bf16[320,128]{1,0:T(8,128)(2,1)S(1)} collective-permute-done((bf16[320,128]{1,0:T(8,128)(2,1)S(1)}, bf16[320,128]{1,0:T(8,128)(2,1)S(1)}, u32[]{:S(2)}, u32[]{:S(2)}) %collective-permute-start.8) | collective-permute-done | bytes 81952 | tf_op jit(solution)/shard_map/ppermute | solution.py:286
  47.5 1.1 %collective-permute-start.11 = (bf16[464,128]{1,0:T(8,128)(2,1)S(1)}, bf16[464,128]{1,0:T(8,128)(2,1)S(1)}, u32[]{:S(2)}, u32[]{:S(2)}) collective-permute-start(bf16[464,128]{1,0:T(8,128)(2,1)S(1)} %pad_maximum_fusion.3), channel_id=1, source_target_pairs={{0,4},{4,0},{8,12},{12,8},{1,5},{5,1},{9,13},{13,9},{2,6},{6,2},{1... | collective-permute-start | bytes 356360 | tf_op jit(solution)/shard_map/ppermute | solution.py:286
  48.6 3.8 %collective-permute-done.11 = bf16[464,128]{1,0:T(8,128)(2,1)S(1)} collective-permute-done((bf16[464,128]{1,0:T(8,128)(2,1)S(1)}, bf16[464,128]{1,0:T(8,128)(2,1)S(1)}, u32[]{:S(2)}, u32[]{:S(2)}) %collective-permute-start.11) | collective-permute-done | bytes 118816 | tf_op jit(solution)/shard_map/ppermute | solution.py:286
  52.5 1.9 %collective-permute-start.12 = (bf16[400,128]{1,0:T(8,128)(2,1)S(1)}, bf16[400,128]{1,0:T(8,128)(2,1)S(1)}, u32[]{:S(2)}, u32[]{:S(2)}) collective-permute-start(bf16[400,128]{1,0:T(8,128)(2,1)S(1)} %pad_maximum_fusion.4), channel_id=1, source_target_pairs={{0,8},{4,12},{8,0},{12,4},{1,9},{5,13},{9,1},{13,5},{2,10},{6,14},... | collective-permute-start | bytes 307208 | tf_op jit(solution)/shard_map/ppermute | solution.py:286
  54.4 0.7 copy-done.6
  55.0 4.9 %shard_map.112 = bf16[64,64,128]{2,1,0:T(8,128)(2,1)} custom-call(f32[4,64,16]{2,1,0:T(8,128)S(1)} %get-tuple-element.19.inv_ref.refs_1_, bf16[1024,32]{1,0:T(8,128)(2,1)S(1)} %get-tuple-element.20.a_ref.refs_2_, bf16[64,512]{1,0:T(8,128)(2,1)S(1)} %get-tuple-element.21.b_ref, bf16[32,4096]{1,0:T(8,128)(2,1)S(1)} %reshape.291.refs_12_.wc_ref.refs_3_, ...), custom_call_target="tpu_custom_call" | custom-call | flops 5000000000 | bytes 8000000 | tf_op jit(solution)/shard_map/pallas_call | solution.py:448
  60.0 0.0 collective-permute-done.12
  60.0 0.4 collective-permute-start.13
  60.4 0.7 %copy.42 = f32[64,64]{1,0:T(8,128)} copy(f32[64,64]{0,1:T(8,128)S(1)} %slice_bitcast_fusion.2) | data formatting | bytes 32768
  61.1 0.8 %copy-done.1 = bf16[16,16,64]{2,1,0:T(8,128)(2,1)S(1)} copy-done((bf16[16,16,64]{2,1,0:T(8,128)(2,1)S(1)}, bf16[16,16,64]{2,1,0:T(8,128)(2,1)}, u32[]{:S(2)}) %copy-start.1) | copy-done | bytes 32792
  61.9 2.0 %shard_map.114 = f32[256,64]{1,0:T(8,128)} custom-call(bf16[32,256]{1,0:T(8,128)(2,1)S(1)} %bitcast.183, bf16[32,256]{1,0:T(8,128)(2,1)S(1)} %bitcast.184, bf16[16,512]{1,0:T(8,128)(2,1)S(1)} %bitcast.185, bf16[16,512]{1,0:T(8,128)(2,1)S(1)} %bitcast.186, bf16[256,64]{1,0:T(8,128)(2,1)S(1)} %bitcast.180, bf16[256,128]{1,0:T(8,128)(2,1)S(1)} %get-tuple-element.18.refs_5_, ...), custom_call_target="tpu_custom_call" | custom-call | tf_op jit(solution)/shard_map/pallas_call | solution.py:458
  63.9 0.4 collective-permute-done.13
  64.4 0.1 collective-permute-start.14
  64.5 0.5 slice_bitcast_fusion.11
  65.0 0.8 %collective-permute-done.14 = bf16[512,128]{1,0:T(8,128)(2,1)S(1)} collective-permute-done((bf16[512,128]{1,0:T(8,128)(2,1)S(1)}, bf16[512,128]{1,0:T(8,128)(2,1)S(1)}, u32[]{:S(2)}, u32[]{:S(2)}) %collective-permute-start.14) | collective-permute-done | bytes 131104 | tf_op jit(solution)/shard_map/ppermute | solution.py:286
  65.9 1.3 %shard_map.115 = f32[32,32,128]{2,1,0:T(8,128)} custom-call(bf16[32,32,128]{2,1,0:T(8,128)(2,1)S(1)} %bitcast.176), custom_call_target="tpu_custom_call" | custom-call | tf_op jit(solution)/shard_map/pallas_call | solution.py:468
  (62 shorter events, 0.6 us)
Async XLA Ops:
  0.6 0.7 copy-start.4
  1.3 0.8 %copy-start = (bf16[16,16,64]{2,1,0:T(8,128)(2,1)S(1)}, bf16[16,16,64]{2,1,0:T(8,128)(2,1)}, u32[]{:S(2)}) copy-start(bf16[16,16,64]{2,1,0:T(8,128)(2,1)} %param.7) | copy-start | bytes 98308
  2.1 0.7 %copy-start.3 = (s32[16,16]{1,0:T(8,128)S(1)}, s32[16,16]{1,0:T(8,128)}, u32[]{:S(2)}) copy-start(s32[16,16]{1,0:T(8,128)} %cell_ref.1) | copy-start | bytes 3076
  2.8 16.5 %copy-start.5 = (bf16[64,64,128]{2,1,0:T(8,128)(2,1)S(1)}, bf16[64,64,128]{2,1,0:T(8,128)(2,1)}, u32[]{:S(2)}) copy-start(bf16[64,64,128]{2,1,0:T(8,128)(2,1)} %refs_0_.1) | copy-start | bytes 3145732
  3.3 11.0 %collective-permute-start.3 = (bf16[256,128]{1,0:T(8,128)(2,1)S(1)}, bf16[256,128]{1,0:T(8,128)(2,1)S(1)}, u32[]{:S(2)}, u32[]{:S(2)}) collective-permute-start(bf16[256,128]{1,0:T(8,128)(2,1)S(1)} %get-tuple-element.18.refs_5_), channel_id=1, source_target_pairs={{0,0},{1,4},{2,8},{3,12},{4,1},{5,5},{6,9},{7,13},{8,2},{9,6},{10,... | collective-permute-start | bytes 196616 | tf_op jit(solution)/shard_map/ppermute | solution.py:339
  3.9 11.9 %collective-permute-start.4 = (bf16[256,128]{1,0:T(8,128)(2,1)S(1)}, bf16[256,128]{1,0:T(8,128)(2,1)S(1)}, u32[]{:S(2)}, u32[]{:S(2)}) collective-permute-start(bf16[256,128]{1,0:T(8,128)(2,1)S(1)} %get-tuple-element.18.refs_5_), channel_id=1, source_target_pairs={{0,4},{1,8},{2,12},{3,0},{4,5},{5,9},{6,13},{7,1},{8,6},{9,10},{10... | collective-permute-start | bytes 196616 | tf_op jit(solution)/shard_map/ppermute | solution.py:339
  8.3 9.6 %collective-permute-start.5 = (bf16[256,128]{1,0:T(8,128)(2,1)S(1)}, bf16[256,128]{1,0:T(8,128)(2,1)S(1)}, u32[]{:S(2)}, u32[]{:S(2)}) collective-permute-start(bf16[256,128]{1,0:T(8,128)(2,1)S(1)} %get-tuple-element.18.refs_5_), channel_id=1, source_target_pairs={{0,8},{1,12},{2,0},{3,4},{4,9},{5,13},{6,1},{7,5},{8,10},{9,14},{1... | collective-permute-start | bytes 196616 | tf_op jit(solution)/shard_map/ppermute | solution.py:339
  11.6 6.3 %collective-permute-start.6 = (bf16[256,128]{1,0:T(8,128)(2,1)S(1)}, bf16[256,128]{1,0:T(8,128)(2,1)S(1)}, u32[]{:S(2)}, u32[]{:S(2)}) collective-permute-start(bf16[256,128]{1,0:T(8,128)(2,1)S(1)} %get-tuple-element.18.refs_5_), channel_id=1, source_target_pairs={{0,12},{1,0},{2,4},{3,8},{4,13},{5,1},{6,5},{7,9},{8,14},{9,2},{10... | collective-permute-start | bytes 196616 | tf_op jit(solution)/shard_map/ppermute | solution.py:339
  14.3 3.8 %collective-permute-start = (bf16[256,128]{1,0:T(8,128)(2,1)S(1)}, bf16[256,128]{1,0:T(8,128)(2,1)S(1)}, u32[]{:S(2)}, u32[]{:S(2)}) collective-permute-start(bf16[256,128]{1,0:T(8,128)(2,1)S(1)} %get-tuple-element.17.refs_0_), channel_id=1, source_target_pairs={{0,1},{1,2},{2,3},{3,0},{4,5},{5,6},{6,7},{7,4},{8,9},{9,10},{10,1... | collective-permute-start | bytes 196616 | tf_op jit(solution)/shard_map/ppermute | solution.py:332
  14.3 5.0 %collective-permute-start.1 = (bf16[256,128]{1,0:T(8,128)(2,1)S(1)}, bf16[256,128]{1,0:T(8,128)(2,1)S(1)}, u32[]{:S(2)}, u32[]{:S(2)}) collective-permute-start(bf16[256,128]{1,0:T(8,128)(2,1)S(1)} %get-tuple-element.17.refs_0_), channel_id=1, source_target_pairs={{0,2},{1,3},{2,0},{3,1},{4,6},{5,7},{6,4},{7,5},{8,10},{9,11},{10,... | collective-permute-start | bytes 196616 | tf_op jit(solution)/shard_map/ppermute | solution.py:332
  15.8 3.5 %collective-permute-start.2 = (bf16[256,128]{1,0:T(8,128)(2,1)S(1)}, bf16[256,128]{1,0:T(8,128)(2,1)S(1)}, u32[]{:S(2)}, u32[]{:S(2)}) collective-permute-start(bf16[256,128]{1,0:T(8,128)(2,1)S(1)} %get-tuple-element.17.refs_0_), channel_id=1, source_target_pairs={{0,3},{1,0},{2,1},{3,2},{4,7},{5,4},{6,5},{7,6},{8,11},{9,8},{10,9... | collective-permute-start | bytes 196616 | tf_op jit(solution)/shard_map/ppermute | solution.py:332
  16.7 1.1 %copy-start.2 = (bf16[64,64]{1,0:T(8,128)(2,1)S(1)}, bf16[64,64]{1,0:T(8,128)(2,1)}, u32[]{:S(2)}) copy-start(bf16[64,64]{1,0:T(8,128)(2,1)} %refs_9_.1) | copy-start | bytes 24580
  36.9 1.6 %collective-permute-start.9 = (bf16[208,128]{1,0:T(8,128)(2,1)S(1)}, bf16[208,128]{1,0:T(8,128)(2,1)S(1)}, u32[]{:S(2)}, u32[]{:S(2)}) collective-permute-start(bf16[208,128]{1,0:T(8,128)(2,1)S(1)} %pad_maximum_fusion.8), channel_id=1, source_target_pairs={{0,1},{1,0},{2,3},{3,2},{4,5},{5,4},{6,7},{7,6},{8,9},{9,8},{10,11... | collective-permute-start | bytes 159752 | tf_op jit(solution)/shard_map/ppermute | solution.py:286
  38.5 4.2 %collective-permute-start.10 = (bf16[208,128]{1,0:T(8,128)(2,1)S(1)}, bf16[208,128]{1,0:T(8,128)(2,1)S(1)}, u32[]{:S(2)}, u32[]{:S(2)}) collective-permute-start(bf16[208,128]{1,0:T(8,128)(2,1)S(1)} %pad_maximum_fusion.9), channel_id=1, source_target_pairs={{0,2},{1,3},{2,0},{3,1},{4,6},{5,7},{6,4},{7,5},{8,10},{9,11},{10,... | collective-permute-start | bytes 159752 | tf_op jit(solution)/shard_map/ppermute | solution.py:286
  39.7 3.1 %collective-permute-start.7 = (bf16[640,128]{1,0:T(8,128)(2,1)S(1)}, bf16[640,128]{1,0:T(8,128)(2,1)S(1)}, u32[]{:S(2)}, u32[]{:S(2)}) collective-permute-start(bf16[640,128]{1,0:T(8,128)(2,1)S(1)} %pad_maximum_fusion.1), channel_id=1, source_target_pairs={{0,1},{1,0},{2,3},{3,2},{4,5},{5,4},{6,7},{7,6},{8,9},{9,8},{10,11... | collective-permute-start | bytes 491528 | tf_op jit(solution)/shard_map/ppermute | solution.py:286
  43.0 4.5 %collective-permute-start.8 = (bf16[320,128]{1,0:T(8,128)(2,1)S(1)}, bf16[320,128]{1,0:T(8,128)(2,1)S(1)}, u32[]{:S(2)}, u32[]{:S(2)}) collective-permute-start(bf16[320,128]{1,0:T(8,128)(2,1)S(1)} %pad_maximum_fusion.5), channel_id=1, source_target_pairs={{0,2},{1,3},{2,0},{3,1},{4,6},{5,7},{6,4},{7,5},{8,10},{9,11},{10,... | collective-permute-start | bytes 245768 | tf_op jit(solution)/shard_map/ppermute | solution.py:286
  47.5 4.9 %collective-permute-start.11 = (bf16[464,128]{1,0:T(8,128)(2,1)S(1)}, bf16[464,128]{1,0:T(8,128)(2,1)S(1)}, u32[]{:S(2)}, u32[]{:S(2)}) collective-permute-start(bf16[464,128]{1,0:T(8,128)(2,1)S(1)} %pad_maximum_fusion.3), channel_id=1, source_target_pairs={{0,4},{4,0},{8,12},{12,8},{1,5},{5,1},{9,13},{13,9},{2,6},{6,2},{1... | collective-permute-start | bytes 356360 | tf_op jit(solution)/shard_map/ppermute | solution.py:286
  52.5 7.4 %collective-permute-start.12 = (bf16[400,128]{1,0:T(8,128)(2,1)S(1)}, bf16[400,128]{1,0:T(8,128)(2,1)S(1)}, u32[]{:S(2)}, u32[]{:S(2)}) collective-permute-start(bf16[400,128]{1,0:T(8,128)(2,1)S(1)} %pad_maximum_fusion.4), channel_id=1, source_target_pairs={{0,8},{4,12},{8,0},{12,4},{1,9},{5,13},{9,1},{13,5},{2,10},{6,14},... | collective-permute-start | bytes 307208 | tf_op jit(solution)/shard_map/ppermute | solution.py:286
  54.4 0.7 copy-start.6
  60.0 4.3 %collective-permute-start.13 = (bf16[256,128]{1,0:T(8,128)(2,1)S(1)}, bf16[256,128]{1,0:T(8,128)(2,1)S(1)}, u32[]{:S(2)}, u32[]{:S(2)}) collective-permute-start(bf16[256,128]{1,0:T(8,128)(2,1)S(1)} %bitcast.196), channel_id=1, source_target_pairs={{0,2},{1,3},{2,0},{3,1},{4,6},{5,7},{6,4},{7,5},{8,10},{9,11},{10,... | collective-permute-start | bytes 196616 | tf_op jit(solution)/shard_map/ppermute | solution.py:286
  61.1 0.8 %copy-start.1 = (bf16[16,16,64]{2,1,0:T(8,128)(2,1)S(1)}, bf16[16,16,64]{2,1,0:T(8,128)(2,1)}, u32[]{:S(2)}) copy-start(bf16[16,16,64]{2,1,0:T(8,128)(2,1)} %param.7) | copy-start | bytes 98308
  64.4 1.4 %collective-permute-start.14 = (bf16[512,128]{1,0:T(8,128)(2,1)S(1)}, bf16[512,128]{1,0:T(8,128)(2,1)S(1)}, u32[]{:S(2)}, u32[]{:S(2)}) collective-permute-start(bf16[512,128]{1,0:T(8,128)(2,1)S(1)} %bitcast.204), channel_id=1, source_target_pairs={{0,1},{1,0},{2,3},{3,2},{4,5},{5,4},{6,7},{7,6},{8,9},{9,8},{10,11... | collective-permute-start | bytes 393224 | tf_op jit(solution)/shard_map/ppermute | solution.py:286

commit v3 on v2

--- a/solution.py
+++ b/solution.py
@@ -57,16 +57,29 @@
     return center * scale, scale
 
 
-def prep_kernel(depth, own, x_ref, cell_ref, line_ref, by_token_ref, by_row_ref):
+def prep_kernel(depth, own, *refs):
+    by_token_ref, by_row_ref, w_ref, wt_ref, x_ref, offset_ref = refs[5:11]
+    cell_ref, line_ref, factors_ref, sem = refs[11:]
     rows = depth * own
+    targets = (x_ref, cell_ref, line_ref, factors_ref, offset_ref)
+    copies = [
+        pltpu.make_async_copy(src, dst, sem.at[k])
+        for k, (src, dst) in enumerate(zip(refs[:5], targets))
+    ]
+    for copy in copies:
+        copy.start()
+    p, q = iota((rows, rows), 0), iota((rows, rows), 1)
+    swap = one_hot(q == (p % depth) * own + p // depth)
+    pick = one_hot(iota((rows, depth), 0) // own == iota((rows, depth), 1))
+    here = iota((rows, own), 0) % own == iota((rows, own), 1)
+    for copy in copies:
+        copy.wait()
     normed, _ = stats(x_ref[...].astype(F32))
     features = normed.shape[1]
     cell = cell_ref[...].astype(F32).astype(BF16)
-    pick = one_hot(iota((rows, depth), 0) // own == iota((rows, depth), 1))
     line = line_ref[...].astype(F32)
     line_column = jnp.sum(pick.astype(F32) * line, axis=1, keepdims=True)
     cells = dot(pick, cell)
-    here = iota((rows, own), 0) % own == iota((rows, own), 1)
     weight = jnp.sum(jnp.where(here, cells, 0.0), axis=1, keepdims=True) * line_column
     masked = normed.astype(BF16).astype(F32) * weight
     wide = jnp.concatenate([masked, jnp.zeros((rows, LANES - features), F32)], axis=1)
@@ -74,9 +87,14 @@
     at = lane == features + iota((rows, LANES), 0) // own
     wide = (wide + jnp.where(at, weight, 0.0)).astype(BF16)
     by_row_ref[...] = wide
-    p, q = iota((rows, rows), 0), iota((rows, rows), 1)
-    swap = one_hot(q == (p % depth) * own + p // depth)
     by_token_ref[...] = dot(swap, wide).astype(BF16)
+    factors = factors_ref[...]
+    width = factors.shape[1]
+    w_ref[...] = jnp.concatenate([factors, jnp.zeros((LANES - features, width), BF16)], axis=0)
+    same = one_hot(iota((width, width), 0) == iota((width, width), 1))
+    turned = lax.dot_general(same, factors, (((1,), (1,)), ((), ())), preferred_element_type=F32)
+    pad = jnp.zeros((width, LANES - features), F32)
+    wt_ref[...] = jnp.concatenate([turned, pad], axis=1).astype(BF16)
 
 
 def scaled_pair(up_ref, inv, at):
@@ -108,7 +126,7 @@
     return jnp.concatenate([ref[at], ref[at + 1]], axis=1)
 
 
-def weight_kernel(depth, n, pieces, *refs):
+def weight_kernel(depth, features, n, pieces, *refs):
     a_refs, b_refs = refs[:pieces], refs[pieces : 2 * pieces]
     up_ref, w_ref, wt_ref, perm_ref, wc_ref = refs[2 * pieces : 2 * pieces + 5]
     outs = refs[2 * pieces + 5 :]
@@ -116,7 +134,6 @@
     bt_ref, at_ref, v_ref, acc_ref = outs[8:]
     g, last = pl.program_id(0), pl.num_programs(0) - 1
     chunk, block, pair = up_ref.shape
-    features = w_ref.shape[0]
     width = w_ref.shape[1] // 2
     r, c = lax.axis_index("row"), lax.axis_index("col")
 
@@ -135,10 +152,7 @@
                 rows = pl.ds(pl.multiple_of(src * own, own), own)
                 for s in range(depth):
                     mj_ref[s, rows, :] = b_refs[k][s * own : (s + 1) * own, :]
-        pad = jnp.zeros((LANES - features, 2 * width), BF16)
-        w = jnp.concatenate([w_ref[...], pad], axis=0)
-        pad = jnp.zeros((2 * width, LANES - features), BF16)
-        wt = jnp.concatenate([wt_ref[...], pad], axis=1)
+        w, wt = w_ref[...], wt_ref[...]
         mi = mi_ref[...]
         a_ref[...] = dot(mi, w[:, :width]).astype(BF16)
         at_ref[...] = dot_nt(wt[:width, :], mi).astype(BF16)
@@ -182,7 +196,7 @@
         dw_ref[...] = acc_ref[...].astype(BF16)
 
 
-def token_kernel(depth, *refs):
+def token_kernel(depth, features, *refs):
     up_ref, inv_ref, a_ref, wc_ref, mi_ref, mj_ref, perm_ref, bias_ref, da_ref = refs[:9]
     small_ref, out_ref, t_ref, db_ref = refs[9:]
     g, last = pl.program_id(0), pl.num_programs(0) - 1
@@ -210,10 +224,10 @@
         right = jnp.zeros((width, LANES), F32)
         for s in range(depth):
             right = right + dot(turned[s * width : (s + 1) * width, :], mj_ref[s])
-        small_ref[0:width, :] = dot(da_ref[...], mi_ref[...]).astype(BF16)
-        small_ref[width : 2 * width, :] = right.astype(BF16)
-        tail = jnp.broadcast_to(bias_ref[0:1, :], (16, LANES))
-        small_ref[2 * width :, :] = tail.astype(BF16)
+        left = dot(da_ref[...], mi_ref[...])
+        small = jnp.concatenate([left[:, :features], right[:, :features]], axis=1)
+        small_ref[0:width, :] = small.astype(BF16)
+        small_ref[width:, :] = jnp.broadcast_to(bias_ref[0:1, :], (16, LANES)).astype(BF16)
 
 
 def update_kernel(depth, inv_ref, a_ref, b_ref, wc_ref, offset_ref, out_ref, t_ref):
@@ -231,19 +245,15 @@
             out_ref[at + k] = value.astype(BF16)
 
 
-def owner_kernel(depth, own, *refs):
-    da_refs, db_refs = refs[:2], refs[2:4]
-    x_ref, message_ref, wt_ref, perm_ref, out_ref = refs[4:]
+def owner_kernel(depth, own, features, *refs):
+    da_refs, db_ref, small_refs = refs[:2], refs[2], refs[3:5]
+    x_ref, message_ref, wt_ref, perm_ref, out_ref, factors_ref, bias_ref = refs[5:]
     rows = depth * own
     width = wt_ref.shape[0] // 2
-    features = x_ref.shape[1]
     p, q = iota((rows, rows), 0), iota((rows, rows), 1)
     swap = one_hot(q == (p % own) * depth + p // own)
-    d_a = jnp.zeros((rows, width), F32)
-    d_b = jnp.zeros((own, width * depth), F32)
-    for k in range(2):
-        d_a = d_a + dot_nt(swap, da_refs[k][...])
-        d_b = d_b + dot_nt(db_refs[k][...], perm_ref[...])
+    d_a = dot_nt(swap, da_refs[0][...]) + dot_nt(swap, da_refs[1][...])
+    d_b = dot_nt(db_ref[...], perm_ref[...])
     d_b = jnp.concatenate([d_b[:, s * width : (s + 1) * width] for s in range(depth)], axis=0)
     highest = lax.Precision.HIGHEST
     wt = wt_ref[...].astype(F32)
@@ -251,11 +261,16 @@
     d_normed = d_normed + jnp.dot(d_b, wt[width:, :], precision=highest, preferred_element_type=F32)
     message = message_ref[...].astype(F32)
     mask = iota((rows, LANES), 1) >= features
-    d_normed = d_normed * jnp.sum(jnp.where(mask, message, 0.0), axis=1, keepdims=True)
+    weight = jnp.sum(jnp.where(mask, message, 0.0), axis=1, keepdims=True)
+    d_normed = d_normed[:, :features] * weight
     normed, scale = stats(x_ref[...].astype(F32))
     mean = jnp.mean(d_normed, axis=-1, keepdims=True)
     along = jnp.mean(d_normed * normed, axis=-1, keepdims=True)
     out_ref[...] = scale * (d_normed - mean - normed * along)
+    small = small_refs[0][...].astype(F32) + small_refs[1][...].astype(F32)
+    turned = small[:width].T
+    factors_ref[...] = jnp.concatenate([turned[:features], turned[features:]], axis=1)
+    bias_ref[...] = small[width : width + 1]
 
 
 def place_kernel(in_ref, out_ref):
@@ -291,11 +306,14 @@
     return got
 
 
-def halves(x, axis, bit):
-    x = x.reshape((x.shape[0] // 2, 2) + x.shape[1:])
+def halves(x, axis, bit, at):
     here = bit_of(axis, bit)
-    keep = lax.dynamic_index_in_dim(x, here, 1, keepdims=False)
-    return keep, lax.dynamic_index_in_dim(x, 1 - here, 1, keepdims=False)
+    keep = lax.dynamic_index_in_dim(x, here, at, keepdims=False)
+    return keep, lax.dynamic_index_in_dim(x, 1 - here, at, keepdims=False)
+
+
+def split_high(x):
+    return x.reshape((2, x.shape[0] // 2) + x.shape[1:])
 
 
 def in_order(mine, other, axis, bit, at):
@@ -340,13 +358,25 @@
 
     r, c = lax.axis_index("row"), lax.axis_index("col")
     x = alignment_embedding.reshape(rows, features)
-    by_token, by_row = call(
+    line = alignment_lines_exist.reshape(1, depth)
+    offset = offset_vector.reshape(1, pair)
+    args = (x, alignment_cell_exists, line, sitewise_factors, offset)
+    out_shapes = [
+        sds((rows, LANES), BF16),
+        sds((rows, LANES), BF16),
+        sds((LANES, 2 * width), BF16),
+        sds((2 * width, LANES), BF16),
+        sds(x.shape, x.dtype),
+        sds(offset.shape, F32),
+    ]
+    by_token, by_row, factors, factors_t, x, offset = call(
         functools.partial(prep_kernel, depth, own),
         (),
-        [full(x.shape), full(alignment_cell_exists.shape), full((1, depth))],
-        [full((rows, LANES))] * 2,
-        [sds((rows, LANES), BF16)] * 2,
-    )(x, alignment_cell_exists, alignment_lines_exist.reshape(1, depth))
+        [pl.BlockSpec(memory_space=pl.ANY)] * len(args),
+        [full(o.shape) for o in out_shapes],
+        out_shapes,
+        [pltpu.VMEM(v.shape, v.dtype) for v in args[1:4]] + [pltpu.SemaphoreType.DMA((5,))],
+    )(*args)
     a_pieces = [by_token] + [along_col(by_token, k) for k in range(1, n)]
     b_pieces = [to_column(by_row, k) for k in range(n)]
     if not split:
@@ -362,7 +392,6 @@
     wide = width * depth
     source = jnp.arange(wide)
     perm = (jnp.arange(wide)[None, :] == (source % width * depth + source // width)[:, None]).astype(BF16)
-    factors_t = sitewise_factors.T
     pairing_wide = pairing_matrix.reshape(width, width * pair)
     up_spec = pl.BlockSpec((chunk, block, pair), lambda g: (g, 0, 0))
     tokens = block * depth
@@ -377,12 +406,12 @@
         sds((width, tokens), BF16),
     ]
     outs = call(
-        functools.partial(weight_kernel, depth, n, pieces),
+        functools.partial(weight_kernel, depth, features, n, pieces),
         (steps,),
         [full(p.shape) for p in a_pieces]
         + [full(p.shape) for p in b_pieces]
         + [up_spec]
-        + [full(v.shape) for v in (sitewise_factors, factors_t, perm, pairing_wide)],
+        + [full(v.shape) for v in (factors, factors_t, perm, pairing_wide)],
         [full(o.shape) for o in out_shapes],
         out_shapes,
         [
@@ -392,25 +421,22 @@
             pltpu.VMEM((width * width, pair), F32),
         ],
         cost(5e9, 8e6),
-    )(*a_pieces, *b_pieces, upstream_adjoint, sitewise_factors, factors_t, perm, pairing_wide)
+    )(*a_pieces, *b_pieces, upstream_adjoint, factors, factors_t, perm, pairing_wide)
     mi, mj, a, b, inv, bias, d_pairing, d_a = outs
 
     bits = n.bit_length() - 1
     d_pairing = d_pairing.reshape(n, -1, LANES)
+    da_all = d_a
     d_a = jnp.stack([lay_out(d_a[:, k * rows : (k + 1) * rows]) for k in range(n)])
-    da_parts = [d_a]
-    for bit in range(bits):
-        keep, go = halves(d_pairing, "col", bit)
-        if bit:
-            d_a = add(*da_parts)
-        da_keep, da_go = halves(d_a, "col", bit)
-        got, da_got = swap_parts([go, da_go], "col", bit, n)
-        d_pairing = add(keep, got)
-        da_parts = [da_keep, da_got.reshape(da_keep.shape)]
-
-    out_shapes = [sds((2 * width + 16, LANES), BF16), sds((block, wide), BF16)]
+    for bit in reversed(range(1, bits)):
+        dp_keep, dp_go = halves(split_high(d_pairing), "col", bit, 0)
+        da_keep, da_go = halves(split_high(d_a), "col", bit, 0)
+        dp_got, da_got = swap_parts([dp_go, da_go], "col", bit, n)
+        d_pairing, d_a = add(dp_keep, dp_got), add(da_keep, da_got)
+
+    out_shapes = [sds((width + 16, LANES), BF16), sds((block, wide), BF16)]
     small, d_b = call(
-        functools.partial(token_kernel, depth),
+        functools.partial(token_kernel, depth, features),
         (steps,),
         [up_spec]
         + [full(v.shape) for v in (inv, a, pairing_wide, mi, mj, perm, bias)]
@@ -419,31 +445,38 @@
         out_shapes,
         [pltpu.VMEM((chunk, wide, pair), BF16), pltpu.VMEM((block, wide), F32)],
         cost(5e9, 8e6),
-    )(upstream_adjoint, inv, a, pairing_wide, mi, mj, perm, bias, outs[7])
-
-    d_b = jnp.stack([lay_out(d_b[k * own : (k + 1) * own]) for k in range(n)])[:, None]
+    )(upstream_adjoint, inv, a, pairing_wide, mi, mj, perm, bias, da_all)
+
+    d_b = jnp.stack([lay_out(d_b[k * own : (k + 1) * own]) for k in range(n)])
+    dp_keep, dp_go = halves(d_pairing, "col", 0, 0)
+    da_keep, da_go = halves(d_a, "col", 0, 0)
+    db_keep, db_go = halves(d_b.reshape((n // 2, 2) + d_b.shape[1:]), "col", 0, 1)
+    parts = swap_parts([dp_go, da_go, db_go, small], "col", 0, n)
+    d_pairing, small = add(dp_keep, parts[0]), add(small, parts[3])
+    da_parts = [da_keep, parts[1]]
+    d_b = in_order(db_keep, parts[2].reshape(db_keep.shape), "col", 0, 1)
+    db_keep, db_go = halves(d_b, "row", 0, 1)
     for bit in range(bits):
-        keep, go = halves(d_b, "col", bit)
-        got, small_got = swap_parts([go, small], "col", bit, n)
-        small = add(small, small_got)
-        d_b = in_order(keep, got.reshape(keep.shape), "col", bit, 1)
-        d_b = d_b.reshape((keep.shape[0], -1) + keep.shape[2:])
-    db_parts = [d_b[0]]
-    for bit in range(bits):
-        if bit:
-            db_parts = [add(*db_parts)]
-        db_keep, db_go = halves(db_parts[0], "row", bit)
-        got, db_got, small_got = swap_parts([d_pairing, db_go, small], "row", bit, n)
-        d_pairing = add(d_pairing, got)
-        small = add(small, small_got)
-        db_parts = [db_keep, db_got.reshape(db_keep.shape)]
+        parts = swap_parts([d_pairing, db_go, small], "row", bit, n)
+        d_pairing, d_b, small = add(d_pairing, parts[0]), add(db_keep, parts[1]), add(small, parts[2])
+        db_keep = db_go = d_b
     d_pairing = d_pairing.reshape(1, -1, LANES)
-    for bit in reversed(range(bits)):
-        (got,) = swap_parts([d_pairing], "col", bit, n)
-        d_pairing = in_order(d_pairing, got.reshape(d_pairing.shape), "col", bit, 1)
+    small_parts = [small, None]
+    for bit in range(1, bits):
+        if bit > 1:
+            small_parts[0] = add(*small_parts)
+        db_keep, db_go = halves(split_high(d_b), "col", bits - bit, 0)
+        parts = swap_parts([d_pairing, db_go, small_parts[0]], "col", bits - bit, n)
+        got = parts[0].reshape(d_pairing.shape)
+        d_pairing = in_order(d_pairing, got, "col", bits - bit, 1)
         d_pairing = d_pairing.reshape((-1,) + d_pairing.shape[2:])
-    d_a = [lay_back(part[0], width, rows) for part in da_parts]
-    d_b = [lay_back(part[0], own, wide) for part in db_parts]
+        mine = bit_of("col", bits - bit) == bit_of("row", bits - bit)
+        d_b = jnp.where(mine, db_keep, parts[1].reshape(db_keep.shape))
+        small_parts[1] = parts[2]
+    (got,) = swap_parts([d_pairing], "col", 0, n)
+    d_pairing = in_order(d_pairing, got.reshape(d_pairing.shape), "col", 0, 1)
+    d_a = [lay_back(part.reshape(-1, LANES), width, rows) for part in da_parts]
+    d_b = lay_back(d_b[0], own, wide)
 
     coupling_update = call(
         functools.partial(update_kernel, depth),
@@ -453,16 +486,17 @@
         sds((block, block, pair), BF16),
         [pltpu.VMEM((chunk, wide, pair), BF16)],
         cost(5e9, 8e6),
-    )(inv, a, b, pairing_wide, offset_vector.reshape(1, pair))
-
-    embedding_adjoint = call(
-        functools.partial(owner_kernel, depth, own),
+    )(inv, a, b, pairing_wide, offset)
+
+    args = (*d_a, d_b, *small_parts, x, by_row, factors_t, perm)
+    out_shapes = [sds((rows, features), F32), sds((features, 2 * width), F32), sds((1, pair), F32)]
+    embedding_adjoint, factors_adjoint, offset_slope = call(
+        functools.partial(owner_kernel, depth, own, features),
         (),
-        [full(v.shape) for v in d_a + d_b]
-        + [full(v.shape) for v in (x, by_row, factors_t, perm)],
-        full((rows, features)),
-        sds((rows, features), F32),
-    )(*d_a, *d_b, x, by_row, factors_t, perm)
+        [full(v.shape) for v in args],
+        [full(o.shape) for o in out_shapes],
+        out_shapes,
+    )(*args)
 
     d_pairing = d_pairing.reshape(width, width, pair)
     placed = call(
@@ -472,14 +506,12 @@
         full((width, width, pair)),
         sds((width, width, pair), F32),
     )(d_pairing)
-    small = small.astype(F32)
-    factors = jnp.concatenate([small[:width], small[width : 2 * width]], axis=0)
     return (
         coupling_update,
         embedding_adjoint.reshape(depth, own, features),
-        factors[:, :features].T,
+        factors_adjoint,
         placed.reshape(width * width, pair),
-        small[2 * width],
+        offset_slope.reshape(pair),
     )
 
 

time: 67.4 us -> 63.9 us (0.948)
  local copies, waits for them, and re-layouts: 6.26 us -> 4.17 us
  starting transfers between devices: 19.7 us -> 18.2 us
    unnamed x20 -> x14, local copies, waits for them, and re-layouts: 4.48 us -> 2.93 us
    ppermute x8 -> x6, starting transfers between devices: 6.44 us -> 4.99 us  [swap_parts(): message = lax.ppermute(message, axis, [(i, i ^ 1 << bit) for i in range(n)])]
    ppermute x8 -> x6, waiting for transfers between devices: 12.2 us -> 11.9 us  [swap_parts(): message = lax.ppermute(message, axis, [(i, i ^ 1 << bit) for i in range(n)])]
  transfers between devices with their start and end apart: 15 -> 13, of which waited for: 8 -> 5; matrix products, arithmetic and copies ran while one was open for 4% -> 2% of each run, Pallas kernels for 10% -> 20%
where the time goes in v3:
time: 63.9 us; the launch traced here: 63.5 us
  Pallas kernels  26.1 us (41%)
  starting transfers between devices  18.2 us (28%)
  waiting for transfers between devices  13.4 us (21%)
  local copies, waits for them, and re-layouts  4.17 us (7%)
  between operations  1.09 us (2%)
    ppermute x6, waiting for transfers between devices, swap_parts(): message = lax.ppermute(message, axis, [(i, i ^ 1 << bit) for i in range(n)])  11.9 us
    pallas_call x1, Pallas kernels, per_device(): call(functools.partial(weight_kernel, depth, features, n, pieces), (steps...  11.6 us
    ppermute x4, starting transfers between devices, to_column(): return lax.ppermute(x, axes, pairs)  11 us
    pallas_call x1, Pallas kernels, per_device(): call(functools.partial(token_kernel, depth, features), (steps,), [up_spec...  5.89 us
    ppermute x6, starting transfers between devices, swap_parts(): message = lax.ppermute(message, axis, [(i, i ^ 1 << bit) for i in range(n)])  4.99 us
    pallas_call x1, Pallas kernels, per_device(): call(functools.partial(update_kernel, depth), (steps,), [full(v.shape) fo...  4.87 us
    unnamed x14, local copies, waits for them, and re-layouts  2.93 us
    ppermute x3, starting transfers between devices, along_col(): return lax.ppermute(x, 'col', [(i, (i + k) % n) for i in range(n)])  2.23 us
  transfers between devices with their start and end apart: 13, of which 5 were waited for; matrix products, arithmetic and copies ran while one was open for 2% of the time, Pallas kernels for 20%

profile of v3, /device:TPU:0, one launch (start us, length us, event | category | flops | bytes accessed | tf_op | source)
XLA Modules:
  0.0 63.5 jit_solution(9661387823301736901)
XLA Ops:
  0.6 0.0 copy-start.3
  0.6 0.0 copy-start.4
  0.7 0.6 %copy-done.3 = s32[16]{0:T(128)S(1)} copy-done((s32[16]{0:T(128)S(1)}, s32[16]{0:T(128)}, u32[]{:S(2)}) %copy-start.3) | copy-done | bytes 88
  1.3 0.0 copy-done.4
  1.3 0.0 copy-start
  1.3 0.8 %copy-done = bf16[16,16,64]{2,1,0:T(8,128)(2,1)S(1)} copy-done((bf16[16,16,64]{2,1,0:T(8,128)(2,1)S(1)}, bf16[16,16,64]{2,1,0:T(8,128)(2,1)}, u32[]{:S(2)}) %copy-start) | copy-done | bytes 32792
  2.1 0.0 copy-start.1
  2.1 0.7 %copy-done.1 = bf16[64,64]{1,0:T(8,128)(2,1)S(1)} copy-done((bf16[64,64]{1,0:T(8,128)(2,1)S(1)}, bf16[64,64]{1,0:T(8,128)(2,1)}, u32[]{:S(2)}) %copy-start.1) | copy-done | bytes 8216
  2.9 0.0 copy-start.2
  2.9 0.7 %copy-done.2 = s32[16,16]{1,0:T(8,128)S(1)} copy-done((s32[16,16]{1,0:T(8,128)S(1)}, s32[16,16]{1,0:T(8,128)}, u32[]{:S(2)}) %copy-start.2) | copy-done | bytes 1048
  3.6 0.0 copy-start.5
  3.6 0.6 shard_map.110
  4.2 0.7 %collective-permute-start.3 = (bf16[256,128]{1,0:T(8,128)(2,1)S(1)}, bf16[256,128]{1,0:T(8,128)(2,1)S(1)}, u32[]{:S(2)}, u32[]{:S(2)}) collective-permute-start(bf16[256,128]{1,0:T(8,128)(2,1)S(1)} %get-tuple-element.25.refs_6_), channel_id=1, source_target_pairs={{0,0},{1,4},{2,8},{3,12},{4,1},{5,5},{6,9},{7,13},{8,2},{9,6},{10,... | collective-permute-start | bytes 196616 | tf_op jit(solution)/shard_map/ppermute | solution.py:357
  4.9 4.3 %collective-permute-start.4 = (bf16[256,128]{1,0:T(8,128)(2,1)S(1)}, bf16[256,128]{1,0:T(8,128)(2,1)S(1)}, u32[]{:S(2)}, u32[]{:S(2)}) collective-permute-start(bf16[256,128]{1,0:T(8,128)(2,1)S(1)} %get-tuple-element.25.refs_6_), channel_id=1, source_target_pairs={{0,4},{1,8},{2,12},{3,0},{4,5},{5,9},{6,13},{7,1},{8,6},{9,10},{10... | collective-permute-start | bytes 196616 | tf_op jit(solution)/shard_map/ppermute | solution.py:357
  9.2 3.4 %collective-permute-start.5 = (bf16[256,128]{1,0:T(8,128)(2,1)S(1)}, bf16[256,128]{1,0:T(8,128)(2,1)S(1)}, u32[]{:S(2)}, u32[]{:S(2)}) collective-permute-start(bf16[256,128]{1,0:T(8,128)(2,1)S(1)} %get-tuple-element.25.refs_6_), channel_id=1, source_target_pairs={{0,8},{1,12},{2,0},{3,4},{4,9},{5,13},{6,1},{7,5},{8,10},{9,14},{1... | collective-permute-start | bytes 196616 | tf_op jit(solution)/shard_map/ppermute | solution.py:357
  12.6 2.6 %collective-permute-start.6 = (bf16[256,128]{1,0:T(8,128)(2,1)S(1)}, bf16[256,128]{1,0:T(8,128)(2,1)S(1)}, u32[]{:S(2)}, u32[]{:S(2)}) collective-permute-start(bf16[256,128]{1,0:T(8,128)(2,1)S(1)} %get-tuple-element.25.refs_6_), channel_id=1, source_target_pairs={{0,12},{1,0},{2,4},{3,8},{4,13},{5,1},{6,5},{7,9},{8,14},{9,2},{10... | collective-permute-start | bytes 196616 | tf_op jit(solution)/shard_map/ppermute | solution.py:357
  15.2 0.0 collective-permute-start
  15.2 0.0 collective-permute-done.3.refs_4_
  15.2 1.5 %collective-permute-start.1 = (bf16[256,128]{1,0:T(8,128)(2,1)S(1)}, bf16[256,128]{1,0:T(8,128)(2,1)S(1)}, u32[]{:S(2)}, u32[]{:S(2)}) collective-permute-start(bf16[256,128]{1,0:T(8,128)(2,1)S(1)} %get-tuple-element.24.refs_0_), channel_id=1, source_target_pairs={{0,2},{1,3},{2,0},{3,1},{4,6},{5,7},{6,4},{7,5},{8,10},{9,11},{10,... | collective-permute-start | bytes 196616 | tf_op jit(solution)/shard_map/ppermute | solution.py:350
  16.7 0.0 collective-permute-done.4.refs_5_
  16.7 0.7 %collective-permute-start.2 = (bf16[256,128]{1,0:T(8,128)(2,1)S(1)}, bf16[256,128]{1,0:T(8,128)(2,1)S(1)}, u32[]{:S(2)}, u32[]{:S(2)}) collective-permute-start(bf16[256,128]{1,0:T(8,128)(2,1)S(1)} %get-tuple-element.24.refs_0_), channel_id=1, source_target_pairs={{0,3},{1,0},{2,1},{3,2},{4,7},{5,4},{6,5},{7,6},{8,11},{9,8},{10,9... | collective-permute-start | bytes 196616 | tf_op jit(solution)/shard_map/ppermute | solution.py:350
  17.5 0.1 fusion.refs_11_.refs_6_.refs_8_
  17.6 1.1 %reshape.208.refs_12_.wc_ref.refs_3_ = bf16[32,4096]{1,0:T(8,128)(2,1)S(1)} reshape(bf16[1024,128]{1,0:T(8,128)(2,1)} %param.11) | data formatting | bytes 524288 | tf_op jit(solution)/shard_map/reshape | solution.py:395
  18.7 0.0 collective-permute-done.5.refs_6_
  18.7 0.0 collective-permute-done.6.refs_7_
  18.7 0.3 collective-permute-done.refs_1_
  19.0 1.2 %collective-permute-done.1.refs_2_ = bf16[256,128]{1,0:T(8,128)(2,1)S(1)} collective-permute-done((bf16[256,128]{1,0:T(8,128)(2,1)S(1)}, bf16[256,128]{1,0:T(8,128)(2,1)S(1)}, u32[]{:S(2)}, u32[]{:S(2)}) %collective-permute-start.1) | collective-permute-done | bytes 65568 | tf_op jit(solution)/shard_map/ppermute | solution.py:350
  20.2 0.0 collective-permute-done.2.refs_3_
  20.2 0.0 copy-done.5
  20.2 11.6 %shard_map.111 = (bf16[1024,128]{1,0:T(8,128)(2,1)S(1)}, bf16[16,64,128]{2,1,0:T(8,128)(2,1)S(1)}, bf16[1024,32]{1,0:T(8,128)(2,1)S(1)}, bf16[64,512]{1,0:T(8,12...) custom-call(bf16[256,128]{1,0:T(8,128)(2,1)S(1)} %get-tuple-element., ...), custom_call_target="tpu_custom_call" | custom-call | flops 5000000000 | bytes 8000000 | tf_op jit(solution)/shard_map/pallas_call | solution.py:408
  31.9 1.2 %collective-permute-start.7 = (bf16[640,128]{1,0:T(8,128)(2,1)S(1)}, bf16[640,128]{1,0:T(8,128)(2,1)S(1)}, u32[]{:S(2)}, u32[]{:S(2)}) collective-permute-start(bf16[640,128]{1,0:T(8,128)(2,1)S(1)} %pad_maximum_fusion.1), channel_id=1, source_target_pairs={{0,2},{1,3},{2,0},{3,1},{4,6},{5,7},{6,4},{7,5},{8,10},{9,11},{10,... | collective-permute-start | bytes 491528 | tf_op jit(solution)/shard_map/ppermute | solution.py:301
  33.1 5.9 %shard_map.113 = (bf16[48,128]{1,0:T(8,128)(2,1)S(1)}, bf16[64,512]{1,0:T(8,128)(2,1)S(1)}) custom-call(bf16[64,64,128]{2,1,0:T(8,128)(2,1)S(1)} %copy-done.5, f32[4,64,16]{2,1,0:T(8,128)S(1)} %get-tuple-element.28.inv_ref.refs_1_, bf16[1024,32]{1,0:T(8,128)(2,1)S(1)} %get-tuple-element.29.a_ref.refs_2_, ...), custom_call_target="tpu_custom_call" | custom-call | flops 5000000000 | bytes 8000000 | tf_op jit(solution)/shard_map/pallas_call | solution.py:438
  39.1 0.0 collective-permute-done.7
  39.3 0.3 collective-permute-start.8
  39.6 1.1 %collective-permute-done.8 = bf16[496,128]{1,0:T(8,128)(2,1)S(1)} collective-permute-done((bf16[496,128]{1,0:T(8,128)(2,1)S(1)}, bf16[496,128]{1,0:T(8,128)(2,1)S(1)}, u32[]{:S(2)}, u32[]{:S(2)}) %collective-permute-start.8) | collective-permute-done | bytes 127008 | tf_op jit(solution)/shard_map/ppermute | solution.py:301
  40.8 0.7 %collective-permute-start.9 = (bf16[432,128]{1,0:T(8,128)(2,1)S(1)}, bf16[432,128]{1,0:T(8,128)(2,1)S(1)}, u32[]{:S(2)}, u32[]{:S(2)}) collective-permute-start(bf16[432,128]{1,0:T(8,128)(2,1)S(1)} %pad_maximum_fusion.4), channel_id=1, source_target_pairs={{0,4},{4,0},{8,12},{12,8},{1,5},{5,1},{9,13},{13,9},{2,6},{6,2},{1... | collective-permute-start | bytes 331784 | tf_op jit(solution)/shard_map/ppermute | solution.py:301
  41.6 4.6 %collective-permute-done.9 = bf16[432,128]{1,0:T(8,128)(2,1)S(1)} collective-permute-done((bf16[432,128]{1,0:T(8,128)(2,1)S(1)}, bf16[432,128]{1,0:T(8,128)(2,1)S(1)}, u32[]{:S(2)}, u32[]{:S(2)}) %collective-permute-start.9) | collective-permute-done | bytes 110624 | tf_op jit(solution)/shard_map/ppermute | solution.py:301
  46.2 1.4 %collective-permute-start.10 = (bf16[432,128]{1,0:T(8,128)(2,1)S(1)}, bf16[432,128]{1,0:T(8,128)(2,1)S(1)}, u32[]{:S(2)}, u32[]{:S(2)}) collective-permute-start(bf16[432,128]{1,0:T(8,128)(2,1)S(1)} %pad_maximum_fusion.5), channel_id=1, source_target_pairs={{0,8},{4,12},{8,0},{12,4},{1,9},{5,13},{9,1},{13,5},{2,10},{6,14},... | collective-permute-start | bytes 331784 | tf_op jit(solution)/shard_map/ppermute | solution.py:301
  47.6 6.2 %collective-permute-done.10 = bf16[432,128]{1,0:T(8,128)(2,1)S(1)} collective-permute-done((bf16[432,128]{1,0:T(8,128)(2,1)S(1)}, bf16[432,128]{1,0:T(8,128)(2,1)S(1)}, u32[]{:S(2)}, u32[]{:S(2)}) %collective-permute-start.10) | collective-permute-done | bytes 110624 | tf_op jit(solution)/shard_map/ppermute | solution.py:301
  53.9 1.3 %collective-permute-start.11 = (bf16[368,128]{1,0:T(8,128)(2,1)S(1)}, bf16[368,128]{1,0:T(8,128)(2,1)S(1)}, u32[]{:S(2)}, u32[]{:S(2)}) collective-permute-start(bf16[368,128]{1,0:T(8,128)(2,1)S(1)} %pad_maximum_fusion.6), channel_id=1, source_target_pairs={{0,2},{1,3},{2,0},{3,1},{4,6},{5,7},{6,4},{7,5},{8,10},{9,11},{10,... | collective-permute-start | bytes 282632 | tf_op jit(solution)/shard_map/ppermute | solution.py:301
  55.2 4.9 %shard_map.112 = bf16[64,64,128]{2,1,0:T(8,128)(2,1)} custom-call(f32[4,64,16]{2,1,0:T(8,128)S(1)} %get-tuple-element.28.inv_ref.refs_1_, bf16[1024,32]{1,0:T(8,128)(2,1)S(1)} %get-tuple-element.29.a_ref.refs_2_, bf16[64,512]{1,0:T(8,128)(2,1)S(1)} %get-tuple-element.30.b_ref, bf16[32,4096]{1,0:T(8,128)(2,1)S(1)} %reshape.208.refs_12_.wc_ref.refs_3_, ...), custom_call_target="tpu_custom_call" | custom-call | flops 5000000000 | bytes 8000000 | tf_op jit(solution)/shard_map/pallas_call | solution.py:481
  60.1 0.0 collective-permute-done.11
  60.2 0.1 collective-permute-start.12
  60.3 1.9 %shard_map.114 = (f32[256,64]{1,0:T(8,128)}, f32[64,64]{1,0:T(8,128)}, f32[1,128]{1,0:T(1,128)}) custom-call(bf16[32,256]{1,0:T(8,128)(2,1)S(1)} %bitcast.137, bf16[32,256]{1,0:T(8,128)(2,1)S(1)} %bitcast.138, bf16[16,512]{1,0:T(8,128)(2,1)S(1)} %bitcast.139, bf16[48,128]{1,0:T(8,128)(2,1)S(1)} %add_convert_fusion.2.refs_3_, ...), custom_call_target="tpu_custom_call" | custom-call | tf_op jit(solution)/shard_map/pallas_call | solution.py:493
  62.2 0.0 collective-permute-done.12
  62.3 1.3 %shard_map.115 = f32[32,32,128]{2,1,0:T(8,128)} custom-call(bf16[32,32,128]{2,1,0:T(8,128)(2,1)S(1)} %bitcast.134), custom_call_target="tpu_custom_call" | custom-call | tf_op jit(solution)/shard_map/pallas_call | solution.py:502
  (48 shorter events, 0.6 us)
Async XLA Ops:
  0.6 0.7 %copy-start.3 = (s32[16]{0:T(128)S(1)}, s32[16]{0:T(128)}, u32[]{:S(2)}) copy-start(s32[16]{0:T(128)} %param.9) | copy-start | bytes 196
  0.6 0.7 %copy-start.4 = (f32[128]{0:T(128)S(1)}, f32[128]{0:T(128)}, u32[]{:S(2)}) copy-start(f32[128]{0:T(128)} %param.12) | copy-start | bytes 1540
  1.3 0.8 %copy-start = (bf16[16,16,64]{2,1,0:T(8,128)(2,1)S(1)}, bf16[16,16,64]{2,1,0:T(8,128)(2,1)}, u32[]{:S(2)}) copy-start(bf16[16,16,64]{2,1,0:T(8,128)(2,1)} %param.7) | copy-start | bytes 98308
  2.1 0.7 %copy-start.1 = (bf16[64,64]{1,0:T(8,128)(2,1)S(1)}, bf16[64,64]{1,0:T(8,128)(2,1)}, u32[]{:S(2)}) copy-start(bf16[64,64]{1,0:T(8,128)(2,1)} %refs_3_.1) | copy-start | bytes 24580
  2.9 0.7 %copy-start.2 = (s32[16,16]{1,0:T(8,128)S(1)}, s32[16,16]{1,0:T(8,128)}, u32[]{:S(2)}) copy-start(s32[16,16]{1,0:T(8,128)} %refs_1_.1) | copy-start | bytes 3076
  3.6 16.7 %copy-start.5 = (bf16[64,64,128]{2,1,0:T(8,128)(2,1)S(1)}, bf16[64,64,128]{2,1,0:T(8,128)(2,1)}, u32[]{:S(2)}) copy-start(bf16[64,64,128]{2,1,0:T(8,128)(2,1)} %refs_0_.1) | copy-start | bytes 3145732
  4.2 11.0 %collective-permute-start.3 = (bf16[256,128]{1,0:T(8,128)(2,1)S(1)}, bf16[256,128]{1,0:T(8,128)(2,1)S(1)}, u32[]{:S(2)}, u32[]{:S(2)}) collective-permute-start(bf16[256,128]{1,0:T(8,128)(2,1)S(1)} %get-tuple-element.25.refs_6_), channel_id=1, source_target_pairs={{0,0},{1,4},{2,8},{3,12},{4,1},{5,5},{6,9},{7,13},{8,2},{9,6},{10,... | collective-permute-start | bytes 196616 | tf_op jit(solution)/shard_map/ppermute | solution.py:357
  4.9 11.9 %collective-permute-start.4 = (bf16[256,128]{1,0:T(8,128)(2,1)S(1)}, bf16[256,128]{1,0:T(8,128)(2,1)S(1)}, u32[]{:S(2)}, u32[]{:S(2)}) collective-permute-start(bf16[256,128]{1,0:T(8,128)(2,1)S(1)} %get-tuple-element.25.refs_6_), channel_id=1, source_target_pairs={{0,4},{1,8},{2,12},{3,0},{4,5},{5,9},{6,13},{7,1},{8,6},{9,10},{10... | collective-permute-start | bytes 196616 | tf_op jit(solution)/shard_map/ppermute | solution.py:357
  9.2 9.5 %collective-permute-start.5 = (bf16[256,128]{1,0:T(8,128)(2,1)S(1)}, bf16[256,128]{1,0:T(8,128)(2,1)S(1)}, u32[]{:S(2)}, u32[]{:S(2)}) collective-permute-start(bf16[256,128]{1,0:T(8,128)(2,1)S(1)} %get-tuple-element.25.refs_6_), channel_id=1, source_target_pairs={{0,8},{1,12},{2,0},{3,4},{4,9},{5,13},{6,1},{7,5},{8,10},{9,14},{1... | collective-permute-start | bytes 196616 | tf_op jit(solution)/shard_map/ppermute | solution.py:357
  12.6 6.1 %collective-permute-start.6 = (bf16[256,128]{1,0:T(8,128)(2,1)S(1)}, bf16[256,128]{1,0:T(8,128)(2,1)S(1)}, u32[]{:S(2)}, u32[]{:S(2)}) collective-permute-start(bf16[256,128]{1,0:T(8,128)(2,1)S(1)} %get-tuple-element.25.refs_6_), channel_id=1, source_target_pairs={{0,12},{1,0},{2,4},{3,8},{4,13},{5,1},{6,5},{7,9},{8,14},{9,2},{10... | collective-permute-start | bytes 196616 | tf_op jit(solution)/shard_map/ppermute | solution.py:357
  15.2 3.8 %collective-permute-start = (bf16[256,128]{1,0:T(8,128)(2,1)S(1)}, bf16[256,128]{1,0:T(8,128)(2,1)S(1)}, u32[]{:S(2)}, u32[]{:S(2)}) collective-permute-start(bf16[256,128]{1,0:T(8,128)(2,1)S(1)} %get-tuple-element.24.refs_0_), channel_id=1, source_target_pairs={{0,1},{1,2},{2,3},{3,0},{4,5},{5,6},{6,7},{7,4},{8,9},{9,10},{10,1... | collective-permute-start | bytes 196616 | tf_op jit(solution)/shard_map/ppermute | solution.py:350
  15.2 5.0 %collective-permute-start.1 = (bf16[256,128]{1,0:T(8,128)(2,1)S(1)}, bf16[256,128]{1,0:T(8,128)(2,1)S(1)}, u32[]{:S(2)}, u32[]{:S(2)}) collective-permute-start(bf16[256,128]{1,0:T(8,128)(2,1)S(1)} %get-tuple-element.24.refs_0_), channel_id=1, source_target_pairs={{0,2},{1,3},{2,0},{3,1},{4,6},{5,7},{6,4},{7,5},{8,10},{9,11},{10,... | collective-permute-start | bytes 196616 | tf_op jit(solution)/shard_map/ppermute | solution.py:350
  16.7 3.5 %collective-permute-start.2 = (bf16[256,128]{1,0:T(8,128)(2,1)S(1)}, bf16[256,128]{1,0:T(8,128)(2,1)S(1)}, u32[]{:S(2)}, u32[]{:S(2)}) collective-permute-start(bf16[256,128]{1,0:T(8,128)(2,1)S(1)} %get-tuple-element.24.refs_0_), channel_id=1, source_target_pairs={{0,3},{1,0},{2,1},{3,2},{4,7},{5,4},{6,5},{7,6},{8,11},{9,8},{10,9... | collective-permute-start | bytes 196616 | tf_op jit(solution)/shard_map/ppermute | solution.py:350
  31.9 7.2 %collective-permute-start.7 = (bf16[640,128]{1,0:T(8,128)(2,1)S(1)}, bf16[640,128]{1,0:T(8,128)(2,1)S(1)}, u32[]{:S(2)}, u32[]{:S(2)}) collective-permute-start(bf16[640,128]{1,0:T(8,128)(2,1)S(1)} %pad_maximum_fusion.1), channel_id=1, source_target_pairs={{0,2},{1,3},{2,0},{3,1},{4,6},{5,7},{6,4},{7,5},{8,10},{9,11},{10,... | collective-permute-start | bytes 491528 | tf_op jit(solution)/shard_map/ppermute | solution.py:301
  39.3 1.4 %collective-permute-start.8 = (bf16[496,128]{1,0:T(8,128)(2,1)S(1)}, bf16[496,128]{1,0:T(8,128)(2,1)S(1)}, u32[]{:S(2)}, u32[]{:S(2)}) collective-permute-start(bf16[496,128]{1,0:T(8,128)(2,1)S(1)} %pad_maximum_fusion.3), channel_id=1, source_target_pairs={{0,1},{1,0},{2,3},{3,2},{4,5},{5,4},{6,7},{7,6},{8,9},{9,8},{10,11... | collective-permute-start | bytes 380936 | tf_op jit(solution)/shard_map/ppermute | solution.py:301
  40.8 5.3 %collective-permute-start.9 = (bf16[432,128]{1,0:T(8,128)(2,1)S(1)}, bf16[432,128]{1,0:T(8,128)(2,1)S(1)}, u32[]{:S(2)}, u32[]{:S(2)}) collective-permute-start(bf16[432,128]{1,0:T(8,128)(2,1)S(1)} %pad_maximum_fusion.4), channel_id=1, source_target_pairs={{0,4},{4,0},{8,12},{12,8},{1,5},{5,1},{9,13},{13,9},{2,6},{6,2},{1... | collective-permute-start | bytes 331784 | tf_op jit(solution)/shard_map/ppermute | solution.py:301
  46.2 7.6 %collective-permute-start.10 = (bf16[432,128]{1,0:T(8,128)(2,1)S(1)}, bf16[432,128]{1,0:T(8,128)(2,1)S(1)}, u32[]{:S(2)}, u32[]{:S(2)}) collective-permute-start(bf16[432,128]{1,0:T(8,128)(2,1)S(1)} %pad_maximum_fusion.5), channel_id=1, source_target_pairs={{0,8},{4,12},{8,0},{12,4},{1,9},{5,13},{9,1},{13,5},{2,10},{6,14},... | collective-permute-start | bytes 331784 | tf_op jit(solution)/shard_map/ppermute | solution.py:301
  53.9 6.2 %collective-permute-start.11 = (bf16[368,128]{1,0:T(8,128)(2,1)S(1)}, bf16[368,128]{1,0:T(8,128)(2,1)S(1)}, u32[]{:S(2)}, u32[]{:S(2)}) collective-permute-start(bf16[368,128]{1,0:T(8,128)(2,1)S(1)} %pad_maximum_fusion.6), channel_id=1, source_target_pairs={{0,2},{1,3},{2,0},{3,1},{4,6},{5,7},{6,4},{7,5},{8,10},{9,11},{10,... | collective-permute-start | bytes 282632 | tf_op jit(solution)/shard_map/ppermute | solution.py:301
  60.2 2.0 %collective-permute-start.12 = (bf16[512,128]{1,0:T(8,128)(2,1)S(1)}, bf16[512,128]{1,0:T(8,128)(2,1)S(1)}, u32[]{:S(2)}, u32[]{:S(2)}) collective-permute-start(bf16[512,128]{1,0:T(8,128)(2,1)S(1)} %bitcast.156), channel_id=1, source_target_pairs={{0,1},{1,0},{2,3},{3,2},{4,5},{5,4},{6,7},{7,6},{8,9},{9,8},{10,11... | collective-permute-start | bytes 393224 | tf_op jit(solution)/shard_map/ppermute | solution.py:301

commit v4 on v3

--- a/solution.py
+++ b/solution.py
@@ -130,8 +130,8 @@
     a_refs, b_refs = refs[:pieces], refs[pieces : 2 * pieces]
     up_ref, w_ref, wt_ref, perm_ref, wc_ref = refs[2 * pieces : 2 * pieces + 5]
     outs = refs[2 * pieces + 5 :]
-    mi_ref, mj_ref, a_ref, b_ref, inv_ref, bias_ref, dw_ref, da_ref = outs[:8]
-    bt_ref, at_ref, v_ref, acc_ref = outs[8:]
+    mi_ref, mj_ref, a_ref, b_ref, bt_ref, inv_ref, bias_ref, dw_ref, left_ref = outs[:9]
+    at_ref, v_ref, acc_ref, wide_ref = outs[9:]
     g, last = pl.program_id(0), pl.num_programs(0) - 1
     chunk, block, pair = up_ref.shape
     width = w_ref.shape[1] // 2
@@ -155,7 +155,8 @@
         w, wt = w_ref[...], wt_ref[...]
         mi = mi_ref[...]
         a_ref[...] = dot(mi, w[:, :width]).astype(BF16)
-        at_ref[...] = dot_nt(wt[:width, :], mi).astype(BF16)
+        same = one_hot(iota((features, LANES), 0) == iota((features, LANES), 1))
+        at_ref[...] = dot_nt(jnp.concatenate([wt[:width, :], same], axis=0), mi).astype(BF16)
         b = jnp.zeros((block, width * depth), F32)
         seen = jnp.zeros((block, LANES), F32)
         for s in range(depth):
@@ -174,6 +175,7 @@
             count = dot_nt(seen_j, seen_i[k * chunk : (k + 1) * chunk, :])
             inv_ref[k] = 1.0 / (count + 0.001)
         acc_ref[...] = jnp.zeros_like(acc_ref)
+        wide_ref[...] = jnp.zeros_like(wide_ref)
         bias_ref[...] = jnp.zeros_like(bias_ref)
 
     bias_ref[0:1, :] += jnp.sum(
@@ -182,23 +184,38 @@
     fill_v(up_ref, inv_ref[g], bt_ref[...], v_ref, depth)
     span = chunk * depth
     a_t = at_ref[:, pl.ds(pl.multiple_of(g * span, span), span)]
-    d_a = jnp.zeros((width, span), F32)
     for e in range(0, width, 2):
-        v = two(v_ref, e)
-        part = dot(a_t, v)
+        part = dot(a_t, two(v_ref, e))
         for k in range(2):
-            acc_ref[(e + k) * width : (e + k + 1) * width, :] += part[:, k * pair : (k + 1) * pair]
-        d_a = d_a + dot_nt(wc_ref[:, e * pair : (e + 2) * pair], v)
-    da_ref[:, pl.ds(pl.multiple_of(g * span, span), span)] = d_a.astype(BF16)
+            rows = slice((e + k) * width, (e + k + 1) * width)
+            acc_ref[rows, :] += part[:width, k * pair : (k + 1) * pair]
+        wide_ref[:, e * pair : (e + 2) * pair] += part[width:]
 
     @pl.when(g == last)
     def _():
         dw_ref[...] = acc_ref[...].astype(BF16)
+        left = jnp.zeros((width, features), F32)
+        for e in range(0, width, 2):
+            lanes = slice(e * pair, (e + 2) * pair)
+            left = left + dot_nt(wc_ref[:, lanes], wide_ref[:, lanes].astype(BF16))
+        left_ref[...] = left
+
+
+def left_kernel(depth, up_ref, inv_ref, bt_ref, wc_ref, out_ref, v_ref):
+    g = pl.program_id(0)
+    chunk, _, pair = up_ref.shape
+    width = wc_ref.shape[0]
+    span = chunk * depth
+    fill_v(up_ref, inv_ref[g], bt_ref[...], v_ref, depth)
+    d_a = jnp.zeros((width, span), F32)
+    for e in range(0, width, 2):
+        d_a = d_a + dot_nt(wc_ref[:, e * pair : (e + 2) * pair], two(v_ref, e))
+    out_ref[:, pl.ds(pl.multiple_of(g * span, span), span)] = d_a.astype(BF16)
 
 
 def token_kernel(depth, features, *refs):
-    up_ref, inv_ref, a_ref, wc_ref, mi_ref, mj_ref, perm_ref, bias_ref, da_ref = refs[:9]
-    small_ref, out_ref, t_ref, db_ref = refs[9:]
+    up_ref, inv_ref, a_ref, wc_ref, mj_ref, perm_ref, bias_ref, left_ref = refs[:8]
+    small_ref, out_ref, t_ref, db_ref = refs[8:]
     g, last = pl.program_id(0), pl.num_programs(0) - 1
     chunk = up_ref.shape[0]
     width = wc_ref.shape[0]
@@ -224,8 +241,7 @@
         right = jnp.zeros((width, LANES), F32)
         for s in range(depth):
             right = right + dot(turned[s * width : (s + 1) * width, :], mj_ref[s])
-        left = dot(da_ref[...], mi_ref[...])
-        small = jnp.concatenate([left[:, :features], right[:, :features]], axis=1)
+        small = jnp.concatenate([left_ref[...], right[:, :features]], axis=1)
         small_ref[0:width, :] = small.astype(BF16)
         small_ref[width:, :] = jnp.broadcast_to(bias_ref[0:1, :], (16, LANES)).astype(BF16)
 
@@ -372,7 +388,7 @@
     by_token, by_row, factors, factors_t, x, offset = call(
         functools.partial(prep_kernel, depth, own),
         (),
-        [pl.BlockSpec(memory_space=pl.ANY)] * len(args),
+        [pl.BlockSpec(memory_space=pltpu.MemorySpace.HBM)] * len(args),
         [full(o.shape) for o in out_shapes],
         out_shapes,
         [pltpu.VMEM(v.shape, v.dtype) for v in args[1:4]] + [pltpu.SemaphoreType.DMA((5,))],
@@ -400,10 +416,11 @@
         sds((depth, block, LANES), BF16),
         sds((tokens, width), BF16),
         sds((block, wide), BF16),
+        sds((wide, block), BF16),
         sds((steps, block, chunk), F32),
         sds((8, pair), F32),
         sds((width * width, pair), BF16),
-        sds((width, tokens), BF16),
+        sds((width, features), F32),
     ]
     outs = call(
         functools.partial(weight_kernel, depth, features, n, pieces),
@@ -415,78 +432,89 @@
         [full(o.shape) for o in out_shapes],
         out_shapes,
         [
-            pltpu.VMEM((wide, block), BF16),
-            pltpu.VMEM((width, tokens), BF16),
+            pltpu.VMEM((width + features, tokens), BF16),
             pltpu.VMEM((width, chunk * depth, pair), BF16),
             pltpu.VMEM((width * width, pair), F32),
+            pltpu.VMEM((features, width * pair), F32),
         ],
         cost(5e9, 8e6),
     )(*a_pieces, *b_pieces, upstream_adjoint, factors, factors_t, perm, pairing_wide)
-    mi, mj, a, b, inv, bias, d_pairing, d_a = outs
+    mi, mj, a, b, b_t, inv, bias, d_pairing, left = outs
 
     bits = n.bit_length() - 1
     d_pairing = d_pairing.reshape(n, -1, LANES)
-    da_all = d_a
-    d_a = jnp.stack([lay_out(d_a[:, k * rows : (k + 1) * rows]) for k in range(n)])
     for bit in reversed(range(1, bits)):
-        dp_keep, dp_go = halves(split_high(d_pairing), "col", bit, 0)
-        da_keep, da_go = halves(split_high(d_a), "col", bit, 0)
-        dp_got, da_got = swap_parts([dp_go, da_go], "col", bit, n)
-        d_pairing, d_a = add(dp_keep, dp_got), add(da_keep, da_got)
+        keep, go = halves(split_high(d_pairing), "col", bit, 0)
+        d_pairing = add(keep, *swap_parts([go], "col", bit, n))
 
     out_shapes = [sds((width + 16, LANES), BF16), sds((block, wide), BF16)]
     small, d_b = call(
         functools.partial(token_kernel, depth, features),
         (steps,),
         [up_spec]
-        + [full(v.shape) for v in (inv, a, pairing_wide, mi, mj, perm, bias)]
-        + [full((width, tokens))],
+        + [full(v.shape) for v in (inv, a, pairing_wide, mj, perm, bias, left)],
         [full(o.shape) for o in out_shapes],
         out_shapes,
         [pltpu.VMEM((chunk, wide, pair), BF16), pltpu.VMEM((block, wide), F32)],
         cost(5e9, 8e6),
-    )(upstream_adjoint, inv, a, pairing_wide, mi, mj, perm, bias, da_all)
+    )(upstream_adjoint, inv, a, pairing_wide, mj, perm, bias, left)
 
     d_b = jnp.stack([lay_out(d_b[k * own : (k + 1) * own]) for k in range(n)])
     dp_keep, dp_go = halves(d_pairing, "col", 0, 0)
-    da_keep, da_go = halves(d_a, "col", 0, 0)
     db_keep, db_go = halves(d_b.reshape((n // 2, 2) + d_b.shape[1:]), "col", 0, 1)
-    parts = swap_parts([dp_go, da_go, db_go, small], "col", 0, n)
-    d_pairing, small = add(dp_keep, parts[0]), add(small, parts[3])
-    da_parts = [da_keep, parts[1]]
-    d_b = in_order(db_keep, parts[2].reshape(db_keep.shape), "col", 0, 1)
+    parts = swap_parts([dp_go, db_go, small], "col", 0, n)
+    d_pairing, small = add(dp_keep, parts[0]), add(small, parts[2])
+    d_b = in_order(db_keep, parts[1].reshape(db_keep.shape), "col", 0, 1)
     db_keep, db_go = halves(d_b, "row", 0, 1)
     for bit in range(bits):
         parts = swap_parts([d_pairing, db_go, small], "row", bit, n)
+        if bit == 0:
+            d_a = call(
+                functools.partial(left_kernel, depth),
+                (steps,),
+                [up_spec] + [full(v.shape) for v in (inv, b_t, pairing_wide)],
+                full((width, tokens)),
+                sds((width, tokens), BF16),
+                [pltpu.VMEM((width, chunk * depth, pair), BF16)],
+                cost(6e9, 8e6),
+            )(upstream_adjoint, inv, b_t, pairing_wide)
+            parts[0], d_a = lax.optimization_barrier((parts[0], d_a))
+            d_a = jnp.stack([lay_out(d_a[:, k * rows : (k + 1) * rows]) for k in range(n)])
+            d_a = d_a.reshape((n // 2, 2) + d_a.shape[1:])
+        if bit == 1:
+            da_keep, da_go = halves(d_a, "col", 0, 1)
+            d_a = add(da_keep, *swap_parts([da_go], "col", 0, n))
+            coupling_update = call(
+                functools.partial(update_kernel, depth),
+                (steps,),
+                [full(v.shape) for v in (inv, a, b, pairing_wide)] + [full((1, pair))],
+                up_spec,
+                sds((block, block, pair), BF16),
+                [pltpu.VMEM((chunk, wide, pair), BF16)],
+                cost(6e9, 8e6),
+            )(inv, a, b, pairing_wide, offset)
+            held = (parts[0], coupling_update, d_a)
+            parts[0], coupling_update, d_a = lax.optimization_barrier(held)
         d_pairing, d_b, small = add(d_pairing, parts[0]), add(db_keep, parts[1]), add(small, parts[2])
         db_keep = db_go = d_b
     d_pairing = d_pairing.reshape(1, -1, LANES)
-    small_parts = [small, None]
-    for bit in range(1, bits):
-        if bit > 1:
-            small_parts[0] = add(*small_parts)
-        db_keep, db_go = halves(split_high(d_b), "col", bits - bit, 0)
-        parts = swap_parts([d_pairing, db_go, small_parts[0]], "col", bits - bit, n)
-        got = parts[0].reshape(d_pairing.shape)
-        d_pairing = in_order(d_pairing, got, "col", bits - bit, 1)
+    small_parts, da_parts = [small], [d_a]
+    for bit in reversed(range(1, bits)):
+        if len(small_parts) > 1:
+            small_parts, da_parts = [add(*small_parts)], [add(*da_parts)]
+        db_keep, db_go = halves(split_high(d_b), "col", bit, 0)
+        da_keep, da_go = halves(split_high(da_parts[0]), "col", bit, 0)
+        parts = swap_parts([d_pairing, db_go, da_go, small_parts[0]], "col", bit, n)
+        d_pairing = in_order(d_pairing, parts[0].reshape(d_pairing.shape), "col", bit, 1)
         d_pairing = d_pairing.reshape((-1,) + d_pairing.shape[2:])
-        mine = bit_of("col", bits - bit) == bit_of("row", bits - bit)
+        mine = bit_of("col", bit) == bit_of("row", bit)
         d_b = jnp.where(mine, db_keep, parts[1].reshape(db_keep.shape))
-        small_parts[1] = parts[2]
+        da_parts = [da_keep, parts[2].reshape(da_keep.shape)]
+        small_parts = [small_parts[0], parts[3]]
     (got,) = swap_parts([d_pairing], "col", 0, n)
     d_pairing = in_order(d_pairing, got.reshape(d_pairing.shape), "col", 0, 1)
     d_a = [lay_back(part.reshape(-1, LANES), width, rows) for part in da_parts]
     d_b = lay_back(d_b[0], own, wide)
-
-    coupling_update = call(
-        functools.partial(update_kernel, depth),
-        (steps,),
-        [full(v.shape) for v in (inv, a, b, pairing_wide)] + [full((1, pair))],
-        up_spec,
-        sds((block, block, pair), BF16),
-        [pltpu.VMEM((chunk, wide, pair), BF16)],
-        cost(5e9, 8e6),
-    )(inv, a, b, pairing_wide, offset)
 
     args = (*d_a, d_b, *small_parts, x, by_row, factors_t, perm)
     out_shapes = [sds((rows, features), F32), sds((features, 2 * width), F32), sds((1, pair), F32)]

time: 63.9 us -> 70.7 us (1.11)
  Pallas kernels: 26.1 us -> 32 us
  waiting for transfers between devices: 13.4 us -> 10.8 us
  local copies, waits for them, and re-layouts: 4.17 us -> 6.41 us
  starting transfers between devices: 18.2 us -> 19.5 us
    pallas_call x0 -> x1, Pallas kernels: none -> 9.37 us  [per_device(): call(functools.partial(left_kernel, depth), (steps,), [up_spec] + [full(v...]
    pallas_call x1, Pallas kernels: 11.6 us -> 8.19 us  [per_device(): call(functools.partial(weight_kernel, depth, features, n, pieces), (steps...]
    ppermute x6 -> x7, waiting for transfers between devices: 11.9 us -> 9.29 us  [swap_parts(): message = lax.ppermute(message, axis, [(i, i ^ 1 << bit) for i in range(n)])]
    slice x7 -> x8, local copies, waits for them, and re-layouts: 0.03 us -> 1.44 us  [swap_parts(): got.append(message[at:at + part.shape[0]])]
    ppermute x6 -> x7, starting transfers between devices: 4.99 us -> 6.25 us  [swap_parts(): message = lax.ppermute(message, axis, [(i, i ^ 1 << bit) for i in range(n)])]
    unnamed x14 -> x18, local copies, waits for them, and re-layouts: 2.93 us -> 3.77 us
  transfers between devices with their start and end apart: 13 -> 14, of which waited for: 5 -> 4; matrix products, arithmetic and copies ran while one was open for 2% -> 2% of each run, Pallas kernels for 20% -> 31%
where the time goes in v4:
time: 70.7 us; the launch traced here: 70.3 us
  Pallas kernels  32 us (45%)
  starting transfers between devices  19.5 us (28%)
  waiting for transfers between devices  10.8 us (15%)
  local copies, waits for them, and re-layouts  6.41 us (9%)
  between operations  1.08 us (2%)
    ppermute x4, starting transfers between devices, to_column(): return lax.ppermute(x, axes, pairs)  11 us
    pallas_call x1, Pallas kernels, per_device(): call(functools.partial(left_kernel, depth), (steps,), [up_spec] + [full(v...  9.37 us
    ppermute x7, waiting for transfers between devices, swap_parts(): message = lax.ppermute(message, axis, [(i, i ^ 1 << bit) for i in range(n)])  9.29 us
    pallas_call x1, Pallas kernels, per_device(): call(functools.partial(weight_kernel, depth, features, n, pieces), (steps...  8.19 us
    ppermute x7, starting transfers between devices, swap_parts(): message = lax.ppermute(message, axis, [(i, i ^ 1 << bit) for i in range(n)])  6.25 us
    pallas_call x1, Pallas kernels, per_device(): call(functools.partial(token_kernel, depth, features), (steps,), [up_spec...  5.83 us
    pallas_call x1, Pallas kernels, per_device(): call(functools.partial(update_kernel, depth), (steps,), [full(v.shape) fo...  4.87 us
    unnamed x18, local copies, waits for them, and re-layouts  3.77 us
  transfers between devices with their start and end apart: 14, of which 4 were waited for; matrix products, arithmetic and copies ran while one was open for 2% of the time, Pallas kernels for 31%

profile of v4, /device:TPU:0, one launch (start us, length us, event | category | flops | bytes accessed | tf_op | source)
XLA Modules:
  0.0 70.3 jit_solution(6944636027666441433)
XLA Ops:
  0.7 0.6 copy-done.3
  1.3 0.0 copy-done.4
  1.3 0.8 %copy-done = bf16[16,16,64]{2,1,0:T(8,128)(2,1)S(1)} copy-done((bf16[16,16,64]{2,1,0:T(8,128)(2,1)S(1)}, bf16[16,16,64]{2,1,0:T(8,128)(2,1)}, u32[]{:S(2)}) %copy-start) | copy-done | bytes 32792
  2.1 0.7 %copy-done.1 = bf16[64,64]{1,0:T(8,128)(2,1)S(1)} copy-done((bf16[64,64]{1,0:T(8,128)(2,1)S(1)}, bf16[64,64]{1,0:T(8,128)(2,1)}, u32[]{:S(2)}) %copy-start.1) | copy-done | bytes 8216
  2.9 0.7 copy-done.2
  3.6 0.6 shard_map.110
  4.2 0.7 collective-permute-start.3
  4.9 4.3 %collective-permute-start.4 = (bf16[256,128]{1,0:T(8,128)(2,1)S(1)}, bf16[256,128]{1,0:T(8,128)(2,1)S(1)}, u32[]{:S(2)}, u32[]{:S(2)}) collective-permute-start(bf16[256,128]{1,0:T(8,128)(2,1)S(1)} %get-tuple-element.30.refs_6_), channel_id=1, source_target_pairs={{0,4},{1,8},{2,12},{3,0},{4,5},{5,9},{6,13},{7,1},{8,6},{9,10},{10... | collective-permute-start | bytes 196616 | tf_op jit(solution)/shard_map/ppermute | solution.py:373
  9.2 3.4 %collective-permute-start.5 = (bf16[256,128]{1,0:T(8,128)(2,1)S(1)}, bf16[256,128]{1,0:T(8,128)(2,1)S(1)}, u32[]{:S(2)}, u32[]{:S(2)}) collective-permute-start(bf16[256,128]{1,0:T(8,128)(2,1)S(1)} %get-tuple-element.30.refs_6_), channel_id=1, source_target_pairs={{0,8},{1,12},{2,0},{3,4},{4,9},{5,13},{6,1},{7,5},{8,10},{9,14},{1... | collective-permute-start | bytes 196616 | tf_op jit(solution)/shard_map/ppermute | solution.py:373
  12.6 2.6 %collective-permute-start.6 = (bf16[256,128]{1,0:T(8,128)(2,1)S(1)}, bf16[256,128]{1,0:T(8,128)(2,1)S(1)}, u32[]{:S(2)}, u32[]{:S(2)}) collective-permute-start(bf16[256,128]{1,0:T(8,128)(2,1)S(1)} %get-tuple-element.30.refs_6_), channel_id=1, source_target_pairs={{0,12},{1,0},{2,4},{3,8},{4,13},{5,1},{6,5},{7,9},{8,14},{9,2},{10... | collective-permute-start | bytes 196616 | tf_op jit(solution)/shard_map/ppermute | solution.py:373
  15.2 0.0 collective-permute-start
  15.2 0.0 collective-permute-done.3.refs_4_
  15.2 1.5 %collective-permute-start.1 = (bf16[256,128]{1,0:T(8,128)(2,1)S(1)}, bf16[256,128]{1,0:T(8,128)(2,1)S(1)}, u32[]{:S(2)}, u32[]{:S(2)}) collective-permute-start(bf16[256,128]{1,0:T(8,128)(2,1)S(1)} %get-tuple-element.29.refs_0_), channel_id=1, source_target_pairs={{0,2},{1,3},{2,0},{3,1},{4,6},{5,7},{6,4},{7,5},{8,10},{9,11},{10,... | collective-permute-start | bytes 196616 | tf_op jit(solution)/shard_map/ppermute | solution.py:366
  16.7 0.0 collective-permute-done.4.refs_5_
  16.7 0.7 %collective-permute-start.2 = (bf16[256,128]{1,0:T(8,128)(2,1)S(1)}, bf16[256,128]{1,0:T(8,128)(2,1)S(1)}, u32[]{:S(2)}, u32[]{:S(2)}) collective-permute-start(bf16[256,128]{1,0:T(8,128)(2,1)S(1)} %get-tuple-element.29.refs_0_), channel_id=1, source_target_pairs={{0,3},{1,0},{2,1},{3,2},{4,7},{5,4},{6,5},{7,6},{8,11},{9,8},{10,9... | collective-permute-start | bytes 196616 | tf_op jit(solution)/shard_map/ppermute | solution.py:366
  17.5 0.1 fusion.refs_11_.refs_5_.refs_8_
  17.6 1.1 %reshape.211.refs_12_.refs_3_.wc_ref = bf16[32,4096]{1,0:T(8,128)(2,1)S(1)} reshape(bf16[1024,128]{1,0:T(8,128)(2,1)} %param.11) | data formatting | bytes 524288 | tf_op jit(solution)/shard_map/reshape | solution.py:411
  18.7 0.0 collective-permute-done.5.refs_6_
  18.7 0.0 collective-permute-done.6.refs_7_
  18.7 0.3 collective-permute-done.refs_1_
  19.0 1.2 %collective-permute-done.1.refs_2_ = bf16[256,128]{1,0:T(8,128)(2,1)S(1)} collective-permute-done((bf16[256,128]{1,0:T(8,128)(2,1)S(1)}, bf16[256,128]{1,0:T(8,128)(2,1)S(1)}, u32[]{:S(2)}, u32[]{:S(2)}) %collective-permute-start.1) | collective-permute-done | bytes 65568 | tf_op jit(solution)/shard_map/ppermute | solution.py:366
  20.2 0.0 collective-permute-done.2.refs_3_
  20.2 8.2 %shard_map.111 = (bf16[1024,128]{1,0:T(8,128)(2,1)}, bf16[16,64,128]{2,1,0:T(8,128)(2,1)S(1)}, bf16[1024,32]{1,0:T(8,128)(2,1)S(1)}, bf16[64,512]{1,0:T(8,128)(2...) custom-call(bf16[256,128]{1,0:T(8,128)(2,1)S(1)} %get-tuple-element., ...), custom_call_target="tpu_custom_call" | custom-call | flops 5000000000 | bytes 8000000 | tf_op jit(solution)/shard_map/pallas_call | solution.py:425
  28.4 1.2 %collective-permute-start.7 = (bf16[512,128]{1,0:T(8,128)(2,1)S(1)}, bf16[512,128]{1,0:T(8,128)(2,1)S(1)}, u32[]{:S(2)}, u32[]{:S(2)}) collective-permute-start(bf16[512,128]{1,0:T(8,128)(2,1)S(1)} %bitcast.159), channel_id=1, source_target_pairs={{0,2},{1,3},{2,0},{3,1},{4,6},{5,7},{6,4},{7,5},{8,10},{9,11},{10,... | collective-permute-start | bytes 393224 | tf_op jit(solution)/shard_map/ppermute | solution.py:317
  29.6 5.8 %shard_map.112 = (bf16[48,128]{1,0:T(8,128)(2,1)S(1)}, bf16[64,512]{1,0:T(8,128)(2,1)S(1)}) custom-call(bf16[64,64,128]{2,1,0:T(8,128)(2,1)S(1)} %copy-done.5, f32[4,64,16]{2,1,0:T(8,128)S(1)} %get-tuple-element.34.refs_1_.inv_ref, bf16[1024,32]{1,0:T(8,128)(2,1)S(1)} %get-tuple-element.35.refs_2_.a_ref, ...), custom_call_target="tpu_custom_call" | custom-call | flops 5000000000 | bytes 8000000 | tf_op jit(solution)/shard_map/pallas_call | solution.py:451
  35.6 0.0 collective-permute-done.7
  35.7 0.3 collective-permute-start.8
  36.0 9.4 %shard_map.113 = bf16[32,1024]{1,0:T(8,128)(2,1)S(1)} custom-call(bf16[64,64,128]{2,1,0:T(8,128)(2,1)S(1)} %copy-done.5, f32[4,64,16]{2,1,0:T(8,128)S(1)} %get-tuple-element.34.refs_1_.inv_ref, bf16[512,64]{1,0:T(8,128)(2,1)S(1)} %get-tuple-element.41.bt_ref, bf16[32,4096]{1,0:T(8,128)(2,1)S(1)} %reshape.211.refs_12_.refs_3_.wc_ref), custom_call_target="tpu_custom_call" | custom-call | flops 6000000000 | bytes 8000000 | tf_op jit(solution)/shard_map/pallas_call | solution.py:472
  45.5 0.6 collective-permute-start.9
  46.2 4.9 %shard_map.114 = bf16[64,64,128]{2,1,0:T(8,128)(2,1)} custom-call(f32[4,64,16]{2,1,0:T(8,128)S(1)} %get-tuple-element.34.refs_1_.inv_ref, bf16[1024,32]{1,0:T(8,128)(2,1)S(1)} %get-tuple-element.35.refs_2_.a_ref, bf16[64,512]{1,0:T(8,128)(2,1)S(1)} %get-tuple-element.43.b_ref, bf16[32,4096]{1,0:T(8,128)(2,1)S(1)} %reshape.211.refs_12_.refs_3_.wc_ref, ...), custom_call_target="tpu_custom_call" | custom-call | flops 6000000000 | bytes 8000000 | tf_op jit(solution)/shard_map/pallas_call | solution.py:487
  51.0 0.0 collective-permute-done.9
  51.0 0.6 copy-done.6
  51.7 0.0 slice-start
  51.8 0.1 collective-permute-start.11
  51.9 0.7 slice-done
  52.6 0.0 slice-start.1
  52.6 0.0 copy-start.7
  52.6 0.7 %slice-done.1 = bf16[128,128]{1,0:T(8,128)(2,1)S(1)} async-done(((bf16[432,128]{1,0:T(8,128)(2,1)}), bf16[128,128]{1,0:T(8,128)(2,1)S(1)}, s32[]{:S(2)}) %slice-start.1) | async-done | bytes 32792 | tf_op jit(solution)/shard_map/slice | solution.py:320
  53.4 0.2 copy-done.7
  53.6 2.5 %collective-permute-start.10 = (bf16[432,128]{1,0:T(8,128)(2,1)S(1)}, bf16[432,128]{1,0:T(8,128)(2,1)S(1)}, u32[]{:S(2)}, u32[]{:S(2)}) collective-permute-start(bf16[432,128]{1,0:T(8,128)(2,1)S(1)} %pad_maximum_fusion.4), channel_id=1, source_target_pairs={{0,8},{4,12},{8,0},{12,4},{1,9},{5,13},{9,1},{13,5},{2,10},{6,14},... | collective-permute-start | bytes 331784 | tf_op jit(solution)/shard_map/ppermute | solution.py:317
  56.1 0.0 collective-permute-done.11
  56.2 5.8 %collective-permute-done.10 = bf16[432,128]{1,0:T(8,128)(2,1)S(1)} collective-permute-done((bf16[432,128]{1,0:T(8,128)(2,1)S(1)}, bf16[432,128]{1,0:T(8,128)(2,1)S(1)}, u32[]{:S(2)}, u32[]{:S(2)}) %collective-permute-start.10) | collective-permute-done | bytes 110624 | tf_op jit(solution)/shard_map/ppermute | solution.py:317
  62.1 1.3 %collective-permute-start.12 = (bf16[432,128]{1,0:T(8,128)(2,1)S(1)}, bf16[432,128]{1,0:T(8,128)(2,1)S(1)}, u32[]{:S(2)}, u32[]{:S(2)}) collective-permute-start(bf16[432,128]{1,0:T(8,128)(2,1)S(1)} %pad_maximum_fusion.5), channel_id=1, source_target_pairs={{0,2},{1,3},{2,0},{3,1},{4,6},{5,7},{6,4},{7,5},{8,10},{9,11},{10,... | collective-permute-start | bytes 331784 | tf_op jit(solution)/shard_map/ppermute | solution.py:317
  63.4 3.5 %collective-permute-done.12 = bf16[432,128]{1,0:T(8,128)(2,1)S(1)} collective-permute-done((bf16[432,128]{1,0:T(8,128)(2,1)S(1)}, bf16[432,128]{1,0:T(8,128)(2,1)S(1)}, u32[]{:S(2)}, u32[]{:S(2)}) %collective-permute-start.12) | collective-permute-done | bytes 110624 | tf_op jit(solution)/shard_map/ppermute | solution.py:317
  67.0 0.1 collective-permute-start.13
  67.1 1.9 %shard_map.115 = (f32[256,64]{1,0:T(8,128)}, f32[64,64]{1,0:T(8,128)}, f32[1,128]{1,0:T(1,128)}) custom-call(bf16[32,256]{1,0:T(8,128)(2,1)S(1)} %bitcast.141, bf16[32,256]{1,0:T(8,128)(2,1)S(1)} %bitcast.143, bf16[16,512]{1,0:T(8,128)(2,1)S(1)} %bitcast.142, bf16[48,128]{1,0:T(8,128)(2,1)S(1)} %add_convert_fusion.2.refs_3_, ...), custom_call_target="tpu_custom_call" | custom-call | tf_op jit(solution)/shard_map/pallas_call | solution.py:521
  69.0 0.0 collective-permute-done.13
  69.1 1.3 %shard_map.116 = f32[32,32,128]{2,1,0:T(8,128)} custom-call(bf16[32,32,128]{2,1,0:T(8,128)(2,1)S(1)} %bitcast.138), custom_call_target="tpu_custom_call" | custom-call | tf_op jit(solution)/shard_map/pallas_call | solution.py:530
  (55 shorter events, 0.6 us)
Async XLA Ops:
  0.6 0.7 copy-start.3
  0.6 0.7 copy-start.4
  1.3 0.8 %copy-start = (bf16[16,16,64]{2,1,0:T(8,128)(2,1)S(1)}, bf16[16,16,64]{2,1,0:T(8,128)(2,1)}, u32[]{:S(2)}) copy-start(bf16[16,16,64]{2,1,0:T(8,128)(2,1)} %param.7) | copy-start | bytes 98308
  2.1 0.7 %copy-start.1 = (bf16[64,64]{1,0:T(8,128)(2,1)S(1)}, bf16[64,64]{1,0:T(8,128)(2,1)}, u32[]{:S(2)}) copy-start(bf16[64,64]{1,0:T(8,128)(2,1)} %refs_3_.1) | copy-start | bytes 24580
  2.9 0.7 copy-start.2
  3.6 16.7 %copy-start.5 = (bf16[64,64,128]{2,1,0:T(8,128)(2,1)S(1)}, bf16[64,64,128]{2,1,0:T(8,128)(2,1)}, u32[]{:S(2)}) copy-start(bf16[64,64,128]{2,1,0:T(8,128)(2,1)} %up_ref.1) | copy-start | bytes 3145732
  4.2 11.0 %collective-permute-start.3 = (bf16[256,128]{1,0:T(8,128)(2,1)S(1)}, bf16[256,128]{1,0:T(8,128)(2,1)S(1)}, u32[]{:S(2)}, u32[]{:S(2)}) collective-permute-start(bf16[256,128]{1,0:T(8,128)(2,1)S(1)} %get-tuple-element.30.refs_6_), channel_id=1, source_target_pairs={{0,0},{1,4},{2,8},{3,12},{4,1},{5,5},{6,9},{7,13},{8,2},{9,6},{10,... | collective-permute-start | bytes 196616 | tf_op jit(solution)/shard_map/ppermute | solution.py:373
  4.9 11.9 %collective-permute-start.4 = (bf16[256,128]{1,0:T(8,128)(2,1)S(1)}, bf16[256,128]{1,0:T(8,128)(2,1)S(1)}, u32[]{:S(2)}, u32[]{:S(2)}) collective-permute-start(bf16[256,128]{1,0:T(8,128)(2,1)S(1)} %get-tuple-element.30.refs_6_), channel_id=1, source_target_pairs={{0,4},{1,8},{2,12},{3,0},{4,5},{5,9},{6,13},{7,1},{8,6},{9,10},{10... | collective-permute-start | bytes 196616 | tf_op jit(solution)/shard_map/ppermute | solution.py:373
  9.2 9.5 %collective-permute-start.5 = (bf16[256,128]{1,0:T(8,128)(2,1)S(1)}, bf16[256,128]{1,0:T(8,128)(2,1)S(1)}, u32[]{:S(2)}, u32[]{:S(2)}) collective-permute-start(bf16[256,128]{1,0:T(8,128)(2,1)S(1)} %get-tuple-element.30.refs_6_), channel_id=1, source_target_pairs={{0,8},{1,12},{2,0},{3,4},{4,9},{5,13},{6,1},{7,5},{8,10},{9,14},{1... | collective-permute-start | bytes 196616 | tf_op jit(solution)/shard_map/ppermute | solution.py:373
  12.6 6.1 %collective-permute-start.6 = (bf16[256,128]{1,0:T(8,128)(2,1)S(1)}, bf16[256,128]{1,0:T(8,128)(2,1)S(1)}, u32[]{:S(2)}, u32[]{:S(2)}) collective-permute-start(bf16[256,128]{1,0:T(8,128)(2,1)S(1)} %get-tuple-element.30.refs_6_), channel_id=1, source_target_pairs={{0,12},{1,0},{2,4},{3,8},{4,13},{5,1},{6,5},{7,9},{8,14},{9,2},{10... | collective-permute-start | bytes 196616 | tf_op jit(solution)/shard_map/ppermute | solution.py:373
  15.2 3.8 %collective-permute-start = (bf16[256,128]{1,0:T(8,128)(2,1)S(1)}, bf16[256,128]{1,0:T(8,128)(2,1)S(1)}, u32[]{:S(2)}, u32[]{:S(2)}) collective-permute-start(bf16[256,128]{1,0:T(8,128)(2,1)S(1)} %get-tuple-element.29.refs_0_), channel_id=1, source_target_pairs={{0,1},{1,2},{2,3},{3,0},{4,5},{5,6},{6,7},{7,4},{8,9},{9,10},{10,1... | collective-permute-start | bytes 196616 | tf_op jit(solution)/shard_map/ppermute | solution.py:366
  15.2 5.0 %collective-permute-start.1 = (bf16[256,128]{1,0:T(8,128)(2,1)S(1)}, bf16[256,128]{1,0:T(8,128)(2,1)S(1)}, u32[]{:S(2)}, u32[]{:S(2)}) collective-permute-start(bf16[256,128]{1,0:T(8,128)(2,1)S(1)} %get-tuple-element.29.refs_0_), channel_id=1, source_target_pairs={{0,2},{1,3},{2,0},{3,1},{4,6},{5,7},{6,4},{7,5},{8,10},{9,11},{10,... | collective-permute-start | bytes 196616 | tf_op jit(solution)/shard_map/ppermute | solution.py:366
  16.7 3.5 %collective-permute-start.2 = (bf16[256,128]{1,0:T(8,128)(2,1)S(1)}, bf16[256,128]{1,0:T(8,128)(2,1)S(1)}, u32[]{:S(2)}, u32[]{:S(2)}) collective-permute-start(bf16[256,128]{1,0:T(8,128)(2,1)S(1)} %get-tuple-element.29.refs_0_), channel_id=1, source_target_pairs={{0,3},{1,0},{2,1},{3,2},{4,7},{5,4},{6,5},{7,6},{8,11},{9,8},{10,9... | collective-permute-start | bytes 196616 | tf_op jit(solution)/shard_map/ppermute | solution.py:366
  28.4 7.1 %collective-permute-start.7 = (bf16[512,128]{1,0:T(8,128)(2,1)S(1)}, bf16[512,128]{1,0:T(8,128)(2,1)S(1)}, u32[]{:S(2)}, u32[]{:S(2)}) collective-permute-start(bf16[512,128]{1,0:T(8,128)(2,1)S(1)} %bitcast.159), channel_id=1, source_target_pairs={{0,2},{1,3},{2,0},{3,1},{4,6},{5,7},{6,4},{7,5},{8,10},{9,11},{10,... | collective-permute-start | bytes 393224 | tf_op jit(solution)/shard_map/ppermute | solution.py:317
  35.7 9.7 %collective-permute-start.8 = (bf16[432,128]{1,0:T(8,128)(2,1)S(1)}, bf16[432,128]{1,0:T(8,128)(2,1)S(1)}, u32[]{:S(2)}, u32[]{:S(2)}) collective-permute-start(bf16[432,128]{1,0:T(8,128)(2,1)S(1)} %pad_maximum_fusion.2), channel_id=1, source_target_pairs={{0,1},{1,0},{2,3},{3,2},{4,5},{5,4},{6,7},{7,6},{8,9},{9,8},{10,11... | collective-permute-start | bytes 331784 | tf_op jit(solution)/shard_map/ppermute | solution.py:317
  45.5 5.5 %collective-permute-start.9 = (bf16[432,128]{1,0:T(8,128)(2,1)S(1)}, bf16[432,128]{1,0:T(8,128)(2,1)S(1)}, u32[]{:S(2)}, u32[]{:S(2)}) collective-permute-start(bf16[432,128]{1,0:T(8,128)(2,1)S(1)} %pad_maximum_fusion.3), channel_id=1, source_target_pairs={{0,4},{4,0},{8,12},{12,8},{1,5},{5,1},{9,13},{13,9},{2,6},{6,2},{1... | collective-permute-start | bytes 331784 | tf_op jit(solution)/shard_map/ppermute | solution.py:317
  51.0 0.6 copy-start.6
  51.7 0.8 %slice-start = ((bf16[432,128]{1,0:T(8,128)(2,1)}), bf16[256,128]{1,0:T(8,128)(2,1)S(1)}, s32[]{:S(2)}) async-start(bf16[432,128]{1,0:T(8,128)(2,1)} %copy-done.6), calls=%async_computation | async-start | bytes 131072 | tf_op jit(solution)/shard_map/slice | solution.py:320
  51.8 4.4 %collective-permute-start.11 = (bf16[128,128]{1,0:T(8,128)(2,1)S(1)}, bf16[128,128]{1,0:T(8,128)(2,1)S(1)}, u32[]{:S(2)}, u32[]{:S(2)}) collective-permute-start(bf16[128,128]{1,0:T(8,128)(2,1)S(1)} %bitcast.174), channel_id=1, source_target_pairs={{0,1},{1,0},{2,3},{3,2},{4,5},{5,4},{6,7},{7,6},{8,9},{9,8},{10,11... | collective-permute-start | bytes 98312 | tf_op jit(solution)/shard_map/ppermute | solution.py:317
  52.6 0.8 %slice-start.1 = ((bf16[432,128]{1,0:T(8,128)(2,1)}), bf16[128,128]{1,0:T(8,128)(2,1)S(1)}, s32[]{:S(2)}) async-start(bf16[432,128]{1,0:T(8,128)(2,1)} %copy-done.6), calls=%async_computation.1 | async-start | bytes 65536 | tf_op jit(solution)/shard_map/slice | solution.py:320
  52.6 1.0 %copy-start.7 = (bf16[432,128]{1,0:T(8,128)(2,1)S(1)}, bf16[432,128]{1,0:T(8,128)(2,1)}, u32[]{:S(2)}) copy-start(bf16[432,128]{1,0:T(8,128)(2,1)} %copy-done.6) | copy-start | bytes 331780
  53.6 8.4 %collective-permute-start.10 = (bf16[432,128]{1,0:T(8,128)(2,1)S(1)}, bf16[432,128]{1,0:T(8,128)(2,1)S(1)}, u32[]{:S(2)}, u32[]{:S(2)}) collective-permute-start(bf16[432,128]{1,0:T(8,128)(2,1)S(1)} %pad_maximum_fusion.4), channel_id=1, source_target_pairs={{0,8},{4,12},{8,0},{12,4},{1,9},{5,13},{9,1},{13,5},{2,10},{6,14},... | collective-permute-start | bytes 331784 | tf_op jit(solution)/shard_map/ppermute | solution.py:317
  62.1 4.8 %collective-permute-start.12 = (bf16[432,128]{1,0:T(8,128)(2,1)S(1)}, bf16[432,128]{1,0:T(8,128)(2,1)S(1)}, u32[]{:S(2)}, u32[]{:S(2)}) collective-permute-start(bf16[432,128]{1,0:T(8,128)(2,1)S(1)} %pad_maximum_fusion.5), channel_id=1, source_target_pairs={{0,2},{1,3},{2,0},{3,1},{4,6},{5,7},{6,4},{7,5},{8,10},{9,11},{10,... | collective-permute-start | bytes 331784 | tf_op jit(solution)/shard_map/ppermute | solution.py:317
  67.0 2.0 %collective-permute-start.13 = (bf16[512,128]{1,0:T(8,128)(2,1)S(1)}, bf16[512,128]{1,0:T(8,128)(2,1)S(1)}, u32[]{:S(2)}, u32[]{:S(2)}) collective-permute-start(bf16[512,128]{1,0:T(8,128)(2,1)S(1)} %bitcast.160), channel_id=1, source_target_pairs={{0,1},{1,0},{2,3},{3,2},{4,5},{5,4},{6,7},{7,6},{8,9},{9,8},{10,11... | collective-permute-start | bytes 393224 | tf_op jit(solution)/shard_map/ppermute | solution.py:317

commit v5 on v4

--- a/solution.py
+++ b/solution.py
@@ -57,44 +57,23 @@
     return center * scale, scale
 
 
-def prep_kernel(depth, own, *refs):
-    by_token_ref, by_row_ref, w_ref, wt_ref, x_ref, offset_ref = refs[5:11]
-    cell_ref, line_ref, factors_ref, sem = refs[11:]
+def prep_kernel(depth, own, x_ref, mask_ref, by_token_ref, by_row_ref):
     rows = depth * own
-    targets = (x_ref, cell_ref, line_ref, factors_ref, offset_ref)
-    copies = [
-        pltpu.make_async_copy(src, dst, sem.at[k])
-        for k, (src, dst) in enumerate(zip(refs[:5], targets))
-    ]
-    for copy in copies:
-        copy.start()
-    p, q = iota((rows, rows), 0), iota((rows, rows), 1)
-    swap = one_hot(q == (p % depth) * own + p // depth)
+    normed, _ = stats(x_ref[...].astype(F32))
+    features = normed.shape[1]
     pick = one_hot(iota((rows, depth), 0) // own == iota((rows, depth), 1))
     here = iota((rows, own), 0) % own == iota((rows, own), 1)
-    for copy in copies:
-        copy.wait()
-    normed, _ = stats(x_ref[...].astype(F32))
-    features = normed.shape[1]
-    cell = cell_ref[...].astype(F32).astype(BF16)
-    line = line_ref[...].astype(F32)
-    line_column = jnp.sum(pick.astype(F32) * line, axis=1, keepdims=True)
-    cells = dot(pick, cell)
-    weight = jnp.sum(jnp.where(here, cells, 0.0), axis=1, keepdims=True) * line_column
+    weight = dot(pick, mask_ref[...])
+    weight = jnp.sum(jnp.where(here, weight, 0.0), axis=1, keepdims=True)
     masked = normed.astype(BF16).astype(F32) * weight
     wide = jnp.concatenate([masked, jnp.zeros((rows, LANES - features), F32)], axis=1)
     lane = iota((rows, LANES), 1)
     at = lane == features + iota((rows, LANES), 0) // own
     wide = (wide + jnp.where(at, weight, 0.0)).astype(BF16)
     by_row_ref[...] = wide
+    p, q = iota((rows, rows), 0), iota((rows, rows), 1)
+    swap = one_hot(q == (p % depth) * own + p // depth)
     by_token_ref[...] = dot(swap, wide).astype(BF16)
-    factors = factors_ref[...]
-    width = factors.shape[1]
-    w_ref[...] = jnp.concatenate([factors, jnp.zeros((LANES - features, width), BF16)], axis=0)
-    same = one_hot(iota((width, width), 0) == iota((width, width), 1))
-    turned = lax.dot_general(same, factors, (((1,), (1,)), ((), ())), preferred_element_type=F32)
-    pad = jnp.zeros((width, LANES - features), F32)
-    wt_ref[...] = jnp.concatenate([turned, pad], axis=1).astype(BF16)
 
 
 def scaled_pair(up_ref, inv, at):
@@ -128,10 +107,10 @@
 
 def weight_kernel(depth, features, n, pieces, *refs):
     a_refs, b_refs = refs[:pieces], refs[pieces : 2 * pieces]
-    up_ref, w_ref, wt_ref, perm_ref, wc_ref = refs[2 * pieces : 2 * pieces + 5]
-    outs = refs[2 * pieces + 5 :]
-    mi_ref, mj_ref, a_ref, b_ref, bt_ref, inv_ref, bias_ref, dw_ref, left_ref = outs[:9]
-    at_ref, v_ref, acc_ref, wide_ref = outs[9:]
+    up_ref, w_ref, perm_ref, wc_ref = refs[2 * pieces : 2 * pieces + 4]
+    outs = refs[2 * pieces + 4 :]
+    mj_ref, a_ref, b_ref, bt_ref, wt_ref, inv_ref, bias_ref, dw_ref, left_ref = outs[:9]
+    mi_ref, at_ref, v_ref, acc_ref, wide_ref = outs[9:]
     g, last = pl.program_id(0), pl.num_programs(0) - 1
     chunk, block, pair = up_ref.shape
     width = w_ref.shape[1] // 2
@@ -152,7 +131,11 @@
                 rows = pl.ds(pl.multiple_of(src * own, own), own)
                 for s in range(depth):
                     mj_ref[s, rows, :] = b_refs[k][s * own : (s + 1) * own, :]
-        w, wt = w_ref[...], wt_ref[...]
+        pad = jnp.zeros((LANES - features, 2 * width), BF16)
+        w = jnp.concatenate([w_ref[...], pad], axis=0)
+        same = one_hot(iota((2 * width, 2 * width), 0) == iota((2 * width, 2 * width), 1))
+        wt = dot_nt(same, w).astype(BF16)
+        wt_ref[...] = wt
         mi = mi_ref[...]
         a_ref[...] = dot(mi, w[:, :width]).astype(BF16)
         same = one_hot(iota((features, LANES), 0) == iota((features, LANES), 1))
@@ -201,16 +184,23 @@
         left_ref[...] = left
 
 
-def left_kernel(depth, up_ref, inv_ref, bt_ref, wc_ref, out_ref, v_ref):
+def left_kernel(depth, up_ref, inv_ref, bt_ref, wc_ref, small_ref, out_ref, pass_ref, v_ref):
     g = pl.program_id(0)
     chunk, _, pair = up_ref.shape
     width = wc_ref.shape[0]
     span = chunk * depth
+
+    @pl.when(g == 0)
+    def _():
+        pass_ref[...] = small_ref[...]
+
     fill_v(up_ref, inv_ref[g], bt_ref[...], v_ref, depth)
-    d_a = jnp.zeros((width, span), F32)
+    d_a = jnp.zeros((span, width), F32)
     for e in range(0, width, 2):
-        d_a = d_a + dot_nt(wc_ref[:, e * pair : (e + 2) * pair], two(v_ref, e))
-    out_ref[:, pl.ds(pl.multiple_of(g * span, span), span)] = d_a.astype(BF16)
+        d_a = d_a + dot_nt(two(v_ref, e), wc_ref[:, e * pair : (e + 2) * pair])
+    same = one_hot(iota((width, width), 0) == iota((width, width), 1))
+    d_a = dot_nt(same, d_a.astype(BF16)).astype(BF16)
+    out_ref[:, pl.ds(pl.multiple_of(g * span, span), span)] = d_a
 
 
 def token_kernel(depth, features, *refs):
@@ -230,12 +220,12 @@
     fill_t(a_chunk, wc_ref, t_ref, depth)
     d_b = db_ref[...]
     for at in range(0, chunk, 2):
-        d_b = d_b + dot_nt(scaled_pair(up_ref, inv, at), two(t_ref, at))
+        d_b = d_b + dot_nt(two(t_ref, at), scaled_pair(up_ref, inv, at))
     db_ref[...] = d_b
 
     @pl.when(g == last)
     def _():
-        d_b = db_ref[...].astype(BF16)
+        d_b = db_ref[...].T.astype(BF16)
         out_ref[...] = d_b
         turned = dot_nt(perm_ref[...], d_b).astype(BF16)
         right = jnp.zeros((width, LANES), F32)
@@ -246,8 +236,16 @@
         small_ref[width:, :] = jnp.broadcast_to(bias_ref[0:1, :], (16, LANES)).astype(BF16)
 
 
-def update_kernel(depth, inv_ref, a_ref, b_ref, wc_ref, offset_ref, out_ref, t_ref):
+def update_kernel(depth, count, *refs):
+    inv_ref, a_ref, b_ref, wc_ref, offset_ref = refs[:5]
+    in_refs, out_ref, pass_refs, t_ref = refs[5 : 5 + count], refs[5 + count], refs[6 + count : -1], refs[-1]
     g = pl.program_id(0)
+
+    @pl.when(g == 0)
+    def _():
+        for src, dst in zip(in_refs, pass_refs):
+            dst[...] = src[...]
+
     chunk, block, pair = out_ref.shape
     span = chunk * depth
     inv = inv_ref[g]
@@ -374,25 +372,15 @@
 
     r, c = lax.axis_index("row"), lax.axis_index("col")
     x = alignment_embedding.reshape(rows, features)
-    line = alignment_lines_exist.reshape(1, depth)
+    mask = (alignment_cell_exists * alignment_lines_exist[:, None]).astype(BF16)
     offset = offset_vector.reshape(1, pair)
-    args = (x, alignment_cell_exists, line, sitewise_factors, offset)
-    out_shapes = [
-        sds((rows, LANES), BF16),
-        sds((rows, LANES), BF16),
-        sds((LANES, 2 * width), BF16),
-        sds((2 * width, LANES), BF16),
-        sds(x.shape, x.dtype),
-        sds(offset.shape, F32),
-    ]
-    by_token, by_row, factors, factors_t, x, offset = call(
+    by_token, by_row = call(
         functools.partial(prep_kernel, depth, own),
         (),
-        [pl.BlockSpec(memory_space=pltpu.MemorySpace.HBM)] * len(args),
-        [full(o.shape) for o in out_shapes],
-        out_shapes,
-        [pltpu.VMEM(v.shape, v.dtype) for v in args[1:4]] + [pltpu.SemaphoreType.DMA((5,))],
-    )(*args)
+        [full(x.shape), full(mask.shape)],
+        [full((rows, LANES))] * 2,
+        [sds((rows, LANES), BF16)] * 2,
+    )(x, mask)
     a_pieces = [by_token] + [along_col(by_token, k) for k in range(1, n)]
     b_pieces = [to_column(by_row, k) for k in range(n)]
     if not split:
@@ -412,11 +400,11 @@
     up_spec = pl.BlockSpec((chunk, block, pair), lambda g: (g, 0, 0))
     tokens = block * depth
     out_shapes = [
-        sds((tokens, LANES), BF16),
         sds((depth, block, LANES), BF16),
         sds((tokens, width), BF16),
         sds((block, wide), BF16),
         sds((wide, block), BF16),
+        sds((2 * width, LANES), BF16),
         sds((steps, block, chunk), F32),
         sds((8, pair), F32),
         sds((width * width, pair), BF16),
@@ -428,18 +416,19 @@
         [full(p.shape) for p in a_pieces]
         + [full(p.shape) for p in b_pieces]
         + [up_spec]
-        + [full(v.shape) for v in (factors, factors_t, perm, pairing_wide)],
+        + [full(v.shape) for v in (sitewise_factors, perm, pairing_wide)],
         [full(o.shape) for o in out_shapes],
         out_shapes,
         [
+            pltpu.VMEM((tokens, LANES), BF16),
             pltpu.VMEM((width + features, tokens), BF16),
             pltpu.VMEM((width, chunk * depth, pair), BF16),
             pltpu.VMEM((width * width, pair), F32),
             pltpu.VMEM((features, width * pair), F32),
         ],
         cost(5e9, 8e6),
-    )(*a_pieces, *b_pieces, upstream_adjoint, factors, factors_t, perm, pairing_wide)
-    mi, mj, a, b, b_t, inv, bias, d_pairing, left = outs
+    )(*a_pieces, *b_pieces, upstream_adjoint, sitewise_factors, perm, pairing_wide)
+    mj, a, b, b_t, factors_t, inv, bias, d_pairing, left = outs
 
     bits = n.bit_length() - 1
     d_pairing = d_pairing.reshape(n, -1, LANES)
@@ -455,7 +444,7 @@
         + [full(v.shape) for v in (inv, a, pairing_wide, mj, perm, bias, left)],
         [full(o.shape) for o in out_shapes],
         out_shapes,
-        [pltpu.VMEM((chunk, wide, pair), BF16), pltpu.VMEM((block, wide), F32)],
+        [pltpu.VMEM((chunk, wide, pair), BF16), pltpu.VMEM((wide, block), F32)],
         cost(5e9, 8e6),
     )(upstream_adjoint, inv, a, pairing_wide, mj, perm, bias, left)
 
@@ -469,32 +458,32 @@
     for bit in range(bits):
         parts = swap_parts([d_pairing, db_go, small], "row", bit, n)
         if bit == 0:
-            d_a = call(
+            out_shapes = [sds((width, tokens), BF16), sds(small.shape, BF16)]
+            d_a, small = call(
                 functools.partial(left_kernel, depth),
                 (steps,),
-                [up_spec] + [full(v.shape) for v in (inv, b_t, pairing_wide)],
-                full((width, tokens)),
-                sds((width, tokens), BF16),
+                [up_spec] + [full(v.shape) for v in (inv, b_t, pairing_wide, small)],
+                [full(o.shape) for o in out_shapes],
+                out_shapes,
                 [pltpu.VMEM((width, chunk * depth, pair), BF16)],
                 cost(6e9, 8e6),
-            )(upstream_adjoint, inv, b_t, pairing_wide)
-            parts[0], d_a = lax.optimization_barrier((parts[0], d_a))
+            )(upstream_adjoint, inv, b_t, pairing_wide, small)
             d_a = jnp.stack([lay_out(d_a[:, k * rows : (k + 1) * rows]) for k in range(n)])
-            d_a = d_a.reshape((n // 2, 2) + d_a.shape[1:])
+            da_keep, da_go = halves(d_a.reshape((n // 2, 2) + d_a.shape[1:]), "col", 0, 1)
+            d_a = add(da_keep, *swap_parts([da_go], "col", 0, n))
         if bit == 1:
-            da_keep, da_go = halves(d_a, "col", 0, 1)
-            d_a = add(da_keep, *swap_parts([da_go], "col", 0, n))
-            coupling_update = call(
-                functools.partial(update_kernel, depth),
+            passed = (small, d_a.reshape(-1, LANES))
+            args = (inv, a, b, pairing_wide, offset) + passed
+            coupling_update, small, d_a = call(
+                functools.partial(update_kernel, depth, len(passed)),
                 (steps,),
-                [full(v.shape) for v in (inv, a, b, pairing_wide)] + [full((1, pair))],
-                up_spec,
-                sds((block, block, pair), BF16),
+                [full(v.shape) for v in args],
+                [up_spec] + [full(v.shape) for v in passed],
+                [sds((block, block, pair), BF16)] + [sds(v.shape, BF16) for v in passed],
                 [pltpu.VMEM((chunk, wide, pair), BF16)],
                 cost(6e9, 8e6),
-            )(inv, a, b, pairing_wide, offset)
-            held = (parts[0], coupling_update, d_a)
-            parts[0], coupling_update, d_a = lax.optimization_barrier(held)
+            )(*args)
+            d_a = d_a.reshape(da_keep.shape)
         d_pairing, d_b, small = add(d_pairing, parts[0]), add(db_keep, parts[1]), add(small, parts[2])
         db_keep = db_go = d_b
     d_pairing = d_pairing.reshape(1, -1, LANES)

time: 70.7 us -> 73.3 us (1.037)
  waiting for transfers between devices: 10.8 us -> 15.9 us
  local copies, waits for them, and re-layouts: 6.41 us -> 3.54 us
  other arithmetic: 0.54 us -> 1.32 us
    ppermute x4, starting transfers between devices: 11 us -> 5.82 us  [to_column(): return lax.ppermute(x, axes, pairs)]
    ppermute x7, waiting for transfers between devices: 9.29 us -> 14.3 us  [swap_parts(): message = lax.ppermute(message, axis, [(i, i ^ 1 << bit) for i in range(n)])]
    ppermute x7, starting transfers between devices: 6.25 us -> 10.6 us  [swap_parts(): message = lax.ppermute(message, axis, [(i, i ^ 1 << bit) for i in range(n)])]
    ppermute x4, waiting for transfers between devices: 0.01 us -> 1.6 us  [to_column(): return lax.ppermute(x, axes, pairs)]
    ppermute x3, waiting for transfers between devices: 1.48 us -> 0.01 us  [along_col(): return lax.ppermute(x, 'col', [(i, (i + k) % n) for i in range(n)])]
    unnamed x18 -> x12, local copies, waits for them, and re-layouts: 3.77 us -> 2.33 us
    slice x8 -> x4, local copies, waits for them, and re-layouts: 1.44 us -> 0.01 us  [swap_parts(): got.append(message[at:at + part.shape[0]])]
    ppermute x3, starting transfers between devices: 2.23 us -> 3.23 us  [along_col(): return lax.ppermute(x, 'col', [(i, (i + k) % n) for i in range(n)])]
  transfers between devices with their start and end apart: 14 -> 14, of which waited for: 4 -> 8; matrix products, arithmetic and copies ran while one was open for 2% -> 2% of each run, Pallas kernels for 31% -> 9%
where the time goes in v5:
time: 73.3 us; the launch traced here: 73 us
  Pallas kernels  31.5 us (43%)
  starting transfers between devices  19.7 us (27%)
  waiting for transfers between devices  15.9 us (22%)
  local copies, waits for them, and re-layouts  3.54 us (5%)
  other arithmetic  1.32 us (2%)
  between operations  1.03 us (1%)
    ppermute x7, waiting for transfers between devices, swap_parts(): message = lax.ppermute(message, axis, [(i, i ^ 1 << bit) for i in range(n)])  14.3 us
    ppermute x7, starting transfers between devices, swap_parts(): message = lax.ppermute(message, axis, [(i, i ^ 1 << bit) for i in range(n)])  10.6 us
    pallas_call x1, Pallas kernels, per_device(): call(functools.partial(left_kernel, depth), (steps,), [up_spec] + [full(v...  9.86 us
    pallas_call x1, Pallas kernels, per_device(): call(functools.partial(weight_kernel, depth, features, n, pieces), (steps...  7.63 us
    ppermute x4, starting transfers between devices, to_column(): return lax.ppermute(x, axes, pairs)  5.82 us
    pallas_call x1, Pallas kernels, per_device(): call(functools.partial(token_kernel, depth, features), (steps,), [up_spec...  5.57 us
    pallas_call x1, Pallas kernels, per_device(): call(functools.partial(update_kernel, depth, len(passed)), (steps,), [ful...  4.9 us
    ppermute x3, starting transfers between devices, along_col(): return lax.ppermute(x, 'col', [(i, (i + k) % n) for i in range(n)])  3.23 us
  transfers between devices with their start and end apart: 14, of which 8 were waited for; matrix products, arithmetic and copies ran while one was open for 2% of the time, Pallas kernels for 9%

profile of v5, /device:TPU:0, one launch (start us, length us, event | category | flops | bytes accessed | tf_op | source)
XLA Modules:
  0.0 73.0 jit_solution(5817815179496613554)
XLA Ops:
  0.6 0.8 %multiply_convert_fusion.mask_ref = bf16[16,16]{1,0:T(8,128)(2,1)S(1)} fusion(s32[16,16]{1,0:T(8,128)} %param.8, s32[16]{0:T(128)} %param.9), kind=kLoop, calls=%fused_computation.61 | loop fusion | flops 512 | bytes 1600 | tf_op jit(solution)/shard_map/convert_element_type | solution.py:375
  1.4 0.0 copy-start
  1.4 0.8 %copy-done = bf16[16,16,64]{2,1,0:T(8,128)(2,1)S(1)} copy-done((bf16[16,16,64]{2,1,0:T(8,128)(2,1)S(1)}, bf16[16,16,64]{2,1,0:T(8,128)(2,1)}, u32[]{:S(2)}) %copy-start) | copy-done | bytes 32792
  2.2 0.0 copy-start.2
  2.2 0.4 shard_map.110
  2.7 2.4 %collective-permute-start.2 = (bf16[256,128]{1,0:T(8,128)(2,1)S(1)}, bf16[256,128]{1,0:T(8,128)(2,1)S(1)}, u32[]{:S(2)}, u32[]{:S(2)}) collective-permute-start(bf16[256,128]{1,0:T(8,128)(2,1)S(1)} %get-tuple-element.26.refs_0_), channel_id=1, source_target_pairs={{0,3},{1,0},{2,1},{3,2},{4,7},{5,4},{6,5},{7,6},{8,11},{9,8},{10,9... | collective-permute-start | bytes 196616 | tf_op jit(solution)/shard_map/ppermute | solution.py:364
  5.1 0.6 collective-permute-start.1
  5.7 0.2 collective-permute-start
  5.9 3.6 %collective-permute-start.6 = (bf16[256,128]{1,0:T(8,128)(2,1)S(1)}, bf16[256,128]{1,0:T(8,128)(2,1)S(1)}, u32[]{:S(2)}, u32[]{:S(2)}) collective-permute-start(bf16[256,128]{1,0:T(8,128)(2,1)S(1)} %get-tuple-element.27.refs_6_), channel_id=1, source_target_pairs={{0,12},{1,0},{2,4},{3,8},{4,13},{5,1},{6,5},{7,9},{8,14},{9,2},{10... | collective-permute-start | bytes 196616 | tf_op jit(solution)/shard_map/ppermute | solution.py:371
  9.5 1.2 %collective-permute-start.5 = (bf16[256,128]{1,0:T(8,128)(2,1)S(1)}, bf16[256,128]{1,0:T(8,128)(2,1)S(1)}, u32[]{:S(2)}, u32[]{:S(2)}) collective-permute-start(bf16[256,128]{1,0:T(8,128)(2,1)S(1)} %get-tuple-element.27.refs_6_), channel_id=1, source_target_pairs={{0,8},{1,12},{2,0},{3,4},{4,9},{5,13},{6,1},{7,5},{8,10},{9,14},{1... | collective-permute-start | bytes 196616 | tf_op jit(solution)/shard_map/ppermute | solution.py:371
  10.7 0.0 collective-permute-done.2.refs_3_
  10.7 0.3 collective-permute-start.4
  11.1 0.0 collective-permute-done.1.refs_2_
  11.1 0.7 collective-permute-start.3
  11.8 0.2 fusion.refs_10_.refs_5_.refs_8_
  11.9 0.0 copy-start.3
  11.9 1.1 %reshape.205.refs_11_.refs_3_.wc_ref = bf16[32,4096]{1,0:T(8,128)(2,1)S(1)} reshape(bf16[1024,128]{1,0:T(8,128)(2,1)} %param.11) | data formatting | bytes 524288 | tf_op jit(solution)/shard_map/reshape | solution.py:399
  13.0 0.0 collective-permute-done.refs_1_
  13.0 0.0 collective-permute-done.6.refs_7_
  13.0 0.8 %collective-permute-done.5.refs_6_ = bf16[256,128]{1,0:T(8,128)(2,1)S(1)} collective-permute-done((bf16[256,128]{1,0:T(8,128)(2,1)S(1)}, bf16[256,128]{1,0:T(8,128)(2,1)S(1)}, u32[]{:S(2)}, u32[]{:S(2)}) %collective-permute-start.5) | collective-permute-done | bytes 65568 | tf_op jit(solution)/shard_map/ppermute | solution.py:371
  13.9 0.8 %collective-permute-done.4.refs_5_ = bf16[256,128]{1,0:T(8,128)(2,1)S(1)} collective-permute-done((bf16[256,128]{1,0:T(8,128)(2,1)S(1)}, bf16[256,128]{1,0:T(8,128)(2,1)S(1)}, u32[]{:S(2)}, u32[]{:S(2)}) %collective-permute-start.4) | collective-permute-done | bytes 65568 | tf_op jit(solution)/shard_map/ppermute | solution.py:371
  14.6 0.0 collective-permute-done.3.refs_4_
  14.6 0.0 copy-done.2
  14.6 0.0 copy-done.3
  14.6 7.6 %shard_map.111 = (bf16[16,64,128]{2,1,0:T(8,128)(2,1)S(1)}, bf16[1024,32]{1,0:T(8,128)(2,1)S(1)}, bf16[64,512]{1,0:T(8,128)(2,1)S(1)}, bf16[512,64]{1,0:T(8,128)...) custom-call(bf16[256,128]{1,0:T(8,128)(2,1)S(1)} %get-tuple-element., ...), custom_call_target="tpu_custom_call" | custom-call | flops 5000000000 | bytes 8000000 | tf_op jit(solution)/shard_map/pallas_call | solution.py:413
  22.3 5.6 %shard_map.112 = (bf16[48,128]{1,0:T(8,128)(2,1)S(1)}, bf16[64,512]{1,0:T(8,128)(2,1)S(1)}) custom-call(bf16[64,64,128]{2,1,0:T(8,128)(2,1)S(1)} %copy-done.2, f32[4,64,16]{2,1,0:T(8,128)S(1)} %get-tuple-element.28.refs_1_.inv_ref.refs_0_, bf16[1024,32]{1,0:T(8,128)(2,1)S(1)} %get-tuple-element.29.refs_2_.refs_1_, ...), custom_call_target="tpu_custom_call" | custom-call | flops 5000000000 | bytes 8000000 | tf_op jit(solution)/shard_map/pallas_call | solution.py:440
  27.9 7.4 %collective-permute-start.7 = (bf16[512,128]{1,0:T(8,128)(2,1)S(1)}, bf16[512,128]{1,0:T(8,128)(2,1)S(1)}, u32[]{:S(2)}, u32[]{:S(2)}) collective-permute-start(bf16[512,128]{1,0:T(8,128)(2,1)S(1)} %bitcast.164), channel_id=1, source_target_pairs={{0,2},{1,3},{2,0},{3,1},{4,6},{5,7},{6,4},{7,5},{8,10},{9,11},{10,... | collective-permute-start | bytes 393224 | tf_op jit(solution)/shard_map/ppermute | solution.py:315
  35.3 3.1 %collective-permute-done.7 = bf16[512,128]{1,0:T(8,128)(2,1)S(1)} collective-permute-done((bf16[512,128]{1,0:T(8,128)(2,1)S(1)}, bf16[512,128]{1,0:T(8,128)(2,1)S(1)}, u32[]{:S(2)}, u32[]{:S(2)}) %collective-permute-start.7) | collective-permute-done | bytes 131104 | tf_op jit(solution)/shard_map/ppermute | solution.py:315
  38.5 0.1 collective-permute-start.8
  38.6 1.3 %collective-permute-done.8 = bf16[432,128]{1,0:T(8,128)(2,1)S(1)} collective-permute-done((bf16[432,128]{1,0:T(8,128)(2,1)S(1)}, bf16[432,128]{1,0:T(8,128)(2,1)S(1)}, u32[]{:S(2)}, u32[]{:S(2)}) %collective-permute-start.8) | collective-permute-done | bytes 110624 | tf_op jit(solution)/shard_map/ppermute | solution.py:315
  39.9 9.9 %shard_map.113 = (bf16[32,1024]{1,0:T(8,128)(2,1)S(1)}, bf16[48,128]{1,0:T(8,128)(2,1)S(1)}) custom-call(bf16[64,64,128]{2,1,0:T(8,128)(2,1)S(1)} %copy-done.2, f32[4,64,16]{2,1,0:T(8,128)S(1)} %get-tuple-element.28.refs_1_.inv_ref.refs_0_, bf16[512,64]{1,0:T(8,128)(2,1)S(1)} %get-tuple-element.31.bt_ref, ...), custom_call_target="tpu_custom_call" | custom-call | flops 6000000000 | bytes 8000000 | tf_op jit(solution)/shard_map/pallas_call | solution.py:462
  49.9 0.2 collective-permute-start.10
  50.2 0.1 collective-permute-start.9
  50.3 0.9 %collective-permute-done.10 = bf16[128,128]{1,0:T(8,128)(2,1)S(1)} collective-permute-done((bf16[128,128]{1,0:T(8,128)(2,1)S(1)}, bf16[128,128]{1,0:T(8,128)(2,1)S(1)}, u32[]{:S(2)}, u32[]{:S(2)}) %collective-permute-start.10) | collective-permute-done | bytes 32800 | tf_op jit(solution)/shard_map/ppermute | solution.py:315
  51.2 4.4 %collective-permute-done.9 = bf16[432,128]{1,0:T(8,128)(2,1)S(1)} collective-permute-done((bf16[432,128]{1,0:T(8,128)(2,1)S(1)}, bf16[432,128]{1,0:T(8,128)(2,1)S(1)}, u32[]{:S(2)}, u32[]{:S(2)}) %collective-permute-start.9) | collective-permute-done | bytes 110624 | tf_op jit(solution)/shard_map/ppermute | solution.py:315
  55.7 0.9 %collective-permute-start.11 = (bf16[432,128]{1,0:T(8,128)(2,1)S(1)}, bf16[432,128]{1,0:T(8,128)(2,1)S(1)}, u32[]{:S(2)}, u32[]{:S(2)}) collective-permute-start(bf16[432,128]{1,0:T(8,128)(2,1)S(1)} %pad_maximum_fusion.4), channel_id=1, source_target_pairs={{0,8},{4,12},{8,0},{12,4},{1,9},{5,13},{9,1},{13,5},{2,10},{6,14},... | collective-permute-start | bytes 331784 | tf_op jit(solution)/shard_map/ppermute | solution.py:315
  56.6 0.0 copy-start.4
  56.6 0.7 copy-done.4
  57.2 4.9 %shard_map.114 = (bf16[64,64,128]{2,1,0:T(8,128)(2,1)}, bf16[48,128]{1,0:T(8,128)(2,1)S(1)}, bf16[128,128]{1,0:T(8,128)(2,1)S(1)}) custom-call(f32[4,64,16]{2,1,0:T(8,128)S(1)} %get-tuple-element.28.refs_1_.inv_ref.refs_0_, bf16[1024,32]{1,0:T(8,128)(2,1)S(1)} %get-tuple-element.29.refs_2_.refs_1_, bf16[64,512]{1,0:T(8,128)(2,1)S(1)} %get-tuple-element.30.refs_2_, ...), custom_call_target="tpu_custom_call" | custom-call | flops 6000000000 | bytes 8000000 | tf_op jit(solution)/shard_map/pallas_call | solution.py:477
  62.1 1.4 %collective-permute-done.11 = bf16[432,128]{1,0:T(8,128)(2,1)S(1)} collective-permute-done((bf16[432,128]{1,0:T(8,128)(2,1)S(1)}, bf16[432,128]{1,0:T(8,128)(2,1)S(1)}, u32[]{:S(2)}, u32[]{:S(2)}) %collective-permute-start.11) | collective-permute-done | bytes 110624 | tf_op jit(solution)/shard_map/ppermute | solution.py:315
  63.6 1.9 %collective-permute-start.12 = (bf16[432,128]{1,0:T(8,128)(2,1)S(1)}, bf16[432,128]{1,0:T(8,128)(2,1)S(1)}, u32[]{:S(2)}, u32[]{:S(2)}) collective-permute-start(bf16[432,128]{1,0:T(8,128)(2,1)S(1)} %pad_maximum_fusion.5), channel_id=1, source_target_pairs={{0,2},{1,3},{2,0},{3,1},{4,6},{5,7},{6,4},{7,5},{8,10},{9,11},{10,... | collective-permute-start | bytes 331784 | tf_op jit(solution)/shard_map/ppermute | solution.py:315
  65.5 3.2 %collective-permute-done.12 = bf16[432,128]{1,0:T(8,128)(2,1)S(1)} collective-permute-done((bf16[432,128]{1,0:T(8,128)(2,1)S(1)}, bf16[432,128]{1,0:T(8,128)(2,1)S(1)}, u32[]{:S(2)}, u32[]{:S(2)}) %collective-permute-start.12) | collective-permute-done | bytes 110624 | tf_op jit(solution)/shard_map/ppermute | solution.py:315
  68.8 0.1 collective-permute-start.13
  68.9 0.0 copy-start.1
  68.9 0.8 %copy-done.1 = bf16[16,16,64]{2,1,0:T(8,128)(2,1)S(1)} copy-done((bf16[16,16,64]{2,1,0:T(8,128)(2,1)S(1)}, bf16[16,16,64]{2,1,0:T(8,128)(2,1)}, u32[]{:S(2)}) %copy-start.1) | copy-done | bytes 32792
  69.7 1.9 %shard_map.115 = (f32[256,64]{1,0:T(8,128)}, f32[64,64]{1,0:T(8,128)}, f32[1,128]{1,0:T(1,128)}) custom-call(bf16[32,256]{1,0:T(8,128)(2,1)S(1)} %bitcast.146, bf16[32,256]{1,0:T(8,128)(2,1)S(1)} %bitcast.148, bf16[16,512]{1,0:T(8,128)(2,1)S(1)} %bitcast.147, bf16[48,128]{1,0:T(8,128)(2,1)S(1)} %add_convert_fusion.2.refs_3_, ...), custom_call_target="tpu_custom_call" | custom-call | tf_op jit(solution)/shard_map/pallas_call | solution.py:510
  71.6 0.0 collective-permute-done.13
  71.7 1.3 %shard_map.116 = f32[32,32,128]{2,1,0:T(8,128)} custom-call(bf16[32,32,128]{2,1,0:T(8,128)(2,1)S(1)} %bitcast.141), custom_call_target="tpu_custom_call" | custom-call | tf_op jit(solution)/shard_map/pallas_call | solution.py:519
  (46 shorter events, 0.6 us)
Async XLA Ops:
  1.4 0.8 %copy-start = (bf16[16,16,64]{2,1,0:T(8,128)(2,1)S(1)}, bf16[16,16,64]{2,1,0:T(8,128)(2,1)}, u32[]{:S(2)}) copy-start(bf16[16,16,64]{2,1,0:T(8,128)(2,1)} %param.7) | copy-start | bytes 98308
  2.2 12.4 %copy-start.2 = (bf16[64,64,128]{2,1,0:T(8,128)(2,1)S(1)}, bf16[64,64,128]{2,1,0:T(8,128)(2,1)}, u32[]{:S(2)}) copy-start(bf16[64,64,128]{2,1,0:T(8,128)(2,1)} %up_ref.1) | copy-start | bytes 3145732
  2.7 8.1 %collective-permute-start.2 = (bf16[256,128]{1,0:T(8,128)(2,1)S(1)}, bf16[256,128]{1,0:T(8,128)(2,1)S(1)}, u32[]{:S(2)}, u32[]{:S(2)}) collective-permute-start(bf16[256,128]{1,0:T(8,128)(2,1)S(1)} %get-tuple-element.26.refs_0_), channel_id=1, source_target_pairs={{0,3},{1,0},{2,1},{3,2},{4,7},{5,4},{6,5},{7,6},{8,11},{9,8},{10,9... | collective-permute-start | bytes 196616 | tf_op jit(solution)/shard_map/ppermute | solution.py:364
  5.1 6.0 %collective-permute-start.1 = (bf16[256,128]{1,0:T(8,128)(2,1)S(1)}, bf16[256,128]{1,0:T(8,128)(2,1)S(1)}, u32[]{:S(2)}, u32[]{:S(2)}) collective-permute-start(bf16[256,128]{1,0:T(8,128)(2,1)S(1)} %get-tuple-element.26.refs_0_), channel_id=1, source_target_pairs={{0,2},{1,3},{2,0},{3,1},{4,6},{5,7},{6,4},{7,5},{8,10},{9,11},{10,... | collective-permute-start | bytes 196616 | tf_op jit(solution)/shard_map/ppermute | solution.py:364
  5.7 7.3 %collective-permute-start = (bf16[256,128]{1,0:T(8,128)(2,1)S(1)}, bf16[256,128]{1,0:T(8,128)(2,1)S(1)}, u32[]{:S(2)}, u32[]{:S(2)}) collective-permute-start(bf16[256,128]{1,0:T(8,128)(2,1)S(1)} %get-tuple-element.26.refs_0_), channel_id=1, source_target_pairs={{0,1},{1,2},{2,3},{3,0},{4,5},{5,6},{6,7},{7,4},{8,9},{9,10},{10,1... | collective-permute-start | bytes 196616 | tf_op jit(solution)/shard_map/ppermute | solution.py:364
  5.9 7.1 %collective-permute-start.6 = (bf16[256,128]{1,0:T(8,128)(2,1)S(1)}, bf16[256,128]{1,0:T(8,128)(2,1)S(1)}, u32[]{:S(2)}, u32[]{:S(2)}) collective-permute-start(bf16[256,128]{1,0:T(8,128)(2,1)S(1)} %get-tuple-element.27.refs_6_), channel_id=1, source_target_pairs={{0,12},{1,0},{2,4},{3,8},{4,13},{5,1},{6,5},{7,9},{8,14},{9,2},{10... | collective-permute-start | bytes 196616 | tf_op jit(solution)/shard_map/ppermute | solution.py:371
  9.5 4.4 %collective-permute-start.5 = (bf16[256,128]{1,0:T(8,128)(2,1)S(1)}, bf16[256,128]{1,0:T(8,128)(2,1)S(1)}, u32[]{:S(2)}, u32[]{:S(2)}) collective-permute-start(bf16[256,128]{1,0:T(8,128)(2,1)S(1)} %get-tuple-element.27.refs_6_), channel_id=1, source_target_pairs={{0,8},{1,12},{2,0},{3,4},{4,9},{5,13},{6,1},{7,5},{8,10},{9,14},{1... | collective-permute-start | bytes 196616 | tf_op jit(solution)/shard_map/ppermute | solution.py:371
  10.7 3.9 %collective-permute-start.4 = (bf16[256,128]{1,0:T(8,128)(2,1)S(1)}, bf16[256,128]{1,0:T(8,128)(2,1)S(1)}, u32[]{:S(2)}, u32[]{:S(2)}) collective-permute-start(bf16[256,128]{1,0:T(8,128)(2,1)S(1)} %get-tuple-element.27.refs_6_), channel_id=1, source_target_pairs={{0,4},{1,8},{2,12},{3,0},{4,5},{5,9},{6,13},{7,1},{8,6},{9,10},{10... | collective-permute-start | bytes 196616 | tf_op jit(solution)/shard_map/ppermute | solution.py:371
  11.1 3.5 %collective-permute-start.3 = (bf16[256,128]{1,0:T(8,128)(2,1)S(1)}, bf16[256,128]{1,0:T(8,128)(2,1)S(1)}, u32[]{:S(2)}, u32[]{:S(2)}) collective-permute-start(bf16[256,128]{1,0:T(8,128)(2,1)S(1)} %get-tuple-element.27.refs_6_), channel_id=1, source_target_pairs={{0,0},{1,4},{2,8},{3,12},{4,1},{5,5},{6,9},{7,13},{8,2},{9,6},{10,... | collective-permute-start | bytes 196616 | tf_op jit(solution)/shard_map/ppermute | solution.py:371
  11.9 2.7 %copy-start.3 = (bf16[64,64]{1,0:T(8,128)(2,1)S(1)}, bf16[64,64]{1,0:T(8,128)(2,1)}, u32[]{:S(2)}) copy-start(bf16[64,64]{1,0:T(8,128)(2,1)} %refs_9_.1) | copy-start | bytes 24580
  27.9 10.5 %collective-permute-start.7 = (bf16[512,128]{1,0:T(8,128)(2,1)S(1)}, bf16[512,128]{1,0:T(8,128)(2,1)S(1)}, u32[]{:S(2)}, u32[]{:S(2)}) collective-permute-start(bf16[512,128]{1,0:T(8,128)(2,1)S(1)} %bitcast.164), channel_id=1, source_target_pairs={{0,2},{1,3},{2,0},{3,1},{4,6},{5,7},{6,4},{7,5},{8,10},{9,11},{10,... | collective-permute-start | bytes 393224 | tf_op jit(solution)/shard_map/ppermute | solution.py:315
  38.5 1.4 %collective-permute-start.8 = (bf16[432,128]{1,0:T(8,128)(2,1)S(1)}, bf16[432,128]{1,0:T(8,128)(2,1)S(1)}, u32[]{:S(2)}, u32[]{:S(2)}) collective-permute-start(bf16[432,128]{1,0:T(8,128)(2,1)S(1)} %pad_maximum_fusion.2), channel_id=1, source_target_pairs={{0,1},{1,0},{2,3},{3,2},{4,5},{5,4},{6,7},{7,6},{8,9},{9,8},{10,11... | collective-permute-start | bytes 331784 | tf_op jit(solution)/shard_map/ppermute | solution.py:315
  49.9 1.3 %collective-permute-start.10 = (bf16[128,128]{1,0:T(8,128)(2,1)S(1)}, bf16[128,128]{1,0:T(8,128)(2,1)S(1)}, u32[]{:S(2)}, u32[]{:S(2)}) collective-permute-start(bf16[128,128]{1,0:T(8,128)(2,1)S(1)} %bitcast.179), channel_id=1, source_target_pairs={{0,1},{1,0},{2,3},{3,2},{4,5},{5,4},{6,7},{7,6},{8,9},{9,8},{10,11... | collective-permute-start | bytes 98312 | tf_op jit(solution)/shard_map/ppermute | solution.py:315
  50.2 5.4 %collective-permute-start.9 = (bf16[432,128]{1,0:T(8,128)(2,1)S(1)}, bf16[432,128]{1,0:T(8,128)(2,1)S(1)}, u32[]{:S(2)}, u32[]{:S(2)}) collective-permute-start(bf16[432,128]{1,0:T(8,128)(2,1)S(1)} %pad_maximum_fusion.3), channel_id=1, source_target_pairs={{0,4},{4,0},{8,12},{12,8},{1,5},{5,1},{9,13},{13,9},{2,6},{6,2},{1... | collective-permute-start | bytes 331784 | tf_op jit(solution)/shard_map/ppermute | solution.py:315
  55.7 7.8 %collective-permute-start.11 = (bf16[432,128]{1,0:T(8,128)(2,1)S(1)}, bf16[432,128]{1,0:T(8,128)(2,1)S(1)}, u32[]{:S(2)}, u32[]{:S(2)}) collective-permute-start(bf16[432,128]{1,0:T(8,128)(2,1)S(1)} %pad_maximum_fusion.4), channel_id=1, source_target_pairs={{0,8},{4,12},{8,0},{12,4},{1,9},{5,13},{9,1},{13,5},{2,10},{6,14},... | collective-permute-start | bytes 331784 | tf_op jit(solution)/shard_map/ppermute | solution.py:315
  56.6 0.7 copy-start.4
  63.6 5.1 %collective-permute-start.12 = (bf16[432,128]{1,0:T(8,128)(2,1)S(1)}, bf16[432,128]{1,0:T(8,128)(2,1)S(1)}, u32[]{:S(2)}, u32[]{:S(2)}) collective-permute-start(bf16[432,128]{1,0:T(8,128)(2,1)S(1)} %pad_maximum_fusion.5), channel_id=1, source_target_pairs={{0,2},{1,3},{2,0},{3,1},{4,6},{5,7},{6,4},{7,5},{8,10},{9,11},{10,... | collective-permute-start | bytes 331784 | tf_op jit(solution)/shard_map/ppermute | solution.py:315
  68.8 2.8 %collective-permute-start.13 = (bf16[512,128]{1,0:T(8,128)(2,1)S(1)}, bf16[512,128]{1,0:T(8,128)(2,1)S(1)}, u32[]{:S(2)}, u32[]{:S(2)}) collective-permute-start(bf16[512,128]{1,0:T(8,128)(2,1)S(1)} %bitcast.162), channel_id=1, source_target_pairs={{0,1},{1,0},{2,3},{3,2},{4,5},{5,4},{6,7},{7,6},{8,9},{9,8},{10,11... | collective-permute-start | bytes 393224 | tf_op jit(solution)/shard_map/ppermute | solution.py:315
  68.9 0.8 %copy-start.1 = (bf16[16,16,64]{2,1,0:T(8,128)(2,1)S(1)}, bf16[16,16,64]{2,1,0:T(8,128)(2,1)}, u32[]{:S(2)}) copy-start(bf16[16,16,64]{2,1,0:T(8,128)(2,1)} %param.7) | copy-start | bytes 98308

commit v6 on v5

--- a/solution.py
+++ b/solution.py
@@ -184,8 +184,8 @@
         left_ref[...] = left
 
 
-def left_kernel(depth, up_ref, inv_ref, bt_ref, wc_ref, small_ref, out_ref, pass_ref, v_ref):
-    g = pl.program_id(0)
+def left_kernel(depth, bit, up_ref, inv_ref, bt_ref, wc_ref, small_ref, keep_ref, go_ref, pass_ref, v_ref, da_ref):
+    g, last = pl.program_id(0), pl.num_programs(0) - 1
     chunk, _, pair = up_ref.shape
     width = wc_ref.shape[0]
     span = chunk * depth
@@ -195,19 +195,27 @@
         pass_ref[...] = small_ref[...]
 
     fill_v(up_ref, inv_ref[g], bt_ref[...], v_ref, depth)
-    d_a = jnp.zeros((span, width), F32)
-    for e in range(0, width, 2):
-        d_a = d_a + dot_nt(two(v_ref, e), wc_ref[:, e * pair : (e + 2) * pair])
+    v = jnp.concatenate([v_ref[e] for e in range(width)], axis=1)
+    d_a = dot_nt(v, wc_ref[...])
     same = one_hot(iota((width, width), 0) == iota((width, width), 1))
     d_a = dot_nt(same, d_a.astype(BF16)).astype(BF16)
-    out_ref[:, pl.ds(pl.multiple_of(g * span, span), span)] = d_a
-
-
-def token_kernel(depth, features, *refs):
+    tiles = span // LANES
+    for k in range(tiles):
+        da_ref[g * tiles + k] = d_a[:, k * LANES : (k + 1) * LANES]
+
+    @pl.when(g == last)
+    def _():
+        half = keep_ref.shape[0]
+        here = (lax.axis_index("col") >> bit) & 1
+        keep_ref[...] = da_ref[pl.ds(here * half, half)]
+        go_ref[...] = da_ref[pl.ds((1 - here) * half, half)]
+
+
+def token_kernel(depth, features, n, *refs):
     up_ref, inv_ref, a_ref, wc_ref, mj_ref, perm_ref, bias_ref, left_ref = refs[:8]
     small_ref, out_ref, t_ref, db_ref = refs[8:]
     g, last = pl.program_id(0), pl.num_programs(0) - 1
-    chunk = up_ref.shape[0]
+    chunk, block = up_ref.shape[:2]
     width = wc_ref.shape[0]
     span = chunk * depth
     inv = inv_ref[g]
@@ -218,15 +226,18 @@
 
     a_chunk = a_ref[pl.ds(pl.multiple_of(g * span, span), span), :]
     fill_t(a_chunk, wc_ref, t_ref, depth)
-    d_b = db_ref[...]
-    for at in range(0, chunk, 2):
-        d_b = d_b + dot_nt(two(t_ref, at), scaled_pair(up_ref, inv, at))
-    db_ref[...] = d_b
+    t = jnp.concatenate([t_ref[i] for i in range(chunk)], axis=1)
+    scaled = jnp.concatenate([scaled_pair(up_ref, inv, at) for at in range(0, chunk, 2)], axis=1)
+    db_ref[...] += dot_nt(t, scaled)
 
     @pl.when(g == last)
     def _():
         d_b = db_ref[...].T.astype(BF16)
-        out_ref[...] = d_b
+        own = block // n
+        for k in range(n):
+            part = d_b[k * own : (k + 1) * own, :]
+            for q in range(part.shape[1] // LANES):
+                out_ref[k, q * own : (q + 1) * own, :] = part[:, q * LANES : (q + 1) * LANES]
         turned = dot_nt(perm_ref[...], d_b).astype(BF16)
         right = jnp.zeros((width, LANES), F32)
         for s in range(depth):
@@ -236,15 +247,12 @@
         small_ref[width:, :] = jnp.broadcast_to(bias_ref[0:1, :], (16, LANES)).astype(BF16)
 
 
-def update_kernel(depth, count, *refs):
-    inv_ref, a_ref, b_ref, wc_ref, offset_ref = refs[:5]
-    in_refs, out_ref, pass_refs, t_ref = refs[5 : 5 + count], refs[5 + count], refs[6 + count : -1], refs[-1]
+def update_kernel(depth, inv_ref, a_ref, b_ref, wc_ref, offset_ref, small_ref, out_ref, pass_ref, t_ref):
     g = pl.program_id(0)
 
     @pl.when(g == 0)
     def _():
-        for src, dst in zip(in_refs, pass_refs):
-            dst[...] = src[...]
+        pass_ref[...] = small_ref[...]
 
     chunk, block, pair = out_ref.shape
     span = chunk * depth
@@ -292,13 +300,6 @@
         out_ref[:, e, :] = in_ref[e].astype(F32)
 
 
-def lay_out(x):
-    rows, lanes = x.shape
-    if lanes % LANES:
-        return x.reshape(-1, LANES)
-    return x.reshape(rows, lanes // LANES, LANES).transpose(1, 0, 2).reshape(-1, LANES)
-
-
 def lay_back(x, rows, lanes):
     if lanes % LANES:
         return x.reshape(rows, lanes)
@@ -312,7 +313,8 @@
 def swap_parts(parts, axis, bit, n):
     parts = [part.reshape(-1, LANES) for part in parts]
     message = jnp.concatenate(parts, axis=0) if len(parts) > 1 else parts[0]
-    message = lax.ppermute(message, axis, [(i, i ^ (1 << bit)) for i in range(n)])
+    pairs = [(i, i ^ (1 << bit)) for i in range(n)]
+    message = lax.ppermute(message, axis, pairs)
     got, at = [], 0
     for part in parts:
         got.append(message[at : at + part.shape[0]])
@@ -436,19 +438,18 @@
         keep, go = halves(split_high(d_pairing), "col", bit, 0)
         d_pairing = add(keep, *swap_parts([go], "col", bit, n))
 
-    out_shapes = [sds((width + 16, LANES), BF16), sds((block, wide), BF16)]
+    out_shapes = [sds((width + 16, LANES), BF16), sds((n, own * wide // LANES, LANES), BF16)]
     small, d_b = call(
-        functools.partial(token_kernel, depth, features),
+        functools.partial(token_kernel, depth, features, n),
         (steps,),
         [up_spec]
         + [full(v.shape) for v in (inv, a, pairing_wide, mj, perm, bias, left)],
         [full(o.shape) for o in out_shapes],
         out_shapes,
         [pltpu.VMEM((chunk, wide, pair), BF16), pltpu.VMEM((wide, block), F32)],
-        cost(5e9, 8e6),
+        cost(8e9, 8e6),
     )(upstream_adjoint, inv, a, pairing_wide, mj, perm, bias, left)
 
-    d_b = jnp.stack([lay_out(d_b[k * own : (k + 1) * own]) for k in range(n)])
     dp_keep, dp_go = halves(d_pairing, "col", 0, 0)
     db_keep, db_go = halves(d_b.reshape((n // 2, 2) + d_b.shape[1:]), "col", 0, 1)
     parts = swap_parts([dp_go, db_go, small], "col", 0, n)
@@ -458,41 +459,43 @@
     for bit in range(bits):
         parts = swap_parts([d_pairing, db_go, small], "row", bit, n)
         if bit == 0:
-            out_shapes = [sds((width, tokens), BF16), sds(small.shape, BF16)]
-            d_a, small = call(
-                functools.partial(left_kernel, depth),
+            coupling_update, small = call(
+                functools.partial(update_kernel, depth),
+                (steps,),
+                [full(v.shape) for v in (inv, a, b, pairing_wide, offset, small)],
+                [up_spec, full(small.shape)],
+                [sds((block, block, pair), BF16), sds(small.shape, BF16)],
+                [pltpu.VMEM((chunk, wide, pair), BF16)],
+                cost(6e9, 8e6),
+            )(inv, a, b, pairing_wide, offset, small)
+        if bit == 1:
+            half = (tokens // LANES // 2, width, LANES)
+            out_shapes = [sds(half, BF16), sds(half, BF16), sds(small.shape, BF16)]
+            *d_a, small = call(
+                functools.partial(left_kernel, depth, bits - 1),
                 (steps,),
                 [up_spec] + [full(v.shape) for v in (inv, b_t, pairing_wide, small)],
                 [full(o.shape) for o in out_shapes],
                 out_shapes,
-                [pltpu.VMEM((width, chunk * depth, pair), BF16)],
+                [
+                    pltpu.VMEM((width, chunk * depth, pair), BF16),
+                    pltpu.VMEM((tokens // LANES, width, LANES), BF16),
+                ],
                 cost(6e9, 8e6),
             )(upstream_adjoint, inv, b_t, pairing_wide, small)
-            d_a = jnp.stack([lay_out(d_a[:, k * rows : (k + 1) * rows]) for k in range(n)])
-            da_keep, da_go = halves(d_a.reshape((n // 2, 2) + d_a.shape[1:]), "col", 0, 1)
-            d_a = add(da_keep, *swap_parts([da_go], "col", 0, n))
-        if bit == 1:
-            passed = (small, d_a.reshape(-1, LANES))
-            args = (inv, a, b, pairing_wide, offset) + passed
-            coupling_update, small, d_a = call(
-                functools.partial(update_kernel, depth, len(passed)),
-                (steps,),
-                [full(v.shape) for v in args],
-                [up_spec] + [full(v.shape) for v in passed],
-                [sds((block, block, pair), BF16)] + [sds(v.shape, BF16) for v in passed],
-                [pltpu.VMEM((chunk, wide, pair), BF16)],
-                cost(6e9, 8e6),
-            )(*args)
-            d_a = d_a.reshape(da_keep.shape)
+            if rows % LANES:
+                shape = (-1, width, LANES // rows, rows)
+                d_a = [part.reshape(shape).transpose(0, 2, 1, 3) for part in d_a]
+            da_keep, da_go = [part.reshape(n // 2, -1, LANES) for part in d_a]
         d_pairing, d_b, small = add(d_pairing, parts[0]), add(db_keep, parts[1]), add(small, parts[2])
         db_keep = db_go = d_b
     d_pairing = d_pairing.reshape(1, -1, LANES)
-    small_parts, da_parts = [small], [d_a]
+    small_parts = [small]
     for bit in reversed(range(1, bits)):
-        if len(small_parts) > 1:
-            small_parts, da_parts = [add(*small_parts)], [add(*da_parts)]
+        if bit < bits - 1:
+            small_parts = [add(*small_parts)]
+            da_keep, da_go = halves(split_high(add(*da_parts)), "col", bit, 0)
         db_keep, db_go = halves(split_high(d_b), "col", bit, 0)
-        da_keep, da_go = halves(split_high(da_parts[0]), "col", bit, 0)
         parts = swap_parts([d_pairing, db_go, da_go, small_parts[0]], "col", bit, n)
         d_pairing = in_order(d_pairing, parts[0].reshape(d_pairing.shape), "col", bit, 1)
         d_pairing = d_pairing.reshape((-1,) + d_pairing.shape[2:])
@@ -500,9 +503,10 @@
         d_b = jnp.where(mine, db_keep, parts[1].reshape(db_keep.shape))
         da_parts = [da_keep, parts[2].reshape(da_keep.shape)]
         small_parts = [small_parts[0], parts[3]]
-    (got,) = swap_parts([d_pairing], "col", 0, n)
+    da_keep, da_go = halves(add(*da_parts), "col", 0, 0)
+    got, da_got = swap_parts([d_pairing, da_go], "col", 0, n)
     d_pairing = in_order(d_pairing, got.reshape(d_pairing.shape), "col", 0, 1)
-    d_a = [lay_back(part.reshape(-1, LANES), width, rows) for part in da_parts]
+    d_a = [lay_back(part.reshape(-1, LANES), width, rows) for part in (da_keep, da_got)]
     d_b = lay_back(d_b[0], own, wide)
 
     args = (*d_a, d_b, *small_parts, x, by_row, factors_t, perm)

time: 73.3 us -> 63.8 us (0.87)
  waiting for transfers between devices: 15.9 us -> 7.38 us
  local copies, waits for them, and re-layouts: 3.54 us -> 2.72 us
    ppermute x7 -> x6, waiting for transfers between devices: 14.3 us -> 5.77 us  [swap_parts(): message = lax.ppermute(message, axis, pairs)]
    unnamed x12 -> x11, local copies, waits for them, and re-layouts: 2.33 us -> 1.51 us
    ppermute x7 -> x6, starting transfers between devices: 10.6 us -> 10.5 us  [swap_parts(): message = lax.ppermute(message, axis, pairs)]
  transfers between devices with their start and end apart: 14 -> 13, of which waited for: 8 -> 5; matrix products, arithmetic and copies ran while one was open for 2% -> 2% of each run, Pallas kernels for 9% -> 32%
where the time goes in v6:
time: 63.8 us; the launch traced here: 63.5 us
  Pallas kernels  31.5 us (49%)
  starting transfers between devices  19.5 us (31%)
  waiting for transfers between devices  7.38 us (12%)
  local copies, waits for them, and re-layouts  2.72 us (4%)
  other arithmetic  1.32 us (2%)
  between operations  1.05 us (2%)
    ppermute x6, starting transfers between devices, swap_parts(): message = lax.ppermute(message, axis, pairs)  10.5 us
    pallas_call x1, Pallas kernels, per_device(): call(functools.partial(left_kernel, depth, bits - 1), (steps,), [up_spec]...  9.82 us
    pallas_call x1, Pallas kernels, per_device(): call(functools.partial(weight_kernel, depth, features, n, pieces), (steps...  7.63 us
    ppermute x4, starting transfers between devices, to_column(): return lax.ppermute(x, axes, pairs)  5.82 us
    ppermute x6, waiting for transfers between devices, swap_parts(): message = lax.ppermute(message, axis, pairs)  5.77 us
    pallas_call x1, Pallas kernels, per_device(): call(functools.partial(token_kernel, depth, features, n), (steps,), [up_s...  5.58 us
    pallas_call x1, Pallas kernels, per_device(): call(functools.partial(update_kernel, depth), (steps,), [full(v.shape) fo...  4.91 us
    ppermute x3, starting transfers between devices, along_col(): return lax.ppermute(x, 'col', [(i, (i + k) % n) for i in range(n)])  3.23 us
  transfers between devices with their start and end apart: 13, of which 5 were waited for; matrix products, arithmetic and copies ran while one was open for 2% of the time, Pallas kernels for 32%

profile of v6, /device:TPU:0, one launch (start us, length us, event | category | flops | bytes accessed | tf_op | source)
XLA Modules:
  0.0 63.5 jit_solution(5666522155501125046)
XLA Ops:
  0.6 0.8 %multiply_convert_fusion.mask_ref = bf16[16,16]{1,0:T(8,128)(2,1)S(1)} fusion(s32[16,16]{1,0:T(8,128)} %param.8, s32[16]{0:T(128)} %param.9), kind=kLoop, calls=%fused_computation.44 | loop fusion | flops 512 | bytes 1600 | tf_op jit(solution)/shard_map/convert_element_type | solution.py:377
  1.4 0.0 copy-start
  1.4 0.8 %copy-done = bf16[16,16,64]{2,1,0:T(8,128)(2,1)S(1)} copy-done((bf16[16,16,64]{2,1,0:T(8,128)(2,1)S(1)}, bf16[16,16,64]{2,1,0:T(8,128)(2,1)}, u32[]{:S(2)}) %copy-start) | copy-done | bytes 32792
  2.2 0.0 copy-start.2
  2.2 0.4 shard_map.110
  2.7 2.4 %collective-permute-start.2 = (bf16[256,128]{1,0:T(8,128)(2,1)S(1)}, bf16[256,128]{1,0:T(8,128)(2,1)S(1)}, u32[]{:S(2)}, u32[]{:S(2)}) collective-permute-start(bf16[256,128]{1,0:T(8,128)(2,1)S(1)} %get-tuple-element.26.refs_0_), channel_id=1, source_target_pairs={{0,3},{1,0},{2,1},{3,2},{4,7},{5,4},{6,5},{7,6},{8,11},{9,8},{10,9... | collective-permute-start | bytes 196616 | tf_op jit(solution)/shard_map/ppermute | solution.py:366
  5.1 0.6 %collective-permute-start.1 = (bf16[256,128]{1,0:T(8,128)(2,1)S(1)}, bf16[256,128]{1,0:T(8,128)(2,1)S(1)}, u32[]{:S(2)}, u32[]{:S(2)}) collective-permute-start(bf16[256,128]{1,0:T(8,128)(2,1)S(1)} %get-tuple-element.26.refs_0_), channel_id=1, source_target_pairs={{0,2},{1,3},{2,0},{3,1},{4,6},{5,7},{6,4},{7,5},{8,10},{9,11},{10,... | collective-permute-start | bytes 196616 | tf_op jit(solution)/shard_map/ppermute | solution.py:366
  5.7 0.2 collective-permute-start
  5.9 3.6 %collective-permute-start.6 = (bf16[256,128]{1,0:T(8,128)(2,1)S(1)}, bf16[256,128]{1,0:T(8,128)(2,1)S(1)}, u32[]{:S(2)}, u32[]{:S(2)}) collective-permute-start(bf16[256,128]{1,0:T(8,128)(2,1)S(1)} %get-tuple-element.27.refs_6_), channel_id=1, source_target_pairs={{0,12},{1,0},{2,4},{3,8},{4,13},{5,1},{6,5},{7,9},{8,14},{9,2},{10... | collective-permute-start | bytes 196616 | tf_op jit(solution)/shard_map/ppermute | solution.py:373
  9.5 1.2 %collective-permute-start.5 = (bf16[256,128]{1,0:T(8,128)(2,1)S(1)}, bf16[256,128]{1,0:T(8,128)(2,1)S(1)}, u32[]{:S(2)}, u32[]{:S(2)}) collective-permute-start(bf16[256,128]{1,0:T(8,128)(2,1)S(1)} %get-tuple-element.27.refs_6_), channel_id=1, source_target_pairs={{0,8},{1,12},{2,0},{3,4},{4,9},{5,13},{6,1},{7,5},{8,10},{9,14},{1... | collective-permute-start | bytes 196616 | tf_op jit(solution)/shard_map/ppermute | solution.py:373
  10.7 0.0 collective-permute-done.2.refs_3_
  10.7 0.3 collective-permute-start.4
  11.1 0.0 collective-permute-done.1.refs_2_
  11.1 0.7 %collective-permute-start.3 = (bf16[256,128]{1,0:T(8,128)(2,1)S(1)}, bf16[256,128]{1,0:T(8,128)(2,1)S(1)}, u32[]{:S(2)}, u32[]{:S(2)}) collective-permute-start(bf16[256,128]{1,0:T(8,128)(2,1)S(1)} %get-tuple-element.27.refs_6_), channel_id=1, source_target_pairs={{0,0},{1,4},{2,8},{3,12},{4,1},{5,5},{6,9},{7,13},{8,2},{9,6},{10,... | collective-permute-start | bytes 196616 | tf_op jit(solution)/shard_map/ppermute | solution.py:373
  11.8 0.2 fusion.refs_10_.refs_5_.refs_8_
  11.9 0.0 copy-start.3
  11.9 1.1 %reshape.174.refs_11_.refs_3_.wc_ref = bf16[32,4096]{1,0:T(8,128)(2,1)S(1)} reshape(bf16[1024,128]{1,0:T(8,128)(2,1)} %param.11) | data formatting | bytes 524288 | tf_op jit(solution)/shard_map/reshape | solution.py:401
  13.0 0.0 collective-permute-done.refs_1_
  13.0 0.0 collective-permute-done.6.refs_7_
  13.0 0.8 %collective-permute-done.5.refs_6_ = bf16[256,128]{1,0:T(8,128)(2,1)S(1)} collective-permute-done((bf16[256,128]{1,0:T(8,128)(2,1)S(1)}, bf16[256,128]{1,0:T(8,128)(2,1)S(1)}, u32[]{:S(2)}, u32[]{:S(2)}) %collective-permute-start.5) | collective-permute-done | bytes 65568 | tf_op jit(solution)/shard_map/ppermute | solution.py:373
  13.9 0.8 %collective-permute-done.4.refs_5_ = bf16[256,128]{1,0:T(8,128)(2,1)S(1)} collective-permute-done((bf16[256,128]{1,0:T(8,128)(2,1)S(1)}, bf16[256,128]{1,0:T(8,128)(2,1)S(1)}, u32[]{:S(2)}, u32[]{:S(2)}) %collective-permute-start.4) | collective-permute-done | bytes 65568 | tf_op jit(solution)/shard_map/ppermute | solution.py:373
  14.6 0.0 collective-permute-done.3.refs_4_
  14.6 0.0 copy-done.2
  14.6 0.0 copy-done.3
  14.6 7.6 %shard_map.111 = (bf16[16,64,128]{2,1,0:T(8,128)(2,1)S(1)}, bf16[1024,32]{1,0:T(8,128)(2,1)S(1)}, bf16[64,512]{1,0:T(8,128)(2,1)S(1)}, bf16[512,64]{1,0:T(8,128)...) custom-call(bf16[256,128]{1,0:T(8,128)(2,1)S(1)} %get-tuple-element., ...), custom_call_target="tpu_custom_call" | custom-call | flops 5000000000 | bytes 8000000 | tf_op jit(solution)/shard_map/pallas_call | solution.py:415
  22.3 7.4 %collective-permute-start.7 = (bf16[512,128]{1,0:T(8,128)(2,1)S(1)}, bf16[512,128]{1,0:T(8,128)(2,1)S(1)}, u32[]{:S(2)}, u32[]{:S(2)}) collective-permute-start(bf16[512,128]{1,0:T(8,128)(2,1)S(1)} %bitcast.101), channel_id=1, source_target_pairs={{0,2},{1,3},{2,0},{3,1},{4,6},{5,7},{6,4},{7,5},{8,10},{9,11},{10,... | collective-permute-start | bytes 393224 | tf_op jit(solution)/shard_map/ppermute | solution.py:317
  29.7 5.6 %shard_map.112 = (bf16[48,128]{1,0:T(8,128)(2,1)S(1)}, bf16[4,64,128]{2,1,0:T(8,128)(2,1)S(1)}) custom-call(bf16[64,64,128]{2,1,0:T(8,128)(2,1)S(1)} %copy-done.2, f32[4,64,16]{2,1,0:T(8,128)S(1)} %get-tuple-element.28.refs_1_.inv_ref, bf16[1024,32]{1,0:T(8,128)(2,1)S(1)} %get-tuple-element.29.refs_2_.a_ref, ...), custom_call_target="tpu_custom_call" | custom-call | flops 8000000000 | bytes 8000000 | tf_op jit(solution)/shard_map/pallas_call | solution.py:442
  35.3 0.0 collective-permute-done.7
  35.4 0.1 collective-permute-start.8
  35.5 1.3 %collective-permute-done.8 = bf16[432,128]{1,0:T(8,128)(2,1)S(1)} collective-permute-done((bf16[432,128]{1,0:T(8,128)(2,1)S(1)}, bf16[432,128]{1,0:T(8,128)(2,1)S(1)}, u32[]{:S(2)}, u32[]{:S(2)}) %collective-permute-start.8) | collective-permute-done | bytes 110624 | tf_op jit(solution)/shard_map/ppermute | solution.py:317
  36.9 0.1 collective-permute-start.9
  37.0 0.0 copy-start.4
  37.0 0.6 %copy-done.4 = f32[128]{0:T(128)S(1)} copy-done((f32[128]{0:T(128)S(1)}, f32[128]{0:T(128)}, u32[]{:S(2)}) %copy-start.4) | copy-done | bytes 536
  37.6 4.9 %shard_map.113 = (bf16[64,64,128]{2,1,0:T(8,128)(2,1)}, bf16[48,128]{1,0:T(8,128)(2,1)S(1)}) custom-call(f32[4,64,16]{2,1,0:T(8,128)S(1)} %get-tuple-element.28.refs_1_.inv_ref, bf16[1024,32]{1,0:T(8,128)(2,1)S(1)} %get-tuple-element.29.refs_2_.a_ref, bf16[64,512]{1,0:T(8,128)(2,1)S(1)} %get-tuple-element.30.b_ref, ...), custom_call_target="tpu_custom_call" | custom-call | flops 6000000000 | bytes 8000000 | tf_op jit(solution)/shard_map/pallas_call | solution.py:462
  42.6 0.0 collective-permute-done.9
  42.7 0.8 %collective-permute-start.10 = (bf16[432,128]{1,0:T(8,128)(2,1)S(1)}, bf16[432,128]{1,0:T(8,128)(2,1)S(1)}, u32[]{:S(2)}, u32[]{:S(2)}) collective-permute-start(bf16[432,128]{1,0:T(8,128)(2,1)S(1)} %pad_maximum_fusion.6), channel_id=1, source_target_pairs={{0,8},{4,12},{8,0},{12,4},{1,9},{5,13},{9,1},{13,5},{2,10},{6,14},... | collective-permute-start | bytes 331784 | tf_op jit(solution)/shard_map/ppermute | solution.py:317
  43.5 9.8 %shard_map.114 = (bf16[4,32,128]{2,1,0:T(8,128)(2,1)S(1)}, bf16[4,32,128]{2,1,0:T(8,128)(2,1)S(1)}, bf16[48,128]{1,0:T(8,128)(2,1)S(1)}) custom-call(bf16[64,64,128]{2,1,0:T(8,128)(2,1)S(1)} %copy-done.2, f32[4,64,16]{2,1,0:T(8,128)S(1)} %get-tuple-element.28.refs_1_.inv_ref, bf16[512,64]{1,0:T(8,128)(2,1)S(1)} %get-tuple-element.38.bt_ref, ...), custom_call_target="tpu_custom_call" | custom-call | flops 6000000000 | bytes 8000000 | tf_op jit(solution)/shard_map/pallas_call | solution.py:474
  53.3 0.0 collective-permute-done.10
  53.4 2.1 %collective-permute-start.11 = (bf16[496,128]{1,0:T(8,128)(2,1)S(1)}, bf16[496,128]{1,0:T(8,128)(2,1)S(1)}, u32[]{:S(2)}, u32[]{:S(2)}) collective-permute-start(bf16[496,128]{1,0:T(8,128)(2,1)S(1)} %pad_maximum_fusion.3), channel_id=1, source_target_pairs={{0,2},{1,3},{2,0},{3,1},{4,6},{5,7},{6,4},{7,5},{8,10},{9,11},{10,... | collective-permute-start | bytes 380936 | tf_op jit(solution)/shard_map/ppermute | solution.py:317
  55.5 3.2 %collective-permute-done.11 = bf16[496,128]{1,0:T(8,128)(2,1)S(1)} collective-permute-done((bf16[496,128]{1,0:T(8,128)(2,1)S(1)}, bf16[496,128]{1,0:T(8,128)(2,1)S(1)}, u32[]{:S(2)}, u32[]{:S(2)}) %collective-permute-start.11) | collective-permute-done | bytes 127008 | tf_op jit(solution)/shard_map/ppermute | solution.py:317
  58.8 0.1 collective-permute-start.12
  58.9 1.3 %collective-permute-done.12 = bf16[576,128]{1,0:T(8,128)(2,1)S(1)} collective-permute-done((bf16[576,128]{1,0:T(8,128)(2,1)S(1)}, bf16[576,128]{1,0:T(8,128)(2,1)S(1)}, u32[]{:S(2)}, u32[]{:S(2)}) %collective-permute-start.12) | collective-permute-done | bytes 147488 | tf_op jit(solution)/shard_map/ppermute | solution.py:317
  60.3 0.0 copy-start.1
  60.4 1.3 %shard_map.116 = f32[32,32,128]{2,1,0:T(8,128)} custom-call(bf16[32,32,128]{2,1,0:T(8,128)(2,1)S(1)} %bitcast.79), custom_call_target="tpu_custom_call" | custom-call | tf_op jit(solution)/shard_map/pallas_call | solution.py:523
  61.6 0.0 copy-done.1
  61.6 1.9 %shard_map.115 = (f32[256,64]{1,0:T(8,128)}, f32[64,64]{1,0:T(8,128)}, f32[1,128]{1,0:T(1,128)}) custom-call(bf16[32,256]{1,0:T(8,128)(2,1)S(1)} %bitcast.85, bf16[32,256]{1,0:T(8,128)(2,1)S(1)} %bitcast.86, bf16[16,512]{1,0:T(8,128)(2,1)S(1)} %bitcast.84, bf16[48,128]{1,0:T(8,128)(2,1)S(1)} %add_convert_fusion.2.refs_3_, ...), custom_call_target="tpu_custom_call" | custom-call | tf_op jit(solution)/shard_map/pallas_call | solution.py:514
  (40 shorter events, 0.5 us)
Async XLA Ops:
  1.4 0.8 %copy-start = (bf16[16,16,64]{2,1,0:T(8,128)(2,1)S(1)}, bf16[16,16,64]{2,1,0:T(8,128)(2,1)}, u32[]{:S(2)}) copy-start(bf16[16,16,64]{2,1,0:T(8,128)(2,1)} %param.7) | copy-start | bytes 98308
  2.2 12.4 %copy-start.2 = (bf16[64,64,128]{2,1,0:T(8,128)(2,1)S(1)}, bf16[64,64,128]{2,1,0:T(8,128)(2,1)}, u32[]{:S(2)}) copy-start(bf16[64,64,128]{2,1,0:T(8,128)(2,1)} %up_ref.1) | copy-start | bytes 3145732
  2.7 8.1 %collective-permute-start.2 = (bf16[256,128]{1,0:T(8,128)(2,1)S(1)}, bf16[256,128]{1,0:T(8,128)(2,1)S(1)}, u32[]{:S(2)}, u32[]{:S(2)}) collective-permute-start(bf16[256,128]{1,0:T(8,128)(2,1)S(1)} %get-tuple-element.26.refs_0_), channel_id=1, source_target_pairs={{0,3},{1,0},{2,1},{3,2},{4,7},{5,4},{6,5},{7,6},{8,11},{9,8},{10,9... | collective-permute-start | bytes 196616 | tf_op jit(solution)/shard_map/ppermute | solution.py:366
  5.1 6.0 %collective-permute-start.1 = (bf16[256,128]{1,0:T(8,128)(2,1)S(1)}, bf16[256,128]{1,0:T(8,128)(2,1)S(1)}, u32[]{:S(2)}, u32[]{:S(2)}) collective-permute-start(bf16[256,128]{1,0:T(8,128)(2,1)S(1)} %get-tuple-element.26.refs_0_), channel_id=1, source_target_pairs={{0,2},{1,3},{2,0},{3,1},{4,6},{5,7},{6,4},{7,5},{8,10},{9,11},{10,... | collective-permute-start | bytes 196616 | tf_op jit(solution)/shard_map/ppermute | solution.py:366
  5.7 7.3 %collective-permute-start = (bf16[256,128]{1,0:T(8,128)(2,1)S(1)}, bf16[256,128]{1,0:T(8,128)(2,1)S(1)}, u32[]{:S(2)}, u32[]{:S(2)}) collective-permute-start(bf16[256,128]{1,0:T(8,128)(2,1)S(1)} %get-tuple-element.26.refs_0_), channel_id=1, source_target_pairs={{0,1},{1,2},{2,3},{3,0},{4,5},{5,6},{6,7},{7,4},{8,9},{9,10},{10,1... | collective-permute-start | bytes 196616 | tf_op jit(solution)/shard_map/ppermute | solution.py:366
  5.9 7.1 %collective-permute-start.6 = (bf16[256,128]{1,0:T(8,128)(2,1)S(1)}, bf16[256,128]{1,0:T(8,128)(2,1)S(1)}, u32[]{:S(2)}, u32[]{:S(2)}) collective-permute-start(bf16[256,128]{1,0:T(8,128)(2,1)S(1)} %get-tuple-element.27.refs_6_), channel_id=1, source_target_pairs={{0,12},{1,0},{2,4},{3,8},{4,13},{5,1},{6,5},{7,9},{8,14},{9,2},{10... | collective-permute-start | bytes 196616 | tf_op jit(solution)/shard_map/ppermute | solution.py:373
  9.5 4.4 %collective-permute-start.5 = (bf16[256,128]{1,0:T(8,128)(2,1)S(1)}, bf16[256,128]{1,0:T(8,128)(2,1)S(1)}, u32[]{:S(2)}, u32[]{:S(2)}) collective-permute-start(bf16[256,128]{1,0:T(8,128)(2,1)S(1)} %get-tuple-element.27.refs_6_), channel_id=1, source_target_pairs={{0,8},{1,12},{2,0},{3,4},{4,9},{5,13},{6,1},{7,5},{8,10},{9,14},{1... | collective-permute-start | bytes 196616 | tf_op jit(solution)/shard_map/ppermute | solution.py:373
  10.7 3.9 %collective-permute-start.4 = (bf16[256,128]{1,0:T(8,128)(2,1)S(1)}, bf16[256,128]{1,0:T(8,128)(2,1)S(1)}, u32[]{:S(2)}, u32[]{:S(2)}) collective-permute-start(bf16[256,128]{1,0:T(8,128)(2,1)S(1)} %get-tuple-element.27.refs_6_), channel_id=1, source_target_pairs={{0,4},{1,8},{2,12},{3,0},{4,5},{5,9},{6,13},{7,1},{8,6},{9,10},{10... | collective-permute-start | bytes 196616 | tf_op jit(solution)/shard_map/ppermute | solution.py:373
  11.1 3.5 %collective-permute-start.3 = (bf16[256,128]{1,0:T(8,128)(2,1)S(1)}, bf16[256,128]{1,0:T(8,128)(2,1)S(1)}, u32[]{:S(2)}, u32[]{:S(2)}) collective-permute-start(bf16[256,128]{1,0:T(8,128)(2,1)S(1)} %get-tuple-element.27.refs_6_), channel_id=1, source_target_pairs={{0,0},{1,4},{2,8},{3,12},{4,1},{5,5},{6,9},{7,13},{8,2},{9,6},{10,... | collective-permute-start | bytes 196616 | tf_op jit(solution)/shard_map/ppermute | solution.py:373
  11.9 2.7 %copy-start.3 = (bf16[64,64]{1,0:T(8,128)(2,1)S(1)}, bf16[64,64]{1,0:T(8,128)(2,1)}, u32[]{:S(2)}) copy-start(bf16[64,64]{1,0:T(8,128)(2,1)} %refs_9_.1) | copy-start | bytes 24580
  22.3 13.0 %collective-permute-start.7 = (bf16[512,128]{1,0:T(8,128)(2,1)S(1)}, bf16[512,128]{1,0:T(8,128)(2,1)S(1)}, u32[]{:S(2)}, u32[]{:S(2)}) collective-permute-start(bf16[512,128]{1,0:T(8,128)(2,1)S(1)} %bitcast.101), channel_id=1, source_target_pairs={{0,2},{1,3},{2,0},{3,1},{4,6},{5,7},{6,4},{7,5},{8,10},{9,11},{10,... | collective-permute-start | bytes 393224 | tf_op jit(solution)/shard_map/ppermute | solution.py:317
  35.4 1.4 %collective-permute-start.8 = (bf16[432,128]{1,0:T(8,128)(2,1)S(1)}, bf16[432,128]{1,0:T(8,128)(2,1)S(1)}, u32[]{:S(2)}, u32[]{:S(2)}) collective-permute-start(bf16[432,128]{1,0:T(8,128)(2,1)S(1)} %pad_maximum_fusion.4), channel_id=1, source_target_pairs={{0,1},{1,0},{2,3},{3,2},{4,5},{5,4},{6,7},{7,6},{8,9},{9,8},{10,11... | collective-permute-start | bytes 331784 | tf_op jit(solution)/shard_map/ppermute | solution.py:317
  36.9 5.6 %collective-permute-start.9 = (bf16[432,128]{1,0:T(8,128)(2,1)S(1)}, bf16[432,128]{1,0:T(8,128)(2,1)S(1)}, u32[]{:S(2)}, u32[]{:S(2)}) collective-permute-start(bf16[432,128]{1,0:T(8,128)(2,1)S(1)} %pad_maximum_fusion.5), channel_id=1, source_target_pairs={{0,4},{4,0},{8,12},{12,8},{1,5},{5,1},{9,13},{13,9},{2,6},{6,2},{1... | collective-permute-start | bytes 331784 | tf_op jit(solution)/shard_map/ppermute | solution.py:317
  37.0 0.7 %copy-start.4 = (f32[128]{0:T(128)S(1)}, f32[128]{0:T(128)}, u32[]{:S(2)}) copy-start(f32[128]{0:T(128)} %param.12) | copy-start | bytes 1540
  42.7 10.6 %collective-permute-start.10 = (bf16[432,128]{1,0:T(8,128)(2,1)S(1)}, bf16[432,128]{1,0:T(8,128)(2,1)S(1)}, u32[]{:S(2)}, u32[]{:S(2)}) collective-permute-start(bf16[432,128]{1,0:T(8,128)(2,1)S(1)} %pad_maximum_fusion.6), channel_id=1, source_target_pairs={{0,8},{4,12},{8,0},{12,4},{1,9},{5,13},{9,1},{13,5},{2,10},{6,14},... | collective-permute-start | bytes 331784 | tf_op jit(solution)/shard_map/ppermute | solution.py:317
  53.4 5.2 %collective-permute-start.11 = (bf16[496,128]{1,0:T(8,128)(2,1)S(1)}, bf16[496,128]{1,0:T(8,128)(2,1)S(1)}, u32[]{:S(2)}, u32[]{:S(2)}) collective-permute-start(bf16[496,128]{1,0:T(8,128)(2,1)S(1)} %pad_maximum_fusion.3), channel_id=1, source_target_pairs={{0,2},{1,3},{2,0},{3,1},{4,6},{5,7},{6,4},{7,5},{8,10},{9,11},{10,... | collective-permute-start | bytes 380936 | tf_op jit(solution)/shard_map/ppermute | solution.py:317
  58.8 1.4 %collective-permute-start.12 = (bf16[576,128]{1,0:T(8,128)(2,1)S(1)}, bf16[576,128]{1,0:T(8,128)(2,1)S(1)}, u32[]{:S(2)}, u32[]{:S(2)}) collective-permute-start(bf16[576,128]{1,0:T(8,128)(2,1)S(1)} %pad_maximum_fusion.1), channel_id=1, source_target_pairs={{0,1},{1,0},{2,3},{3,2},{4,5},{5,4},{6,7},{7,6},{8,9},{9,8},{10,11... | collective-permute-start | bytes 442376 | tf_op jit(solution)/shard_map/ppermute | solution.py:317
  60.3 1.3 %copy-start.1 = (bf16[16,16,64]{2,1,0:T(8,128)(2,1)S(1)}, bf16[16,16,64]{2,1,0:T(8,128)(2,1)}, u32[]{:S(2)}) copy-start(bf16[16,16,64]{2,1,0:T(8,128)(2,1)} %param.7) | copy-start | bytes 98308

commit v7 on v6

--- a/solution.py
+++ b/solution.py
@@ -10,7 +10,7 @@
 F32 = jnp.float32
 BF16 = jnp.bfloat16
 LANES = 128
-VMEM_LIMIT = 40 * 1024 * 1024
+VMEM_LIMIT = 32 * 1024 * 1024
 NT = (((1,), (1,)), ((), ()))
 
 
@@ -76,61 +76,38 @@
     by_token_ref[...] = dot(swap, wide).astype(BF16)
 
 
-def scaled_pair(up_ref, inv, at):
-    parts = [up_ref[i].astype(F32) * inv[:, i : i + 1] for i in (at, at + 1)]
-    return jnp.concatenate(parts, axis=1).astype(BF16)
-
-
-def fill_v(up_ref, inv, bt, v_ref, depth):
-    chunk, _, pair = up_ref.shape
+def two(ref, at):
+    return jnp.concatenate([ref[at], ref[at + 1]], axis=1)
+
+
+def fill_v(g_ref, bt, v_ref, depth):
+    chunk, _, pair = g_ref.shape
     width = v_ref.shape[0]
     for at in range(0, chunk, 2):
-        v = dot(bt, scaled_pair(up_ref, inv, at)).astype(BF16)
+        v = dot(bt, two(g_ref, at)).astype(BF16)
         for k in range(2):
             part = v[:, k * pair : (k + 1) * pair].reshape(width, depth, pair)
             v_ref[:, (at + k) * depth : (at + k + 1) * depth, :] = part
 
 
-def fill_t(a_chunk, wc_ref, t_ref, depth):
-    chunk, rows, pair = t_ref.shape
-    width = rows // depth
-    for e in range(0, width, 2):
-        t = dot(a_chunk, wc_ref[:, e * pair : (e + 2) * pair]).astype(BF16)
-        for k in range(2):
-            part = t[:, k * pair : (k + 1) * pair].reshape(chunk, depth, pair)
-            t_ref[:, (e + k) * depth : (e + k + 1) * depth, :] = part
-
-
-def two(ref, at):
-    return jnp.concatenate([ref[at], ref[at + 1]], axis=1)
-
-
-def weight_kernel(depth, features, n, pieces, *refs):
-    a_refs, b_refs = refs[:pieces], refs[pieces : 2 * pieces]
-    up_ref, w_ref, perm_ref, wc_ref = refs[2 * pieces : 2 * pieces + 4]
-    outs = refs[2 * pieces + 4 :]
-    mj_ref, a_ref, b_ref, bt_ref, wt_ref, inv_ref, bias_ref, dw_ref, left_ref = outs[:9]
-    mi_ref, at_ref, v_ref, acc_ref, wide_ref = outs[9:]
-    g, last = pl.program_id(0), pl.num_programs(0) - 1
-    chunk, block, pair = up_ref.shape
+def row_kernel(depth, features, n, pieces, *refs):
+    a_refs, (w_ref, wc_ref) = refs[:pieces], refs[pieces : pieces + 2]
+    t_ref, at_ref, seen_ref, wt_ref, mi_ref, a_ref = refs[pieces + 2 :]
+    g = pl.program_id(0)
+    chunk, wide, pair = t_ref.shape
+    block = seen_ref.shape[0]
     width = w_ref.shape[1] // 2
-    r, c = lax.axis_index("row"), lax.axis_index("col")
 
     @pl.when(g == 0)
     def _():
         if pieces == 1:
             mi_ref[...] = a_refs[0][...]
-            mj_ref[...] = b_refs[0][...]
         else:
-            own = block // pieces
+            c = lax.axis_index("col")
+            size = a_refs[0].shape[0]
             for k in range(pieces):
                 src = lax.rem(c - k + n, n)
-                rows = pl.ds(pl.multiple_of(src * own * depth, own * depth), own * depth)
-                mi_ref[rows, :] = a_refs[k][...]
-                src = lax.rem(r - k + n, n)
-                rows = pl.ds(pl.multiple_of(src * own, own), own)
-                for s in range(depth):
-                    mj_ref[s, rows, :] = b_refs[k][s * own : (s + 1) * own, :]
+                mi_ref[pl.ds(pl.multiple_of(src * size, size), size), :] = a_refs[k][...]
         pad = jnp.zeros((LANES - features, 2 * width), BF16)
         w = jnp.concatenate([w_ref[...], pad], axis=0)
         same = one_hot(iota((2 * width, 2 * width), 0) == iota((2 * width, 2 * width), 1))
@@ -140,31 +117,70 @@
         a_ref[...] = dot(mi, w[:, :width]).astype(BF16)
         same = one_hot(iota((features, LANES), 0) == iota((features, LANES), 1))
         at_ref[...] = dot_nt(jnp.concatenate([wt[:width, :], same], axis=0), mi).astype(BF16)
+        rows = block * depth
+        gather = one_hot(iota((block, rows), 0) == iota((block, rows), 1) // depth)
+        seen_ref[...] = dot(gather, mi).astype(BF16)
+
+    span = chunk * depth
+    a_chunk = a_ref[pl.ds(pl.multiple_of(g * span, span), span), :]
+    for e in range(0, width, 2):
+        t = dot(a_chunk, wc_ref[:, e * pair : (e + 2) * pair]).astype(BF16)
+        for k in range(2):
+            part = t[:, k * pair : (k + 1) * pair].reshape(chunk, depth, pair)
+            t_ref[:, (e + k) * depth : (e + k + 1) * depth, :] = part
+
+
+def weight_kernel(depth, features, n, pieces, *refs):
+    b_refs = refs[:pieces]
+    up_ref, w_ref, perm_ref, wc_ref, at_ref, seen_ref, offset_ref = refs[pieces : pieces + 7]
+    outs = refs[pieces + 7 :]
+    g_ref, mj_ref, b_ref, bt_ref, inv_ref, bias_ref, dw_ref, left_ref, pass_ref = outs[:9]
+    v_ref, acc_ref, wide_ref = outs[9:]
+    g, last = pl.program_id(0), pl.num_programs(0) - 1
+    chunk, block, pair = up_ref.shape
+    width = w_ref.shape[1] // 2
+
+    @pl.when(g == 0)
+    def _():
+        if pieces == 1:
+            mj_ref[...] = b_refs[0][...]
+        else:
+            r = lax.axis_index("row")
+            own = block // pieces
+            for k in range(pieces):
+                src = lax.rem(r - k + n, n)
+                rows = pl.ds(pl.multiple_of(src * own, own), own)
+                for s in range(depth):
+                    mj_ref[s, rows, :] = b_refs[k][s * own : (s + 1) * own, :]
+        pad = jnp.zeros((LANES - features, width), BF16)
+        w = jnp.concatenate([w_ref[:, width:], pad], axis=0)
         b = jnp.zeros((block, width * depth), F32)
         seen = jnp.zeros((block, LANES), F32)
         for s in range(depth):
             mj = mj_ref[s]
             seen = seen + mj.astype(F32)
-            part = dot(mj, w[:, width:]).astype(BF16)
+            part = dot(mj, w).astype(BF16)
             b = b + dot(part, perm_ref[s * width : (s + 1) * width, :])
         b_ref[...] = b.astype(BF16)
         bt_ref[...] = b.T.astype(BF16)
         keep = iota((block, LANES), 1) >= features
-        seen_j = jnp.where(keep, seen, 0.0).astype(BF16)
-        rows = block * depth
-        gather = one_hot(iota((block, rows), 0) == iota((block, rows), 1) // depth)
-        seen_i = dot(gather, mi).astype(BF16)
+        seen = jnp.where(keep, seen, 0.0).astype(BF16)
         for k in range(block // chunk):
-            count = dot_nt(seen_j, seen_i[k * chunk : (k + 1) * chunk, :])
+            count = dot_nt(seen, seen_ref[k * chunk : (k + 1) * chunk, :])
             inv_ref[k] = 1.0 / (count + 0.001)
         acc_ref[...] = jnp.zeros_like(acc_ref)
         wide_ref[...] = jnp.zeros_like(wide_ref)
         bias_ref[...] = jnp.zeros_like(bias_ref)
-
-    bias_ref[0:1, :] += jnp.sum(
-        jnp.sum(up_ref[...].astype(F32), axis=0), axis=0, keepdims=True
-    )
-    fill_v(up_ref, inv_ref[g], bt_ref[...], v_ref, depth)
+        pass_ref[...] = offset_ref[...]
+
+    inv = inv_ref[g]
+    bias = jnp.zeros((block, pair), F32)
+    for i in range(chunk):
+        up = up_ref[i].astype(F32)
+        bias = bias + up
+        g_ref[i] = (up * inv[:, i : i + 1]).astype(BF16)
+    bias_ref[0:1, :] += jnp.sum(bias, axis=0, keepdims=True)
+    fill_v(g_ref, bt_ref[...], v_ref, depth)
     span = chunk * depth
     a_t = at_ref[:, pl.ds(pl.multiple_of(g * span, span), span)]
     for e in range(0, width, 2):
@@ -184,19 +200,23 @@
         left_ref[...] = left
 
 
-def left_kernel(depth, bit, up_ref, inv_ref, bt_ref, wc_ref, small_ref, keep_ref, go_ref, pass_ref, v_ref, da_ref):
+def left_kernel(depth, bit, g_ref, bt_ref, wd_ref, small_ref, keep_ref, go_ref, pass_ref, v_ref, da_ref):
     g, last = pl.program_id(0), pl.num_programs(0) - 1
-    chunk, _, pair = up_ref.shape
-    width = wc_ref.shape[0]
+    chunk, _, pair = g_ref.shape
+    width = wd_ref.shape[1]
     span = chunk * depth
 
     @pl.when(g == 0)
     def _():
         pass_ref[...] = small_ref[...]
 
-    fill_v(up_ref, inv_ref[g], bt_ref[...], v_ref, depth)
-    v = jnp.concatenate([v_ref[e] for e in range(width)], axis=1)
-    d_a = dot_nt(v, wc_ref[...])
+    fill_v(g_ref, bt_ref[...], v_ref, depth)
+    d_a = []
+    each = width // 4
+    for e in range(0, width, each):
+        v = jnp.concatenate([v_ref[e + k] for k in range(each)], axis=1)
+        d_a.append(dot(v, wd_ref[e * pair : (e + each) * pair, :]))
+    d_a = (d_a[0] + d_a[1]) + (d_a[2] + d_a[3])
     same = one_hot(iota((width, width), 0) == iota((width, width), 1))
     d_a = dot_nt(same, d_a.astype(BF16)).astype(BF16)
     tiles = span // LANES
@@ -211,23 +231,17 @@
         go_ref[...] = da_ref[pl.ds((1 - here) * half, half)]
 
 
-def token_kernel(depth, features, n, *refs):
-    up_ref, inv_ref, a_ref, wc_ref, mj_ref, perm_ref, bias_ref, left_ref = refs[:8]
-    small_ref, out_ref, t_ref, db_ref = refs[8:]
+def token_kernel(depth, features, n, g_ref, t_ref, mj_ref, perm_ref, bias_ref, left_ref, small_ref, out_ref, db_ref):
     g, last = pl.program_id(0), pl.num_programs(0) - 1
-    chunk, block = up_ref.shape[:2]
-    width = wc_ref.shape[0]
-    span = chunk * depth
-    inv = inv_ref[g]
+    chunk, block = g_ref.shape[:2]
+    width = left_ref.shape[0]
 
     @pl.when(g == 0)
     def _():
         db_ref[...] = jnp.zeros_like(db_ref)
 
-    a_chunk = a_ref[pl.ds(pl.multiple_of(g * span, span), span), :]
-    fill_t(a_chunk, wc_ref, t_ref, depth)
     t = jnp.concatenate([t_ref[i] for i in range(chunk)], axis=1)
-    scaled = jnp.concatenate([scaled_pair(up_ref, inv, at) for at in range(0, chunk, 2)], axis=1)
+    scaled = jnp.concatenate([g_ref[i] for i in range(chunk)], axis=1)
     db_ref[...] += dot_nt(t, scaled)
 
     @pl.when(g == last)
@@ -247,7 +261,7 @@
         small_ref[width:, :] = jnp.broadcast_to(bias_ref[0:1, :], (16, LANES)).astype(BF16)
 
 
-def update_kernel(depth, inv_ref, a_ref, b_ref, wc_ref, offset_ref, small_ref, out_ref, pass_ref, t_ref):
+def update_kernel(inv_ref, b_ref, t_ref, offset_ref, small_ref, out_ref, pass_ref):
     g = pl.program_id(0)
 
     @pl.when(g == 0)
@@ -255,9 +269,7 @@
         pass_ref[...] = small_ref[...]
 
     chunk, block, pair = out_ref.shape
-    span = chunk * depth
     inv = inv_ref[g]
-    fill_t(a_ref[pl.ds(pl.multiple_of(g * span, span), span), :], wc_ref, t_ref, depth)
     b = b_ref[...]
     offset = offset_ref[...]
     for at in range(0, chunk, 2):
@@ -269,7 +281,10 @@
 
 def owner_kernel(depth, own, features, *refs):
     da_refs, db_ref, small_refs = refs[:2], refs[2], refs[3:5]
-    x_ref, message_ref, wt_ref, perm_ref, out_ref, factors_ref, bias_ref = refs[5:]
+    x_ref, message_ref, wt_ref, perm_ref, dw_ref = refs[5:10]
+    out_ref, factors_ref, bias_ref, placed_ref = refs[10:]
+    for e in range(dw_ref.shape[0]):
+        placed_ref[:, e, :] = dw_ref[e].astype(F32)
     rows = depth * own
     width = wt_ref.shape[0] // 2
     p, q = iota((rows, rows), 0), iota((rows, rows), 1)
@@ -295,11 +310,6 @@
     bias_ref[...] = small[width : width + 1]
 
 
-def place_kernel(in_ref, out_ref):
-    for e in range(in_ref.shape[0]):
-        out_ref[:, e, :] = in_ref[e].astype(F32)
-
-
 def lay_back(x, rows, lanes):
     if lanes % LANES:
         return x.reshape(rows, lanes)
@@ -396,41 +406,54 @@
     pieces = len(a_pieces)
 
     wide = width * depth
+    tokens = block * depth
     source = jnp.arange(wide)
     perm = (jnp.arange(wide)[None, :] == (source % width * depth + source // width)[:, None]).astype(BF16)
     pairing_wide = pairing_matrix.reshape(width, width * pair)
+    pairing_t = pairing_wide.T
     up_spec = pl.BlockSpec((chunk, block, pair), lambda g: (g, 0, 0))
-    tokens = block * depth
+    t_spec = pl.BlockSpec((chunk, wide, pair), lambda g: (g, 0, 0))
+    out_shapes = [
+        sds((width + features, tokens), BF16),
+        sds((block, LANES), BF16),
+        sds((2 * width, LANES), BF16),
+    ]
+    args = (*a_pieces, sitewise_factors, pairing_wide)
+    t, a_t, seen, factors_t = call(
+        functools.partial(row_kernel, depth, features, n, pieces),
+        (steps,),
+        [full(v.shape) for v in args],
+        [t_spec] + [full(o.shape) for o in out_shapes],
+        [sds((block, wide, pair), BF16)] + out_shapes,
+        [pltpu.VMEM((tokens, LANES), BF16), pltpu.VMEM((tokens, width), BF16)],
+        cost(3e9, 8e6),
+    )(*args)
+
     out_shapes = [
         sds((depth, block, LANES), BF16),
-        sds((tokens, width), BF16),
         sds((block, wide), BF16),
         sds((wide, block), BF16),
-        sds((2 * width, LANES), BF16),
         sds((steps, block, chunk), F32),
         sds((8, pair), F32),
         sds((width * width, pair), BF16),
         sds((width, features), F32),
+        sds((1, pair), F32),
     ]
+    args = (sitewise_factors, perm, pairing_wide, a_t, seen, offset)
     outs = call(
         functools.partial(weight_kernel, depth, features, n, pieces),
         (steps,),
-        [full(p.shape) for p in a_pieces]
-        + [full(p.shape) for p in b_pieces]
-        + [up_spec]
-        + [full(v.shape) for v in (sitewise_factors, perm, pairing_wide)],
-        [full(o.shape) for o in out_shapes],
-        out_shapes,
+        [full(p.shape) for p in b_pieces] + [up_spec] + [full(v.shape) for v in args],
+        [up_spec] + [full(o.shape) for o in out_shapes],
+        [sds(upstream_adjoint.shape, BF16)] + out_shapes,
         [
-            pltpu.VMEM((tokens, LANES), BF16),
-            pltpu.VMEM((width + features, tokens), BF16),
             pltpu.VMEM((width, chunk * depth, pair), BF16),
             pltpu.VMEM((width * width, pair), F32),
             pltpu.VMEM((features, width * pair), F32),
         ],
         cost(5e9, 8e6),
-    )(*a_pieces, *b_pieces, upstream_adjoint, sitewise_factors, perm, pairing_wide)
-    mj, a, b, b_t, factors_t, inv, bias, d_pairing, left = outs
+    )(*b_pieces, upstream_adjoint, *args)
+    scaled, mj, b, b_t, inv, bias, d_pairing, left, offset = outs
 
     bits = n.bit_length() - 1
     d_pairing = d_pairing.reshape(n, -1, LANES)
@@ -442,13 +465,12 @@
     small, d_b = call(
         functools.partial(token_kernel, depth, features, n),
         (steps,),
-        [up_spec]
-        + [full(v.shape) for v in (inv, a, pairing_wide, mj, perm, bias, left)],
+        [up_spec, t_spec] + [full(v.shape) for v in (mj, perm, bias, left)],
         [full(o.shape) for o in out_shapes],
         out_shapes,
-        [pltpu.VMEM((chunk, wide, pair), BF16), pltpu.VMEM((wide, block), F32)],
-        cost(8e9, 8e6),
-    )(upstream_adjoint, inv, a, pairing_wide, mj, perm, bias, left)
+        [pltpu.VMEM((wide, block), F32)],
+        cost(6e9, 16e6),
+    )(scaled, t, mj, perm, bias, left)
 
     dp_keep, dp_go = halves(d_pairing, "col", 0, 0)
     db_keep, db_go = halves(d_b.reshape((n // 2, 2) + d_b.shape[1:]), "col", 0, 1)
@@ -459,22 +481,25 @@
     for bit in range(bits):
         parts = swap_parts([d_pairing, db_go, small], "row", bit, n)
         if bit == 0:
+            args = (inv, b, t, offset, small)
+            specs = [full(v.shape) for v in args]
+            specs[2] = t_spec
             coupling_update, small = call(
-                functools.partial(update_kernel, depth),
+                update_kernel,
                 (steps,),
-                [full(v.shape) for v in (inv, a, b, pairing_wide, offset, small)],
+                specs,
                 [up_spec, full(small.shape)],
                 [sds((block, block, pair), BF16), sds(small.shape, BF16)],
-                [pltpu.VMEM((chunk, wide, pair), BF16)],
+                (),
                 cost(6e9, 8e6),
-            )(inv, a, b, pairing_wide, offset, small)
+            )(*args)
         if bit == 1:
             half = (tokens // LANES // 2, width, LANES)
             out_shapes = [sds(half, BF16), sds(half, BF16), sds(small.shape, BF16)]
             *d_a, small = call(
                 functools.partial(left_kernel, depth, bits - 1),
                 (steps,),
-                [up_spec] + [full(v.shape) for v in (inv, b_t, pairing_wide, small)],
+                [up_spec] + [full(v.shape) for v in (b_t, pairing_t, small)],
                 [full(o.shape) for o in out_shapes],
                 out_shapes,
                 [
@@ -482,7 +507,7 @@
                     pltpu.VMEM((tokens // LANES, width, LANES), BF16),
                 ],
                 cost(6e9, 8e6),
-            )(upstream_adjoint, inv, b_t, pairing_wide, small)
+            )(scaled, b_t, pairing_t, small)
             if rows % LANES:
                 shape = (-1, width, LANES // rows, rows)
                 d_a = [part.reshape(shape).transpose(0, 2, 1, 3) for part in d_a]
@@ -509,24 +534,21 @@
     d_a = [lay_back(part.reshape(-1, LANES), width, rows) for part in (da_keep, da_got)]
     d_b = lay_back(d_b[0], own, wide)
 
-    args = (*d_a, d_b, *small_parts, x, by_row, factors_t, perm)
-    out_shapes = [sds((rows, features), F32), sds((features, 2 * width), F32), sds((1, pair), F32)]
-    embedding_adjoint, factors_adjoint, offset_slope = call(
+    d_pairing = d_pairing.reshape(width, width, pair)
+    args = (*d_a, d_b, *small_parts, x, by_row, factors_t, perm, d_pairing)
+    out_shapes = [
+        sds((rows, features), F32),
+        sds((features, 2 * width), F32),
+        sds((1, pair), F32),
+        sds((width, width, pair), F32),
+    ]
+    embedding_adjoint, factors_adjoint, offset_slope, placed = call(
         functools.partial(owner_kernel, depth, own, features),
         (),
         [full(v.shape) for v in args],
         [full(o.shape) for o in out_shapes],
         out_shapes,
     )(*args)
-
-    d_pairing = d_pairing.reshape(width, width, pair)
-    placed = call(
-        place_kernel,
-        (),
-        [full(d_pairing.shape)],
-        full((width, width, pair)),
-        sds((width, width, pair), F32),
-    )(d_pairing)
     return (
         coupling_update,
         embedding_adjoint.reshape(depth, own, features),

time: 63.8 us -> 64.6 us (1.013)
  Pallas kernels: 31.5 us -> 25.1 us
  local copies, waits for them, and re-layouts: 2.72 us -> 7.43 us
  other arithmetic: 1.32 us -> 3.51 us
  waiting for transfers between devices: 7.38 us -> 8.15 us
    ppermute x6, starting transfers between devices: 10.5 us -> 4.8 us  [swap_parts(): message = lax.ppermute(message, axis, pairs)]
    pallas_call x1, Pallas kernels: 9.82 us -> 5.46 us  [per_device(): call(functools.partial(left_kernel, depth, bits - 1), (steps,), [up_spec]...]
    ppermute x4, starting transfers between devices: 5.82 us -> 9.61 us  [to_column(): return lax.ppermute(x, axes, pairs)]
    unnamed x11 -> x15, local copies, waits for them, and re-layouts: 1.51 us -> 4.96 us
    ppermute x6, waiting for transfers between devices: 5.77 us -> 8.13 us  [swap_parts(): message = lax.ppermute(message, axis, pairs)]
    pallas_call x1, Pallas kernels: 5.58 us -> 3.41 us  [per_device(): call(functools.partial(token_kernel, depth, features, n), (steps,), [up_s...]
    ppermute x4, waiting for transfers between devices: 1.6 us -> 0.01 us  [to_column(): return lax.ppermute(x, axes, pairs)]
    convert_element_type x10, other arithmetic: 0.2 us -> 1.74 us  [add(): (mine.astype(F32) + other.astype(F32)).astype(BF16)]
  transfers between devices with their start and end apart: 13 -> 13, of which waited for: 5 -> 5; matrix products, arithmetic and copies ran while one was open for 2% -> 3% of each run, Pallas kernels for 32% -> 23%
where the time goes in v7:
time: 64.6 us; the launch traced here: 64.1 us
  Pallas kernels  25.1 us (39%)
  starting transfers between devices  18.9 us (29%)
  waiting for transfers between devices  8.15 us (13%)
  local copies, waits for them, and re-layouts  7.43 us (12%)
  other arithmetic  3.51 us (5%)
  between operations  1.02 us (2%)
    ppermute x4, starting transfers between devices, to_column(): return lax.ppermute(x, axes, pairs)  9.61 us
    ppermute x6, waiting for transfers between devices, swap_parts(): message = lax.ppermute(message, axis, pairs)  8.13 us
    pallas_call x1, Pallas kernels, per_device(): call(functools.partial(weight_kernel, depth, features, n, pieces), (steps...  7.33 us
    pallas_call x1, Pallas kernels, per_device(): call(functools.partial(left_kernel, depth, bits - 1), (steps,), [up_spec]...  5.46 us
    unnamed x15, local copies, waits for them, and re-layouts  4.96 us
    ppermute x6, starting transfers between devices, swap_parts(): message = lax.ppermute(message, axis, pairs)  4.8 us
    ppermute x3, starting transfers between devices, along_col(): return lax.ppermute(x, 'col', [(i, (i + k) % n) for i in range(n)])  4.46 us
    pallas_call x1, Pallas kernels, per_device(): call(functools.partial(token_kernel, depth, features, n), (steps,), [up_s...  3.41 us
  transfers between devices with their start and end apart: 13, of which 5 were waited for; matrix products, arithmetic and copies ran while one was open for 3% of the time, Pallas kernels for 23%

profile of v7, /device:TPU:0, one launch (start us, length us, event | category | flops | bytes accessed | tf_op | source)
XLA Modules:
  0.0 64.1 jit_solution(11361656796996598122)
XLA Ops:
  0.6 0.0 copy-start.4
  0.6 0.8 %multiply_convert_fusion.mask_ref = bf16[16,16]{1,0:T(8,128)(2,1)S(1)} fusion(s32[16,16]{1,0:T(8,128)} %param.8, s32[16]{0:T(128)} %param.9), kind=kLoop, calls=%fused_computation.44 | loop fusion | flops 512 | bytes 1600 | tf_op jit(solution)/shard_map/convert_element_type | solution.py:387
  1.4 0.8 %copy-done = bf16[16,16,64]{2,1,0:T(8,128)(2,1)S(1)} copy-done((bf16[16,16,64]{2,1,0:T(8,128)(2,1)S(1)}, bf16[16,16,64]{2,1,0:T(8,128)(2,1)}, u32[]{:S(2)}) %copy-start) | copy-done | bytes 32792
  2.3 0.4 shard_map.110
  2.7 0.5 collective-permute-start.4
  3.2 2.6 %collective-permute-start.5 = (bf16[256,128]{1,0:T(8,128)(2,1)S(1)}, bf16[256,128]{1,0:T(8,128)(2,1)S(1)}, u32[]{:S(2)}, u32[]{:S(2)}) collective-permute-start(bf16[256,128]{1,0:T(8,128)(2,1)S(1)} %get-tuple-element.32.refs_0_), channel_id=1, source_target_pairs={{0,2},{1,3},{2,0},{3,1},{4,6},{5,7},{6,4},{7,5},{8,10},{9,11},{10,... | collective-permute-start | bytes 196616 | tf_op jit(solution)/shard_map/ppermute | solution.py:376
  5.8 1.4 %collective-permute-start.6 = (bf16[256,128]{1,0:T(8,128)(2,1)S(1)}, bf16[256,128]{1,0:T(8,128)(2,1)S(1)}, u32[]{:S(2)}, u32[]{:S(2)}) collective-permute-start(bf16[256,128]{1,0:T(8,128)(2,1)S(1)} %get-tuple-element.32.refs_0_), channel_id=1, source_target_pairs={{0,3},{1,0},{2,1},{3,2},{4,7},{5,4},{6,5},{7,6},{8,11},{9,8},{10,9... | collective-permute-start | bytes 196616 | tf_op jit(solution)/shard_map/ppermute | solution.py:376
  7.1 0.7 %collective-permute-start = (bf16[256,128]{1,0:T(8,128)(2,1)S(1)}, bf16[256,128]{1,0:T(8,128)(2,1)S(1)}, u32[]{:S(2)}, u32[]{:S(2)}) collective-permute-start(bf16[256,128]{1,0:T(8,128)(2,1)S(1)} %get-tuple-element.31.refs_6_), channel_id=1, source_target_pairs={{0,0},{1,4},{2,8},{3,12},{4,1},{5,5},{6,9},{7,13},{8,2},{9,6},{10,... | collective-permute-start | bytes 196616 | tf_op jit(solution)/shard_map/ppermute | solution.py:383
  7.8 2.9 %collective-permute-start.1 = (bf16[256,128]{1,0:T(8,128)(2,1)S(1)}, bf16[256,128]{1,0:T(8,128)(2,1)S(1)}, u32[]{:S(2)}, u32[]{:S(2)}) collective-permute-start(bf16[256,128]{1,0:T(8,128)(2,1)S(1)} %get-tuple-element.31.refs_6_), channel_id=1, source_target_pairs={{0,4},{1,8},{2,12},{3,0},{4,5},{5,9},{6,13},{7,1},{8,6},{9,10},{10... | collective-permute-start | bytes 196616 | tf_op jit(solution)/shard_map/ppermute | solution.py:383
  10.7 0.2 fusion.refs_6_.perm_ref.refs_8_
  10.9 1.1 %reshape.174.refs_5_.refs_7_ = bf16[32,4096]{1,0:T(8,128)(2,1)S(1)} reshape(bf16[1024,128]{1,0:T(8,128)(2,1)} %param.11) | data formatting | bytes 524288 | tf_op jit(solution)/shard_map/reshape | solution.py:412
  11.9 0.0 collective-permute-done.4.refs_1_
  12.0 2.7 %collective-permute-start.2 = (bf16[256,128]{1,0:T(8,128)(2,1)S(1)}, bf16[256,128]{1,0:T(8,128)(2,1)S(1)}, u32[]{:S(2)}, u32[]{:S(2)}) collective-permute-start(bf16[256,128]{1,0:T(8,128)(2,1)S(1)} %get-tuple-element.31.refs_6_), channel_id=1, source_target_pairs={{0,8},{1,12},{2,0},{3,4},{4,9},{5,13},{6,1},{7,5},{8,10},{9,14},{1... | collective-permute-start | bytes 196616 | tf_op jit(solution)/shard_map/ppermute | solution.py:383
  14.7 0.0 collective-permute-done.5.refs_2_
  14.7 3.4 %collective-permute-start.3 = (bf16[256,128]{1,0:T(8,128)(2,1)S(1)}, bf16[256,128]{1,0:T(8,128)(2,1)S(1)}, u32[]{:S(2)}, u32[]{:S(2)}) collective-permute-start(bf16[256,128]{1,0:T(8,128)(2,1)S(1)} %get-tuple-element.31.refs_6_), channel_id=1, source_target_pairs={{0,12},{1,0},{2,4},{3,8},{4,13},{5,1},{6,5},{7,9},{8,14},{9,2},{10... | collective-permute-start | bytes 196616 | tf_op jit(solution)/shard_map/ppermute | solution.py:383
  18.0 0.0 collective-permute-done.6.refs_3_
  18.0 0.7 %copy-done.3 = bf16[64,64]{1,0:T(8,128)(2,1)S(1)} copy-done((bf16[64,64]{1,0:T(8,128)(2,1)S(1)}, bf16[64,64]{1,0:T(8,128)(2,1)}, u32[]{:S(2)}) %copy-start.3) | copy-done | bytes 8216
  18.7 3.1 %shard_map.111 = (bf16[64,512,128]{2,1,0:T(8,128)(2,1)S(1)}, bf16[96,1024]{1,0:T(8,128)(2,1)S(1)}, bf16[64,128]{1,0:T(8,128)(2,1)S(1)}, bf16[64,128]{1,0:T(8,128)(2,1)S(1)}) custom-call(bf16[256,128]{1,0:T(8,128)(2,1)S(1)} %get-tuple-element.32.refs_0_, bf16[256,128]{1,0:T(8,128)(2,1)S(1)} %collective-permute-done.4.refs_1_, ...), custom_call_target="tpu_custom_call" | custom-call | flops 3000000000 | bytes 8000000 | tf_op jit(solution)/shard_map/pallas_call | solution.py:422
  21.9 0.0 copy-start.5
  21.9 0.0 collective-permute-done.refs_0_
  21.9 0.0 collective-permute-done.1.refs_1_
  21.9 0.0 collective-permute-done.2.refs_2_
  21.9 0.0 collective-permute-done.3.refs_3_
  21.9 0.0 copy-done.4
  22.0 0.0 copy-done.2
  22.0 7.3 %shard_map.112 = (bf16[64,64,128]{2,1,0:T(8,128)(2,1)S(1)}, bf16[16,64,128]{2,1,0:T(8,128)(2,1)S(1)}, bf16[64,512]{1,0:T(8,128)(2,1)S(1)}, bf16[512,64]{1,0:T(8,...) custom-call(bf16[256,128]{1,0:T(8,128)(2,1)S(1)} %collective-permute, ...), custom_call_target="tpu_custom_call" | custom-call | flops 5000000000 | bytes 8000000 | tf_op jit(solution)/shard_map/pallas_call | solution.py:443
  29.3 0.3 collective-permute-start.7
  29.6 3.4 %shard_map.113 = (bf16[48,128]{1,0:T(8,128)(2,1)S(1)}, bf16[4,64,128]{2,1,0:T(8,128)(2,1)S(1)}) custom-call(bf16[64,64,128]{2,1,0:T(8,128)(2,1)S(1)} %get-tuple-element.39.g_ref, bf16[64,512,128]{2,1,0:T(8,128)(2,1)S(1)} %get-tuple-element.37.t_ref, bf16[16,64,128]{2,1,0:T(8,128)(2,1)S(1)} %get-tuple-element.40.mj_ref, ...), custom_call_target="tpu_custom_call" | custom-call | flops 6000000000 | bytes 16000000 | tf_op jit(solution)/shard_map/pallas_call | solution.py:465
  33.1 1.3 %collective-permute-done.7 = bf16[512,128]{1,0:T(8,128)(2,1)S(1)} collective-permute-done((bf16[512,128]{1,0:T(8,128)(2,1)S(1)}, bf16[512,128]{1,0:T(8,128)(2,1)S(1)}, u32[]{:S(2)}, u32[]{:S(2)}) %collective-permute-start.7) | collective-permute-done | bytes 131104 | tf_op jit(solution)/shard_map/ppermute | solution.py:327
  34.4 0.7 %pad_maximum_fusion.4 = bf16[432,128]{1,0:T(8,128)(2,1)} fusion(bf16[48,128]{1,0:T(8,128)(2,1)S(1)} %get-tuple-element.43, bf16[128,128]{1,0:T(8,128)(2,1)S(1)} %bitcast.98, bf16[256,128]{1,0:T(8,128)(2,1)S(1)} %dynamic-slice_bitcast_fusion), kind=kLoop, calls=%fused_computation.14 | loop fusion | flops 331776 | bytes 221184 | tf_op jit(solution)/shard_map/concatenate | solution.py:325
  35.1 0.0 collective-permute-start.8
  35.1 0.5 copy.20
  35.6 1.1 %collective-permute-done.8 = bf16[432,128]{1,0:T(8,128)(2,1)} collective-permute-done((bf16[432,128]{1,0:T(8,128)(2,1)}, bf16[432,128]{1,0:T(8,128)(2,1)}, u32[]{:S(2)}, u32[]{:S(2)}) %collective-permute-start.8) | collective-permute-done | bytes 110624 | tf_op jit(solution)/shard_map/ppermute | solution.py:327
  36.7 0.9 %fusion.2 = bf16[256,128]{1,0:T(8,128)(2,1)S(1)} fusion(bf16[432,128]{1,0:T(8,128)(2,1)} %collective-permute-done.8, bf16[2,256,128]{2,1,0:T(8,128)(2,1)S(1)} %fusion.1, s32[]{:T(128)S(6)} %select_n.125), kind=kLoop, calls=%fused_computation.8 | loop fusion | flops 131072 | bytes 196612 | tf_op jit(solution)/shard_map/convert_element_type | solution.py:353
  37.6 0.7 %add_convert_fusion.4.small_ref = bf16[48,128]{1,0:T(8,128)(2,1)S(1)} fusion(bf16[48,128]{1,0:T(8,128)(2,1)S(1)} %get-tuple-element.43, bf16[432,128]{1,0:T(8,128)(2,1)} %collective-permute-done.8), kind=kLoop, calls=%fused_computation.37 | loop fusion | flops 24576 | bytes 36864 | tf_op jit(solution)/shard_map/convert_element_type | solution.py:353
  38.3 0.8 %slice.62 = bf16[128,128]{1,0:T(8,128)(2,1)S(1)} slice(bf16[432,128]{1,0:T(8,128)(2,1)} %collective-permute-done.8), slice={[256:384], [0:128]} | slice | bytes 65536 | tf_op jit(solution)/shard_map/slice | solution.py:330
  39.1 1.1 %collective-permute-start.9 = (bf16[432,128]{1,0:T(8,128)(2,1)S(1)}, bf16[432,128]{1,0:T(8,128)(2,1)S(1)}, u32[]{:S(2)}, u32[]{:S(2)}) collective-permute-start(bf16[432,128]{1,0:T(8,128)(2,1)S(1)} %pad_maximum_fusion.5), channel_id=1, source_target_pairs={{0,4},{4,0},{8,12},{12,8},{1,5},{5,1},{9,13},{13,9},{2,6},{6,2},{1... | collective-permute-start | bytes 331784 | tf_op jit(solution)/shard_map/ppermute | solution.py:327
  40.3 3.4 %copy-done.6 = bf16[64,512,128]{2,1,0:T(8,128)(2,1)S(1)} copy-done((bf16[64,512,128]{2,1,0:T(8,128)(2,1)S(1)}, bf16[64,512,128]{2,1,0:T(8,128)(2,1)}, u32[]{:S(2)}) %copy-start.6) | copy-done | bytes 8388632
  43.6 2.9 %shard_map.114 = (bf16[64,64,128]{2,1,0:T(8,128)(2,1)}, bf16[48,128]{1,0:T(8,128)(2,1)S(1)}) custom-call(f32[4,64,16]{2,1,0:T(8,128)S(1)} %get-tuple-element.35.inv_ref, bf16[64,512]{1,0:T(8,128)(2,1)S(1)} %get-tuple-element.36.b_ref, bf16[64,512,128]{2,1,0:T(8,128)(2,1)S(1)} %copy-done.6, f32[1,128]{1,0:T(1,128)S(1)} %get-tuple-element.38.offset_ref, ...), custom_call_target="tpu_custom_call" | custom-call | flops 6000000000 | bytes 8000000 | tf_op jit(solution)/shard_map/pallas_call | solution.py:487
  46.5 0.0 collective-permute-done.9
  46.6 2.2 %collective-permute-start.10 = (bf16[432,128]{1,0:T(8,128)(2,1)S(1)}, bf16[432,128]{1,0:T(8,128)(2,1)S(1)}, u32[]{:S(2)}, u32[]{:S(2)}) collective-permute-start(bf16[432,128]{1,0:T(8,128)(2,1)S(1)} %pad_maximum_fusion.6), channel_id=1, source_target_pairs={{0,8},{4,12},{8,0},{12,4},{1,9},{5,13},{9,1},{13,5},{2,10},{6,14},... | collective-permute-start | bytes 331784 | tf_op jit(solution)/shard_map/ppermute | solution.py:327
  48.9 5.5 %shard_map.115 = (bf16[4,32,128]{2,1,0:T(8,128)(2,1)S(1)}, bf16[4,32,128]{2,1,0:T(8,128)(2,1)S(1)}, bf16[48,128]{1,0:T(8,128)(2,1)S(1)}) custom-call(bf16[64,64,128]{2,1,0:T(8,128)(2,1)S(1)} %get-tuple-element.39.g_ref, bf16[512,64]{1,0:T(8,128)(2,1)S(1)} %get-tuple-element.47.bt_ref, bf16[4096,32]{1,0:T(8,128)(2,1)S(1)} %bitcast.80, ...), custom_call_target="tpu_custom_call" | custom-call | flops 6000000000 | bytes 8000000 | tf_op jit(solution)/shard_map/pallas_call | solution.py:499
  54.3 0.5 collective-permute-done.10
  54.9 1.1 %collective-permute-start.11 = (bf16[496,128]{1,0:T(8,128)(2,1)S(1)}, bf16[496,128]{1,0:T(8,128)(2,1)S(1)}, u32[]{:S(2)}, u32[]{:S(2)}) collective-permute-start(bf16[496,128]{1,0:T(8,128)(2,1)S(1)} %pad_maximum_fusion.3), channel_id=1, source_target_pairs={{0,2},{1,3},{2,0},{3,1},{4,6},{5,7},{6,4},{7,5},{8,10},{9,11},{10,... | collective-permute-start | bytes 380936 | tf_op jit(solution)/shard_map/ppermute | solution.py:327
  56.0 3.9 %collective-permute-done.11 = bf16[496,128]{1,0:T(8,128)(2,1)S(1)} collective-permute-done((bf16[496,128]{1,0:T(8,128)(2,1)S(1)}, bf16[496,128]{1,0:T(8,128)(2,1)S(1)}, u32[]{:S(2)}, u32[]{:S(2)}) %collective-permute-start.11) | collective-permute-done | bytes 127008 | tf_op jit(solution)/shard_map/ppermute | solution.py:327
  60.0 0.1 collective-permute-start.12
  60.1 1.3 %collective-permute-done.12 = bf16[576,128]{1,0:T(8,128)(2,1)S(1)} collective-permute-done((bf16[576,128]{1,0:T(8,128)(2,1)S(1)}, bf16[576,128]{1,0:T(8,128)(2,1)S(1)}, u32[]{:S(2)}, u32[]{:S(2)}) %collective-permute-start.12) | collective-permute-done | bytes 147488 | tf_op jit(solution)/shard_map/ppermute | solution.py:327
  61.6 2.4 %shard_map.116 = (f32[256,64]{1,0:T(8,128)}, f32[64,64]{1,0:T(8,128)}, f32[1,128]{1,0:T(1,128)}, f32[32,32,128]{2,1,0:T(8,128)}) custom-call(bf16[32,256]{1,0:T(8,128)(2,1)S(1)} %bitcast.87, bf16[32,256]{1,0:T(8,128)(2,1)S(1)} %bitcast.88, bf16[16,512]{1,0:T(8,128)(2,1)S(1)} %bitcast.86, bf16[48,128]{1,0:T(8,128)(2,1)S(1)} %add_convert_fusion.2.refs_3_, ...), custom_call_target="tpu_custom_call" | custom-call | tf_op jit(solution)/shard_map/pallas_call | solution.py:545
  (43 shorter events, 0.5 us)
Async XLA Ops:
  0.6 21.3 %copy-start.4 = (f32[128]{0:T(128)S(1)}, f32[128]{0:T(128)}, u32[]{:S(2)}) copy-start(f32[128]{0:T(128)} %param.12) | copy-start | bytes 1540
  1.4 0.8 %copy-start = (bf16[16,16,64]{2,1,0:T(8,128)(2,1)S(1)}, bf16[16,16,64]{2,1,0:T(8,128)(2,1)}, u32[]{:S(2)}) copy-start(bf16[16,16,64]{2,1,0:T(8,128)(2,1)} %param.7) | copy-start | bytes 98308
  2.3 19.7 %copy-start.2 = (bf16[64,64,128]{2,1,0:T(8,128)(2,1)S(1)}, bf16[64,64,128]{2,1,0:T(8,128)(2,1)}, u32[]{:S(2)}) copy-start(bf16[64,64,128]{2,1,0:T(8,128)(2,1)} %refs_4_.3) | copy-start | bytes 3145732
  2.7 9.3 %collective-permute-start.4 = (bf16[256,128]{1,0:T(8,128)(2,1)S(1)}, bf16[256,128]{1,0:T(8,128)(2,1)S(1)}, u32[]{:S(2)}, u32[]{:S(2)}) collective-permute-start(bf16[256,128]{1,0:T(8,128)(2,1)S(1)} %get-tuple-element.32.refs_0_), channel_id=1, source_target_pairs={{0,1},{1,2},{2,3},{3,0},{4,5},{5,6},{6,7},{7,4},{8,9},{9,10},{10,1... | collective-permute-start | bytes 196616 | tf_op jit(solution)/shard_map/ppermute | solution.py:376
  3.2 11.5 %collective-permute-start.5 = (bf16[256,128]{1,0:T(8,128)(2,1)S(1)}, bf16[256,128]{1,0:T(8,128)(2,1)S(1)}, u32[]{:S(2)}, u32[]{:S(2)}) collective-permute-start(bf16[256,128]{1,0:T(8,128)(2,1)S(1)} %get-tuple-element.32.refs_0_), channel_id=1, source_target_pairs={{0,2},{1,3},{2,0},{3,1},{4,6},{5,7},{6,4},{7,5},{8,10},{9,11},{10,... | collective-permute-start | bytes 196616 | tf_op jit(solution)/shard_map/ppermute | solution.py:376
  5.8 12.3 %collective-permute-start.6 = (bf16[256,128]{1,0:T(8,128)(2,1)S(1)}, bf16[256,128]{1,0:T(8,128)(2,1)S(1)}, u32[]{:S(2)}, u32[]{:S(2)}) collective-permute-start(bf16[256,128]{1,0:T(8,128)(2,1)S(1)} %get-tuple-element.32.refs_0_), channel_id=1, source_target_pairs={{0,3},{1,0},{2,1},{3,2},{4,7},{5,4},{6,5},{7,6},{8,11},{9,8},{10,9... | collective-permute-start | bytes 196616 | tf_op jit(solution)/shard_map/ppermute | solution.py:376
  7.1 14.8 %collective-permute-start = (bf16[256,128]{1,0:T(8,128)(2,1)S(1)}, bf16[256,128]{1,0:T(8,128)(2,1)S(1)}, u32[]{:S(2)}, u32[]{:S(2)}) collective-permute-start(bf16[256,128]{1,0:T(8,128)(2,1)S(1)} %get-tuple-element.31.refs_6_), channel_id=1, source_target_pairs={{0,0},{1,4},{2,8},{3,12},{4,1},{5,5},{6,9},{7,13},{8,2},{9,6},{10,... | collective-permute-start | bytes 196616 | tf_op jit(solution)/shard_map/ppermute | solution.py:383
  7.8 14.1 %collective-permute-start.1 = (bf16[256,128]{1,0:T(8,128)(2,1)S(1)}, bf16[256,128]{1,0:T(8,128)(2,1)S(1)}, u32[]{:S(2)}, u32[]{:S(2)}) collective-permute-start(bf16[256,128]{1,0:T(8,128)(2,1)S(1)} %get-tuple-element.31.refs_6_), channel_id=1, source_target_pairs={{0,4},{1,8},{2,12},{3,0},{4,5},{5,9},{6,13},{7,1},{8,6},{9,10},{10... | collective-permute-start | bytes 196616 | tf_op jit(solution)/shard_map/ppermute | solution.py:383
  12.0 10.0 %collective-permute-start.2 = (bf16[256,128]{1,0:T(8,128)(2,1)S(1)}, bf16[256,128]{1,0:T(8,128)(2,1)S(1)}, u32[]{:S(2)}, u32[]{:S(2)}) collective-permute-start(bf16[256,128]{1,0:T(8,128)(2,1)S(1)} %get-tuple-element.31.refs_6_), channel_id=1, source_target_pairs={{0,8},{1,12},{2,0},{3,4},{4,9},{5,13},{6,1},{7,5},{8,10},{9,14},{1... | collective-permute-start | bytes 196616 | tf_op jit(solution)/shard_map/ppermute | solution.py:383
  14.7 7.3 %collective-permute-start.3 = (bf16[256,128]{1,0:T(8,128)(2,1)S(1)}, bf16[256,128]{1,0:T(8,128)(2,1)S(1)}, u32[]{:S(2)}, u32[]{:S(2)}) collective-permute-start(bf16[256,128]{1,0:T(8,128)(2,1)S(1)} %get-tuple-element.31.refs_6_), channel_id=1, source_target_pairs={{0,12},{1,0},{2,4},{3,8},{4,13},{5,1},{6,5},{7,9},{8,14},{9,2},{10... | collective-permute-start | bytes 196616 | tf_op jit(solution)/shard_map/ppermute | solution.py:383
  18.0 0.7 %copy-start.3 = (bf16[64,64]{1,0:T(8,128)(2,1)S(1)}, bf16[64,64]{1,0:T(8,128)(2,1)}, u32[]{:S(2)}) copy-start(bf16[64,64]{1,0:T(8,128)(2,1)} %refs_5_.1) | copy-start | bytes 24580
  21.9 7.7 %copy-start.5 = (bf16[64,512,128]{2,1,0:T(8,128)(2,1)}, bf16[64,512,128]{2,1,0:T(8,128)(2,1)S(1)}, u32[]{:S(2)}) copy-start(bf16[64,512,128]{2,1,0:T(8,128)(2,1)S(1)} %get-tuple-element.37.t_ref) | copy-start | bytes 25165828
  29.3 5.0 %collective-permute-start.7 = (bf16[512,128]{1,0:T(8,128)(2,1)S(1)}, bf16[512,128]{1,0:T(8,128)(2,1)S(1)}, u32[]{:S(2)}, u32[]{:S(2)}) collective-permute-start(bf16[512,128]{1,0:T(8,128)(2,1)S(1)} %bitcast.102), channel_id=1, source_target_pairs={{0,2},{1,3},{2,0},{3,1},{4,6},{5,7},{6,4},{7,5},{8,10},{9,11},{10,... | collective-permute-start | bytes 393224 | tf_op jit(solution)/shard_map/ppermute | solution.py:327
  35.1 1.7 %collective-permute-start.8 = (bf16[432,128]{1,0:T(8,128)(2,1)}, bf16[432,128]{1,0:T(8,128)(2,1)}, u32[]{:S(2)}, u32[]{:S(2)}) collective-permute-start(bf16[432,128]{1,0:T(8,128)(2,1)} %pad_maximum_fusion.4), channel_id=1, source_target_pairs={{0,1},{1,0},{2,3},{3,2},{4,5},{5,4},{6,7},{7,6},{8,9},{9,8},{10,11... | collective-permute-start | bytes 331784 | tf_op jit(solution)/shard_map/ppermute | solution.py:327
  39.1 7.4 %collective-permute-start.9 = (bf16[432,128]{1,0:T(8,128)(2,1)S(1)}, bf16[432,128]{1,0:T(8,128)(2,1)S(1)}, u32[]{:S(2)}, u32[]{:S(2)}) collective-permute-start(bf16[432,128]{1,0:T(8,128)(2,1)S(1)} %pad_maximum_fusion.5), channel_id=1, source_target_pairs={{0,4},{4,0},{8,12},{12,8},{1,5},{5,1},{9,13},{13,9},{2,6},{6,2},{1... | collective-permute-start | bytes 331784 | tf_op jit(solution)/shard_map/ppermute | solution.py:327
  40.3 3.4 %copy-start.6 = (bf16[64,512,128]{2,1,0:T(8,128)(2,1)S(1)}, bf16[64,512,128]{2,1,0:T(8,128)(2,1)}, u32[]{:S(2)}) copy-start(bf16[64,512,128]{2,1,0:T(8,128)(2,1)} %copy-done.5) | copy-start | bytes 25165828
  46.6 8.2 %collective-permute-start.10 = (bf16[432,128]{1,0:T(8,128)(2,1)S(1)}, bf16[432,128]{1,0:T(8,128)(2,1)S(1)}, u32[]{:S(2)}, u32[]{:S(2)}) collective-permute-start(bf16[432,128]{1,0:T(8,128)(2,1)S(1)} %pad_maximum_fusion.6), channel_id=1, source_target_pairs={{0,8},{4,12},{8,0},{12,4},{1,9},{5,13},{9,1},{13,5},{2,10},{6,14},... | collective-permute-start | bytes 331784 | tf_op jit(solution)/shard_map/ppermute | solution.py:327
  48.9 12.7 %copy-start.1 = (bf16[16,16,64]{2,1,0:T(8,128)(2,1)S(1)}, bf16[16,16,64]{2,1,0:T(8,128)(2,1)}, u32[]{:S(2)}) copy-start(bf16[16,16,64]{2,1,0:T(8,128)(2,1)} %param.7) | copy-start | bytes 98308
  54.9 5.0 %collective-permute-start.11 = (bf16[496,128]{1,0:T(8,128)(2,1)S(1)}, bf16[496,128]{1,0:T(8,128)(2,1)S(1)}, u32[]{:S(2)}, u32[]{:S(2)}) collective-permute-start(bf16[496,128]{1,0:T(8,128)(2,1)S(1)} %pad_maximum_fusion.3), channel_id=1, source_target_pairs={{0,2},{1,3},{2,0},{3,1},{4,6},{5,7},{6,4},{7,5},{8,10},{9,11},{10,... | collective-permute-start | bytes 380936 | tf_op jit(solution)/shard_map/ppermute | solution.py:327
  60.0 1.4 %collective-permute-start.12 = (bf16[576,128]{1,0:T(8,128)(2,1)S(1)}, bf16[576,128]{1,0:T(8,128)(2,1)S(1)}, u32[]{:S(2)}, u32[]{:S(2)}) collective-permute-start(bf16[576,128]{1,0:T(8,128)(2,1)S(1)} %pad_maximum_fusion.1), channel_id=1, source_target_pairs={{0,1},{1,0},{2,3},{3,2},{4,5},{5,4},{6,7},{7,6},{8,9},{9,8},{10,11... | collective-permute-start | bytes 442376 | tf_op jit(solution)/shard_map/ppermute | solution.py:327

commit v8 on v7

--- a/solution.py
+++ b/solution.py
@@ -10,7 +10,7 @@
 F32 = jnp.float32
 BF16 = jnp.bfloat16
 LANES = 128
-VMEM_LIMIT = 32 * 1024 * 1024
+VMEM_LIMIT = 16 * 1024 * 1024
 NT = (((1,), (1,)), ((), ()))
 
 
@@ -57,23 +57,23 @@
     return center * scale, scale
 
 
-def prep_kernel(depth, own, x_ref, mask_ref, by_token_ref, by_row_ref):
+def prep_kernel(depth, own, x_ref, mask_ref, by_token_ref, by_row_ref, mask_out_ref):
     rows = depth * own
     normed, _ = stats(x_ref[...].astype(F32))
-    features = normed.shape[1]
     pick = one_hot(iota((rows, depth), 0) // own == iota((rows, depth), 1))
     here = iota((rows, own), 0) % own == iota((rows, own), 1)
-    weight = dot(pick, mask_ref[...])
-    weight = jnp.sum(jnp.where(here, weight, 0.0), axis=1, keepdims=True)
+    mask = mask_ref[...]
+    weight = jnp.sum(jnp.where(here, dot(pick, mask), 0.0), axis=1, keepdims=True)
     masked = normed.astype(BF16).astype(F32) * weight
-    wide = jnp.concatenate([masked, jnp.zeros((rows, LANES - features), F32)], axis=1)
-    lane = iota((rows, LANES), 1)
-    at = lane == features + iota((rows, LANES), 0) // own
-    wide = (wide + jnp.where(at, weight, 0.0)).astype(BF16)
-    by_row_ref[...] = wide
+    half = rows // 2
+    by_row_ref[...] = jnp.concatenate([masked[:half], masked[half:]], axis=1).astype(BF16)
     p, q = iota((rows, rows), 0), iota((rows, rows), 1)
     swap = one_hot(q == (p % depth) * own + p // depth)
-    by_token_ref[...] = dot(swap, wide).astype(BF16)
+    turned = dot(swap, masked.astype(BF16))
+    by_token_ref[...] = jnp.concatenate([turned[:half], turned[half:]], axis=1).astype(BF16)
+    pad = jnp.zeros((LANES - depth, own), BF16)
+    same = one_hot(iota((own, own), 0) == iota((own, own), 1))
+    mask_out_ref[...] = dot_nt(same, jnp.concatenate([mask, pad], axis=0)).astype(BF16)
 
 
 def two(ref, at):
@@ -90,36 +90,25 @@
             v_ref[:, (at + k) * depth : (at + k + 1) * depth, :] = part
 
 
-def row_kernel(depth, features, n, pieces, *refs):
-    a_refs, (w_ref, wc_ref) = refs[:pieces], refs[pieces : pieces + 2]
-    t_ref, at_ref, seen_ref, wt_ref, mi_ref, a_ref = refs[pieces + 2 :]
+def row_kernel(depth, features, mi_ref, w_ref, wide_ref, t_ref, at_ref, wt_ref, wc_ref, a_ref, rows_ref):
     g = pl.program_id(0)
     chunk, wide, pair = t_ref.shape
-    block = seen_ref.shape[0]
     width = w_ref.shape[1] // 2
 
     @pl.when(g == 0)
     def _():
-        if pieces == 1:
-            mi_ref[...] = a_refs[0][...]
-        else:
-            c = lax.axis_index("col")
-            size = a_refs[0].shape[0]
-            for k in range(pieces):
-                src = lax.rem(c - k + n, n)
-                mi_ref[pl.ds(pl.multiple_of(src * size, size), size), :] = a_refs[k][...]
-        pad = jnp.zeros((LANES - features, 2 * width), BF16)
-        w = jnp.concatenate([w_ref[...], pad], axis=0)
+        rows_ref[...] = wide_ref[...].astype(F32)
+        for e in range(width):
+            part = rows_ref[pl.ds(e, width, stride=width), :]
+            wc_ref[:, e * pair : (e + 1) * pair] = part.astype(BF16)
+        w = w_ref[...]
         same = one_hot(iota((2 * width, 2 * width), 0) == iota((2 * width, 2 * width), 1))
         wt = dot_nt(same, w).astype(BF16)
         wt_ref[...] = wt
         mi = mi_ref[...]
         a_ref[...] = dot(mi, w[:, :width]).astype(BF16)
-        same = one_hot(iota((features, LANES), 0) == iota((features, LANES), 1))
+        same = one_hot(iota((features, features), 0) == iota((features, features), 1))
         at_ref[...] = dot_nt(jnp.concatenate([wt[:width, :], same], axis=0), mi).astype(BF16)
-        rows = block * depth
-        gather = one_hot(iota((block, rows), 0) == iota((block, rows), 1) // depth)
-        seen_ref[...] = dot(gather, mi).astype(BF16)
 
     span = chunk * depth
     a_chunk = a_ref[pl.ds(pl.multiple_of(g * span, span), span), :]
@@ -130,43 +119,25 @@
             t_ref[:, (e + k) * depth : (e + k + 1) * depth, :] = part
 
 
-def weight_kernel(depth, features, n, pieces, *refs):
-    b_refs = refs[:pieces]
-    up_ref, w_ref, perm_ref, wc_ref, at_ref, seen_ref, offset_ref = refs[pieces : pieces + 7]
-    outs = refs[pieces + 7 :]
-    g_ref, mj_ref, b_ref, bt_ref, inv_ref, bias_ref, dw_ref, left_ref, pass_ref = outs[:9]
-    v_ref, acc_ref, wide_ref = outs[9:]
+def weight_kernel(depth, features, *refs):
+    up_ref, mj_ref, seen_j_ref, seen_i_ref, w_ref, perm_ref, wc_ref, at_ref, offset_ref = refs[:9]
+    g_ref, b_ref, bt_ref, inv_ref, bias_ref, dw_ref, left_ref, pass_ref = refs[9:17]
+    v_ref, acc_ref, wide_ref = refs[17:]
     g, last = pl.program_id(0), pl.num_programs(0) - 1
     chunk, block, pair = up_ref.shape
     width = w_ref.shape[1] // 2
 
     @pl.when(g == 0)
     def _():
-        if pieces == 1:
-            mj_ref[...] = b_refs[0][...]
-        else:
-            r = lax.axis_index("row")
-            own = block // pieces
-            for k in range(pieces):
-                src = lax.rem(r - k + n, n)
-                rows = pl.ds(pl.multiple_of(src * own, own), own)
-                for s in range(depth):
-                    mj_ref[s, rows, :] = b_refs[k][s * own : (s + 1) * own, :]
-        pad = jnp.zeros((LANES - features, width), BF16)
-        w = jnp.concatenate([w_ref[:, width:], pad], axis=0)
+        w = w_ref[:, width:]
         b = jnp.zeros((block, width * depth), F32)
-        seen = jnp.zeros((block, LANES), F32)
         for s in range(depth):
-            mj = mj_ref[s]
-            seen = seen + mj.astype(F32)
-            part = dot(mj, w).astype(BF16)
+            part = dot(mj_ref[s], w).astype(BF16)
             b = b + dot(part, perm_ref[s * width : (s + 1) * width, :])
         b_ref[...] = b.astype(BF16)
         bt_ref[...] = b.T.astype(BF16)
-        keep = iota((block, LANES), 1) >= features
-        seen = jnp.where(keep, seen, 0.0).astype(BF16)
         for k in range(block // chunk):
-            count = dot_nt(seen, seen_ref[k * chunk : (k + 1) * chunk, :])
+            count = dot_nt(seen_j_ref[...], seen_i_ref[k * chunk : (k + 1) * chunk, :])
             inv_ref[k] = 1.0 / (count + 0.001)
         acc_ref[...] = jnp.zeros_like(acc_ref)
         wide_ref[...] = jnp.zeros_like(wide_ref)
@@ -253,22 +224,25 @@
             for q in range(part.shape[1] // LANES):
                 out_ref[k, q * own : (q + 1) * own, :] = part[:, q * LANES : (q + 1) * LANES]
         turned = dot_nt(perm_ref[...], d_b).astype(BF16)
-        right = jnp.zeros((width, LANES), F32)
+        right = jnp.zeros((width, features), F32)
         for s in range(depth):
             right = right + dot(turned[s * width : (s + 1) * width, :], mj_ref[s])
-        small = jnp.concatenate([left_ref[...], right[:, :features]], axis=1)
+        small = jnp.concatenate([left_ref[...], right], axis=1)
         small_ref[0:width, :] = small.astype(BF16)
         small_ref[width:, :] = jnp.broadcast_to(bias_ref[0:1, :], (16, LANES)).astype(BF16)
 
 
-def update_kernel(inv_ref, b_ref, t_ref, offset_ref, small_ref, out_ref, pass_ref):
+def update_kernel(inv_ref, b_ref, t_ref, offset_ref, wc_ref, small_ref, out_ref, wd_ref, pass_ref):
     g = pl.program_id(0)
+    chunk, block, pair = out_ref.shape
 
     @pl.when(g == 0)
     def _():
         pass_ref[...] = small_ref[...]
-
-    chunk, block, pair = out_ref.shape
+        same = one_hot(iota((2 * pair, 2 * pair), 0) == iota((2 * pair, 2 * pair), 1))
+        for at in range(0, wd_ref.shape[0], 2 * pair):
+            wd_ref[at : at + 2 * pair, :] = dot_nt(same, wc_ref[:, at : at + 2 * pair]).astype(BF16)
+
     inv = inv_ref[g]
     b = b_ref[...]
     offset = offset_ref[...]
@@ -281,7 +255,7 @@
 
 def owner_kernel(depth, own, features, *refs):
     da_refs, db_ref, small_refs = refs[:2], refs[2], refs[3:5]
-    x_ref, message_ref, wt_ref, perm_ref, dw_ref = refs[5:10]
+    x_ref, mask_ref, wt_ref, perm_ref, dw_ref = refs[5:10]
     out_ref, factors_ref, bias_ref, placed_ref = refs[10:]
     for e in range(dw_ref.shape[0]):
         placed_ref[:, e, :] = dw_ref[e].astype(F32)
@@ -296,10 +270,10 @@
     wt = wt_ref[...].astype(F32)
     d_normed = jnp.dot(d_a, wt[:width, :], precision=highest, preferred_element_type=F32)
     d_normed = d_normed + jnp.dot(d_b, wt[width:, :], precision=highest, preferred_element_type=F32)
-    message = message_ref[...].astype(F32)
-    mask = iota((rows, LANES), 1) >= features
-    weight = jnp.sum(jnp.where(mask, message, 0.0), axis=1, keepdims=True)
-    d_normed = d_normed[:, :features] * weight
+    pick = one_hot(iota((rows, depth), 0) // own == iota((rows, depth), 1))
+    here = iota((rows, own), 0) % own == iota((rows, own), 1)
+    weight = jnp.sum(jnp.where(here, dot(pick, mask_ref[...]), 0.0), axis=1, keepdims=True)
+    d_normed = d_normed * weight
     normed, scale = stats(x_ref[...].astype(F32))
     mean = jnp.mean(d_normed, axis=-1, keepdims=True)
     along = jnp.mean(d_normed * normed, axis=-1, keepdims=True)
@@ -372,65 +346,64 @@
     axes = ("row", "col")
     sds = jax.ShapeDtypeStruct
 
-    def along_col(x, k):
-        return lax.ppermute(x, "col", [(i, (i + k) % n) for i in range(n)])
-
-    def along_row(x, k):
-        return lax.ppermute(x, "row", [(i, (i + k) % n) for i in range(n)])
-
-    def to_column(x, k):
-        pairs = [(i * n + j, (j + k) % n * n + i) for i in range(n) for j in range(n)]
-        return lax.ppermute(x, axes, pairs)
-
-    r, c = lax.axis_index("row"), lax.axis_index("col")
+    bits = n.bit_length() - 1
     x = alignment_embedding.reshape(rows, features)
     mask = (alignment_cell_exists * alignment_lines_exist[:, None]).astype(BF16)
     offset = offset_vector.reshape(1, pair)
-    by_token, by_row = call(
+    out_shapes = [sds((rows // 2, LANES), BF16)] * 2 + [sds((own, LANES), BF16)]
+    by_token, by_row, mask_t = call(
         functools.partial(prep_kernel, depth, own),
         (),
         [full(x.shape), full(mask.shape)],
-        [full((rows, LANES))] * 2,
-        [sds((rows, LANES), BF16)] * 2,
+        [full(o.shape) for o in out_shapes],
+        out_shapes,
     )(x, mask)
-    a_pieces = [by_token] + [along_col(by_token, k) for k in range(1, n)]
-    b_pieces = [to_column(by_row, k) for k in range(n)]
-    if not split:
-        order = (c - jnp.arange(n)) % n
-        held = jnp.zeros((n, rows, LANES), BF16).at[order].set(jnp.stack(a_pieces))
-        a_pieces = [held.reshape(block * depth, LANES)]
-        order = (r - jnp.arange(n)) % n
-        held = jnp.zeros((n, depth, own, LANES), BF16)
-        held = held.at[order].set(jnp.stack(b_pieces).reshape(n, depth, own, LANES))
-        b_pieces = [held.transpose(1, 0, 2, 3).reshape(depth, block, LANES)]
-    pieces = len(a_pieces)
+    held = jnp.concatenate([by_row, mask_t], axis=0)[None]
+    for bit in reversed(range(bits)):
+        (got,) = swap_parts([held], "row", bit, n)
+        held = in_order(held, got.reshape(held.shape), "row", bit, 1)
+        held = held.reshape((-1,) + held.shape[2:])
+    held = held[:, None]
+    for bit in reversed(range(bits)):
+        keep, go = halves(split_high(held), "col", bit, 0)
+        (got,) = swap_parts([go], "col", bit, n)
+        held = in_order(keep, got.reshape(keep.shape), "col", bit, 2)
+        held = held.reshape((keep.shape[0], -1) + keep.shape[2:])
+    seen_j = held[0, :, rows // 2 :].reshape(block, LANES)
+    parts = held[0, :, : rows // 2].reshape(n, depth // 2, own, 2, features)
+    mj = parts.transpose(3, 1, 0, 2, 4).reshape(depth, block, features)
+    held = jnp.concatenate([by_token, mask_t], axis=0)[None]
+    for bit in reversed(range(bits)):
+        (got,) = swap_parts([held], "col", bit, n)
+        held = in_order(held, got.reshape(held.shape), "col", bit, 1)
+        held = held.reshape((-1,) + held.shape[2:])
+    seen_i = held[:, rows // 2 :].reshape(block, LANES)
+    parts = held[:, : rows // 2].reshape(n, rows // 2, 2, features)
+    mi = parts.transpose(0, 2, 1, 3).reshape(block * depth, features)
 
     wide = width * depth
     tokens = block * depth
     source = jnp.arange(wide)
     perm = (jnp.arange(wide)[None, :] == (source % width * depth + source // width)[:, None]).astype(BF16)
-    pairing_wide = pairing_matrix.reshape(width, width * pair)
-    pairing_t = pairing_wide.T
     up_spec = pl.BlockSpec((chunk, block, pair), lambda g: (g, 0, 0))
     t_spec = pl.BlockSpec((chunk, wide, pair), lambda g: (g, 0, 0))
     out_shapes = [
         sds((width + features, tokens), BF16),
-        sds((block, LANES), BF16),
-        sds((2 * width, LANES), BF16),
+        sds((2 * width, features), BF16),
+        sds((width, width * pair), BF16),
     ]
-    args = (*a_pieces, sitewise_factors, pairing_wide)
-    t, a_t, seen, factors_t = call(
-        functools.partial(row_kernel, depth, features, n, pieces),
+    args = (mi, sitewise_factors, pairing_matrix)
+    t, a_t, factors_t, pairing_wide = call(
+        functools.partial(row_kernel, depth, features),
         (steps,),
         [full(v.shape) for v in args],
         [t_spec] + [full(o.shape) for o in out_shapes],
         [sds((block, wide, pair), BF16)] + out_shapes,
-        [pltpu.VMEM((tokens, LANES), BF16), pltpu.VMEM((tokens, width), BF16)],
-        cost(3e9, 8e6),
+        [pltpu.VMEM((tokens, width), BF16), pltpu.VMEM((width * width, pair), F32)],
+        cost(4e9, 8e6),
     )(*args)
 
     out_shapes = [
-        sds((depth, block, LANES), BF16),
         sds((block, wide), BF16),
         sds((wide, block), BF16),
         sds((steps, block, chunk), F32),
@@ -439,11 +412,11 @@
         sds((width, features), F32),
         sds((1, pair), F32),
     ]
-    args = (sitewise_factors, perm, pairing_wide, a_t, seen, offset)
+    args = (mj, seen_j, seen_i, sitewise_factors, perm, pairing_wide, a_t, offset)
     outs = call(
-        functools.partial(weight_kernel, depth, features, n, pieces),
+        functools.partial(weight_kernel, depth, features),
         (steps,),
-        [full(p.shape) for p in b_pieces] + [up_spec] + [full(v.shape) for v in args],
+        [up_spec] + [full(v.shape) for v in args],
         [up_spec] + [full(o.shape) for o in out_shapes],
         [sds(upstream_adjoint.shape, BF16)] + out_shapes,
         [
@@ -452,10 +425,9 @@
             pltpu.VMEM((features, width * pair), F32),
         ],
         cost(5e9, 8e6),
-    )(*b_pieces, upstream_adjoint, *args)
-    scaled, mj, b, b_t, inv, bias, d_pairing, left, offset = outs
-
-    bits = n.bit_length() - 1
+    )(upstream_adjoint, *args)
+    scaled, b, b_t, inv, bias, d_pairing, left, offset = outs
+
     d_pairing = d_pairing.reshape(n, -1, LANES)
     for bit in reversed(range(1, bits)):
         keep, go = halves(split_high(d_pairing), "col", bit, 0)
@@ -481,15 +453,19 @@
     for bit in range(bits):
         parts = swap_parts([d_pairing, db_go, small], "row", bit, n)
         if bit == 0:
-            args = (inv, b, t, offset, small)
+            args = (inv, b, t, offset, pairing_wide, small)
             specs = [full(v.shape) for v in args]
             specs[2] = t_spec
-            coupling_update, small = call(
+            coupling_update, pairing_t, small = call(
                 update_kernel,
                 (steps,),
                 specs,
-                [up_spec, full(small.shape)],
-                [sds((block, block, pair), BF16), sds(small.shape, BF16)],
+                [up_spec, full((width * pair, width)), full(small.shape)],
+                [
+                    sds((block, block, pair), BF16),
+                    sds((width * pair, width), BF16),
+                    sds(small.shape, BF16),
+                ],
                 (),
                 cost(6e9, 8e6),
             )(*args)
@@ -535,7 +511,7 @@
     d_b = lay_back(d_b[0], own, wide)
 
     d_pairing = d_pairing.reshape(width, width, pair)
-    args = (*d_a, d_b, *small_parts, x, by_row, factors_t, perm, d_pairing)
+    args = (*d_a, d_b, *small_parts, x, mask, factors_t, perm, d_pairing)
     out_shapes = [
         sds((rows, features), F32),
         sds((features, 2 * width), F32),

time: 64.6 us -> 71 us (1.099)
  waiting for transfers between devices: 8.15 us -> 17.1 us
  starting transfers between devices: 18.9 us -> 13.9 us
  local copies, waits for them, and re-layouts: 7.43 us -> 10.8 us
  other arithmetic: 3.51 us -> 1.49 us
  Pallas kernels: 25.1 us -> 26.1 us
    ppermute x7 -> x0, starting transfers between devices: 14.1 us -> none  [the longest x4 9.61 us: to_column(): return lax.ppermute(x, axes, pairs)]
    ppermute x6 -> x12, starting transfers between devices: 4.8 us -> 13.9 us  [swap_parts(): message = lax.ppermute(message, axis, pairs)]
    ppermute x6 -> x12, waiting for transfers between devices: 8.13 us -> 17.1 us  [swap_parts(): message = lax.ppermute(message, axis, pairs)]
    unnamed x15 -> x28, local copies, waits for them, and re-layouts: 4.96 us -> 10.1 us
    reshape x2 -> x0, local copies, waits for them, and re-layouts: 1.58 us -> none  [per_device(): pairing_wide = pairing_matrix.reshape(width, width * pair)]
    convert_element_type x10, other arithmetic: 1.74 us -> 0.19 us  [add(): (mine.astype(F32) + other.astype(F32)).astype(BF16)]
    pallas_call x3, Pallas kernels: 13.3 us -> 14.3 us  [the longest x1 7.3 us: per_device(): call(functools.partial(weight_kernel, depth, features), (steps,), [up_spe...]
    slice x7, local copies, waits for them, and re-layouts: 0.79 us -> 0.03 us  [swap_parts(): got.append(message[at:at + part.shape[0]])]
  transfers between devices with their start and end apart: 13 -> 12, of which waited for: 5 -> 7; matrix products, arithmetic and copies ran while one was open for 3% -> 1% of each run, Pallas kernels for 23% -> 22%
where the time goes in v8:
time: 71 us; the launch traced here: 70.7 us
  Pallas kernels  26.1 us (37%)
  waiting for transfers between devices  17.1 us (24%)
  starting transfers between devices  13.9 us (20%)
  local copies, waits for them, and re-layouts  10.8 us (15%)
  other arithmetic  1.49 us (2%)
  between operations  1.24 us (2%)
    ppermute x12, waiting for transfers between devices, swap_parts(): message = lax.ppermute(message, axis, pairs)  17.1 us
    ppermute x12, starting transfers between devices, swap_parts(): message = lax.ppermute(message, axis, pairs)  13.9 us
    unnamed x28, local copies, waits for them, and re-layouts  10.1 us
    pallas_call x1, Pallas kernels, per_device(): call(functools.partial(weight_kernel, depth, features), (steps,), [up_spe...  7.3 us
    pallas_call x1, Pallas kernels, per_device(): call(functools.partial(left_kernel, depth, bits - 1), (steps,), [up_spec]...  5.42 us
    pallas_call x1, Pallas kernels, per_device(): call(update_kernel, (steps,), specs, [up_spec, full((width * pair, width)...  3.57 us
    pallas_call x1, Pallas kernels, per_device(): call(functools.partial(token_kernel, depth, features, n), (steps,), [up_s...  3.45 us
    pallas_call x1, Pallas kernels, per_device(): call(functools.partial(row_kernel, depth, features), (steps,), [full(v.sh...  3.44 us
  transfers between devices with their start and end apart: 12, of which 7 were waited for; matrix products, arithmetic and copies ran while one was open for 1% of the time, Pallas kernels for 22%

profile of v8, /device:TPU:0, one launch (start us, length us, event | category | flops | bytes accessed | tf_op | source)
XLA Modules:
  0.0 70.7 jit_solution(3258943368552749828)
XLA Ops:
  0.6 0.8 %multiply_convert_fusion.mask_ref.refs_6_ = bf16[16,16]{1,0:T(8,128)(2,1)S(1)} fusion(s32[16,16]{1,0:T(8,128)} %param.8, s32[16]{0:T(128)} %param.9), kind=kLoop, calls=%fused_computation.78 | loop fusion | flops 512 | bytes 1600 | tf_op jit(solution)/shard_map/convert_element_type | solution.py:351
  1.4 0.8 %copy-done = bf16[16,16,64]{2,1,0:T(8,128)(2,1)S(1)} copy-done((bf16[16,16,64]{2,1,0:T(8,128)(2,1)S(1)}, bf16[16,16,64]{2,1,0:T(8,128)(2,1)}, u32[]{:S(2)}) %copy-start) | copy-done | bytes 32792
  2.2 0.5 shard_map.110
  2.8 3.0 %collective-permute-start.4 = (bf16[144,128]{1,0:T(8,128)(2,1)S(1)}, bf16[144,128]{1,0:T(8,128)(2,1)S(1)}, u32[]{:S(2)}, u32[]{:S(2)}) collective-permute-start(bf16[144,128]{1,0:T(8,128)(2,1)S(1)} %get-tuple-element.79), channel_id=1, source_target_pairs={{0,2},{1,3},{2,0},{3,1},{4,6},{5,7},{6,4},{7,5},{8,10},{9,11},{10,... | collective-permute-start | bytes 110600 | tf_op jit(solution)/shard_map/ppermute | solution.py:301
  5.8 2.6 %collective-permute-start = (bf16[144,128]{1,0:T(8,128)(2,1)S(1)}, bf16[144,128]{1,0:T(8,128)(2,1)S(1)}, u32[]{:S(2)}, u32[]{:S(2)}) collective-permute-start(bf16[144,128]{1,0:T(8,128)(2,1)S(1)} %get-tuple-element.80), channel_id=1, source_target_pairs={{0,8},{4,12},{8,0},{12,4},{1,9},{5,13},{9,1},{13,5},{2,10},{6,14},... | collective-permute-start | bytes 110600 | tf_op jit(solution)/shard_map/ppermute | solution.py:301
  8.4 0.2 fusion.refs_5_.perm_ref.refs_8_
  8.5 2.1 %collective-permute-done = bf16[144,128]{1,0:T(8,128)(2,1)S(1)} collective-permute-done((bf16[144,128]{1,0:T(8,128)(2,1)S(1)}, bf16[144,128]{1,0:T(8,128)(2,1)S(1)}, u32[]{:S(2)}, u32[]{:S(2)}) %collective-permute-start) | collective-permute-done | bytes 36896 | tf_op jit(solution)/shard_map/ppermute | solution.py:301
  10.6 1.6 %collective-permute-start.1 = (bf16[288,128]{1,0:T(8,128)(2,1)S(1)}, bf16[288,128]{1,0:T(8,128)(2,1)S(1)}, u32[]{:S(2)}, u32[]{:S(2)}) collective-permute-start(bf16[288,128]{1,0:T(8,128)(2,1)S(1)} %bitcast.165), channel_id=1, source_target_pairs={{0,4},{4,0},{8,12},{12,8},{1,5},{5,1},{9,13},{13,9},{2,6},{6,2},{1... | collective-permute-start | bytes 221192 | tf_op jit(solution)/shard_map/ppermute | solution.py:301
  12.3 0.0 collective-permute-done.4
  12.3 0.1 collective-permute-start.5
  12.4 2.7 %collective-permute-done.1 = bf16[288,128]{1,0:T(8,128)(2,1)S(1)} collective-permute-done((bf16[288,128]{1,0:T(8,128)(2,1)S(1)}, bf16[288,128]{1,0:T(8,128)(2,1)S(1)}, u32[]{:S(2)}, u32[]{:S(2)}) %collective-permute-start.1) | collective-permute-done | bytes 73760 | tf_op jit(solution)/shard_map/ppermute | solution.py:301
  15.1 0.6 collective-permute-start.2
  15.7 0.0 collective-permute-done.5
  15.8 0.1 copy.20
  15.9 0.2 copy.21
  16.1 3.4 %collective-permute-done.2 = bf16[288,128]{1,0:T(8,128)(2,1)S(1)} collective-permute-done((bf16[288,128]{1,0:T(8,128)(2,1)S(1)}, bf16[288,128]{1,0:T(8,128)(2,1)S(1)}, u32[]{:S(2)}, u32[]{:S(2)}) %collective-permute-start.2) | collective-permute-done | bytes 73760 | tf_op jit(solution)/shard_map/ppermute | solution.py:301
  19.5 0.0 copy-start.5
  19.6 0.0 copy-start.6
  19.6 0.0 copy-start.2
  19.6 0.1 collective-permute-start.3
  19.7 0.0 copy-start.3
  19.7 1.0 %copy-done.3 = bf16[1024,128]{1,0:T(8,128)(2,1)S(1)} copy-done((bf16[1024,128]{1,0:T(8,128)(2,1)S(1)}, bf16[1024,128]{1,0:T(8,128)(2,1)}, u32[]{:S(2)}) %copy-start.3) | copy-done | bytes 262168
  20.7 0.7 %copy-done.4 = bf16[64,64]{1,0:T(8,128)(2,1)S(1)} copy-done((bf16[64,64]{1,0:T(8,128)(2,1)S(1)}, bf16[64,64]{1,0:T(8,128)(2,1)}, u32[]{:S(2)}) %copy-start.4) | copy-done | bytes 8216
  21.4 3.4 %shard_map.111 = (bf16[64,512,128]{2,1,0:T(8,128)(2,1)S(1)}, bf16[96,1024]{1,0:T(8,128)(2,1)S(1)}, bf16[64,64]{1,0:T(8,128)(2,1)S(1)}, bf16[32,4096]{1,0:T(8,128)(2,1)S(1)}) custom-call(bf16[1024,64]{1,0:T(8,128)(2,1)S(1)} %bitcast.126, bf16[64,64]{1,0:T(8,128)(2,1)S(1)} %copy-done.4, bf16[1024,128]{1,0:T(8,128)(2,1)S(1)} %copy-done.3), custom_call_target="tpu_custom_call" | custom-call | flops 4000000000 | bytes 8000000 | tf_op jit(solution)/shard_map/pallas_call | solution.py:396
  24.9 3.3 %copy-done.7 = bf16[64,512,128]{2,1,0:T(8,128)(2,1)} copy-done((bf16[64,512,128]{2,1,0:T(8,128)(2,1)}, bf16[64,512,128]{2,1,0:T(8,128)(2,1)S(1)}, u32[]{:S(2)}) %copy-start.7) | copy-done | bytes 8388632
  28.2 0.0 collective-permute-done.3
  28.2 0.1 reshape_squeeze.9
  28.4 0.0 slice-start
  28.5 0.0 slice-start.1
  28.5 7.3 %shard_map.112 = (bf16[64,64,128]{2,1,0:T(8,128)(2,1)S(1)}, bf16[64,512]{1,0:T(8,128)(2,1)S(1)}, bf16[512,64]{1,0:T(8,128)(2,1)S(1)}, f32[4,64,16]{2,1,0:T(8,128...) custom-call(bf16[64,64,128]{2,1,0:T(8,128)(2,1)S(1)} %copy-done.2, ...), custom_call_target="tpu_custom_call" | custom-call | flops 5000000000 | bytes 8000000 | tf_op jit(solution)/shard_map/pallas_call | solution.py:416
  35.8 0.6 collective-permute-start.6
  36.5 3.4 %shard_map.113 = (bf16[48,128]{1,0:T(8,128)(2,1)S(1)}, bf16[4,64,128]{2,1,0:T(8,128)(2,1)S(1)}) custom-call(bf16[64,64,128]{2,1,0:T(8,128)(2,1)S(1)} %get-tuple-element.41.g_ref, bf16[64,512,128]{2,1,0:T(8,128)(2,1)S(1)} %bitcast.144, bf16[16,64,64]{2,1,0:T(8,128)(2,1)S(1)} %bitcast.130, bf16[512,512]{1,0:T(8,128)(2,1)S(1)} %fusion.refs_5_.perm_ref.refs_8_, ...), custom_call_target="tpu_custom_call" | custom-call | flops 6000000000 | bytes 16000000 | tf_op jit(solution)/shard_map/pallas_call | solution.py:437
  39.9 1.8 %collective-permute-done.6 = bf16[512,128]{1,0:T(8,128)(2,1)S(1)} collective-permute-done((bf16[512,128]{1,0:T(8,128)(2,1)S(1)}, bf16[512,128]{1,0:T(8,128)(2,1)S(1)}, u32[]{:S(2)}, u32[]{:S(2)}) %collective-permute-start.6) | collective-permute-done | bytes 131104 | tf_op jit(solution)/shard_map/ppermute | solution.py:301
  41.8 0.1 collective-permute-start.7
  41.9 1.3 %collective-permute-done.7 = bf16[432,128]{1,0:T(8,128)(2,1)S(1)} collective-permute-done((bf16[432,128]{1,0:T(8,128)(2,1)S(1)}, bf16[432,128]{1,0:T(8,128)(2,1)S(1)}, u32[]{:S(2)}, u32[]{:S(2)}) %collective-permute-start.7) | collective-permute-done | bytes 110624 | tf_op jit(solution)/shard_map/ppermute | solution.py:301
  43.3 1.6 %collective-permute-start.8 = (bf16[432,128]{1,0:T(8,128)(2,1)S(1)}, bf16[432,128]{1,0:T(8,128)(2,1)S(1)}, u32[]{:S(2)}, u32[]{:S(2)}) collective-permute-start(bf16[432,128]{1,0:T(8,128)(2,1)S(1)} %pad_maximum_fusion.7), channel_id=1, source_target_pairs={{0,4},{4,0},{8,12},{12,8},{1,5},{5,1},{9,13},{13,9},{2,6},{6,2},{1... | collective-permute-start | bytes 331784 | tf_op jit(solution)/shard_map/ppermute | solution.py:301
  45.0 3.4 %copy-done.8 = bf16[64,512,128]{2,1,0:T(8,128)(2,1)S(1)} copy-done((bf16[64,512,128]{2,1,0:T(8,128)(2,1)S(1)}, bf16[64,512,128]{2,1,0:T(8,128)(2,1)}, u32[]{:S(2)}) %copy-start.8) | copy-done | bytes 8388632
  48.3 0.8 %copy-done.10 = bf16[64,512]{1,0:T(8,128)(2,1)S(1)} copy-done((bf16[64,512]{1,0:T(8,128)(2,1)S(1)}, bf16[64,512]{1,0:T(8,128)(2,1)}, u32[]{:S(2)}) %copy-start.10) | copy-done | bytes 65560
  49.2 3.6 %shard_map.114 = (bf16[64,64,128]{2,1,0:T(8,128)(2,1)}, bf16[4096,32]{1,0:T(8,128)(2,1)S(1)}, bf16[48,128]{1,0:T(8,128)(2,1)S(1)}) custom-call(f32[4,64,16]{2,1,0:T(8,128)S(1)} %get-tuple-element.37.inv_ref, bf16[64,512]{1,0:T(8,128)(2,1)S(1)} %copy-done.10, bf16[64,512,128]{2,1,0:T(8,128)(2,1)S(1)} %copy-done.8, f32[1,128]{1,0:T(1,128)S(1)} %get-tuple-element.40.offset_ref, ...), custom_call_target="tpu_custom_call" | custom-call | flops 6000000000 | bytes 8000000 | tf_op jit(solution)/shard_map/pallas_call | solution.py:459
  52.7 0.0 collective-permute-done.8
  52.9 2.9 %collective-permute-start.9 = (bf16[432,128]{1,0:T(8,128)(2,1)S(1)}, bf16[432,128]{1,0:T(8,128)(2,1)S(1)}, u32[]{:S(2)}, u32[]{:S(2)}) collective-permute-start(bf16[432,128]{1,0:T(8,128)(2,1)S(1)} %pad_maximum_fusion.8), channel_id=1, source_target_pairs={{0,8},{4,12},{8,0},{12,4},{1,9},{5,13},{9,1},{13,5},{2,10},{6,14},... | collective-permute-start | bytes 331784 | tf_op jit(solution)/shard_map/ppermute | solution.py:301
  55.8 5.4 %shard_map.115 = (bf16[4,32,128]{2,1,0:T(8,128)(2,1)S(1)}, bf16[4,32,128]{2,1,0:T(8,128)(2,1)S(1)}, bf16[48,128]{1,0:T(8,128)(2,1)S(1)}) custom-call(bf16[64,64,128]{2,1,0:T(8,128)(2,1)S(1)} %get-tuple-element.41.g_ref, bf16[512,64]{1,0:T(8,128)(2,1)S(1)} %get-tuple-element.48.bt_ref, bf16[4096,32]{1,0:T(8,128)(2,1)S(1)} %get-tuple-element.49.wd_ref, ...), custom_call_target="tpu_custom_call" | custom-call | flops 6000000000 | bytes 8000000 | tf_op jit(solution)/shard_map/pallas_call | solution.py:475
  61.2 0.0 collective-permute-done.9
  61.4 0.6 collective-permute-start.10
  61.9 4.6 %collective-permute-done.10 = bf16[496,128]{1,0:T(8,128)(2,1)S(1)} collective-permute-done((bf16[496,128]{1,0:T(8,128)(2,1)S(1)}, bf16[496,128]{1,0:T(8,128)(2,1)S(1)}, u32[]{:S(2)}, u32[]{:S(2)}) %collective-permute-start.10) | collective-permute-done | bytes 127008 | tf_op jit(solution)/shard_map/ppermute | solution.py:301
  66.6 0.1 collective-permute-start.11
  66.7 1.3 %collective-permute-done.11 = bf16[576,128]{1,0:T(8,128)(2,1)S(1)} collective-permute-done((bf16[576,128]{1,0:T(8,128)(2,1)S(1)}, bf16[576,128]{1,0:T(8,128)(2,1)S(1)}, u32[]{:S(2)}, u32[]{:S(2)}) %collective-permute-start.11) | collective-permute-done | bytes 147488 | tf_op jit(solution)/shard_map/ppermute | solution.py:301
  68.2 2.4 %shard_map.116 = (f32[256,64]{1,0:T(8,128)}, f32[64,64]{1,0:T(8,128)}, f32[1,128]{1,0:T(1,128)}, f32[32,32,128]{2,1,0:T(8,128)}) custom-call(bf16[32,256]{1,0:T(8,128)(2,1)S(1)} %bitcast.136, bf16[32,256]{1,0:T(8,128)(2,1)S(1)} %bitcast.137, bf16[16,512]{1,0:T(8,128)(2,1)S(1)} %bitcast.135, bf16[48,128]{1,0:T(8,128)(2,1)S(1)} %add_convert_fusion.2.refs_3_, ...), custom_call_target="tpu_custom_call" | custom-call | tf_op jit(solution)/shard_map/pallas_call | solution.py:521
  (75 shorter events, 0.8 us)
Async XLA Ops:
  1.4 0.8 %copy-start = (bf16[16,16,64]{2,1,0:T(8,128)(2,1)S(1)}, bf16[16,16,64]{2,1,0:T(8,128)(2,1)}, u32[]{:S(2)}) copy-start(bf16[16,16,64]{2,1,0:T(8,128)(2,1)} %param.7) | copy-start | bytes 98308
  2.8 9.5 %collective-permute-start.4 = (bf16[144,128]{1,0:T(8,128)(2,1)S(1)}, bf16[144,128]{1,0:T(8,128)(2,1)S(1)}, u32[]{:S(2)}, u32[]{:S(2)}) collective-permute-start(bf16[144,128]{1,0:T(8,128)(2,1)S(1)} %get-tuple-element.79), channel_id=1, source_target_pairs={{0,2},{1,3},{2,0},{3,1},{4,6},{5,7},{6,4},{7,5},{8,10},{9,11},{10,... | collective-permute-start | bytes 110600 | tf_op jit(solution)/shard_map/ppermute | solution.py:301
  5.8 4.9 %collective-permute-start = (bf16[144,128]{1,0:T(8,128)(2,1)S(1)}, bf16[144,128]{1,0:T(8,128)(2,1)S(1)}, u32[]{:S(2)}, u32[]{:S(2)}) collective-permute-start(bf16[144,128]{1,0:T(8,128)(2,1)S(1)} %get-tuple-element.80), channel_id=1, source_target_pairs={{0,8},{4,12},{8,0},{12,4},{1,9},{5,13},{9,1},{13,5},{2,10},{6,14},... | collective-permute-start | bytes 110600 | tf_op jit(solution)/shard_map/ppermute | solution.py:301
  10.6 4.4 %collective-permute-start.1 = (bf16[288,128]{1,0:T(8,128)(2,1)S(1)}, bf16[288,128]{1,0:T(8,128)(2,1)S(1)}, u32[]{:S(2)}, u32[]{:S(2)}) collective-permute-start(bf16[288,128]{1,0:T(8,128)(2,1)S(1)} %bitcast.165), channel_id=1, source_target_pairs={{0,4},{4,0},{8,12},{12,8},{1,5},{5,1},{9,13},{13,9},{2,6},{6,2},{1... | collective-permute-start | bytes 221192 | tf_op jit(solution)/shard_map/ppermute | solution.py:301
  12.3 3.4 %collective-permute-start.5 = (bf16[288,128]{1,0:T(8,128)(2,1)S(1)}, bf16[288,128]{1,0:T(8,128)(2,1)S(1)}, u32[]{:S(2)}, u32[]{:S(2)}) collective-permute-start(bf16[288,128]{1,0:T(8,128)(2,1)S(1)} %bitcast.164), channel_id=1, source_target_pairs={{0,1},{1,0},{2,3},{3,2},{4,5},{5,4},{6,7},{7,6},{8,9},{9,8},{10,11... | collective-permute-start | bytes 221192 | tf_op jit(solution)/shard_map/ppermute | solution.py:301
  15.1 4.4 %collective-permute-start.2 = (bf16[288,128]{1,0:T(8,128)(2,1)S(1)}, bf16[288,128]{1,0:T(8,128)(2,1)S(1)}, u32[]{:S(2)}, u32[]{:S(2)}) collective-permute-start(bf16[288,128]{1,0:T(8,128)(2,1)S(1)} %bitcast.162), channel_id=1, source_target_pairs={{0,2},{1,3},{2,0},{3,1},{4,6},{5,7},{6,4},{7,5},{8,10},{9,11},{10,... | collective-permute-start | bytes 221192 | tf_op jit(solution)/shard_map/ppermute | solution.py:301
  19.5 8.9 %copy-start.5 = (bf16[64,64]{1,0:T(8,128)(2,1)S(1)}, bf16[64,64]{1,0:T(8,128)(2,1)}, u32[]{:S(2)}) copy-start(bf16[64,64]{1,0:T(8,128)(2,1)} %refs_4_.1) | copy-start | bytes 24580
  19.6 8.9 %copy-start.6 = (f32[128]{0:T(128)S(1)}, f32[128]{0:T(128)}, u32[]{:S(2)}) copy-start(f32[128]{0:T(128)} %param.12) | copy-start | bytes 1540
  19.6 8.9 %copy-start.2 = (bf16[64,64,128]{2,1,0:T(8,128)(2,1)S(1)}, bf16[64,64,128]{2,1,0:T(8,128)(2,1)}, u32[]{:S(2)}) copy-start(bf16[64,64,128]{2,1,0:T(8,128)(2,1)} %refs_0_.1) | copy-start | bytes 3145732
  19.6 8.5 %collective-permute-start.3 = (bf16[288,128]{1,0:T(8,128)(2,1)S(1)}, bf16[288,128]{1,0:T(8,128)(2,1)S(1)}, u32[]{:S(2)}, u32[]{:S(2)}) collective-permute-start(bf16[288,128]{1,0:T(8,128)(2,1)S(1)} %bitcast.163), channel_id=1, source_target_pairs={{0,1},{1,0},{2,3},{3,2},{4,5},{5,4},{6,7},{7,6},{8,9},{9,8},{10,11... | collective-permute-start | bytes 221192 | tf_op jit(solution)/shard_map/ppermute | solution.py:301
  19.7 1.0 %copy-start.3 = (bf16[1024,128]{1,0:T(8,128)(2,1)S(1)}, bf16[1024,128]{1,0:T(8,128)(2,1)}, u32[]{:S(2)}) copy-start(bf16[1024,128]{1,0:T(8,128)(2,1)} %wide_ref.1) | copy-start | bytes 786436
  20.7 0.7 %copy-start.4 = (bf16[64,64]{1,0:T(8,128)(2,1)S(1)}, bf16[64,64]{1,0:T(8,128)(2,1)}, u32[]{:S(2)}) copy-start(bf16[64,64]{1,0:T(8,128)(2,1)} %refs_4_.1) | copy-start | bytes 24580
  24.9 3.3 %copy-start.7 = (bf16[64,512,128]{2,1,0:T(8,128)(2,1)}, bf16[64,512,128]{2,1,0:T(8,128)(2,1)S(1)}, u32[]{:S(2)}) copy-start(bf16[64,512,128]{2,1,0:T(8,128)(2,1)S(1)} %get-tuple-element.39.t_ref) | copy-start | bytes 25165828
  28.4 8.1 %slice-start = ((s8[8388608]{0:T(1024)(128)(4,1)}), s8[4194304]{0:T(1024)(128)(4,1)S(1)}, s32[]{:S(2)}) async-start(s8[8388608]{0:T(1024)(128)(4,1)} %bitcast.143), calls=%async_computation | async-start | bytes 8388608
  28.5 8.0 %slice-start.1 = ((s8[8388608]{0:T(1024)(128)(4,1)}), s8[4194304]{0:T(1024)(128)(4,1)S(1)}, s32[]{:S(2)}) async-start(s8[8388608]{0:T(1024)(128)(4,1)} %bitcast.143), calls=%async_computation.1 | async-start | bytes 8388608
  35.8 4.1 %copy-start.9 = (bf16[64,512]{1,0:T(8,128)(2,1)}, bf16[64,512]{1,0:T(8,128)(2,1)S(1)}, u32[]{:S(2)}) copy-start(bf16[64,512]{1,0:T(8,128)(2,1)S(1)} %get-tuple-element.38.b_ref) | copy-start | bytes 196612
  35.8 5.9 %collective-permute-start.6 = (bf16[512,128]{1,0:T(8,128)(2,1)S(1)}, bf16[512,128]{1,0:T(8,128)(2,1)S(1)}, u32[]{:S(2)}, u32[]{:S(2)}) collective-permute-start(bf16[512,128]{1,0:T(8,128)(2,1)S(1)} %bitcast.159), channel_id=1, source_target_pairs={{0,2},{1,3},{2,0},{3,1},{4,6},{5,7},{6,4},{7,5},{8,10},{9,11},{10,... | collective-permute-start | bytes 393224 | tf_op jit(solution)/shard_map/ppermute | solution.py:301
  41.8 1.4 %collective-permute-start.7 = (bf16[432,128]{1,0:T(8,128)(2,1)S(1)}, bf16[432,128]{1,0:T(8,128)(2,1)S(1)}, u32[]{:S(2)}, u32[]{:S(2)}) collective-permute-start(bf16[432,128]{1,0:T(8,128)(2,1)S(1)} %pad_maximum_fusion.6), channel_id=1, source_target_pairs={{0,1},{1,0},{2,3},{3,2},{4,5},{5,4},{6,7},{7,6},{8,9},{9,8},{10,11... | collective-permute-start | bytes 331784 | tf_op jit(solution)/shard_map/ppermute | solution.py:301
  43.3 9.4 %collective-permute-start.8 = (bf16[432,128]{1,0:T(8,128)(2,1)S(1)}, bf16[432,128]{1,0:T(8,128)(2,1)S(1)}, u32[]{:S(2)}, u32[]{:S(2)}) collective-permute-start(bf16[432,128]{1,0:T(8,128)(2,1)S(1)} %pad_maximum_fusion.7), channel_id=1, source_target_pairs={{0,4},{4,0},{8,12},{12,8},{1,5},{5,1},{9,13},{13,9},{2,6},{6,2},{1... | collective-permute-start | bytes 331784 | tf_op jit(solution)/shard_map/ppermute | solution.py:301
  44.9 3.4 %copy-start.8 = (bf16[64,512,128]{2,1,0:T(8,128)(2,1)S(1)}, bf16[64,512,128]{2,1,0:T(8,128)(2,1)}, u32[]{:S(2)}) copy-start(bf16[64,512,128]{2,1,0:T(8,128)(2,1)} %copy-done.7) | copy-start | bytes 25165828
  48.3 0.8 %copy-start.10 = (bf16[64,512]{1,0:T(8,128)(2,1)S(1)}, bf16[64,512]{1,0:T(8,128)(2,1)}, u32[]{:S(2)}) copy-start(bf16[64,512]{1,0:T(8,128)(2,1)} %copy-done.9) | copy-start | bytes 196612
  52.9 8.4 %collective-permute-start.9 = (bf16[432,128]{1,0:T(8,128)(2,1)S(1)}, bf16[432,128]{1,0:T(8,128)(2,1)S(1)}, u32[]{:S(2)}, u32[]{:S(2)}) collective-permute-start(bf16[432,128]{1,0:T(8,128)(2,1)S(1)} %pad_maximum_fusion.8), channel_id=1, source_target_pairs={{0,8},{4,12},{8,0},{12,4},{1,9},{5,13},{9,1},{13,5},{2,10},{6,14},... | collective-permute-start | bytes 331784 | tf_op jit(solution)/shard_map/ppermute | solution.py:301
  55.8 12.4 %copy-start.1 = (bf16[16,16,64]{2,1,0:T(8,128)(2,1)S(1)}, bf16[16,16,64]{2,1,0:T(8,128)(2,1)}, u32[]{:S(2)}) copy-start(bf16[16,16,64]{2,1,0:T(8,128)(2,1)} %param.7) | copy-start | bytes 98308
  61.4 5.1 %collective-permute-start.10 = (bf16[496,128]{1,0:T(8,128)(2,1)S(1)}, bf16[496,128]{1,0:T(8,128)(2,1)S(1)}, u32[]{:S(2)}, u32[]{:S(2)}) collective-permute-start(bf16[496,128]{1,0:T(8,128)(2,1)S(1)} %pad_maximum_fusion.5), channel_id=1, source_target_pairs={{0,2},{1,3},{2,0},{3,1},{4,6},{5,7},{6,4},{7,5},{8,10},{9,11},{10,... | collective-permute-start | bytes 380936 | tf_op jit(solution)/shard_map/ppermute | solution.py:301
  66.6 1.4 %collective-permute-start.11 = (bf16[576,128]{1,0:T(8,128)(2,1)S(1)}, bf16[576,128]{1,0:T(8,128)(2,1)S(1)}, u32[]{:S(2)}, u32[]{:S(2)}) collective-permute-start(bf16[576,128]{1,0:T(8,128)(2,1)S(1)} %pad_maximum_fusion.3), channel_id=1, source_target_pairs={{0,1},{1,0},{2,3},{3,2},{4,5},{5,4},{6,7},{7,6},{8,9},{9,8},{10,11... | collective-permute-start | bytes 442376 | tf_op jit(solution)/shard_map/ppermute | solution.py:301

commit v9 on v8

--- a/solution.py
+++ b/solution.py
@@ -10,7 +10,7 @@
 F32 = jnp.float32
 BF16 = jnp.bfloat16
 LANES = 128
-VMEM_LIMIT = 16 * 1024 * 1024
+VMEM_LIMIT = 57 * 1024 * 1024
 NT = (((1,), (1,)), ((), ()))
 
 
@@ -57,8 +57,11 @@
     return center * scale, scale
 
 
-def prep_kernel(depth, own, x_ref, mask_ref, by_token_ref, by_row_ref, mask_out_ref):
+def prep_kernel(depth, own, x_ref, cell_ref, line_ref, by_token_ref, by_row_ref, mask_out_ref, mask_ref):
     rows = depth * own
+    same = iota((depth, depth), 0) == iota((depth, depth), 1)
+    line = jnp.sum(jnp.where(same, line_ref[...].astype(F32), 0.0), axis=1, keepdims=True)
+    mask_ref[...] = (cell_ref[...].astype(F32) * line).astype(BF16)
     normed, _ = stats(x_ref[...].astype(F32))
     pick = one_hot(iota((rows, depth), 0) // own == iota((rows, depth), 1))
     here = iota((rows, own), 0) % own == iota((rows, own), 1)
@@ -322,6 +325,14 @@
     return jnp.stack([low, jnp.where(first, other, mine)], axis=at)
 
 
+def unswap(x, axis):
+    n = x.shape[0]
+    for bit in range(n.bit_length() - 1):
+        y = x.reshape((n >> (bit + 1), 2, 1 << bit) + x.shape[1:])
+        x = jnp.where(bit_of(axis, bit) == 0, y, y[:, ::-1]).reshape(x.shape)
+    return x
+
+
 def add(mine, other):
     other = other.reshape(mine.shape)
     return lax.optimization_barrier((mine.astype(F32) + other.astype(F32)).astype(BF16))
@@ -348,38 +359,33 @@
 
     bits = n.bit_length() - 1
     x = alignment_embedding.reshape(rows, features)
-    mask = (alignment_cell_exists * alignment_lines_exist[:, None]).astype(BF16)
     offset = offset_vector.reshape(1, pair)
-    out_shapes = [sds((rows // 2, LANES), BF16)] * 2 + [sds((own, LANES), BF16)]
-    by_token, by_row, mask_t = call(
+    args = (x, alignment_cell_exists, alignment_lines_exist.reshape(1, depth))
+    out_shapes = [sds((rows // 2, LANES), BF16)] * 2 + [sds((own, LANES), BF16), sds((depth, own), BF16)]
+    by_token, by_row, mask_t, mask = call(
         functools.partial(prep_kernel, depth, own),
-        (),
-        [full(x.shape), full(mask.shape)],
+        (1,),
+        [full(v.shape) for v in args],
         [full(o.shape) for o in out_shapes],
         out_shapes,
-    )(x, mask)
-    held = jnp.concatenate([by_row, mask_t], axis=0)[None]
-    for bit in reversed(range(bits)):
-        (got,) = swap_parts([held], "row", bit, n)
-        held = in_order(held, got.reshape(held.shape), "row", bit, 1)
-        held = held.reshape((-1,) + held.shape[2:])
-    held = held[:, None]
-    for bit in reversed(range(bits)):
-        keep, go = halves(split_high(held), "col", bit, 0)
-        (got,) = swap_parts([go], "col", bit, n)
-        held = in_order(keep, got.reshape(keep.shape), "col", bit, 2)
-        held = held.reshape((keep.shape[0], -1) + keep.shape[2:])
-    seen_j = held[0, :, rows // 2 :].reshape(block, LANES)
-    parts = held[0, :, : rows // 2].reshape(n, depth // 2, own, 2, features)
-    mj = parts.transpose(3, 1, 0, 2, 4).reshape(depth, block, features)
-    held = jnp.concatenate([by_token, mask_t], axis=0)[None]
-    for bit in reversed(range(bits)):
-        (got,) = swap_parts([held], "col", bit, n)
-        held = in_order(held, got.reshape(held.shape), "col", bit, 1)
-        held = held.reshape((-1,) + held.shape[2:])
+    )(*args)
+    message = jnp.concatenate([by_token, mask_t], axis=0)
+    held = [message]
+    for k in range(1, n):
+        held.append(lax.ppermute(message, "col", [(j, j ^ k) for j in range(n)]))
+    held = unswap(jnp.stack(held), "col")
     seen_i = held[:, rows // 2 :].reshape(block, LANES)
     parts = held[:, : rows // 2].reshape(n, rows // 2, 2, features)
     mi = parts.transpose(0, 2, 1, 3).reshape(block * depth, features)
+    message = jnp.concatenate([by_row, mask_t], axis=0)
+    held = []
+    for k in range(n):
+        pairs = [(i * n + j, (j ^ k) * n + i) for i in range(n) for j in range(n)]
+        held.append(lax.ppermute(message, axes, pairs))
+    held = unswap(jnp.stack(held), "row")
+    seen_j = held[:, rows // 2 :].reshape(block, LANES)
+    parts = held[:, : rows // 2].reshape(n, depth // 2, own, 2, features)
+    mj = parts.transpose(3, 1, 0, 2, 4).reshape(depth, block, features)
 
     wide = width * depth
     tokens = block * depth

time: 71 us -> 85.3 us (1.20)
  Pallas kernels: 26.1 us -> 43.2 us
  waiting for transfers between devices: 17.1 us -> 6.87 us
  other arithmetic: 1.49 us -> 6.64 us
  starting transfers between devices: 13.9 us -> 17.1 us
  local copies, waits for them, and re-layouts: 10.8 us -> 9.6 us
    ppermute x12 -> x6, waiting for transfers between devices: 17.1 us -> 4.84 us  [swap_parts(): message = lax.ppermute(message, axis, pairs)]
    ppermute x0 -> x7, starting transfers between devices: none -> 11.8 us  [the longest x4 7.19 us: per_device(): held.append(lax.ppermute(message, axes, pairs))]
    unnamed x28 -> x10, local copies, waits for them, and re-layouts: 10.1 us -> 1.39 us
    ppermute x12 -> x6, starting transfers between devices: 13.9 us -> 5.32 us  [swap_parts(): message = lax.ppermute(message, axis, pairs)]
    pallas_call x1, Pallas kernels: 3.45 us -> 7.18 us  [per_device(): call(functools.partial(token_kernel, depth, features, n), (steps,), [up_s...]
    pallas_call x1, Pallas kernels: 3.44 us -> 6.62 us  [per_device(): call(functools.partial(row_kernel, depth, features), (steps,), [full(v.sh...]
    pallas_call x1, Pallas kernels: 3.57 us -> 6.56 us  [per_device(): call(update_kernel, (steps,), specs, [up_spec, full((width * pair, width)...]
    convert_element_type x10, other arithmetic: 0.19 us -> 3.07 us  [add(): (mine.astype(F32) + other.astype(F32)).astype(BF16)]
  transfers between devices with their start and end apart: 12 -> 13, of which waited for: 7 -> 3; matrix products, arithmetic and copies ran while one was open for 1% -> 5% of each run, Pallas kernels for 22% -> 25%
where the time goes in v9:
time: 85.3 us; the launch traced here: 84.3 us
  Pallas kernels  43.2 us (51%)
  starting transfers between devices  17.1 us (20%)
  local copies, waits for them, and re-layouts  9.6 us (11%)
  waiting for transfers between devices  6.87 us (8%)
  other arithmetic  6.64 us (8%)
  between operations  0.93 us (1%)
    pallas_call x1, Pallas kernels, per_device(): call(functools.partial(weight_kernel, depth, features), (steps,), [up_spe...  9.76 us
    pallas_call x1, Pallas kernels, per_device(): call(functools.partial(left_kernel, depth, bits - 1), (steps,), [up_spec]...  7.38 us
    ppermute x4, starting transfers between devices, per_device(): held.append(lax.ppermute(message, axes, pairs))  7.19 us
    pallas_call x1, Pallas kernels, per_device(): call(functools.partial(token_kernel, depth, features, n), (steps,), [up_s...  7.18 us
    pallas_call x1, Pallas kernels, per_device(): call(functools.partial(row_kernel, depth, features), (steps,), [full(v.sh...  6.62 us
    pallas_call x1, Pallas kernels, per_device(): call(update_kernel, (steps,), specs, [up_spec, full((width * pair, width)...  6.56 us
    ppermute x6, starting transfers between devices, swap_parts(): message = lax.ppermute(message, axis, pairs)  5.32 us
    ppermute x6, waiting for transfers between devices, swap_parts(): message = lax.ppermute(message, axis, pairs)  4.84 us
  transfers between devices with their start and end apart: 13, of which 3 were waited for; matrix products, arithmetic and copies ran while one was open for 5% of the time, Pallas kernels for 25%

profile of v9, /device:TPU:0, one launch (start us, length us, event | category | flops | bytes accessed | tf_op | source)
XLA Modules:
  0.0 84.3 jit_solution(311803597800652064)
XLA Ops:
  0.6 2.0 %shard_map.110 = (bf16[128,128]{1,0:T(8,128)(2,1)}, bf16[128,128]{1,0:T(8,128)(2,1)}, bf16[16,128]{1,0:T(8,128)(2,1)}, bf16[16,16]{1,0:T(8,128)(2,1)}) custom-call(bf16[256,64]{1,0:T(8,128)(2,1)} %bitcast.121, s32[16,16]{1,0:T(8,128)} %cell_ref.1, s32[1,16]{1,0:T(1,128)} %bitcast.152), custom_call_target="tpu_custom_call" | custom-call | tf_op jit(solution)/shard_map/pallas_call | solution.py:365
  2.7 0.8 constant_dynamic-update-slice_fusion.1
  3.5 0.7 constant_dynamic-update-slice_fusion.2
  4.2 5.0 %collective-permute-start.3 = (bf16[144,128]{1,0:T(8,128)(2,1)S(1)}, bf16[144,128]{1,0:T(8,128)(2,1)S(1)}, u32[]{:S(2)}, u32[]{:S(2)}) collective-permute-start(bf16[144,128]{1,0:T(8,128)(2,1)S(1)} %get-tuple-element.70), channel_id=1, source_target_pairs={{0,12},{1,8},{2,4},{3,0},{4,13},{5,9},{6,5},{7,1},{8,14},{9,10},{1... | collective-permute-start | bytes 110600 | tf_op jit(solution)/shard_map/ppermute | solution.py:384
  9.2 1.5 %collective-permute-start.2 = (bf16[144,128]{1,0:T(8,128)(2,1)S(1)}, bf16[144,128]{1,0:T(8,128)(2,1)S(1)}, u32[]{:S(2)}, u32[]{:S(2)}) collective-permute-start(bf16[144,128]{1,0:T(8,128)(2,1)S(1)} %get-tuple-element.70), channel_id=1, source_target_pairs={{0,8},{1,12},{2,0},{3,4},{4,9},{5,13},{6,1},{7,5},{8,10},{9,14},{1... | collective-permute-start | bytes 110600 | tf_op jit(solution)/shard_map/ppermute | solution.py:384
  10.7 0.0 collective-permute-start.1
  10.7 0.7 collective-permute-start
  11.4 3.2 %collective-permute-start.6 = (bf16[144,128]{1,0:T(8,128)(2,1)S(1)}, bf16[144,128]{1,0:T(8,128)(2,1)S(1)}, u32[]{:S(2)}, u32[]{:S(2)}) collective-permute-start(bf16[144,128]{1,0:T(8,128)(2,1)S(1)} %get-tuple-element.69), channel_id=1, source_target_pairs={{0,3},{1,2},{2,1},{3,0},{4,7},{5,6},{6,5},{7,4},{8,11},{9,10},{10,... | collective-permute-start | bytes 110600 | tf_op jit(solution)/shard_map/ppermute | solution.py:375
  14.6 1.0 %fusion.refs_5_.perm_ref.refs_8_ = bf16[512,512]{1,0:T(8,128)(2,1)} fusion(s32[512]{0:T(512)S(1)} %fusion.15), kind=kLoop, calls=%fused_computation.1 | loop fusion | flops 524288 | bytes 526336 | tf_op jit(solution)/shard_map/convert_element_type | solution.py:393
  15.6 0.0 collective-permute-done.3
  15.6 1.1 %collective-permute-start.5 = (bf16[144,128]{1,0:T(8,128)(2,1)S(1)}, bf16[144,128]{1,0:T(8,128)(2,1)S(1)}, u32[]{:S(2)}, u32[]{:S(2)}) collective-permute-start(bf16[144,128]{1,0:T(8,128)(2,1)S(1)} %get-tuple-element.69), channel_id=1, source_target_pairs={{0,2},{1,3},{2,0},{3,1},{4,6},{5,7},{6,4},{7,5},{8,10},{9,11},{10,... | collective-permute-start | bytes 110600 | tf_op jit(solution)/shard_map/ppermute | solution.py:375
  16.7 0.0 collective-permute-done.2
  16.7 0.2 collective-permute-start.4
  16.9 0.0 collective-permute-done.1
  17.0 0.6 slice.77
  17.6 2.0 %collective-permute-done.5 = bf16[144,128]{1,0:T(8,128)(2,1)S(1)} collective-permute-done((bf16[144,128]{1,0:T(8,128)(2,1)S(1)}, bf16[144,128]{1,0:T(8,128)(2,1)S(1)}, u32[]{:S(2)}, u32[]{:S(2)}) %collective-permute-start.5) | collective-permute-done | bytes 36896 | tf_op jit(solution)/shard_map/ppermute | solution.py:375
  19.8 0.1 copy.19
  20.0 0.7 copy.20
  20.7 0.8 %copy.21 = bf16[4,2,128,64]{3,2,1,0:T(8,128)(2,1)} copy(bf16[4,2,128,64]{2,3,1,0:T(8,128)(2,1)S(1)} %bitcast.113) | data formatting | bytes 262144 | tf_op jit(solution)/shard_map/transpose | solution.py:379
  21.5 0.1 reshape.206
  21.7 0.8 copy.18
  22.4 6.6 %shard_map.111 = (bf16[64,512,128]{2,1,0:T(8,128)(2,1)}, bf16[96,1024]{1,0:T(8,128)(2,1)}, bf16[64,64]{1,0:T(8,128)(2,1)}, bf16[32,4096]{1,0:T(8,128)(2,1)}) custom-call(bf16[1024,64]{1,0:T(8,128)(2,1)} %bitcast.116, bf16[64,64]{1,0:T(8,128)(2,1)} %refs_4_.1, bf16[1024,128]{1,0:T(8,128)(2,1)} %wide_ref.1), custom_call_target="tpu_custom_call" | custom-call | flops 4000000000 | bytes 8000000 | tf_op jit(solution)/shard_map/pallas_call | solution.py:402
  29.0 9.8 %shard_map.112 = (bf16[64,64,128]{2,1,0:T(8,128)(2,1)}, bf16[64,512]{1,0:T(8,128)(2,1)}, bf16[512,64]{1,0:T(8,128)(2,1)}, f32[4,64,16]{2,1,0:T(8,128)}, f32[8,12...) custom-call(bf16[64,64,128]{2,1,0:T(8,128)(2,1)} %refs_0_.1, ...), custom_call_target="tpu_custom_call" | custom-call | flops 5000000000 | bytes 8000000 | tf_op jit(solution)/shard_map/pallas_call | solution.py:422
  38.8 0.9 %constant_dynamic-slice_fusion.2 = bf16[1,2,256,128]{3,2,1,0:T(8,128)(2,1)S(1)} fusion(bf16[2,2,256,128]{3,2,1,0:T(8,128)(2,1)} %bitcast.119, s32[]{:T(128)S(6)} %select_n.159), kind=kLoop, calls=%fused_computation.65 | loop fusion | bytes 262148 | tf_op jit(solution)/shard_map/jit(dynamic_index_in_dim)/dynamic_slice | solution.py:315
  39.7 1.3 %collective-permute-start.7 = (bf16[512,128]{1,0:T(8,128)(2,1)S(1)}, bf16[512,128]{1,0:T(8,128)(2,1)S(1)}, u32[]{:S(2)}, u32[]{:S(2)}) collective-permute-start(bf16[512,128]{1,0:T(8,128)(2,1)S(1)} %bitcast.129), channel_id=1, source_target_pairs={{0,2},{1,3},{2,0},{3,1},{4,6},{5,7},{6,4},{7,5},{8,10},{9,11},{10,... | collective-permute-start | bytes 393224 | tf_op jit(solution)/shard_map/ppermute | solution.py:304
  41.0 7.2 %shard_map.113 = (bf16[48,128]{1,0:T(8,128)(2,1)}, bf16[4,64,128]{2,1,0:T(8,128)(2,1)}) custom-call(bf16[64,64,128]{2,1,0:T(8,128)(2,1)} %get-tuple-element.42.g_ref, bf16[64,512,128]{2,1,0:T(8,128)(2,1)} %get-tuple-element.40.t_ref, bf16[16,64,64]{2,1,0:T(8,128)(2,1)} %bitcast.118, bf16[512,512]{1,0:T(8,128)(2,1)} %fusion.refs_5_.perm_ref.refs_8_, ...), custom_call_target="tpu_custom_call" | custom-call | flops 6000000000 | bytes 16000000 | tf_op jit(solution)/shard_map/pallas_call | solution.py:443
  48.2 0.8 constant_dynamic-slice_fusion.1
  49.1 0.7 pad_maximum_fusion.6
  49.8 1.3 %collective-permute-done.8 = bf16[432,128]{1,0:T(8,128)(2,1)S(1)} collective-permute-done((bf16[432,128]{1,0:T(8,128)(2,1)S(1)}, bf16[432,128]{1,0:T(8,128)(2,1)S(1)}, u32[]{:S(2)}, u32[]{:S(2)}) %collective-permute-start.8) | collective-permute-done | bytes 110624 | tf_op jit(solution)/shard_map/ppermute | solution.py:304
  51.1 0.7 add_convert_fusion.4.small_ref
  51.8 0.8 bitcast_select_fusion.2
  52.7 1.4 %collective-permute-start.9 = (bf16[432,128]{1,0:T(8,128)(2,1)S(1)}, bf16[432,128]{1,0:T(8,128)(2,1)S(1)}, u32[]{:S(2)}, u32[]{:S(2)}) collective-permute-start(bf16[432,128]{1,0:T(8,128)(2,1)S(1)} %pad_maximum_fusion.7), channel_id=1, source_target_pairs={{0,4},{4,0},{8,12},{12,8},{1,5},{5,1},{9,13},{13,9},{2,6},{6,2},{1... | collective-permute-start | bytes 331784 | tf_op jit(solution)/shard_map/ppermute | solution.py:304
  54.1 6.6 %shard_map.114 = (bf16[64,64,128]{2,1,0:T(8,128)(2,1)}, bf16[4096,32]{1,0:T(8,128)(2,1)}, bf16[48,128]{1,0:T(8,128)(2,1)}) custom-call(f32[4,64,16]{2,1,0:T(8,128)} %get-tuple-element.38.inv_ref, bf16[64,512]{1,0:T(8,128)(2,1)} %get-tuple-element.39.b_ref, bf16[64,512,128]{2,1,0:T(8,128)(2,1)} %get-tuple-element.40.t_ref, ...), custom_call_target="tpu_custom_call" | custom-call | flops 6000000000 | bytes 8000000 | tf_op jit(solution)/shard_map/pallas_call | solution.py:465
  60.6 0.7 add_convert_fusion.3.small_ref
  61.4 1.0 %collective-permute-start.10 = (bf16[432,128]{1,0:T(8,128)(2,1)S(1)}, bf16[432,128]{1,0:T(8,128)(2,1)S(1)}, u32[]{:S(2)}, u32[]{:S(2)}) collective-permute-start(bf16[432,128]{1,0:T(8,128)(2,1)S(1)} %pad_maximum_fusion.8), channel_id=1, source_target_pairs={{0,8},{4,12},{8,0},{12,4},{1,9},{5,13},{9,1},{13,5},{2,10},{6,14},... | collective-permute-start | bytes 331784 | tf_op jit(solution)/shard_map/ppermute | solution.py:304
  62.5 7.4 %shard_map.115 = (bf16[4,32,128]{2,1,0:T(8,128)(2,1)}, bf16[4,32,128]{2,1,0:T(8,128)(2,1)}, bf16[48,128]{1,0:T(8,128)(2,1)}) custom-call(bf16[64,64,128]{2,1,0:T(8,128)(2,1)} %get-tuple-element.42.g_ref, bf16[512,64]{1,0:T(8,128)(2,1)} %get-tuple-element.49.bt_ref, bf16[4096,32]{1,0:T(8,128)(2,1)} %get-tuple-element.50.wd_ref, bf16[48,128]{1,0:T(8,128)(2,1)} %copy-done.3), custom_call_target="tpu_custom_call" | custom-call | flops 6000000000 | bytes 8000000 | tf_op jit(solution)/shard_map/pallas_call | solution.py:481
  69.9 0.7 add_convert_fusion.2.refs_3_
  70.7 0.8 pad_maximum_fusion.5
  71.4 1.5 %collective-permute-start.11 = (bf16[496,128]{1,0:T(8,128)(2,1)S(1)}, bf16[496,128]{1,0:T(8,128)(2,1)S(1)}, u32[]{:S(2)}, u32[]{:S(2)}) collective-permute-start(bf16[496,128]{1,0:T(8,128)(2,1)S(1)} %pad_maximum_fusion.5), channel_id=1, source_target_pairs={{0,2},{1,3},{2,0},{3,1},{4,6},{5,7},{6,4},{7,5},{8,10},{9,11},{10,... | collective-permute-start | bytes 380936 | tf_op jit(solution)/shard_map/ppermute | solution.py:304
  72.9 3.5 %collective-permute-done.11 = bf16[496,128]{1,0:T(8,128)(2,1)S(1)} collective-permute-done((bf16[496,128]{1,0:T(8,128)(2,1)S(1)}, bf16[496,128]{1,0:T(8,128)(2,1)S(1)}, u32[]{:S(2)}, u32[]{:S(2)}) %collective-permute-start.11) | collective-permute-done | bytes 127008 | tf_op jit(solution)/shard_map/ppermute | solution.py:304
  76.4 0.8 fusion.5
  77.3 0.1 collective-permute-start.12
  77.4 0.6 copy.37
  78.0 0.6 copy.38
  78.6 0.6 slice.93.refs_4_
  79.3 0.7 copy.27
  80.0 0.6 copy.36
  80.6 3.7 %shard_map.116 = (f32[256,64]{1,0:T(8,128)}, f32[64,64]{1,0:T(8,128)}, f32[1,128]{1,0:T(1,128)}, f32[32,32,128]{2,1,0:T(8,128)}) custom-call(bf16[32,256]{1,0:T(8,128)(2,1)} %bitcast.139, bf16[32,256]{1,0:T(8,128)(2,1)} %bitcast.140, bf16[16,512]{1,0:T(8,128)(2,1)} %bitcast.138, bf16[48,128]{1,0:T(8,128)(2,1)} %copy-done.1, bf16[48,128]{1,0:T(8,128)(2,1)} %slice.93.refs_4_, ...), custom_call_target="tpu_custom_call" | custom-call | tf_op jit(solution)/shard_map/pallas_call | solution.py:527
  (51 shorter events, 0.7 us)
Async XLA Ops:
  4.2 11.4 %collective-permute-start.3 = (bf16[144,128]{1,0:T(8,128)(2,1)S(1)}, bf16[144,128]{1,0:T(8,128)(2,1)S(1)}, u32[]{:S(2)}, u32[]{:S(2)}) collective-permute-start(bf16[144,128]{1,0:T(8,128)(2,1)S(1)} %get-tuple-element.70), channel_id=1, source_target_pairs={{0,12},{1,8},{2,4},{3,0},{4,13},{5,9},{6,5},{7,1},{8,14},{9,10},{1... | collective-permute-start | bytes 110600 | tf_op jit(solution)/shard_map/ppermute | solution.py:384
  9.2 7.5 %collective-permute-start.2 = (bf16[144,128]{1,0:T(8,128)(2,1)S(1)}, bf16[144,128]{1,0:T(8,128)(2,1)S(1)}, u32[]{:S(2)}, u32[]{:S(2)}) collective-permute-start(bf16[144,128]{1,0:T(8,128)(2,1)S(1)} %get-tuple-element.70), channel_id=1, source_target_pairs={{0,8},{1,12},{2,0},{3,4},{4,9},{5,13},{6,1},{7,5},{8,10},{9,14},{1... | collective-permute-start | bytes 110600 | tf_op jit(solution)/shard_map/ppermute | solution.py:384
  10.7 6.2 %collective-permute-start.1 = (bf16[144,128]{1,0:T(8,128)(2,1)S(1)}, bf16[144,128]{1,0:T(8,128)(2,1)S(1)}, u32[]{:S(2)}, u32[]{:S(2)}) collective-permute-start(bf16[144,128]{1,0:T(8,128)(2,1)S(1)} %get-tuple-element.70), channel_id=1, source_target_pairs={{0,4},{1,0},{2,12},{3,8},{4,5},{5,1},{6,13},{7,9},{8,6},{9,2},{10,... | collective-permute-start | bytes 110600 | tf_op jit(solution)/shard_map/ppermute | solution.py:384
  10.7 6.2 %collective-permute-start = (bf16[144,128]{1,0:T(8,128)(2,1)S(1)}, bf16[144,128]{1,0:T(8,128)(2,1)S(1)}, u32[]{:S(2)}, u32[]{:S(2)}) collective-permute-start(bf16[144,128]{1,0:T(8,128)(2,1)S(1)} %get-tuple-element.70), channel_id=1, source_target_pairs={{0,0},{1,4},{2,8},{3,12},{4,1},{5,5},{6,9},{7,13},{8,2},{9,6},{10,... | collective-permute-start | bytes 110600 | tf_op jit(solution)/shard_map/ppermute | solution.py:384
  11.4 6.3 %collective-permute-start.6 = (bf16[144,128]{1,0:T(8,128)(2,1)S(1)}, bf16[144,128]{1,0:T(8,128)(2,1)S(1)}, u32[]{:S(2)}, u32[]{:S(2)}) collective-permute-start(bf16[144,128]{1,0:T(8,128)(2,1)S(1)} %get-tuple-element.69), channel_id=1, source_target_pairs={{0,3},{1,2},{2,1},{3,0},{4,7},{5,6},{6,5},{7,4},{8,11},{9,10},{10,... | collective-permute-start | bytes 110600 | tf_op jit(solution)/shard_map/ppermute | solution.py:375
  15.6 4.1 %collective-permute-start.5 = (bf16[144,128]{1,0:T(8,128)(2,1)S(1)}, bf16[144,128]{1,0:T(8,128)(2,1)S(1)}, u32[]{:S(2)}, u32[]{:S(2)}) collective-permute-start(bf16[144,128]{1,0:T(8,128)(2,1)S(1)} %get-tuple-element.69), channel_id=1, source_target_pairs={{0,2},{1,3},{2,0},{3,1},{4,6},{5,7},{6,4},{7,5},{8,10},{9,11},{10,... | collective-permute-start | bytes 110600 | tf_op jit(solution)/shard_map/ppermute | solution.py:375
  16.7 2.9 %collective-permute-start.4 = (bf16[144,128]{1,0:T(8,128)(2,1)S(1)}, bf16[144,128]{1,0:T(8,128)(2,1)S(1)}, u32[]{:S(2)}, u32[]{:S(2)}) collective-permute-start(bf16[144,128]{1,0:T(8,128)(2,1)S(1)} %get-tuple-element.69), channel_id=1, source_target_pairs={{0,1},{1,0},{2,3},{3,2},{4,5},{5,4},{6,7},{7,6},{8,9},{9,8},{10,11... | collective-permute-start | bytes 110600 | tf_op jit(solution)/shard_map/ppermute | solution.py:375
  39.7 9.3 %collective-permute-start.7 = (bf16[512,128]{1,0:T(8,128)(2,1)S(1)}, bf16[512,128]{1,0:T(8,128)(2,1)S(1)}, u32[]{:S(2)}, u32[]{:S(2)}) collective-permute-start(bf16[512,128]{1,0:T(8,128)(2,1)S(1)} %bitcast.129), channel_id=1, source_target_pairs={{0,2},{1,3},{2,0},{3,1},{4,6},{5,7},{6,4},{7,5},{8,10},{9,11},{10,... | collective-permute-start | bytes 393224 | tf_op jit(solution)/shard_map/ppermute | solution.py:304
  41.0 7.9 %copy-start = (bf16[1024,128]{1,0:T(8,128)(2,1)S(1)}, bf16[1024,128]{1,0:T(8,128)(2,1)}, u32[]{:S(2)}) copy-start(bf16[1024,128]{1,0:T(8,128)(2,1)} %get-tuple-element.46) | copy-start | bytes 786436
  49.8 1.3 %collective-permute-start.8 = (bf16[432,128]{1,0:T(8,128)(2,1)S(1)}, bf16[432,128]{1,0:T(8,128)(2,1)S(1)}, u32[]{:S(2)}, u32[]{:S(2)}) collective-permute-start(bf16[432,128]{1,0:T(8,128)(2,1)S(1)} %pad_maximum_fusion.6), channel_id=1, source_target_pairs={{0,1},{1,0},{2,3},{3,2},{4,5},{5,4},{6,7},{7,6},{8,9},{9,8},{10,11... | collective-permute-start | bytes 331784 | tf_op jit(solution)/shard_map/ppermute | solution.py:304
  51.8 2.2 %copy-start.2 = (bf16[48,128]{1,0:T(8,128)(2,1)}, bf16[48,128]{1,0:T(8,128)(2,1)S(1)}, u32[]{:S(2)}) copy-start(bf16[48,128]{1,0:T(8,128)(2,1)S(1)} %add_convert_fusion.4.small_ref) | copy-start | bytes 36868
  52.7 8.0 %collective-permute-start.9 = (bf16[432,128]{1,0:T(8,128)(2,1)S(1)}, bf16[432,128]{1,0:T(8,128)(2,1)S(1)}, u32[]{:S(2)}, u32[]{:S(2)}) collective-permute-start(bf16[432,128]{1,0:T(8,128)(2,1)S(1)} %pad_maximum_fusion.7), channel_id=1, source_target_pairs={{0,4},{4,0},{8,12},{12,8},{1,5},{5,1},{9,13},{13,9},{2,6},{6,2},{1... | collective-permute-start | bytes 331784 | tf_op jit(solution)/shard_map/ppermute | solution.py:304
  61.4 1.1 %copy-start.3 = (bf16[48,128]{1,0:T(8,128)(2,1)}, bf16[48,128]{1,0:T(8,128)(2,1)S(1)}, u32[]{:S(2)}) copy-start(bf16[48,128]{1,0:T(8,128)(2,1)S(1)} %add_convert_fusion.3.small_ref) | copy-start | bytes 36868
  61.4 8.4 %collective-permute-start.10 = (bf16[432,128]{1,0:T(8,128)(2,1)S(1)}, bf16[432,128]{1,0:T(8,128)(2,1)S(1)}, u32[]{:S(2)}, u32[]{:S(2)}) collective-permute-start(bf16[432,128]{1,0:T(8,128)(2,1)S(1)} %pad_maximum_fusion.8), channel_id=1, source_target_pairs={{0,8},{4,12},{8,0},{12,4},{1,9},{5,13},{9,1},{13,5},{2,10},{6,14},... | collective-permute-start | bytes 331784 | tf_op jit(solution)/shard_map/ppermute | solution.py:304
  70.6 10.1 %copy-start.1 = (bf16[48,128]{1,0:T(8,128)(2,1)}, bf16[48,128]{1,0:T(8,128)(2,1)S(1)}, u32[]{:S(2)}) copy-start(bf16[48,128]{1,0:T(8,128)(2,1)S(1)} %add_convert_fusion.2.refs_3_) | copy-start | bytes 36868
  71.4 5.0 %collective-permute-start.11 = (bf16[496,128]{1,0:T(8,128)(2,1)S(1)}, bf16[496,128]{1,0:T(8,128)(2,1)S(1)}, u32[]{:S(2)}, u32[]{:S(2)}) collective-permute-start(bf16[496,128]{1,0:T(8,128)(2,1)S(1)} %pad_maximum_fusion.5), channel_id=1, source_target_pairs={{0,2},{1,3},{2,0},{3,1},{4,6},{5,7},{6,4},{7,5},{8,10},{9,11},{10,... | collective-permute-start | bytes 380936 | tf_op jit(solution)/shard_map/ppermute | solution.py:304
  77.3 1.9 %collective-permute-start.12 = (bf16[576,128]{1,0:T(8,128)(2,1)S(1)}, bf16[576,128]{1,0:T(8,128)(2,1)S(1)}, u32[]{:S(2)}, u32[]{:S(2)}) collective-permute-start(bf16[576,128]{1,0:T(8,128)(2,1)S(1)} %pad_maximum_fusion.3), channel_id=1, source_target_pairs={{0,1},{1,0},{2,3},{3,2},{4,5},{5,4},{6,7},{7,6},{8,9},{9,8},{10,11... | collective-permute-start | bytes 442376 | tf_op jit(solution)/shard_map/ppermute | solution.py:304

commit v10 on v9

--- a/solution.py
+++ b/solution.py
@@ -10,7 +10,7 @@
 F32 = jnp.float32
 BF16 = jnp.bfloat16
 LANES = 128
-VMEM_LIMIT = 57 * 1024 * 1024
+VMEM_LIMIT = 24 * 1024 * 1024
 NT = (((1,), (1,)), ((), ()))
 
 
@@ -57,26 +57,23 @@
     return center * scale, scale
 
 
-def prep_kernel(depth, own, x_ref, cell_ref, line_ref, by_token_ref, by_row_ref, mask_out_ref, mask_ref):
+def prep_kernel(depth, own, features, x_ref, by_token_ref, by_row_ref):
     rows = depth * own
-    same = iota((depth, depth), 0) == iota((depth, depth), 1)
-    line = jnp.sum(jnp.where(same, line_ref[...].astype(F32), 0.0), axis=1, keepdims=True)
-    mask_ref[...] = (cell_ref[...].astype(F32) * line).astype(BF16)
-    normed, _ = stats(x_ref[...].astype(F32))
-    pick = one_hot(iota((rows, depth), 0) // own == iota((rows, depth), 1))
-    here = iota((rows, own), 0) % own == iota((rows, own), 1)
-    mask = mask_ref[...]
-    weight = jnp.sum(jnp.where(here, dot(pick, mask), 0.0), axis=1, keepdims=True)
+    half = rows // 2
+    x = x_ref[...].astype(F32)
+    weight = x[:, features : features + 1]
+    normed, _ = stats(x[:, :features])
     masked = normed.astype(BF16).astype(F32) * weight
-    half = rows // 2
-    by_row_ref[...] = jnp.concatenate([masked[:half], masked[half:]], axis=1).astype(BF16)
+    by_row_ref[:half, :] = jnp.concatenate([masked[:half], masked[half:]], axis=1).astype(BF16)
     p, q = iota((rows, rows), 0), iota((rows, rows), 1)
     swap = one_hot(q == (p % depth) * own + p // depth)
     turned = dot(swap, masked.astype(BF16))
-    by_token_ref[...] = jnp.concatenate([turned[:half], turned[half:]], axis=1).astype(BF16)
-    pad = jnp.zeros((LANES - depth, own), BF16)
-    same = one_hot(iota((own, own), 0) == iota((own, own), 1))
-    mask_out_ref[...] = dot_nt(same, jnp.concatenate([mask, pad], axis=0)).astype(BF16)
+    by_token_ref[:half, :] = jnp.concatenate([turned[:half], turned[half:]], axis=1).astype(BF16)
+    here = one_hot(iota((own, rows), 0) == iota((own, rows), 1) % own)
+    at = iota((rows, LANES), 1) == iota((rows, LANES), 0) // own
+    mask = dot(here, jnp.where(at, weight, 0.0).astype(BF16)).astype(BF16)
+    by_row_ref[half:, :] = mask
+    by_token_ref[half:, :] = mask
 
 
 def two(ref, at):
@@ -93,33 +90,31 @@
             v_ref[:, (at + k) * depth : (at + k + 1) * depth, :] = part
 
 
-def row_kernel(depth, features, mi_ref, w_ref, wide_ref, t_ref, at_ref, wt_ref, wc_ref, a_ref, rows_ref):
-    g = pl.program_id(0)
+def fill_t(a_chunk, wc_ref, t_ref, depth):
     chunk, wide, pair = t_ref.shape
-    width = w_ref.shape[1] // 2
-
-    @pl.when(g == 0)
-    def _():
-        rows_ref[...] = wide_ref[...].astype(F32)
-        for e in range(width):
-            part = rows_ref[pl.ds(e, width, stride=width), :]
-            wc_ref[:, e * pair : (e + 1) * pair] = part.astype(BF16)
-        w = w_ref[...]
-        same = one_hot(iota((2 * width, 2 * width), 0) == iota((2 * width, 2 * width), 1))
-        wt = dot_nt(same, w).astype(BF16)
-        wt_ref[...] = wt
-        mi = mi_ref[...]
-        a_ref[...] = dot(mi, w[:, :width]).astype(BF16)
-        same = one_hot(iota((features, features), 0) == iota((features, features), 1))
-        at_ref[...] = dot_nt(jnp.concatenate([wt[:width, :], same], axis=0), mi).astype(BF16)
-
-    span = chunk * depth
-    a_chunk = a_ref[pl.ds(pl.multiple_of(g * span, span), span), :]
+    width = wide // depth
     for e in range(0, width, 2):
         t = dot(a_chunk, wc_ref[:, e * pair : (e + 2) * pair]).astype(BF16)
         for k in range(2):
             part = t[:, k * pair : (k + 1) * pair].reshape(chunk, depth, pair)
             t_ref[:, (e + k) * depth : (e + k + 1) * depth, :] = part
+
+
+def row_kernel(mi_ref, w_ref, wide_ref, a_ref, at_ref, wt_ref, wc_ref, rows_ref):
+    features, width = w_ref.shape[0], w_ref.shape[1] // 2
+    pair = wide_ref.shape[1]
+    rows_ref[...] = wide_ref[...].astype(F32)
+    for e in range(width):
+        part = rows_ref[pl.ds(e, width, stride=width), :]
+        wc_ref[:, e * pair : (e + 1) * pair] = part.astype(BF16)
+    w = w_ref[...]
+    same = one_hot(iota((2 * width, 2 * width), 0) == iota((2 * width, 2 * width), 1))
+    wt = dot_nt(same, w).astype(BF16)
+    wt_ref[...] = wt
+    mi = mi_ref[...]
+    a_ref[...] = dot(mi, w[:, :width]).astype(BF16)
+    same = one_hot(iota((features, features), 0) == iota((features, features), 1))
+    at_ref[...] = dot_nt(jnp.concatenate([wt[:width, :], same], axis=0), mi).astype(BF16)
 
 
 def weight_kernel(depth, features, *refs):
@@ -205,7 +200,9 @@
         go_ref[...] = da_ref[pl.ds((1 - here) * half, half)]
 
 
-def token_kernel(depth, features, n, g_ref, t_ref, mj_ref, perm_ref, bias_ref, left_ref, small_ref, out_ref, db_ref):
+def token_kernel(depth, features, n, *refs):
+    g_ref, a_ref, wc_ref, mj_ref, perm_ref, bias_ref, left_ref = refs[:7]
+    small_ref, out_ref, t_ref, db_ref = refs[7:]
     g, last = pl.program_id(0), pl.num_programs(0) - 1
     chunk, block = g_ref.shape[:2]
     width = left_ref.shape[0]
@@ -214,6 +211,8 @@
     def _():
         db_ref[...] = jnp.zeros_like(db_ref)
 
+    span = chunk * depth
+    fill_t(a_ref[pl.ds(pl.multiple_of(g * span, span), span), :], wc_ref, t_ref, depth)
     t = jnp.concatenate([t_ref[i] for i in range(chunk)], axis=1)
     scaled = jnp.concatenate([g_ref[i] for i in range(chunk)], axis=1)
     db_ref[...] += dot_nt(t, scaled)
@@ -235,7 +234,8 @@
         small_ref[width:, :] = jnp.broadcast_to(bias_ref[0:1, :], (16, LANES)).astype(BF16)
 
 
-def update_kernel(inv_ref, b_ref, t_ref, offset_ref, wc_ref, small_ref, out_ref, wd_ref, pass_ref):
+def update_kernel(depth, *refs):
+    inv_ref, a_ref, b_ref, offset_ref, wc_ref, small_ref, out_ref, wd_ref, pass_ref, t_ref = refs
     g = pl.program_id(0)
     chunk, block, pair = out_ref.shape
 
@@ -246,6 +246,8 @@
         for at in range(0, wd_ref.shape[0], 2 * pair):
             wd_ref[at : at + 2 * pair, :] = dot_nt(same, wc_ref[:, at : at + 2 * pair]).astype(BF16)
 
+    span = chunk * depth
+    fill_t(a_ref[pl.ds(pl.multiple_of(g * span, span), span), :], wc_ref, t_ref, depth)
     inv = inv_ref[g]
     b = b_ref[...]
     offset = offset_ref[...]
@@ -258,8 +260,8 @@
 
 def owner_kernel(depth, own, features, *refs):
     da_refs, db_ref, small_refs = refs[:2], refs[2], refs[3:5]
-    x_ref, mask_ref, wt_ref, perm_ref, dw_ref = refs[5:10]
-    out_ref, factors_ref, bias_ref, placed_ref = refs[10:]
+    x_ref, wt_ref, perm_ref, dw_ref = refs[5:9]
+    out_ref, factors_ref, bias_ref, placed_ref = refs[9:]
     for e in range(dw_ref.shape[0]):
         placed_ref[:, e, :] = dw_ref[e].astype(F32)
     rows = depth * own
@@ -273,11 +275,9 @@
     wt = wt_ref[...].astype(F32)
     d_normed = jnp.dot(d_a, wt[:width, :], precision=highest, preferred_element_type=F32)
     d_normed = d_normed + jnp.dot(d_b, wt[width:, :], precision=highest, preferred_element_type=F32)
-    pick = one_hot(iota((rows, depth), 0) // own == iota((rows, depth), 1))
-    here = iota((rows, own), 0) % own == iota((rows, own), 1)
-    weight = jnp.sum(jnp.where(here, dot(pick, mask_ref[...]), 0.0), axis=1, keepdims=True)
-    d_normed = d_normed * weight
-    normed, scale = stats(x_ref[...].astype(F32))
+    x = x_ref[...].astype(F32)
+    d_normed = d_normed * x[:, features : features + 1]
+    normed, scale = stats(x[:, :features])
     mean = jnp.mean(d_normed, axis=-1, keepdims=True)
     along = jnp.mean(d_normed * normed, axis=-1, keepdims=True)
     out_ref[...] = scale * (d_normed - mean - normed * along)
@@ -358,18 +358,19 @@
     sds = jax.ShapeDtypeStruct
 
     bits = n.bit_length() - 1
-    x = alignment_embedding.reshape(rows, features)
+    mask = (alignment_cell_exists * alignment_lines_exist[:, None]).astype(BF16)
+    mask = jnp.broadcast_to(mask[:, :, None], (depth, own, LANES - features))
+    x = jnp.concatenate([alignment_embedding, mask], axis=2).reshape(rows, LANES)
     offset = offset_vector.reshape(1, pair)
-    args = (x, alignment_cell_exists, alignment_lines_exist.reshape(1, depth))
-    out_shapes = [sds((rows // 2, LANES), BF16)] * 2 + [sds((own, LANES), BF16), sds((depth, own), BF16)]
-    by_token, by_row, mask_t, mask = call(
-        functools.partial(prep_kernel, depth, own),
-        (1,),
-        [full(v.shape) for v in args],
+    out_shapes = [sds((rows // 2 + own, LANES), BF16)] * 2
+    by_token, by_row = call(
+        functools.partial(prep_kernel, depth, own, features),
+        (),
+        [full(x.shape)],
         [full(o.shape) for o in out_shapes],
         out_shapes,
-    )(*args)
-    message = jnp.concatenate([by_token, mask_t], axis=0)
+    )(x)
+    message = by_token
     held = [message]
     for k in range(1, n):
         held.append(lax.ppermute(message, "col", [(j, j ^ k) for j in range(n)]))
@@ -377,7 +378,7 @@
     seen_i = held[:, rows // 2 :].reshape(block, LANES)
     parts = held[:, : rows // 2].reshape(n, rows // 2, 2, features)
     mi = parts.transpose(0, 2, 1, 3).reshape(block * depth, features)
-    message = jnp.concatenate([by_row, mask_t], axis=0)
+    message = by_row
     held = []
     for k in range(n):
         pairs = [(i * n + j, (j ^ k) * n + i) for i in range(n) for j in range(n)]
@@ -392,21 +393,20 @@
     source = jnp.arange(wide)
     perm = (jnp.arange(wide)[None, :] == (source % width * depth + source // width)[:, None]).astype(BF16)
     up_spec = pl.BlockSpec((chunk, block, pair), lambda g: (g, 0, 0))
-    t_spec = pl.BlockSpec((chunk, wide, pair), lambda g: (g, 0, 0))
+    args = (mi, sitewise_factors, pairing_matrix)
     out_shapes = [
+        sds((tokens, width), BF16),
         sds((width + features, tokens), BF16),
         sds((2 * width, features), BF16),
         sds((width, width * pair), BF16),
     ]
-    args = (mi, sitewise_factors, pairing_matrix)
-    t, a_t, factors_t, pairing_wide = call(
-        functools.partial(row_kernel, depth, features),
-        (steps,),
+    a, a_t, factors_t, pairing_wide = call(
+        row_kernel,
+        (),
         [full(v.shape) for v in args],
-        [t_spec] + [full(o.shape) for o in out_shapes],
-        [sds((block, wide, pair), BF16)] + out_shapes,
-        [pltpu.VMEM((tokens, width), BF16), pltpu.VMEM((width * width, pair), F32)],
-        cost(4e9, 8e6),
+        [full(o.shape) for o in out_shapes],
+        out_shapes,
+        [pltpu.VMEM((width * width, pair), F32)],
     )(*args)
 
     out_shapes = [
@@ -443,12 +443,12 @@
     small, d_b = call(
         functools.partial(token_kernel, depth, features, n),
         (steps,),
-        [up_spec, t_spec] + [full(v.shape) for v in (mj, perm, bias, left)],
+        [up_spec] + [full(v.shape) for v in (a, pairing_wide, mj, perm, bias, left)],
         [full(o.shape) for o in out_shapes],
         out_shapes,
-        [pltpu.VMEM((wide, block), F32)],
-        cost(6e9, 16e6),
-    )(scaled, t, mj, perm, bias, left)
+        [pltpu.VMEM((chunk, wide, pair), BF16), pltpu.VMEM((wide, block), F32)],
+        cost(8e9, 8e6),
+    )(scaled, a, pairing_wide, mj, perm, bias, left)
 
     dp_keep, dp_go = halves(d_pairing, "col", 0, 0)
     db_keep, db_go = halves(d_b.reshape((n // 2, 2) + d_b.shape[1:]), "col", 0, 1)
@@ -459,20 +459,18 @@
     for bit in range(bits):
         parts = swap_parts([d_pairing, db_go, small], "row", bit, n)
         if bit == 0:
-            args = (inv, b, t, offset, pairing_wide, small)
-            specs = [full(v.shape) for v in args]
-            specs[2] = t_spec
+            args = (inv, a, b, offset, pairing_wide, small)
             coupling_update, pairing_t, small = call(
-                update_kernel,
+                functools.partial(update_kernel, depth),
                 (steps,),
-                specs,
+                [full(v.shape) for v in args],
                 [up_spec, full((width * pair, width)), full(small.shape)],
                 [
                     sds((block, block, pair), BF16),
                     sds((width * pair, width), BF16),
                     sds(small.shape, BF16),
                 ],
-                (),
+                [pltpu.VMEM((chunk, wide, pair), BF16)],
                 cost(6e9, 8e6),
             )(*args)
         if bit == 1:
@@ -517,7 +515,7 @@
     d_b = lay_back(d_b[0], own, wide)
 
     d_pairing = d_pairing.reshape(width, width, pair)
-    args = (*d_a, d_b, *small_parts, x, mask, factors_t, perm, d_pairing)
+    args = (*d_a, d_b, *small_parts, x, factors_t, perm, d_pairing)
     out_shapes = [
         sds((rows, features), F32),
         sds((features, 2 * width), F32),

time: 85.3 us -> 61.5 us (0.72)
  Pallas kernels: 43.2 us -> 27.5 us
  local copies, waits for them, and re-layouts: 9.6 us -> 3.11 us
  other arithmetic: 6.64 us -> 1.63 us
  waiting for transfers between devices: 6.87 us -> 10.7 us
    pallas_call x3, Pallas kernels: 15.2 us -> 6.76 us  [the longest x1 5.55 us: per_device(): call(functools.partial(update_kernel, depth), (steps,), [full(v.shape) fo...]
    ppermute x6, waiting for transfers between devices: 4.84 us -> 8.09 us  [swap_parts(): message = lax.ppermute(message, axis, pairs)]
    convert_element_type x10, other arithmetic: 3.07 us -> 0.19 us  [add(): (mine.astype(F32) + other.astype(F32)).astype(BF16)]
    pallas_call x1, Pallas kernels: 9.76 us -> 7.27 us  [per_device(): call(functools.partial(weight_kernel, depth, features), (steps,), [up_spe...]
    pallas_call x1, Pallas kernels: 7.38 us -> 5.44 us  [per_device(): call(functools.partial(left_kernel, depth, bits - 1), (steps,), [up_spec]...]
    dynamic_slice x2, local copies, waits for them, and re-layouts: 1.68 us -> 0.02 us  [halves(): return (keep, lax.dynamic_index_in_dim(x, 1 - here, at, keepdims=False))]
    pallas_call x1, Pallas kernels: 7.18 us -> 5.56 us  [per_device(): call(functools.partial(token_kernel, depth, features, n), (steps,), [up_s...]
    concatenate x5, other arithmetic: 1.52 us -> 0.06 us  [swap_parts(): message = jnp.concatenate(parts, axis=0) if len(parts) > 1 else parts[0]]
  transfers between devices with their start and end apart: 13 -> 13, of which waited for: 3 -> 5; matrix products, arithmetic and copies ran while one was open for 5% -> 0% of each run, Pallas kernels for 25% -> 27%
where the time goes in v10:
time: 61.5 us; the launch traced here: 61.3 us
  Pallas kernels  27.5 us (45%)
  starting transfers between devices  17.2 us (28%)
  waiting for transfers between devices  10.7 us (17%)
  local copies, waits for them, and re-layouts  3.11 us (5%)
  other arithmetic  1.63 us (3%)
  between operations  1.18 us (2%)
    ppermute x6, waiting for transfers between devices, swap_parts(): message = lax.ppermute(message, axis, pairs)  8.09 us
    pallas_call x1, Pallas kernels, per_device(): call(functools.partial(weight_kernel, depth, features), (steps,), [up_spe...  7.27 us
    ppermute x4, starting transfers between devices, per_device(): held.append(lax.ppermute(message, axes, pairs))  7.25 us
    pallas_call x1, Pallas kernels, per_device(): call(functools.partial(token_kernel, depth, features, n), (steps,), [up_s...  5.56 us
    pallas_call x1, Pallas kernels, per_device(): call(functools.partial(update_kernel, depth), (steps,), [full(v.shape) fo...  5.55 us
    pallas_call x1, Pallas kernels, per_device(): call(functools.partial(left_kernel, depth, bits - 1), (steps,), [up_spec]...  5.44 us
    ppermute x6, starting transfers between devices, swap_parts(): message = lax.ppermute(message, axis, pairs)  5.36 us
    ppermute x3, starting transfers between devices, per_device(): held.append(lax.ppermute(message, 'col', [(j, j ^ k) for j in range(n)]))  4.64 us
  transfers between devices with their start and end apart: 13, of which 5 were waited for; matrix products, arithmetic and copies ran while one was open for 0% of the time, Pallas kernels for 27%

profile of v10, /device:TPU:0, one launch (start us, length us, event | category | flops | bytes accessed | tf_op | source)
XLA Modules:
  0.0 61.3 jit_solution(10434571643541544488)
XLA Ops:
  0.6 0.8 %multiply_convert_fusion = bf16[16,16]{1,0:T(8,128)(2,1)S(1)} fusion(s32[16,16]{1,0:T(8,128)} %param.8, s32[16]{0:T(128)} %param.9), kind=kLoop, calls=%fused_computation.53 | loop fusion | flops 512 | bytes 1600 | tf_op jit(solution)/shard_map/convert_element_type | solution.py:361
  1.4 0.1 broadcast_in_dim.2
  1.6 0.1 pad_maximum_fusion.9
  1.7 0.5 shard_map.110
  2.2 5.1 %collective-permute-start.3 = (bf16[144,128]{1,0:T(8,128)(2,1)S(1)}, bf16[144,128]{1,0:T(8,128)(2,1)S(1)}, u32[]{:S(2)}, u32[]{:S(2)}) collective-permute-start(bf16[144,128]{1,0:T(8,128)(2,1)S(1)} %get-tuple-element.31), channel_id=1, source_target_pairs={{0,12},{1,8},{2,4},{3,0},{4,13},{5,9},{6,5},{7,1},{8,14},{9,10},{1... | collective-permute-start | bytes 110600 | tf_op jit(solution)/shard_map/ppermute | solution.py:385
  7.3 1.5 %collective-permute-start.2 = (bf16[144,128]{1,0:T(8,128)(2,1)S(1)}, bf16[144,128]{1,0:T(8,128)(2,1)S(1)}, u32[]{:S(2)}, u32[]{:S(2)}) collective-permute-start(bf16[144,128]{1,0:T(8,128)(2,1)S(1)} %get-tuple-element.31), channel_id=1, source_target_pairs={{0,8},{1,12},{2,0},{3,4},{4,9},{5,13},{6,1},{7,5},{8,10},{9,14},{1... | collective-permute-start | bytes 110600 | tf_op jit(solution)/shard_map/ppermute | solution.py:385
  8.8 0.0 collective-permute-start.1
  8.8 0.7 %collective-permute-start = (bf16[144,128]{1,0:T(8,128)(2,1)S(1)}, bf16[144,128]{1,0:T(8,128)(2,1)S(1)}, u32[]{:S(2)}, u32[]{:S(2)}) collective-permute-start(bf16[144,128]{1,0:T(8,128)(2,1)S(1)} %get-tuple-element.31), channel_id=1, source_target_pairs={{0,0},{1,4},{2,8},{3,12},{4,1},{5,5},{6,9},{7,13},{8,2},{9,6},{10,... | collective-permute-start | bytes 110600 | tf_op jit(solution)/shard_map/ppermute | solution.py:385
  9.4 3.3 %collective-permute-start.6 = (bf16[144,128]{1,0:T(8,128)(2,1)S(1)}, bf16[144,128]{1,0:T(8,128)(2,1)S(1)}, u32[]{:S(2)}, u32[]{:S(2)}) collective-permute-start(bf16[144,128]{1,0:T(8,128)(2,1)S(1)} %get-tuple-element.32), channel_id=1, source_target_pairs={{0,3},{1,2},{2,1},{3,0},{4,7},{5,6},{6,5},{7,4},{8,11},{9,10},{10,... | collective-permute-start | bytes 110600 | tf_op jit(solution)/shard_map/ppermute | solution.py:376
  12.7 0.2 fusion.refs_5_.refs_4_.refs_7_
  12.9 0.0 collective-permute-done.3
  12.9 1.2 %collective-permute-start.5 = (bf16[144,128]{1,0:T(8,128)(2,1)S(1)}, bf16[144,128]{1,0:T(8,128)(2,1)S(1)}, u32[]{:S(2)}, u32[]{:S(2)}) collective-permute-start(bf16[144,128]{1,0:T(8,128)(2,1)S(1)} %get-tuple-element.32), channel_id=1, source_target_pairs={{0,2},{1,3},{2,0},{3,1},{4,6},{5,7},{6,4},{7,5},{8,10},{9,11},{10,... | collective-permute-start | bytes 110600 | tf_op jit(solution)/shard_map/ppermute | solution.py:376
  14.1 0.0 collective-permute-done.2
  14.1 0.2 collective-permute-start.4
  14.3 0.0 collective-permute-done.1
  14.4 2.6 %collective-permute-done.5 = bf16[144,128]{1,0:T(8,128)(2,1)S(1)} collective-permute-done((bf16[144,128]{1,0:T(8,128)(2,1)S(1)}, bf16[144,128]{1,0:T(8,128)(2,1)S(1)}, u32[]{:S(2)}, u32[]{:S(2)}) %collective-permute-start.5) | collective-permute-done | bytes 36896 | tf_op jit(solution)/shard_map/ppermute | solution.py:376
  17.2 0.1 copy.19
  17.4 0.0 copy-start.2
  17.4 0.1 copy.20
  17.5 0.2 copy.21
  17.7 0.1 reshape.204
  17.8 0.0 copy-start
  17.8 0.0 copy-start.1
  17.9 0.9 %copy-done = bf16[1024,128]{1,0:T(8,128)(2,1)S(1)} copy-done((bf16[1024,128]{1,0:T(8,128)(2,1)S(1)}, bf16[1024,128]{1,0:T(8,128)(2,1)}, u32[]{:S(2)}) %copy-start) | copy-done | bytes 262168
  18.8 0.7 %shard_map.111 = (bf16[1024,32]{1,0:T(8,128)(2,1)S(1)}, bf16[96,1024]{1,0:T(8,128)(2,1)S(1)}, bf16[64,64]{1,0:T(8,128)(2,1)S(1)}, bf16[32,4096]{1,0:T(8,128)(2,1)S(1)}) custom-call(bf16[1024,64]{1,0:T(8,128)(2,1)S(1)} %bitcast.104, bf16[64,64]{1,0:T(8,128)(2,1)S(1)} %copy-done.1, bf16[1024,128]{1,0:T(8,128)(2,1)S(1)} %copy-done), custom_call_target="tpu_custom_call" | custom-call | tf_op jit(solution)/shard_map/pallas_call | solution.py:403
  19.4 0.0 copy-start.3
  19.5 0.6 %copy-done.3 = f32[128]{0:T(128)S(1)} copy-done((f32[128]{0:T(128)S(1)}, f32[128]{0:T(128)}, u32[]{:S(2)}) %copy-start.3) | copy-done | bytes 536
  20.1 7.3 %shard_map.112 = (bf16[64,64,128]{2,1,0:T(8,128)(2,1)S(1)}, bf16[64,512]{1,0:T(8,128)(2,1)S(1)}, bf16[512,64]{1,0:T(8,128)(2,1)S(1)}, f32[4,64,16]{2,1,0:T(8,128...) custom-call(bf16[64,64,128]{2,1,0:T(8,128)(2,1)S(1)} %copy-done.2, ...), custom_call_target="tpu_custom_call" | custom-call | flops 5000000000 | bytes 8000000 | tf_op jit(solution)/shard_map/pallas_call | solution.py:422
  27.4 0.0 copy-start.6
  27.4 0.6 %copy-done.4 = f32[4,64,16]{2,1,0:T(8,128)} copy-done((f32[4,64,16]{2,1,0:T(8,128)}, f32[4,64,16]{2,1,0:T(8,128)S(1)}, u32[]{:S(2)}) %copy-start.4) | copy-done | bytes 16408
  28.1 0.0 copy-done.6
  28.1 1.7 %collective-permute-start.7 = (bf16[512,128]{1,0:T(8,128)(2,1)S(1)}, bf16[512,128]{1,0:T(8,128)(2,1)S(1)}, u32[]{:S(2)}, u32[]{:S(2)}) collective-permute-start(bf16[512,128]{1,0:T(8,128)(2,1)S(1)} %bitcast.138), channel_id=1, source_target_pairs={{0,2},{1,3},{2,0},{3,1},{4,6},{5,7},{6,4},{7,5},{8,10},{9,11},{10,... | collective-permute-start | bytes 393224 | tf_op jit(solution)/shard_map/ppermute | solution.py:304
  29.8 5.6 %shard_map.113 = (bf16[48,128]{1,0:T(8,128)(2,1)S(1)}, bf16[4,64,128]{2,1,0:T(8,128)(2,1)S(1)}) custom-call(bf16[64,64,128]{2,1,0:T(8,128)(2,1)S(1)} %get-tuple-element.39.refs_0_.g_ref, bf16[1024,32]{1,0:T(8,128)(2,1)S(1)} %get-tuple-element.36.refs_1_, bf16[32,4096]{1,0:T(8,128)(2,1)S(1)} %get-tuple-element.33.refs_6_.refs_2_.refs_4_, ...), custom_call_target="tpu_custom_call" | custom-call | flops 8000000000 | bytes 8000000 | tf_op jit(solution)/shard_map/pallas_call | solution.py:443
  35.4 0.0 collective-permute-done.7
  35.5 0.1 collective-permute-start.8
  35.6 1.3 %collective-permute-done.8 = bf16[432,128]{1,0:T(8,128)(2,1)S(1)} collective-permute-done((bf16[432,128]{1,0:T(8,128)(2,1)S(1)}, bf16[432,128]{1,0:T(8,128)(2,1)S(1)}, u32[]{:S(2)}, u32[]{:S(2)}) %collective-permute-start.8) | collective-permute-done | bytes 110624 | tf_op jit(solution)/shard_map/ppermute | solution.py:304
  37.0 0.0 copy-start.5
  37.0 0.0 copy-start.7
  37.0 1.2 %collective-permute-start.9 = (bf16[432,128]{1,0:T(8,128)(2,1)S(1)}, bf16[432,128]{1,0:T(8,128)(2,1)S(1)}, u32[]{:S(2)}, u32[]{:S(2)}) collective-permute-start(bf16[432,128]{1,0:T(8,128)(2,1)S(1)} %pad_maximum_fusion.7), channel_id=1, source_target_pairs={{0,4},{4,0},{8,12},{12,8},{1,5},{5,1},{9,13},{13,9},{2,6},{6,2},{1... | collective-permute-start | bytes 331784 | tf_op jit(solution)/shard_map/ppermute | solution.py:304
  38.3 5.5 %shard_map.114 = (bf16[64,64,128]{2,1,0:T(8,128)(2,1)}, bf16[4096,32]{1,0:T(8,128)(2,1)S(1)}, bf16[48,128]{1,0:T(8,128)(2,1)S(1)}) custom-call(f32[4,64,16]{2,1,0:T(8,128)S(1)} %copy-done.5, bf16[1024,32]{1,0:T(8,128)(2,1)S(1)} %get-tuple-element.36.refs_1_, bf16[64,512]{1,0:T(8,128)(2,1)S(1)} %copy-done.7, f32[1,128]{1,0:T(1,128)S(1)} %get-tuple-element.38.refs_3_, ...), custom_call_target="tpu_custom_call" | custom-call | flops 6000000000 | bytes 8000000 | tf_op jit(solution)/shard_map/pallas_call | solution.py:463
  43.9 0.7 %collective-permute-start.10 = (bf16[432,128]{1,0:T(8,128)(2,1)S(1)}, bf16[432,128]{1,0:T(8,128)(2,1)S(1)}, u32[]{:S(2)}, u32[]{:S(2)}) collective-permute-start(bf16[432,128]{1,0:T(8,128)(2,1)S(1)} %pad_maximum_fusion.8), channel_id=1, source_target_pairs={{0,8},{4,12},{8,0},{12,4},{1,9},{5,13},{9,1},{13,5},{2,10},{6,14},... | collective-permute-start | bytes 331784 | tf_op jit(solution)/shard_map/ppermute | solution.py:304
  44.7 5.4 %shard_map.115 = (bf16[4,32,128]{2,1,0:T(8,128)(2,1)S(1)}, bf16[4,32,128]{2,1,0:T(8,128)(2,1)S(1)}, bf16[48,128]{1,0:T(8,128)(2,1)S(1)}) custom-call(bf16[64,64,128]{2,1,0:T(8,128)(2,1)S(1)} %get-tuple-element.39.refs_0_.g_ref, bf16[512,64]{1,0:T(8,128)(2,1)S(1)} %get-tuple-element.46.bt_ref, bf16[4096,32]{1,0:T(8,128)(2,1)S(1)} %get-tuple-element.47.wd_ref, ...), custom_call_target="tpu_custom_call" | custom-call | flops 6000000000 | bytes 8000000 | tf_op jit(solution)/shard_map/pallas_call | solution.py:479
  50.1 2.0 %collective-permute-done.10 = bf16[432,128]{1,0:T(8,128)(2,1)S(1)} collective-permute-done((bf16[432,128]{1,0:T(8,128)(2,1)S(1)}, bf16[432,128]{1,0:T(8,128)(2,1)S(1)}, u32[]{:S(2)}, u32[]{:S(2)}) %collective-permute-start.10) | collective-permute-done | bytes 110624 | tf_op jit(solution)/shard_map/ppermute | solution.py:304
  52.2 1.5 %collective-permute-start.11 = (bf16[496,128]{1,0:T(8,128)(2,1)S(1)}, bf16[496,128]{1,0:T(8,128)(2,1)S(1)}, u32[]{:S(2)}, u32[]{:S(2)}) collective-permute-start(bf16[496,128]{1,0:T(8,128)(2,1)S(1)} %pad_maximum_fusion.5), channel_id=1, source_target_pairs={{0,2},{1,3},{2,0},{3,1},{4,6},{5,7},{6,4},{7,5},{8,10},{9,11},{10,... | collective-permute-start | bytes 380936 | tf_op jit(solution)/shard_map/ppermute | solution.py:304
  53.7 3.5 %collective-permute-done.11 = bf16[496,128]{1,0:T(8,128)(2,1)S(1)} collective-permute-done((bf16[496,128]{1,0:T(8,128)(2,1)S(1)}, bf16[496,128]{1,0:T(8,128)(2,1)S(1)}, u32[]{:S(2)}, u32[]{:S(2)}) %collective-permute-start.11) | collective-permute-done | bytes 127008 | tf_op jit(solution)/shard_map/ppermute | solution.py:304
  57.3 0.1 collective-permute-start.12
  57.4 1.3 %collective-permute-done.12 = bf16[576,128]{1,0:T(8,128)(2,1)S(1)} collective-permute-done((bf16[576,128]{1,0:T(8,128)(2,1)S(1)}, bf16[576,128]{1,0:T(8,128)(2,1)S(1)}, u32[]{:S(2)}, u32[]{:S(2)}) %collective-permute-start.12) | collective-permute-done | bytes 147488 | tf_op jit(solution)/shard_map/ppermute | solution.py:304
  58.9 2.4 %shard_map.116 = (f32[256,64]{1,0:T(8,128)}, f32[64,64]{1,0:T(8,128)}, f32[1,128]{1,0:T(1,128)}, f32[32,32,128]{2,1,0:T(8,128)}) custom-call(bf16[32,256]{1,0:T(8,128)(2,1)S(1)} %bitcast.112, bf16[32,256]{1,0:T(8,128)(2,1)S(1)} %bitcast.113, bf16[16,512]{1,0:T(8,128)(2,1)S(1)} %bitcast.111, bf16[48,128]{1,0:T(8,128)(2,1)S(1)} %add_convert_fusion.2.refs_3_, ...), custom_call_target="tpu_custom_call" | custom-call | tf_op jit(solution)/shard_map/pallas_call | solution.py:525
  (62 shorter events, 0.8 us)
Async XLA Ops:
  0.6 0.9 %copy-start.8 = (bf16[16,16,64]{2,1,0:T(8,128)(2,1)S(1)}, bf16[16,16,64]{2,1,0:T(8,128)(2,1)}, u32[]{:S(2)}) copy-start(bf16[16,16,64]{2,1,0:T(8,128)(2,1)} %param.7) | copy-start | bytes 98308
  2.2 10.7 %collective-permute-start.3 = (bf16[144,128]{1,0:T(8,128)(2,1)S(1)}, bf16[144,128]{1,0:T(8,128)(2,1)S(1)}, u32[]{:S(2)}, u32[]{:S(2)}) collective-permute-start(bf16[144,128]{1,0:T(8,128)(2,1)S(1)} %get-tuple-element.31), channel_id=1, source_target_pairs={{0,12},{1,8},{2,4},{3,0},{4,13},{5,9},{6,5},{7,1},{8,14},{9,10},{1... | collective-permute-start | bytes 110600 | tf_op jit(solution)/shard_map/ppermute | solution.py:385
  7.3 6.8 %collective-permute-start.2 = (bf16[144,128]{1,0:T(8,128)(2,1)S(1)}, bf16[144,128]{1,0:T(8,128)(2,1)S(1)}, u32[]{:S(2)}, u32[]{:S(2)}) collective-permute-start(bf16[144,128]{1,0:T(8,128)(2,1)S(1)} %get-tuple-element.31), channel_id=1, source_target_pairs={{0,8},{1,12},{2,0},{3,4},{4,9},{5,13},{6,1},{7,5},{8,10},{9,14},{1... | collective-permute-start | bytes 110600 | tf_op jit(solution)/shard_map/ppermute | solution.py:385
  8.8 5.5 %collective-permute-start.1 = (bf16[144,128]{1,0:T(8,128)(2,1)S(1)}, bf16[144,128]{1,0:T(8,128)(2,1)S(1)}, u32[]{:S(2)}, u32[]{:S(2)}) collective-permute-start(bf16[144,128]{1,0:T(8,128)(2,1)S(1)} %get-tuple-element.31), channel_id=1, source_target_pairs={{0,4},{1,0},{2,12},{3,8},{4,5},{5,1},{6,13},{7,9},{8,6},{9,2},{10,... | collective-permute-start | bytes 110600 | tf_op jit(solution)/shard_map/ppermute | solution.py:385
  8.8 5.5 %collective-permute-start = (bf16[144,128]{1,0:T(8,128)(2,1)S(1)}, bf16[144,128]{1,0:T(8,128)(2,1)S(1)}, u32[]{:S(2)}, u32[]{:S(2)}) collective-permute-start(bf16[144,128]{1,0:T(8,128)(2,1)S(1)} %get-tuple-element.31), channel_id=1, source_target_pairs={{0,0},{1,4},{2,8},{3,12},{4,1},{5,5},{6,9},{7,13},{8,2},{9,6},{10,... | collective-permute-start | bytes 110600 | tf_op jit(solution)/shard_map/ppermute | solution.py:385
  9.4 5.0 %collective-permute-start.6 = (bf16[144,128]{1,0:T(8,128)(2,1)S(1)}, bf16[144,128]{1,0:T(8,128)(2,1)S(1)}, u32[]{:S(2)}, u32[]{:S(2)}) collective-permute-start(bf16[144,128]{1,0:T(8,128)(2,1)S(1)} %get-tuple-element.32), channel_id=1, source_target_pairs={{0,3},{1,2},{2,1},{3,0},{4,7},{5,6},{6,5},{7,4},{8,11},{9,10},{10,... | collective-permute-start | bytes 110600 | tf_op jit(solution)/shard_map/ppermute | solution.py:376
  12.9 4.2 %collective-permute-start.5 = (bf16[144,128]{1,0:T(8,128)(2,1)S(1)}, bf16[144,128]{1,0:T(8,128)(2,1)S(1)}, u32[]{:S(2)}, u32[]{:S(2)}) collective-permute-start(bf16[144,128]{1,0:T(8,128)(2,1)S(1)} %get-tuple-element.32), channel_id=1, source_target_pairs={{0,2},{1,3},{2,0},{3,1},{4,6},{5,7},{6,4},{7,5},{8,10},{9,11},{10,... | collective-permute-start | bytes 110600 | tf_op jit(solution)/shard_map/ppermute | solution.py:376
  14.1 2.9 %collective-permute-start.4 = (bf16[144,128]{1,0:T(8,128)(2,1)S(1)}, bf16[144,128]{1,0:T(8,128)(2,1)S(1)}, u32[]{:S(2)}, u32[]{:S(2)}) collective-permute-start(bf16[144,128]{1,0:T(8,128)(2,1)S(1)} %get-tuple-element.32), channel_id=1, source_target_pairs={{0,1},{1,0},{2,3},{3,2},{4,5},{5,4},{6,7},{7,6},{8,9},{9,8},{10,11... | collective-permute-start | bytes 110600 | tf_op jit(solution)/shard_map/ppermute | solution.py:376
  17.4 2.1 %copy-start.2 = (bf16[64,64,128]{2,1,0:T(8,128)(2,1)S(1)}, bf16[64,64,128]{2,1,0:T(8,128)(2,1)}, u32[]{:S(2)}) copy-start(bf16[64,64,128]{2,1,0:T(8,128)(2,1)} %refs_0_.1) | copy-start | bytes 3145732
  17.8 1.0 %copy-start = (bf16[1024,128]{1,0:T(8,128)(2,1)S(1)}, bf16[1024,128]{1,0:T(8,128)(2,1)}, u32[]{:S(2)}) copy-start(bf16[1024,128]{1,0:T(8,128)(2,1)} %wide_ref.1) | copy-start | bytes 786436
  17.8 0.9 %copy-start.1 = (bf16[64,64]{1,0:T(8,128)(2,1)S(1)}, bf16[64,64]{1,0:T(8,128)(2,1)}, u32[]{:S(2)}) copy-start(bf16[64,64]{1,0:T(8,128)(2,1)} %refs_4_.1) | copy-start | bytes 24580
  19.4 0.7 %copy-start.3 = (f32[128]{0:T(128)S(1)}, f32[128]{0:T(128)}, u32[]{:S(2)}) copy-start(f32[128]{0:T(128)} %param.12) | copy-start | bytes 1540
  27.4 0.7 %copy-start.4 = (f32[4,64,16]{2,1,0:T(8,128)}, f32[4,64,16]{2,1,0:T(8,128)S(1)}, u32[]{:S(2)}) copy-start(f32[4,64,16]{2,1,0:T(8,128)S(1)} %get-tuple-element.35.refs_0_) | copy-start | bytes 49156
  27.4 0.7 %copy-start.6 = (bf16[64,512]{1,0:T(8,128)(2,1)}, bf16[64,512]{1,0:T(8,128)(2,1)S(1)}, u32[]{:S(2)}) copy-start(bf16[64,512]{1,0:T(8,128)(2,1)S(1)} %get-tuple-element.37.refs_2_) | copy-start | bytes 196612
  28.1 7.3 %collective-permute-start.7 = (bf16[512,128]{1,0:T(8,128)(2,1)S(1)}, bf16[512,128]{1,0:T(8,128)(2,1)S(1)}, u32[]{:S(2)}, u32[]{:S(2)}) collective-permute-start(bf16[512,128]{1,0:T(8,128)(2,1)S(1)} %bitcast.138), channel_id=1, source_target_pairs={{0,2},{1,3},{2,0},{3,1},{4,6},{5,7},{6,4},{7,5},{8,10},{9,11},{10,... | collective-permute-start | bytes 393224 | tf_op jit(solution)/shard_map/ppermute | solution.py:304
  35.5 1.4 %collective-permute-start.8 = (bf16[432,128]{1,0:T(8,128)(2,1)S(1)}, bf16[432,128]{1,0:T(8,128)(2,1)S(1)}, u32[]{:S(2)}, u32[]{:S(2)}) collective-permute-start(bf16[432,128]{1,0:T(8,128)(2,1)S(1)} %pad_maximum_fusion.6), channel_id=1, source_target_pairs={{0,1},{1,0},{2,3},{3,2},{4,5},{5,4},{6,7},{7,6},{8,9},{9,8},{10,11... | collective-permute-start | bytes 331784 | tf_op jit(solution)/shard_map/ppermute | solution.py:304
  37.0 1.3 %copy-start.5 = (f32[4,64,16]{2,1,0:T(8,128)S(1)}, f32[4,64,16]{2,1,0:T(8,128)}, u32[]{:S(2)}) copy-start(f32[4,64,16]{2,1,0:T(8,128)} %copy-done.4) | copy-start | bytes 49156
  37.0 1.3 %copy-start.7 = (bf16[64,512]{1,0:T(8,128)(2,1)S(1)}, bf16[64,512]{1,0:T(8,128)(2,1)}, u32[]{:S(2)}) copy-start(bf16[64,512]{1,0:T(8,128)(2,1)} %copy-done.6) | copy-start | bytes 196612
  37.0 6.8 %collective-permute-start.9 = (bf16[432,128]{1,0:T(8,128)(2,1)S(1)}, bf16[432,128]{1,0:T(8,128)(2,1)S(1)}, u32[]{:S(2)}, u32[]{:S(2)}) collective-permute-start(bf16[432,128]{1,0:T(8,128)(2,1)S(1)} %pad_maximum_fusion.7), channel_id=1, source_target_pairs={{0,4},{4,0},{8,12},{12,8},{1,5},{5,1},{9,13},{13,9},{2,6},{6,2},{1... | collective-permute-start | bytes 331784 | tf_op jit(solution)/shard_map/ppermute | solution.py:304
  43.9 8.2 %collective-permute-start.10 = (bf16[432,128]{1,0:T(8,128)(2,1)S(1)}, bf16[432,128]{1,0:T(8,128)(2,1)S(1)}, u32[]{:S(2)}, u32[]{:S(2)}) collective-permute-start(bf16[432,128]{1,0:T(8,128)(2,1)S(1)} %pad_maximum_fusion.8), channel_id=1, source_target_pairs={{0,8},{4,12},{8,0},{12,4},{1,9},{5,13},{9,1},{13,5},{2,10},{6,14},... | collective-permute-start | bytes 331784 | tf_op jit(solution)/shard_map/ppermute | solution.py:304
  52.2 5.0 %collective-permute-start.11 = (bf16[496,128]{1,0:T(8,128)(2,1)S(1)}, bf16[496,128]{1,0:T(8,128)(2,1)S(1)}, u32[]{:S(2)}, u32[]{:S(2)}) collective-permute-start(bf16[496,128]{1,0:T(8,128)(2,1)S(1)} %pad_maximum_fusion.5), channel_id=1, source_target_pairs={{0,2},{1,3},{2,0},{3,1},{4,6},{5,7},{6,4},{7,5},{8,10},{9,11},{10,... | collective-permute-start | bytes 380936 | tf_op jit(solution)/shard_map/ppermute | solution.py:304
  57.3 1.4 %collective-permute-start.12 = (bf16[576,128]{1,0:T(8,128)(2,1)S(1)}, bf16[576,128]{1,0:T(8,128)(2,1)S(1)}, u32[]{:S(2)}, u32[]{:S(2)}) collective-permute-start(bf16[576,128]{1,0:T(8,128)(2,1)S(1)} %pad_maximum_fusion.3), channel_id=1, source_target_pairs={{0,1},{1,0},{2,3},{3,2},{4,5},{5,4},{6,7},{7,6},{8,9},{9,8},{10,11... | collective-permute-start | bytes 442376 | tf_op jit(solution)/shard_map/ppermute | solution.py:304

commit v11 on v10

--- a/solution.py
+++ b/solution.py
@@ -100,54 +100,55 @@
             t_ref[:, (e + k) * depth : (e + k + 1) * depth, :] = part
 
 
-def row_kernel(mi_ref, w_ref, wide_ref, a_ref, at_ref, wt_ref, wc_ref, rows_ref):
-    features, width = w_ref.shape[0], w_ref.shape[1] // 2
+def factor_kernel(w_ref, wide_ref, offset_ref, wt_ref, wc_ref, pass_ref, rows_ref):
+    width = w_ref.shape[1] // 2
     pair = wide_ref.shape[1]
+    pass_ref[...] = offset_ref[...]
     rows_ref[...] = wide_ref[...].astype(F32)
     for e in range(width):
         part = rows_ref[pl.ds(e, width, stride=width), :]
         wc_ref[:, e * pair : (e + 1) * pair] = part.astype(BF16)
-    w = w_ref[...]
     same = one_hot(iota((2 * width, 2 * width), 0) == iota((2 * width, 2 * width), 1))
-    wt = dot_nt(same, w).astype(BF16)
-    wt_ref[...] = wt
-    mi = mi_ref[...]
-    a_ref[...] = dot(mi, w[:, :width]).astype(BF16)
-    same = one_hot(iota((features, features), 0) == iota((features, features), 1))
-    at_ref[...] = dot_nt(jnp.concatenate([wt[:width, :], same], axis=0), mi).astype(BF16)
+    wt_ref[...] = dot_nt(same, w_ref[...]).astype(BF16)
 
 
 def weight_kernel(depth, features, *refs):
-    up_ref, mj_ref, seen_j_ref, seen_i_ref, w_ref, perm_ref, wc_ref, at_ref, offset_ref = refs[:9]
-    g_ref, b_ref, bt_ref, inv_ref, bias_ref, dw_ref, left_ref, pass_ref = refs[9:17]
-    v_ref, acc_ref, wide_ref = refs[17:]
+    up_ref, mi_ref, mj_ref, seen_i_ref, seen_j_ref, wt_ref, perm_ref, wc_ref = refs[:8]
+    g_ref, a_ref, b_ref, bt_ref, inv_ref, bias_ref, dw_ref, left_ref = refs[8:16]
+    at_ref, v_ref, acc_ref, wide_ref = refs[16:]
     g, last = pl.program_id(0), pl.num_programs(0) - 1
     chunk, block, pair = up_ref.shape
-    width = w_ref.shape[1] // 2
+    part_size = inv_ref.shape[2]
+    width = wt_ref.shape[0] // 2
 
     @pl.when(g == 0)
     def _():
-        w = w_ref[:, width:]
+        wt = wt_ref[...]
+        mi = mi_ref[...]
+        a_ref[...] = dot_nt(mi, wt[:width, :]).astype(BF16)
+        same = one_hot(iota((features, features), 0) == iota((features, features), 1))
+        at_ref[...] = dot_nt(jnp.concatenate([wt[:width, :], same], axis=0), mi).astype(BF16)
         b = jnp.zeros((block, width * depth), F32)
         for s in range(depth):
-            part = dot(mj_ref[s], w).astype(BF16)
+            part = dot_nt(mj_ref[s], wt[width:, :]).astype(BF16)
             b = b + dot(part, perm_ref[s * width : (s + 1) * width, :])
         b_ref[...] = b.astype(BF16)
         bt_ref[...] = b.T.astype(BF16)
-        for k in range(block // chunk):
-            count = dot_nt(seen_j_ref[...], seen_i_ref[k * chunk : (k + 1) * chunk, :])
+        for k in range(block // part_size):
+            rows = slice(k * part_size, (k + 1) * part_size)
+            count = dot_nt(seen_j_ref[...], seen_i_ref[rows, :])
             inv_ref[k] = 1.0 / (count + 0.001)
         acc_ref[...] = jnp.zeros_like(acc_ref)
         wide_ref[...] = jnp.zeros_like(wide_ref)
         bias_ref[...] = jnp.zeros_like(bias_ref)
-        pass_ref[...] = offset_ref[...]
-
-    inv = inv_ref[g]
+
     bias = jnp.zeros((block, pair), F32)
-    for i in range(chunk):
-        up = up_ref[i].astype(F32)
-        bias = bias + up
-        g_ref[i] = (up * inv[:, i : i + 1]).astype(BF16)
+    for k in range(chunk // part_size):
+        inv = inv_ref[g * (chunk // part_size) + k]
+        for i in range(part_size):
+            up = up_ref[k * part_size + i].astype(F32)
+            bias = bias + up
+            g_ref[k * part_size + i] = (up * inv[:, i : i + 1]).astype(BF16)
     bias_ref[0:1, :] += jnp.sum(bias, axis=0, keepdims=True)
     fill_v(g_ref, bt_ref[...], v_ref, depth)
     span = chunk * depth
@@ -169,15 +170,19 @@
         left_ref[...] = left
 
 
-def left_kernel(depth, bit, g_ref, bt_ref, wd_ref, small_ref, keep_ref, go_ref, pass_ref, v_ref, da_ref):
+def left_kernel(depth, bit, *refs):
+    g_ref, bt_ref, wc_ref, small_ref, keep_ref, go_ref, pass_ref, v_ref, wd_ref, da_ref = refs
     g, last = pl.program_id(0), pl.num_programs(0) - 1
     chunk, _, pair = g_ref.shape
-    width = wd_ref.shape[1]
+    width = wc_ref.shape[0]
     span = chunk * depth
 
     @pl.when(g == 0)
     def _():
         pass_ref[...] = small_ref[...]
+        same = one_hot(iota((2 * pair, 2 * pair), 0) == iota((2 * pair, 2 * pair), 1))
+        for at in range(0, wd_ref.shape[0], 2 * pair):
+            wd_ref[at : at + 2 * pair, :] = dot_nt(same, wc_ref[:, at : at + 2 * pair]).astype(BF16)
 
     fill_v(g_ref, bt_ref[...], v_ref, depth)
     d_a = []
@@ -202,7 +207,7 @@
 
 def token_kernel(depth, features, n, *refs):
     g_ref, a_ref, wc_ref, mj_ref, perm_ref, bias_ref, left_ref = refs[:7]
-    small_ref, out_ref, t_ref, db_ref = refs[7:]
+    small_ref, out_ref, t_ref, db_ref = refs[-4:]
     g, last = pl.program_id(0), pl.num_programs(0) - 1
     chunk, block = g_ref.shape[:2]
     width = left_ref.shape[0]
@@ -235,16 +240,13 @@
 
 
 def update_kernel(depth, *refs):
-    inv_ref, a_ref, b_ref, offset_ref, wc_ref, small_ref, out_ref, wd_ref, pass_ref, t_ref = refs
+    inv_ref, a_ref, b_ref, offset_ref, wc_ref, small_ref, out_ref, pass_ref, t_ref = refs
     g = pl.program_id(0)
     chunk, block, pair = out_ref.shape
 
     @pl.when(g == 0)
     def _():
         pass_ref[...] = small_ref[...]
-        same = one_hot(iota((2 * pair, 2 * pair), 0) == iota((2 * pair, 2 * pair), 1))
-        for at in range(0, wd_ref.shape[0], 2 * pair):
-            wd_ref[at : at + 2 * pair, :] = dot_nt(same, wc_ref[:, at : at + 2 * pair]).astype(BF16)
 
     span = chunk * depth
     fill_t(a_ref[pl.ds(pl.multiple_of(g * span, span), span), :], wc_ref, t_ref, depth)
@@ -393,15 +395,14 @@
     source = jnp.arange(wide)
     perm = (jnp.arange(wide)[None, :] == (source % width * depth + source // width)[:, None]).astype(BF16)
     up_spec = pl.BlockSpec((chunk, block, pair), lambda g: (g, 0, 0))
-    args = (mi, sitewise_factors, pairing_matrix)
+    args = (sitewise_factors, pairing_matrix, offset)
     out_shapes = [
-        sds((tokens, width), BF16),
-        sds((width + features, tokens), BF16),
         sds((2 * width, features), BF16),
         sds((width, width * pair), BF16),
+        sds((1, pair), F32),
     ]
-    a, a_t, factors_t, pairing_wide = call(
-        row_kernel,
+    factors_t, pairing_wide, offset = call(
+        factor_kernel,
         (),
         [full(v.shape) for v in args],
         [full(o.shape) for o in out_shapes],
@@ -410,29 +411,32 @@
     )(*args)
 
     out_shapes = [
+        sds((tokens, width), BF16),
         sds((block, wide), BF16),
         sds((wide, block), BF16),
         sds((steps, block, chunk), F32),
         sds((8, pair), F32),
         sds((width * width, pair), BF16),
         sds((width, features), F32),
-        sds((1, pair), F32),
     ]
-    args = (mj, seen_j, seen_i, sitewise_factors, perm, pairing_wide, a_t, offset)
+    args = (mi, mj, seen_i, seen_j, factors_t, perm, pairing_wide)
+    large = 2 * chunk
+    large_spec = pl.BlockSpec((large, block, pair), lambda g: (g, 0, 0))
     outs = call(
         functools.partial(weight_kernel, depth, features),
-        (steps,),
-        [up_spec] + [full(v.shape) for v in args],
-        [up_spec] + [full(o.shape) for o in out_shapes],
+        (block // large,),
+        [large_spec] + [full(v.shape) for v in args],
+        [large_spec] + [full(o.shape) for o in out_shapes],
         [sds(upstream_adjoint.shape, BF16)] + out_shapes,
         [
-            pltpu.VMEM((width, chunk * depth, pair), BF16),
+            pltpu.VMEM((width + features, tokens), BF16),
+            pltpu.VMEM((width, large * depth, pair), BF16),
             pltpu.VMEM((width * width, pair), F32),
             pltpu.VMEM((features, width * pair), F32),
         ],
         cost(5e9, 8e6),
     )(upstream_adjoint, *args)
-    scaled, b, b_t, inv, bias, d_pairing, left, offset = outs
+    scaled, a, b, b_t, inv, bias, d_pairing, left = outs
 
     d_pairing = d_pairing.reshape(n, -1, LANES)
     for bit in reversed(range(1, bits)):
@@ -443,12 +447,14 @@
     small, d_b = call(
         functools.partial(token_kernel, depth, features, n),
         (steps,),
-        [up_spec] + [full(v.shape) for v in (a, pairing_wide, mj, perm, bias, left)],
+        [up_spec]
+        + [full(v.shape) for v in (a, pairing_wide, mj, perm, bias, left)]
+        + [pl.BlockSpec(memory_space=pl.ANY)] * 4,
         [full(o.shape) for o in out_shapes],
         out_shapes,
         [pltpu.VMEM((chunk, wide, pair), BF16), pltpu.VMEM((wide, block), F32)],
         cost(8e9, 8e6),
-    )(scaled, a, pairing_wide, mj, perm, bias, left)
+    )(scaled, a, pairing_wide, mj, perm, bias, left, b, b_t, inv, offset)
 
     dp_keep, dp_go = halves(d_pairing, "col", 0, 0)
     db_keep, db_go = halves(d_b.reshape((n // 2, 2) + d_b.shape[1:]), "col", 0, 1)
@@ -460,16 +466,12 @@
         parts = swap_parts([d_pairing, db_go, small], "row", bit, n)
         if bit == 0:
             args = (inv, a, b, offset, pairing_wide, small)
-            coupling_update, pairing_t, small = call(
+            coupling_update, small = call(
                 functools.partial(update_kernel, depth),
                 (steps,),
                 [full(v.shape) for v in args],
-                [up_spec, full((width * pair, width)), full(small.shape)],
-                [
-                    sds((block, block, pair), BF16),
-                    sds((width * pair, width), BF16),
-                    sds(small.shape, BF16),
-                ],
+                [up_spec, full(small.shape)],
+                [sds((block, block, pair), BF16), sds(small.shape, BF16)],
                 [pltpu.VMEM((chunk, wide, pair), BF16)],
                 cost(6e9, 8e6),
             )(*args)
@@ -479,15 +481,16 @@
             *d_a, small = call(
                 functools.partial(left_kernel, depth, bits - 1),
                 (steps,),
-                [up_spec] + [full(v.shape) for v in (b_t, pairing_t, small)],
+                [up_spec] + [full(v.shape) for v in (b_t, pairing_wide, small)],
                 [full(o.shape) for o in out_shapes],
                 out_shapes,
                 [
                     pltpu.VMEM((width, chunk * depth, pair), BF16),
+                    pltpu.VMEM((width * pair, width), BF16),
                     pltpu.VMEM((tokens // LANES, width, LANES), BF16),
                 ],
                 cost(6e9, 8e6),
-            )(scaled, b_t, pairing_t, small)
+            )(scaled, b_t, pairing_wide, small)
             if rows % LANES:
                 shape = (-1, width, LANES // rows, rows)
                 d_a = [part.reshape(shape).transpose(0, 2, 1, 3) for part in d_a]

time: 61.5 us -> 60.2 us (0.979)
  waiting for transfers between devices: 10.7 us -> 9.94 us
  Pallas kernels: 27.5 us -> 26.8 us
    ppermute x6, waiting for transfers between devices: 8.09 us -> 7.32 us  [swap_parts(): message = lax.ppermute(message, axis, pairs)]
    pallas_call x1, Pallas kernels: 5.44 us -> 6.1 us  [per_device(): call(functools.partial(left_kernel, depth, bits - 1), (steps,), [up_spec]...]
    pallas_call x1, Pallas kernels: 5.55 us -> 4.89 us  [per_device(): call(functools.partial(update_kernel, depth), (steps,), [full(v.shape) fo...]
    pallas_call x2, Pallas kernels: 7.96 us -> 7.31 us  [the longest x1 6.84 us: per_device(): call(functools.partial(weight_kernel, depth, features), (block // large,)...]
    unnamed x19 -> x23, local copies, waits for them, and re-layouts: 2.22 us -> 2.25 us
  transfers between devices with their start and end apart: 13 -> 13, of which waited for: 5 -> 5; matrix products, arithmetic and copies ran while one was open for 0% -> 0% of each run, Pallas kernels for 27% -> 28%
where the time goes in v11:
time: 60.2 us; the launch traced here: 59.9 us
  Pallas kernels  26.8 us (45%)
  starting transfers between devices  17.2 us (29%)
  waiting for transfers between devices  9.94 us (17%)
  local copies, waits for them, and re-layouts  3.14 us (5%)
  other arithmetic  1.62 us (3%)
  between operations  1.17 us (2%)
    ppermute x6, waiting for transfers between devices, swap_parts(): message = lax.ppermute(message, axis, pairs)  7.32 us
    ppermute x4, starting transfers between devices, per_device(): held.append(lax.ppermute(message, axes, pairs))  7.25 us
    pallas_call x1, Pallas kernels, per_device(): call(functools.partial(weight_kernel, depth, features), (block // large,)...  6.84 us
    pallas_call x1, Pallas kernels, per_device(): call(functools.partial(left_kernel, depth, bits - 1), (steps,), [up_spec]...  6.1 us
    pallas_call x1, Pallas kernels, per_device(): call(functools.partial(token_kernel, depth, features, n), (steps,), [up_s...  5.54 us
    ppermute x6, starting transfers between devices, swap_parts(): message = lax.ppermute(message, axis, pairs)  5.43 us
    pallas_call x1, Pallas kernels, per_device(): call(functools.partial(update_kernel, depth), (steps,), [full(v.shape) fo...  4.89 us
    ppermute x3, starting transfers between devices, per_device(): held.append(lax.ppermute(message, 'col', [(j, j ^ k) for j in range(n)]))  4.57 us
  transfers between devices with their start and end apart: 13, of which 5 were waited for; matrix products, arithmetic and copies ran while one was open for 0% of the time, Pallas kernels for 28%

profile of v11, /device:TPU:0, one launch (start us, length us, event | category | flops | bytes accessed | tf_op | source)
XLA Modules:
  0.0 59.9 jit_solution(13198290656957634111)
XLA Ops:
  0.6 0.8 %multiply_convert_fusion = bf16[16,16]{1,0:T(8,128)(2,1)S(1)} fusion(s32[16,16]{1,0:T(8,128)} %param.8, s32[16]{0:T(128)} %param.9), kind=kLoop, calls=%fused_computation.53 | loop fusion | flops 512 | bytes 1600 | tf_op jit(solution)/shard_map/convert_element_type | solution.py:363
  1.4 0.1 broadcast_in_dim.2
  1.6 0.1 pad_maximum_fusion.9
  1.7 0.5 shard_map.110
  2.2 5.1 %collective-permute-start.6 = (bf16[144,128]{1,0:T(8,128)(2,1)S(1)}, bf16[144,128]{1,0:T(8,128)(2,1)S(1)}, u32[]{:S(2)}, u32[]{:S(2)}) collective-permute-start(bf16[144,128]{1,0:T(8,128)(2,1)S(1)} %get-tuple-element.30), channel_id=1, source_target_pairs={{0,12},{1,8},{2,4},{3,0},{4,13},{5,9},{6,5},{7,1},{8,14},{9,10},{1... | collective-permute-start | bytes 110600 | tf_op jit(solution)/shard_map/ppermute | solution.py:387
  7.3 1.5 %collective-permute-start.5 = (bf16[144,128]{1,0:T(8,128)(2,1)S(1)}, bf16[144,128]{1,0:T(8,128)(2,1)S(1)}, u32[]{:S(2)}, u32[]{:S(2)}) collective-permute-start(bf16[144,128]{1,0:T(8,128)(2,1)S(1)} %get-tuple-element.30), channel_id=1, source_target_pairs={{0,8},{1,12},{2,0},{3,4},{4,9},{5,13},{6,1},{7,5},{8,10},{9,14},{1... | collective-permute-start | bytes 110600 | tf_op jit(solution)/shard_map/ppermute | solution.py:387
  8.8 0.0 collective-permute-start.4
  8.8 0.7 %collective-permute-start.3 = (bf16[144,128]{1,0:T(8,128)(2,1)S(1)}, bf16[144,128]{1,0:T(8,128)(2,1)S(1)}, u32[]{:S(2)}, u32[]{:S(2)}) collective-permute-start(bf16[144,128]{1,0:T(8,128)(2,1)S(1)} %get-tuple-element.30), channel_id=1, source_target_pairs={{0,0},{1,4},{2,8},{3,12},{4,1},{5,5},{6,9},{7,13},{8,2},{9,6},{10,... | collective-permute-start | bytes 110600 | tf_op jit(solution)/shard_map/ppermute | solution.py:387
  9.4 3.3 %collective-permute-start.2 = (bf16[144,128]{1,0:T(8,128)(2,1)S(1)}, bf16[144,128]{1,0:T(8,128)(2,1)S(1)}, u32[]{:S(2)}, u32[]{:S(2)}) collective-permute-start(bf16[144,128]{1,0:T(8,128)(2,1)S(1)} %get-tuple-element.29), channel_id=1, source_target_pairs={{0,3},{1,2},{2,1},{3,0},{4,7},{5,6},{6,5},{7,4},{8,11},{9,10},{10,... | collective-permute-start | bytes 110600 | tf_op jit(solution)/shard_map/ppermute | solution.py:378
  12.7 0.2 fusion.refs_6_.refs_4_.refs_7_
  12.9 0.0 copy-start.1
  12.9 0.0 copy-start.2
  12.9 0.7 %copy-done = bf16[1024,128]{1,0:T(8,128)(2,1)S(1)} copy-done((bf16[1024,128]{1,0:T(8,128)(2,1)S(1)}, bf16[1024,128]{1,0:T(8,128)(2,1)}, u32[]{:S(2)}) %copy-start) | copy-done | bytes 262168
  13.7 0.5 shard_map.111
  14.1 0.0 collective-permute-done.6
  14.1 1.1 %collective-permute-start.1 = (bf16[144,128]{1,0:T(8,128)(2,1)S(1)}, bf16[144,128]{1,0:T(8,128)(2,1)S(1)}, u32[]{:S(2)}, u32[]{:S(2)}) collective-permute-start(bf16[144,128]{1,0:T(8,128)(2,1)S(1)} %get-tuple-element.29), channel_id=1, source_target_pairs={{0,2},{1,3},{2,0},{3,1},{4,6},{5,7},{6,4},{7,5},{8,10},{9,11},{10,... | collective-permute-start | bytes 110600 | tf_op jit(solution)/shard_map/ppermute | solution.py:378
  15.3 0.0 collective-permute-done.5
  15.3 0.2 collective-permute-start
  15.4 0.0 collective-permute-done.4
  15.6 2.6 %collective-permute-done.1 = bf16[144,128]{1,0:T(8,128)(2,1)S(1)} collective-permute-done((bf16[144,128]{1,0:T(8,128)(2,1)S(1)}, bf16[144,128]{1,0:T(8,128)(2,1)S(1)}, u32[]{:S(2)}, u32[]{:S(2)}) %collective-permute-start.1) | collective-permute-done | bytes 36896 | tf_op jit(solution)/shard_map/ppermute | solution.py:378
  18.3 0.1 copy.18
  18.5 0.0 copy-start.3
  18.6 0.1 copy.21
  18.6 0.2 copy.19
  18.8 0.1 reshape.208
  19.0 0.7 %copy-done.3 = bf16[64,64,128]{2,1,0:T(8,128)(2,1)S(1)} copy-done((bf16[64,64,128]{2,1,0:T(8,128)(2,1)S(1)}, bf16[64,64,128]{2,1,0:T(8,128)(2,1)}, u32[]{:S(2)}) %copy-start.3) | copy-done | bytes 1048600
  19.7 6.8 %shard_map.112 = (bf16[64,64,128]{2,1,0:T(8,128)(2,1)S(1)}, bf16[1024,32]{1,0:T(8,128)(2,1)S(1)}, bf16[64,512]{1,0:T(8,128)(2,1)S(1)}, bf16[512,64]{1,0:T(8,128)...) custom-call(bf16[64,64,128]{2,1,0:T(8,128)(2,1)S(1)} %copy-done.3, ...), custom_call_target="tpu_custom_call" | custom-call | flops 5000000000 | bytes 8000000 | tf_op jit(solution)/shard_map/pallas_call | solution.py:425
  26.6 1.1 %collective-permute-start.7 = (bf16[512,128]{1,0:T(8,128)(2,1)S(1)}, bf16[512,128]{1,0:T(8,128)(2,1)S(1)}, u32[]{:S(2)}, u32[]{:S(2)}) collective-permute-start(bf16[512,128]{1,0:T(8,128)(2,1)S(1)} %bitcast.138), channel_id=1, source_target_pairs={{0,2},{1,3},{2,0},{3,1},{4,6},{5,7},{6,4},{7,5},{8,10},{9,11},{10,... | collective-permute-start | bytes 393224 | tf_op jit(solution)/shard_map/ppermute | solution.py:306
  27.7 5.5 %shard_map.113 = (bf16[48,128]{1,0:T(8,128)(2,1)S(1)}, bf16[4,64,128]{2,1,0:T(8,128)(2,1)S(1)}) custom-call(bf16[64,64,128]{2,1,0:T(8,128)(2,1)S(1)} %get-tuple-element.37.refs_0_, bf16[1024,32]{1,0:T(8,128)(2,1)S(1)} %get-tuple-element.34.refs_1_, bf16[32,4096]{1,0:T(8,128)(2,1)S(1)} %get-tuple-element.32.refs_7_.refs_2_.refs_4_, ...), custom_call_target="tpu_custom_call" | custom-call | flops 8000000000 | bytes 8000000 | tf_op jit(solution)/shard_map/pallas_call | solution.py:447
  33.3 0.6 %copy-done.8 = bf16[64,512]{1,0:T(8,128)(2,1)} copy-done((bf16[64,512]{1,0:T(8,128)(2,1)}, bf16[64,512]{1,0:T(8,128)(2,1)S(1)}, u32[]{:S(2)}) %copy-start.8) | copy-done | bytes 65560
  33.9 0.0 collective-permute-done.7
  34.0 0.1 collective-permute-start.8
  34.1 1.3 %collective-permute-done.8 = bf16[432,128]{1,0:T(8,128)(2,1)S(1)} collective-permute-done((bf16[432,128]{1,0:T(8,128)(2,1)S(1)}, bf16[432,128]{1,0:T(8,128)(2,1)S(1)}, u32[]{:S(2)}, u32[]{:S(2)}) %collective-permute-start.8) | collective-permute-done | bytes 110624 | tf_op jit(solution)/shard_map/ppermute | solution.py:306
  35.5 0.0 copy-start.7
  35.5 0.0 copy-start.9
  35.6 1.9 %collective-permute-start.9 = (bf16[432,128]{1,0:T(8,128)(2,1)S(1)}, bf16[432,128]{1,0:T(8,128)(2,1)S(1)}, u32[]{:S(2)}, u32[]{:S(2)}) collective-permute-start(bf16[432,128]{1,0:T(8,128)(2,1)S(1)} %pad_maximum_fusion.7), channel_id=1, source_target_pairs={{0,4},{4,0},{8,12},{12,8},{1,5},{5,1},{9,13},{13,9},{2,6},{6,2},{1... | collective-permute-start | bytes 331784 | tf_op jit(solution)/shard_map/ppermute | solution.py:306
  37.5 4.9 %shard_map.114 = (bf16[64,64,128]{2,1,0:T(8,128)(2,1)}, bf16[48,128]{1,0:T(8,128)(2,1)S(1)}) custom-call(f32[4,64,16]{2,1,0:T(8,128)S(1)} %copy-done.7, bf16[1024,32]{1,0:T(8,128)(2,1)S(1)} %get-tuple-element.34.refs_1_, bf16[64,512]{1,0:T(8,128)(2,1)S(1)} %copy-done.9, f32[1,128]{1,0:T(1,128)S(1)} %get-tuple-element.36.refs_10_.refs_3_, ...), custom_call_target="tpu_custom_call" | custom-call | flops 6000000000 | bytes 8000000 | tf_op jit(solution)/shard_map/pallas_call | solution.py:469
  42.4 0.0 collective-permute-done.9
  42.5 0.0 copy-start.5
  42.5 0.7 %collective-permute-start.10 = (bf16[432,128]{1,0:T(8,128)(2,1)S(1)}, bf16[432,128]{1,0:T(8,128)(2,1)S(1)}, u32[]{:S(2)}, u32[]{:S(2)}) collective-permute-start(bf16[432,128]{1,0:T(8,128)(2,1)S(1)} %pad_maximum_fusion.8), channel_id=1, source_target_pairs={{0,8},{4,12},{8,0},{12,4},{1,9},{5,13},{9,1},{13,5},{2,10},{6,14},... | collective-permute-start | bytes 331784 | tf_op jit(solution)/shard_map/ppermute | solution.py:306
  43.2 0.1 copy-done.5
  43.4 6.1 %shard_map.115 = (bf16[4,32,128]{2,1,0:T(8,128)(2,1)S(1)}, bf16[4,32,128]{2,1,0:T(8,128)(2,1)S(1)}, bf16[48,128]{1,0:T(8,128)(2,1)S(1)}) custom-call(bf16[64,64,128]{2,1,0:T(8,128)(2,1)S(1)} %get-tuple-element.37.refs_0_, bf16[512,64]{1,0:T(8,128)(2,1)S(1)} %copy-done.5, bf16[32,4096]{1,0:T(8,128)(2,1)S(1)} %get-tuple-element.32.refs_7_.refs_2_.refs_4_, ...), custom_call_target="tpu_custom_call" | custom-call | flops 6000000000 | bytes 8000000 | tf_op jit(solution)/shard_map/pallas_call | solution.py:481
  49.5 1.2 %collective-permute-done.10 = bf16[432,128]{1,0:T(8,128)(2,1)S(1)} collective-permute-done((bf16[432,128]{1,0:T(8,128)(2,1)S(1)}, bf16[432,128]{1,0:T(8,128)(2,1)S(1)}, u32[]{:S(2)}, u32[]{:S(2)}) %collective-permute-start.10) | collective-permute-done | bytes 110624 | tf_op jit(solution)/shard_map/ppermute | solution.py:306
  50.8 1.5 %collective-permute-start.11 = (bf16[496,128]{1,0:T(8,128)(2,1)S(1)}, bf16[496,128]{1,0:T(8,128)(2,1)S(1)}, u32[]{:S(2)}, u32[]{:S(2)}) collective-permute-start(bf16[496,128]{1,0:T(8,128)(2,1)S(1)} %pad_maximum_fusion.5), channel_id=1, source_target_pairs={{0,2},{1,3},{2,0},{3,1},{4,6},{5,7},{6,4},{7,5},{8,10},{9,11},{10,... | collective-permute-start | bytes 380936 | tf_op jit(solution)/shard_map/ppermute | solution.py:306
  52.3 3.5 %collective-permute-done.11 = bf16[496,128]{1,0:T(8,128)(2,1)S(1)} collective-permute-done((bf16[496,128]{1,0:T(8,128)(2,1)S(1)}, bf16[496,128]{1,0:T(8,128)(2,1)S(1)}, u32[]{:S(2)}, u32[]{:S(2)}) %collective-permute-start.11) | collective-permute-done | bytes 127008 | tf_op jit(solution)/shard_map/ppermute | solution.py:306
  55.9 0.1 collective-permute-start.12
  56.0 1.3 %collective-permute-done.12 = bf16[576,128]{1,0:T(8,128)(2,1)S(1)} collective-permute-done((bf16[576,128]{1,0:T(8,128)(2,1)S(1)}, bf16[576,128]{1,0:T(8,128)(2,1)S(1)}, u32[]{:S(2)}, u32[]{:S(2)}) %collective-permute-start.12) | collective-permute-done | bytes 147488 | tf_op jit(solution)/shard_map/ppermute | solution.py:306
  57.5 2.4 %shard_map.116 = (f32[256,64]{1,0:T(8,128)}, f32[64,64]{1,0:T(8,128)}, f32[1,128]{1,0:T(1,128)}, f32[32,32,128]{2,1,0:T(8,128)}) custom-call(bf16[32,256]{1,0:T(8,128)(2,1)S(1)} %bitcast.112, bf16[32,256]{1,0:T(8,128)(2,1)S(1)} %bitcast.113, bf16[16,512]{1,0:T(8,128)(2,1)S(1)} %bitcast.111, bf16[48,128]{1,0:T(8,128)(2,1)S(1)} %add_convert_fusion.2.refs_3_, ...), custom_call_target="tpu_custom_call" | custom-call | tf_op jit(solution)/shard_map/pallas_call | solution.py:528
  (66 shorter events, 0.8 us)
Async XLA Ops:
  0.6 0.9 %copy-start.10 = (bf16[16,16,64]{2,1,0:T(8,128)(2,1)S(1)}, bf16[16,16,64]{2,1,0:T(8,128)(2,1)}, u32[]{:S(2)}) copy-start(bf16[16,16,64]{2,1,0:T(8,128)(2,1)} %param.7) | copy-start | bytes 98308
  2.2 11.9 %collective-permute-start.6 = (bf16[144,128]{1,0:T(8,128)(2,1)S(1)}, bf16[144,128]{1,0:T(8,128)(2,1)S(1)}, u32[]{:S(2)}, u32[]{:S(2)}) collective-permute-start(bf16[144,128]{1,0:T(8,128)(2,1)S(1)} %get-tuple-element.30), channel_id=1, source_target_pairs={{0,12},{1,8},{2,4},{3,0},{4,13},{5,9},{6,5},{7,1},{8,14},{9,10},{1... | collective-permute-start | bytes 110600 | tf_op jit(solution)/shard_map/ppermute | solution.py:387
  7.3 8.0 %collective-permute-start.5 = (bf16[144,128]{1,0:T(8,128)(2,1)S(1)}, bf16[144,128]{1,0:T(8,128)(2,1)S(1)}, u32[]{:S(2)}, u32[]{:S(2)}) collective-permute-start(bf16[144,128]{1,0:T(8,128)(2,1)S(1)} %get-tuple-element.30), channel_id=1, source_target_pairs={{0,8},{1,12},{2,0},{3,4},{4,9},{5,13},{6,1},{7,5},{8,10},{9,14},{1... | collective-permute-start | bytes 110600 | tf_op jit(solution)/shard_map/ppermute | solution.py:387
  8.8 6.7 %collective-permute-start.4 = (bf16[144,128]{1,0:T(8,128)(2,1)S(1)}, bf16[144,128]{1,0:T(8,128)(2,1)S(1)}, u32[]{:S(2)}, u32[]{:S(2)}) collective-permute-start(bf16[144,128]{1,0:T(8,128)(2,1)S(1)} %get-tuple-element.30), channel_id=1, source_target_pairs={{0,4},{1,0},{2,12},{3,8},{4,5},{5,1},{6,13},{7,9},{8,6},{9,2},{10,... | collective-permute-start | bytes 110600 | tf_op jit(solution)/shard_map/ppermute | solution.py:387
  8.8 6.7 %collective-permute-start.3 = (bf16[144,128]{1,0:T(8,128)(2,1)S(1)}, bf16[144,128]{1,0:T(8,128)(2,1)S(1)}, u32[]{:S(2)}, u32[]{:S(2)}) collective-permute-start(bf16[144,128]{1,0:T(8,128)(2,1)S(1)} %get-tuple-element.30), channel_id=1, source_target_pairs={{0,0},{1,4},{2,8},{3,12},{4,1},{5,5},{6,9},{7,13},{8,2},{9,6},{10,... | collective-permute-start | bytes 110600 | tf_op jit(solution)/shard_map/ppermute | solution.py:387
  9.4 6.2 %collective-permute-start.2 = (bf16[144,128]{1,0:T(8,128)(2,1)S(1)}, bf16[144,128]{1,0:T(8,128)(2,1)S(1)}, u32[]{:S(2)}, u32[]{:S(2)}) collective-permute-start(bf16[144,128]{1,0:T(8,128)(2,1)S(1)} %get-tuple-element.29), channel_id=1, source_target_pairs={{0,3},{1,2},{2,1},{3,0},{4,7},{5,6},{6,5},{7,4},{8,11},{9,10},{10,... | collective-permute-start | bytes 110600 | tf_op jit(solution)/shard_map/ppermute | solution.py:378
  12.7 0.9 %copy-start = (bf16[1024,128]{1,0:T(8,128)(2,1)S(1)}, bf16[1024,128]{1,0:T(8,128)(2,1)}, u32[]{:S(2)}) copy-start(bf16[1024,128]{1,0:T(8,128)(2,1)} %wide_ref.1) | copy-start | bytes 786436
  12.9 0.8 %copy-start.1 = (bf16[64,64]{1,0:T(8,128)(2,1)S(1)}, bf16[64,64]{1,0:T(8,128)(2,1)}, u32[]{:S(2)}) copy-start(bf16[64,64]{1,0:T(8,128)(2,1)} %w_ref.1) | copy-start | bytes 24580
  12.9 0.8 %copy-start.2 = (f32[128]{0:T(128)S(1)}, f32[128]{0:T(128)}, u32[]{:S(2)}) copy-start(f32[128]{0:T(128)} %param.12) | copy-start | bytes 1540
  14.1 4.1 %collective-permute-start.1 = (bf16[144,128]{1,0:T(8,128)(2,1)S(1)}, bf16[144,128]{1,0:T(8,128)(2,1)S(1)}, u32[]{:S(2)}, u32[]{:S(2)}) collective-permute-start(bf16[144,128]{1,0:T(8,128)(2,1)S(1)} %get-tuple-element.29), channel_id=1, source_target_pairs={{0,2},{1,3},{2,0},{3,1},{4,6},{5,7},{6,4},{7,5},{8,10},{9,11},{10,... | collective-permute-start | bytes 110600 | tf_op jit(solution)/shard_map/ppermute | solution.py:378
  15.3 2.9 %collective-permute-start = (bf16[144,128]{1,0:T(8,128)(2,1)S(1)}, bf16[144,128]{1,0:T(8,128)(2,1)S(1)}, u32[]{:S(2)}, u32[]{:S(2)}) collective-permute-start(bf16[144,128]{1,0:T(8,128)(2,1)S(1)} %get-tuple-element.29), channel_id=1, source_target_pairs={{0,1},{1,0},{2,3},{3,2},{4,5},{5,4},{6,7},{7,6},{8,9},{9,8},{10,11... | collective-permute-start | bytes 110600 | tf_op jit(solution)/shard_map/ppermute | solution.py:378
  18.5 1.2 %copy-start.3 = (bf16[64,64,128]{2,1,0:T(8,128)(2,1)S(1)}, bf16[64,64,128]{2,1,0:T(8,128)(2,1)}, u32[]{:S(2)}) copy-start(bf16[64,64,128]{2,1,0:T(8,128)(2,1)} %refs_0_.1) | copy-start | bytes 3145732
  26.5 1.2 %copy-start.4 = (bf16[512,64]{1,0:T(8,128)(2,1)}, bf16[512,64]{1,0:T(8,128)(2,1)S(1)}, u32[]{:S(2)}) copy-start(bf16[512,64]{1,0:T(8,128)(2,1)S(1)} %get-tuple-element.40.refs_8_.refs_1_) | copy-start | bytes 196612
  26.5 1.2 %copy-start.6 = (f32[4,64,16]{2,1,0:T(8,128)}, f32[4,64,16]{2,1,0:T(8,128)S(1)}, u32[]{:S(2)}) copy-start(f32[4,64,16]{2,1,0:T(8,128)S(1)} %get-tuple-element.33.refs_9_.refs_0_) | copy-start | bytes 49156
  26.6 7.3 %collective-permute-start.7 = (bf16[512,128]{1,0:T(8,128)(2,1)S(1)}, bf16[512,128]{1,0:T(8,128)(2,1)S(1)}, u32[]{:S(2)}, u32[]{:S(2)}) collective-permute-start(bf16[512,128]{1,0:T(8,128)(2,1)S(1)} %bitcast.138), channel_id=1, source_target_pairs={{0,2},{1,3},{2,0},{3,1},{4,6},{5,7},{6,4},{7,5},{8,10},{9,11},{10,... | collective-permute-start | bytes 393224 | tf_op jit(solution)/shard_map/ppermute | solution.py:306
  33.3 0.6 %copy-start.8 = (bf16[64,512]{1,0:T(8,128)(2,1)}, bf16[64,512]{1,0:T(8,128)(2,1)S(1)}, u32[]{:S(2)}) copy-start(bf16[64,512]{1,0:T(8,128)(2,1)S(1)} %get-tuple-element.35.refs_7_.refs_2_) | copy-start | bytes 196612
  34.0 1.4 %collective-permute-start.8 = (bf16[432,128]{1,0:T(8,128)(2,1)S(1)}, bf16[432,128]{1,0:T(8,128)(2,1)S(1)}, u32[]{:S(2)}, u32[]{:S(2)}) collective-permute-start(bf16[432,128]{1,0:T(8,128)(2,1)S(1)} %pad_maximum_fusion.6), channel_id=1, source_target_pairs={{0,1},{1,0},{2,3},{3,2},{4,5},{5,4},{6,7},{7,6},{8,9},{9,8},{10,11... | collective-permute-start | bytes 331784 | tf_op jit(solution)/shard_map/ppermute | solution.py:306
  35.5 2.0 %copy-start.7 = (f32[4,64,16]{2,1,0:T(8,128)S(1)}, f32[4,64,16]{2,1,0:T(8,128)}, u32[]{:S(2)}) copy-start(f32[4,64,16]{2,1,0:T(8,128)} %copy-done.6) | copy-start | bytes 49156
  35.5 2.0 %copy-start.9 = (bf16[64,512]{1,0:T(8,128)(2,1)S(1)}, bf16[64,512]{1,0:T(8,128)(2,1)}, u32[]{:S(2)}) copy-start(bf16[64,512]{1,0:T(8,128)(2,1)} %copy-done.8) | copy-start | bytes 196612
  35.6 6.8 %collective-permute-start.9 = (bf16[432,128]{1,0:T(8,128)(2,1)S(1)}, bf16[432,128]{1,0:T(8,128)(2,1)S(1)}, u32[]{:S(2)}, u32[]{:S(2)}) collective-permute-start(bf16[432,128]{1,0:T(8,128)(2,1)S(1)} %pad_maximum_fusion.7), channel_id=1, source_target_pairs={{0,4},{4,0},{8,12},{12,8},{1,5},{5,1},{9,13},{13,9},{2,6},{6,2},{1... | collective-permute-start | bytes 331784 | tf_op jit(solution)/shard_map/ppermute | solution.py:306
  42.5 0.9 %copy-start.5 = (bf16[512,64]{1,0:T(8,128)(2,1)S(1)}, bf16[512,64]{1,0:T(8,128)(2,1)}, u32[]{:S(2)}) copy-start(bf16[512,64]{1,0:T(8,128)(2,1)} %copy-done.4) | copy-start | bytes 196612
  42.5 8.2 %collective-permute-start.10 = (bf16[432,128]{1,0:T(8,128)(2,1)S(1)}, bf16[432,128]{1,0:T(8,128)(2,1)S(1)}, u32[]{:S(2)}, u32[]{:S(2)}) collective-permute-start(bf16[432,128]{1,0:T(8,128)(2,1)S(1)} %pad_maximum_fusion.8), channel_id=1, source_target_pairs={{0,8},{4,12},{8,0},{12,4},{1,9},{5,13},{9,1},{13,5},{2,10},{6,14},... | collective-permute-start | bytes 331784 | tf_op jit(solution)/shard_map/ppermute | solution.py:306
  50.8 5.0 %collective-permute-start.11 = (bf16[496,128]{1,0:T(8,128)(2,1)S(1)}, bf16[496,128]{1,0:T(8,128)(2,1)S(1)}, u32[]{:S(2)}, u32[]{:S(2)}) collective-permute-start(bf16[496,128]{1,0:T(8,128)(2,1)S(1)} %pad_maximum_fusion.5), channel_id=1, source_target_pairs={{0,2},{1,3},{2,0},{3,1},{4,6},{5,7},{6,4},{7,5},{8,10},{9,11},{10,... | collective-permute-start | bytes 380936 | tf_op jit(solution)/shard_map/ppermute | solution.py:306
  55.9 1.4 %collective-permute-start.12 = (bf16[576,128]{1,0:T(8,128)(2,1)S(1)}, bf16[576,128]{1,0:T(8,128)(2,1)S(1)}, u32[]{:S(2)}, u32[]{:S(2)}) collective-permute-start(bf16[576,128]{1,0:T(8,128)(2,1)S(1)} %pad_maximum_fusion.3), channel_id=1, source_target_pairs={{0,1},{1,0},{2,3},{3,2},{4,5},{5,4},{6,7},{7,6},{8,9},{9,8},{10,11... | collective-permute-start | bytes 442376 | tf_op jit(solution)/shard_map/ppermute | solution.py:306

commit v12 on v11

--- a/solution.py
+++ b/solution.py
@@ -100,56 +100,97 @@
             t_ref[:, (e + k) * depth : (e + k + 1) * depth, :] = part
 
 
-def factor_kernel(w_ref, wide_ref, offset_ref, wt_ref, wc_ref, pass_ref, rows_ref):
-    width = w_ref.shape[1] // 2
+def held_b(held_ref, block, width, depth):
+    at = block * depth
+    tiles = width * depth // LANES
+    return jnp.concatenate([held_ref[at + k * block : at + (k + 1) * block, :] for k in range(tiles)], axis=1)
+
+
+def factor_kernel(own, pieces, w_ref, wide_ref, offset_ref, up_ref, *refs):
+    wt_ref, wc_ref, pass_ref, bias_ref, a_ref, at_ref, seen_ref, rows_ref, mi_ref = refs[pieces:]
+    features, width = w_ref.shape[0], w_ref.shape[1] // 2
     pair = wide_ref.shape[1]
+    if own % 16 == 0:
+        half = refs[0].shape[1] - own
+        for k in range(pieces):
+            for core in range(2):
+                at = ((lax.axis_index("col") >> 1) ^ k) * 2 + core
+                for q in range(2):
+                    rows = pl.ds(pl.multiple_of((at * 2 + q) * half, half), half)
+                    mi_ref[rows, :] = refs[k][core, :half, q * features : (q + 1) * features]
+                rows = pl.ds(pl.multiple_of(at * own, own), own)
+                seen_ref[rows, :] = refs[k][core, half:, :]
+    else:
+        mi_ref[...] = refs[0][...]
+        seen_ref[...] = refs[1][...]
     pass_ref[...] = offset_ref[...]
     rows_ref[...] = wide_ref[...].astype(F32)
     for e in range(width):
         part = rows_ref[pl.ds(e, width, stride=width), :]
         wc_ref[:, e * pair : (e + 1) * pair] = part.astype(BF16)
     same = one_hot(iota((2 * width, 2 * width), 0) == iota((2 * width, 2 * width), 1))
-    wt_ref[...] = dot_nt(same, w_ref[...]).astype(BF16)
-
-
-def weight_kernel(depth, features, *refs):
-    up_ref, mi_ref, mj_ref, seen_i_ref, seen_j_ref, wt_ref, perm_ref, wc_ref = refs[:8]
-    g_ref, a_ref, b_ref, bt_ref, inv_ref, bias_ref, dw_ref, left_ref = refs[8:16]
-    at_ref, v_ref, acc_ref, wide_ref = refs[16:]
+    wt = dot_nt(same, w_ref[...]).astype(BF16)
+    wt_ref[...] = wt
+    mi = mi_ref[...]
+    a_ref[...] = dot_nt(mi, wt[:width, :]).astype(BF16)
+    same = one_hot(iota((features, features), 0) == iota((features, features), 1))
+    at_ref[...] = dot_nt(jnp.concatenate([wt[:width, :], same], axis=0), mi).astype(BF16)
+    bias = [jnp.zeros(up_ref.shape[1:], F32)] * 2
+    for i in range(up_ref.shape[0]):
+        bias[i % 2] = bias[i % 2] + up_ref[i].astype(F32)
+    bias = jnp.sum(bias[0] + bias[1], axis=0, keepdims=True)
+    bias_ref[...] = jnp.broadcast_to(bias, bias_ref.shape)
+
+
+def weight_kernel(depth, features, own, pieces, part_size, *refs):
+    up_ref, a_ref, at_ref, seen_i_ref, wt_ref, perm_ref, wc_ref = refs[:7]
+    j_refs, refs = refs[7 : 7 + pieces], refs[7 + pieces :]
+    g_ref, held_ref, dw_ref, left_ref, mj_ref, seen_j_ref, bt_ref, inv_ref, v_ref, acc_ref, wide_ref = refs
     g, last = pl.program_id(0), pl.num_programs(0) - 1
     chunk, block, pair = up_ref.shape
-    part_size = inv_ref.shape[2]
     width = wt_ref.shape[0] // 2
 
     @pl.when(g == 0)
     def _():
+        if own % 16 == 0:
+            half = depth // 2
+            for k in range(pieces):
+                for core in range(2):
+                    at = ((lax.axis_index("row") >> 1) ^ k) * 2 + core
+                    rows = pl.ds(pl.multiple_of(at * own, own), own)
+                    seen_j_ref[rows, :] = j_refs[k][core, :own, :]
+                    for s in range(depth):
+                        lanes = slice(s // half * features, (s // half + 1) * features)
+                        start = own + s % half * own
+                        mj_ref[s, rows, :] = j_refs[k][core, start : start + own, lanes]
+        else:
+            mj_ref[...] = j_refs[0][...]
+            seen_j_ref[...] = j_refs[1][...]
         wt = wt_ref[...]
-        mi = mi_ref[...]
-        a_ref[...] = dot_nt(mi, wt[:width, :]).astype(BF16)
-        same = one_hot(iota((features, features), 0) == iota((features, features), 1))
-        at_ref[...] = dot_nt(jnp.concatenate([wt[:width, :], same], axis=0), mi).astype(BF16)
         b = jnp.zeros((block, width * depth), F32)
         for s in range(depth):
             part = dot_nt(mj_ref[s], wt[width:, :]).astype(BF16)
             b = b + dot(part, perm_ref[s * width : (s + 1) * width, :])
-        b_ref[...] = b.astype(BF16)
         bt_ref[...] = b.T.astype(BF16)
+        at = block * depth
+        held_ref[:at, :width] = a_ref[...]
+        for k in range(width * depth // LANES):
+            held_ref[at : at + block, :] = b[:, k * LANES : (k + 1) * LANES].astype(BF16)
+            at += block
         for k in range(block // part_size):
             rows = slice(k * part_size, (k + 1) * part_size)
             count = dot_nt(seen_j_ref[...], seen_i_ref[rows, :])
             inv_ref[k] = 1.0 / (count + 0.001)
+            held_ref[at : at + block, :part_size] = count.astype(BF16)
+            at += block
         acc_ref[...] = jnp.zeros_like(acc_ref)
         wide_ref[...] = jnp.zeros_like(wide_ref)
-        bias_ref[...] = jnp.zeros_like(bias_ref)
-
-    bias = jnp.zeros((block, pair), F32)
+
     for k in range(chunk // part_size):
         inv = inv_ref[g * (chunk // part_size) + k]
         for i in range(part_size):
             up = up_ref[k * part_size + i].astype(F32)
-            bias = bias + up
             g_ref[k * part_size + i] = (up * inv[:, i : i + 1]).astype(BF16)
-    bias_ref[0:1, :] += jnp.sum(bias, axis=0, keepdims=True)
     fill_v(g_ref, bt_ref[...], v_ref, depth)
     span = chunk * depth
     a_t = at_ref[:, pl.ds(pl.multiple_of(g * span, span), span)]
@@ -171,15 +212,16 @@
 
 
 def left_kernel(depth, bit, *refs):
-    g_ref, bt_ref, wc_ref, small_ref, keep_ref, go_ref, pass_ref, v_ref, wd_ref, da_ref = refs
+    g_ref, held_ref, wc_ref, small_ref, keep_ref, go_ref, pass_ref, v_ref, wd_ref, da_ref, bt_ref = refs
     g, last = pl.program_id(0), pl.num_programs(0) - 1
-    chunk, _, pair = g_ref.shape
+    chunk, block, pair = g_ref.shape
     width = wc_ref.shape[0]
     span = chunk * depth
 
     @pl.when(g == 0)
     def _():
         pass_ref[...] = small_ref[...]
+        bt_ref[...] = held_b(held_ref, block, width, depth).astype(F32).T.astype(BF16)
         same = one_hot(iota((2 * pair, 2 * pair), 0) == iota((2 * pair, 2 * pair), 1))
         for at in range(0, wd_ref.shape[0], 2 * pair):
             wd_ref[at : at + 2 * pair, :] = dot_nt(same, wc_ref[:, at : at + 2 * pair]).astype(BF16)
@@ -206,8 +248,8 @@
 
 
 def token_kernel(depth, features, n, *refs):
-    g_ref, a_ref, wc_ref, mj_ref, perm_ref, bias_ref, left_ref = refs[:7]
-    small_ref, out_ref, t_ref, db_ref = refs[-4:]
+    g_ref, held_ref, wc_ref, mj_ref, perm_ref, bias_ref, left_ref = refs[:7]
+    small_ref, out_ref, t_ref, db_ref = refs[7:]
     g, last = pl.program_id(0), pl.num_programs(0) - 1
     chunk, block = g_ref.shape[:2]
     width = left_ref.shape[0]
@@ -217,7 +259,7 @@
         db_ref[...] = jnp.zeros_like(db_ref)
 
     span = chunk * depth
-    fill_t(a_ref[pl.ds(pl.multiple_of(g * span, span), span), :], wc_ref, t_ref, depth)
+    fill_t(held_ref[pl.ds(pl.multiple_of(g * span, span), span), :width], wc_ref, t_ref, depth)
     t = jnp.concatenate([t_ref[i] for i in range(chunk)], axis=1)
     scaled = jnp.concatenate([g_ref[i] for i in range(chunk)], axis=1)
     db_ref[...] += dot_nt(t, scaled)
@@ -240,18 +282,21 @@
 
 
 def update_kernel(depth, *refs):
-    inv_ref, a_ref, b_ref, offset_ref, wc_ref, small_ref, out_ref, pass_ref, t_ref = refs
+    held_ref, offset_ref, wc_ref, small_ref, out_ref, pass_ref, t_ref = refs
     g = pl.program_id(0)
     chunk, block, pair = out_ref.shape
+    width = wc_ref.shape[0]
 
     @pl.when(g == 0)
     def _():
         pass_ref[...] = small_ref[...]
 
     span = chunk * depth
-    fill_t(a_ref[pl.ds(pl.multiple_of(g * span, span), span), :], wc_ref, t_ref, depth)
-    inv = inv_ref[g]
-    b = b_ref[...]
+    fill_t(held_ref[pl.ds(pl.multiple_of(g * span, span), span), :width], wc_ref, t_ref, depth)
+    rows = held_ref.shape[0] - (pl.num_programs(0) - g) * block
+    count = held_ref[pl.ds(pl.multiple_of(rows, block), block), :chunk]
+    inv = 1.0 / (count.astype(F32) + 0.001)
+    b = held_b(held_ref, block, width, depth)
     offset = offset_ref[...]
     for at in range(0, chunk, 2):
         part = dot(b, two(t_ref, at))
@@ -331,7 +376,7 @@
     n = x.shape[0]
     for bit in range(n.bit_length() - 1):
         y = x.reshape((n >> (bit + 1), 2, 1 << bit) + x.shape[1:])
-        x = jnp.where(bit_of(axis, bit) == 0, y, y[:, ::-1]).reshape(x.shape)
+        x = jnp.where(bit_of(axis, bit + 1) == 0, y, y[:, ::-1]).reshape(x.shape)
     return x
 
 
@@ -372,71 +417,80 @@
         [full(o.shape) for o in out_shapes],
         out_shapes,
     )(x)
-    message = by_token
+    message = jnp.concatenate([by_token, by_row[: rows // 2]], axis=0)
+    both = in_order(message, *swap_parts([message], "col", 0, n), "col", 0, 0)
+    message = both[:, : rows // 2 + own]
     held = [message]
-    for k in range(1, n):
+    for k in range(2, n, 2):
         held.append(lax.ppermute(message, "col", [(j, j ^ k) for j in range(n)]))
-    held = unswap(jnp.stack(held), "col")
-    seen_i = held[:, rows // 2 :].reshape(block, LANES)
-    parts = held[:, : rows // 2].reshape(n, rows // 2, 2, features)
-    mi = parts.transpose(0, 2, 1, 3).reshape(block * depth, features)
-    message = by_row
+    a_pieces = held
+    if own % 16:
+        held = unswap(jnp.stack(held), "col").reshape((n,) + message.shape[1:])
+        parts = held[:, : rows // 2].reshape(n, rows // 2, 2, features)
+        mi = parts.transpose(0, 2, 1, 3).reshape(block * depth, features)
+        a_pieces = [mi, held[:, rows // 2 :].reshape(block, LANES)]
+    message = both[:, rows // 2 :]
     held = []
-    for k in range(n):
+    for k in range(0, n, 2):
         pairs = [(i * n + j, (j ^ k) * n + i) for i in range(n) for j in range(n)]
         held.append(lax.ppermute(message, axes, pairs))
-    held = unswap(jnp.stack(held), "row")
-    seen_j = held[:, rows // 2 :].reshape(block, LANES)
-    parts = held[:, : rows // 2].reshape(n, depth // 2, own, 2, features)
-    mj = parts.transpose(3, 1, 0, 2, 4).reshape(depth, block, features)
+    j_pieces = held
+    if own % 16:
+        held = unswap(jnp.stack(held), "row").reshape((n,) + message.shape[1:])
+        parts = held[:, own:].reshape(n, depth // 2, own, 2, features)
+        mj = parts.transpose(3, 1, 0, 2, 4).reshape(depth, block, features)
+        j_pieces = [mj, held[:, :own].reshape(block, LANES)]
 
     wide = width * depth
     tokens = block * depth
     source = jnp.arange(wide)
     perm = (jnp.arange(wide)[None, :] == (source % width * depth + source // width)[:, None]).astype(BF16)
     up_spec = pl.BlockSpec((chunk, block, pair), lambda g: (g, 0, 0))
-    args = (sitewise_factors, pairing_matrix, offset)
+    args = (sitewise_factors, pairing_matrix, offset, upstream_adjoint, *a_pieces)
     out_shapes = [
         sds((2 * width, features), BF16),
         sds((width, width * pair), BF16),
         sds((1, pair), F32),
+        sds((8, pair), F32),
+        sds((tokens, width), BF16),
+        sds((width + features, tokens), BF16),
+        sds((block, LANES), BF16),
     ]
-    factors_t, pairing_wide, offset = call(
-        factor_kernel,
+    factors_t, pairing_wide, offset, bias, a, a_t, seen = call(
+        functools.partial(factor_kernel, own, len(a_pieces)),
         (),
         [full(v.shape) for v in args],
         [full(o.shape) for o in out_shapes],
         out_shapes,
-        [pltpu.VMEM((width * width, pair), F32)],
+        [pltpu.VMEM((width * width, pair), F32), pltpu.VMEM((tokens, features), BF16)],
+        cost(3e9, 4e6),
     )(*args)
 
     out_shapes = [
-        sds((tokens, width), BF16),
-        sds((block, wide), BF16),
-        sds((wide, block), BF16),
-        sds((steps, block, chunk), F32),
-        sds((8, pair), F32),
+        sds((tokens + block * wide // LANES + block * steps, LANES), BF16),
         sds((width * width, pair), BF16),
         sds((width, features), F32),
+        sds((depth, block, features), BF16),
     ]
-    args = (mi, mj, seen_i, seen_j, factors_t, perm, pairing_wide)
+    args = (a, a_t, seen, factors_t, perm, pairing_wide, *j_pieces)
     large = 2 * chunk
     large_spec = pl.BlockSpec((large, block, pair), lambda g: (g, 0, 0))
-    outs = call(
-        functools.partial(weight_kernel, depth, features),
+    scaled, held, d_pairing, left, mj = call(
+        functools.partial(weight_kernel, depth, features, own, len(j_pieces), chunk),
         (block // large,),
         [large_spec] + [full(v.shape) for v in args],
         [large_spec] + [full(o.shape) for o in out_shapes],
         [sds(upstream_adjoint.shape, BF16)] + out_shapes,
         [
-            pltpu.VMEM((width + features, tokens), BF16),
+            pltpu.VMEM((block, LANES), BF16),
+            pltpu.VMEM((wide, block), BF16),
+            pltpu.VMEM((steps, block, chunk), F32),
             pltpu.VMEM((width, large * depth, pair), BF16),
             pltpu.VMEM((width * width, pair), F32),
             pltpu.VMEM((features, width * pair), F32),
         ],
         cost(5e9, 8e6),
     )(upstream_adjoint, *args)
-    scaled, a, b, b_t, inv, bias, d_pairing, left = outs
 
     d_pairing = d_pairing.reshape(n, -1, LANES)
     for bit in reversed(range(1, bits)):
@@ -448,13 +502,12 @@
         functools.partial(token_kernel, depth, features, n),
         (steps,),
         [up_spec]
-        + [full(v.shape) for v in (a, pairing_wide, mj, perm, bias, left)]
-        + [pl.BlockSpec(memory_space=pl.ANY)] * 4,
+        + [full(v.shape) for v in (held, pairing_wide, mj, perm, bias, left)],
         [full(o.shape) for o in out_shapes],
         out_shapes,
         [pltpu.VMEM((chunk, wide, pair), BF16), pltpu.VMEM((wide, block), F32)],
         cost(8e9, 8e6),
-    )(scaled, a, pairing_wide, mj, perm, bias, left, b, b_t, inv, offset)
+    )(scaled, held, pairing_wide, mj, perm, bias, left)
 
     dp_keep, dp_go = halves(d_pairing, "col", 0, 0)
     db_keep, db_go = halves(d_b.reshape((n // 2, 2) + d_b.shape[1:]), "col", 0, 1)
@@ -465,7 +518,7 @@
     for bit in range(bits):
         parts = swap_parts([d_pairing, db_go, small], "row", bit, n)
         if bit == 0:
-            args = (inv, a, b, offset, pairing_wide, small)
+            args = (held, offset, pairing_wide, small)
             coupling_update, small = call(
                 functools.partial(update_kernel, depth),
                 (steps,),
@@ -481,16 +534,17 @@
             *d_a, small = call(
                 functools.partial(left_kernel, depth, bits - 1),
                 (steps,),
-                [up_spec] + [full(v.shape) for v in (b_t, pairing_wide, small)],
+                [up_spec] + [full(v.shape) for v in (held, pairing_wide, small)],
                 [full(o.shape) for o in out_shapes],
                 out_shapes,
                 [
                     pltpu.VMEM((width, chunk * depth, pair), BF16),
                     pltpu.VMEM((width * pair, width), BF16),
                     pltpu.VMEM((tokens // LANES, width, LANES), BF16),
+                    pltpu.VMEM((wide, block), BF16),
                 ],
                 cost(6e9, 8e6),
-            )(scaled, b_t, pairing_wide, small)
+            )(scaled, held, pairing_wide, small)
             if rows % LANES:
                 shape = (-1, width, LANES // rows, rows)
                 d_a = [part.reshape(shape).transpose(0, 2, 1, 3) for part in d_a]

time: 60.2 us -> 56.3 us (0.935)
  starting transfers between devices: 17.2 us -> 13 us
  waiting for transfers between devices: 9.94 us -> 13 us
  local copies, waits for them, and re-layouts: 3.14 us -> 0.28 us
    ppermute x4 -> x2, waiting for transfers between devices: 0.01 us -> 3.71 us  [per_device(): held.append(lax.ppermute(message, axes, pairs))]
    ppermute x4 -> x2, starting transfers between devices: 7.25 us -> 4.56 us  [per_device(): held.append(lax.ppermute(message, axes, pairs))]
    ppermute x3 -> x1, waiting for transfers between devices: 2.62 us -> 0.01 us  [per_device(): held.append(lax.ppermute(message, 'col', [(j, j ^ k) for j in range(n)]))]
    unnamed x23 -> x11, local copies, waits for them, and re-layouts: 2.25 us -> 0.03 us
    ppermute x6 -> x7, waiting for transfers between devices: 7.32 us -> 9.27 us  [swap_parts(): message = lax.ppermute(message, axis, pairs)]
    ppermute x3 -> x1, starting transfers between devices: 4.57 us -> 2.9 us  [per_device(): held.append(lax.ppermute(message, 'col', [(j, j ^ k) for j in range(n)]))]
    ppermute x6 -> x7, starting transfers between devices: 5.43 us -> 5.56 us  [swap_parts(): message = lax.ppermute(message, axis, pairs)]
  transfers between devices with their start and end apart: 13 -> 10, of which waited for: 5 -> 7; matrix products, arithmetic and copies ran while one was open for 0% -> 0% of each run, Pallas kernels for 28% -> 31%
where the time goes in v12:
time: 56.3 us; the launch traced here: 56.1 us
  Pallas kernels  27.2 us (48%)
  starting transfers between devices  13 us (23%)
  waiting for transfers between devices  13 us (23%)
  other arithmetic  1.56 us (3%)
  between operations  1.06 us (2%)
    ppermute x7, waiting for transfers between devices, swap_parts(): message = lax.ppermute(message, axis, pairs)  9.27 us
    pallas_call x1, Pallas kernels, per_device(): call(functools.partial(weight_kernel, depth, features, own, len(j_pieces)...  6.81 us
    pallas_call x1, Pallas kernels, per_device(): call(functools.partial(left_kernel, depth, bits - 1), (steps,), [up_spec]...  6.11 us
    ppermute x7, starting transfers between devices, swap_parts(): message = lax.ppermute(message, axis, pairs)  5.56 us
    pallas_call x1, Pallas kernels, per_device(): call(functools.partial(token_kernel, depth, features, n), (steps,), [up_s...  5.56 us
    pallas_call x1, Pallas kernels, per_device(): call(functools.partial(update_kernel, depth), (steps,), [full(v.shape) fo...  4.92 us
    ppermute x2, starting transfers between devices, per_device(): held.append(lax.ppermute(message, axes, pairs))  4.56 us
    ppermute x2, waiting for transfers between devices, per_device(): held.append(lax.ppermute(message, axes, pairs))  3.71 us
  transfers between devices with their start and end apart: 10, of which 7 were waited for; matrix products, arithmetic and copies ran while one was open for 0% of the time, Pallas kernels for 31%

profile of v12, /device:TPU:0, one launch (start us, length us, event | category | flops | bytes accessed | tf_op | source)
XLA Modules:
  0.0 56.1 jit_solution(2161585757030014545)
XLA Ops:
  0.6 0.0 copy-start.4
  0.6 0.0 copy-start
  0.7 0.9 %multiply_convert_fusion = bf16[16,16]{1,0:T(8,128)(2,1)S(1)} fusion(s32[16,16]{1,0:T(8,128)} %param.8, s32[16]{0:T(128)} %param.9), kind=kLoop, calls=%fused_computation.52 | loop fusion | flops 512 | bytes 1600 | tf_op jit(solution)/shard_map/convert_element_type | solution.py:408
  1.5 0.1 broadcast_in_dim.2
  1.6 0.0 copy-done.4
  1.6 0.1 pad_maximum_fusion.9
  1.7 0.5 shard_map.110
  2.3 0.5 collective-permute-start
  2.8 0.9 %collective-permute-done = bf16[272,128]{1,0:T(8,128)(2,1)S(1)} collective-permute-done((bf16[272,128]{1,0:T(8,128)(2,1)S(1)}, bf16[272,128]{1,0:T(8,128)(2,1)S(1)}, u32[]{:S(2)}, u32[]{:S(2)}) %collective-permute-start) | collective-permute-done | bytes 69664 | tf_op jit(solution)/shard_map/ppermute | solution.py:351
  3.8 0.0 copy-start.1
  3.8 2.9 %collective-permute-start.1 = (bf16[2,144,128]{2,1,0:T(8,128)(2,1)S(1)}, bf16[2,144,128]{2,1,0:T(8,128)(2,1)S(1)}, u32[]{:S(2)}, u32[]{:S(2)}) collective-permute-start(bf16[2,144,128]{2,1,0:T(8,128)(2,1)S(1)} %get-tuple-element.60.refs_0_), channel_id=1, source_target_pairs={{0,2},{1,3},{2,0},{3,1},{4,6},{5,7},{6,4},{7,5},{8,10},{9,11},{10,... | collective-permute-start | bytes 221192 | tf_op jit(solution)/shard_map/ppermute | solution.py:425
  6.7 0.1 fusion.refs_5_.refs_4_.refs_7_
  6.8 0.0 copy-start.2
  6.9 0.0 copy-start.3
  6.9 0.7 %collective-permute-start.2 = (bf16[2,144,128]{2,1,0:T(8,128)(2,1)S(1)}, bf16[2,144,128]{2,1,0:T(8,128)(2,1)S(1)}, u32[]{:S(2)}, u32[]{:S(2)}) collective-permute-start(bf16[2,144,128]{2,1,0:T(8,128)(2,1)S(1)} %get-tuple-element.59), channel_id=1, source_target_pairs={{0,0},{1,4},{2,8},{3,12},{4,1},{5,5},{6,9},{7,13},{8,2},{9,6},{10,... | collective-permute-start | bytes 221192 | tf_op jit(solution)/shard_map/ppermute | solution.py:436
  7.5 3.9 %collective-permute-start.3 = (bf16[2,144,128]{2,1,0:T(8,128)(2,1)S(1)}, bf16[2,144,128]{2,1,0:T(8,128)(2,1)S(1)}, u32[]{:S(2)}, u32[]{:S(2)}) collective-permute-start(bf16[2,144,128]{2,1,0:T(8,128)(2,1)S(1)} %get-tuple-element.59), channel_id=1, source_target_pairs={{0,8},{1,12},{2,0},{3,4},{4,9},{5,13},{6,1},{7,5},{8,10},{9,14},{1... | collective-permute-start | bytes 221192 | tf_op jit(solution)/shard_map/ppermute | solution.py:436
  11.4 0.0 collective-permute-done.1.refs_1_
  11.4 0.0 copy-done
  11.4 0.0 copy-done.1
  11.5 0.0 copy-done.2
  11.5 0.0 copy-done.3
  11.5 0.8 %shard_map.111 = (bf16[64,64]{1,0:T(8,128)(2,1)S(1)}, bf16[32,4096]{1,0:T(8,128)(2,1)S(1)}, f32[1,128]{1,0:T(1,128)S(1)}, f32[8,128]{1,0:T(8,128)S(1)}, bf16[102...) custom-call(bf16[64,64]{1,0:T(8,128)(2,1)S(1)} %copy-done.2, ...), custom_call_target="tpu_custom_call" | custom-call | flops 3000000000 | bytes 4000000 | tf_op jit(solution)/shard_map/pallas_call | solution.py:459
  12.3 0.0 collective-permute-done.2.refs_7_
  12.3 3.7 %collective-permute-done.3.refs_8_ = bf16[2,144,128]{2,1,0:T(8,128)(2,1)S(1)} collective-permute-done((bf16[2,144,128]{2,1,0:T(8,128)(2,1)S(1)}, bf16[2,144,128]{2,1,0:T(8,128)(2,1)S(1)}, u32[]{:S(2)}, u32[]{:S(2)}) %collective-permute-start.3) | collective-permute-done | bytes 73760 | tf_op jit(solution)/shard_map/ppermute | solution.py:436
  16.0 6.8 %shard_map.112 = (bf16[64,64,128]{2,1,0:T(8,128)(2,1)S(1)}, bf16[1536,128]{1,0:T(8,128)(2,1)S(1)}, bf16[1024,128]{1,0:T(8,128)(2,1)S(1)}, f32[32,64]{1,0:T(8,128)S(1)}, bf16[16,64,64]{2,1,0:T(8,128)(2,1)S(1)}) custom-call(bf16[64,64,128]{2,1,0:T(8,128)(2,1)S(1)} %copy-done, bf16[1024,32]{1,0:T(8,128)(2,1)S(1)} %get-tuple-element.32.refs_1_, ...), custom_call_target="tpu_custom_call" | custom-call | flops 5000000000 | bytes 8000000 | tf_op jit(solution)/shard_map/pallas_call | solution.py:478
  22.9 2.6 %collective-permute-start.4 = (bf16[512,128]{1,0:T(8,128)(2,1)S(1)}, bf16[512,128]{1,0:T(8,128)(2,1)S(1)}, u32[]{:S(2)}, u32[]{:S(2)}) collective-permute-start(bf16[512,128]{1,0:T(8,128)(2,1)S(1)} %bitcast.104), channel_id=1, source_target_pairs={{0,2},{1,3},{2,0},{3,1},{4,6},{5,7},{6,4},{7,5},{8,10},{9,11},{10,... | collective-permute-start | bytes 393224 | tf_op jit(solution)/shard_map/ppermute | solution.py:351
  25.5 5.6 %shard_map.113 = (bf16[48,128]{1,0:T(8,128)(2,1)S(1)}, bf16[4,64,128]{2,1,0:T(8,128)(2,1)S(1)}) custom-call(bf16[64,64,128]{2,1,0:T(8,128)(2,1)S(1)} %get-tuple-element.39.refs_0_, bf16[1536,128]{1,0:T(8,128)(2,1)S(1)} %get-tuple-element.37.refs_1_.refs_0_, bf16[32,4096]{1,0:T(8,128)(2,1)S(1)} %get-tuple-element.36.refs_6_.refs_2_, ...), custom_call_target="tpu_custom_call" | custom-call | flops 8000000000 | bytes 8000000 | tf_op jit(solution)/shard_map/pallas_call | solution.py:501
  31.1 0.0 collective-permute-done.4
  31.2 0.8 %collective-permute-start.5 = (bf16[432,128]{1,0:T(8,128)(2,1)S(1)}, bf16[432,128]{1,0:T(8,128)(2,1)S(1)}, u32[]{:S(2)}, u32[]{:S(2)}) collective-permute-start(bf16[432,128]{1,0:T(8,128)(2,1)S(1)} %pad_maximum_fusion.4), channel_id=1, source_target_pairs={{0,1},{1,0},{2,3},{3,2},{4,5},{5,4},{6,7},{7,6},{8,9},{9,8},{10,11... | collective-permute-start | bytes 331784 | tf_op jit(solution)/shard_map/ppermute | solution.py:351
  32.0 1.0 %collective-permute-done.5 = bf16[432,128]{1,0:T(8,128)(2,1)S(1)} collective-permute-done((bf16[432,128]{1,0:T(8,128)(2,1)S(1)}, bf16[432,128]{1,0:T(8,128)(2,1)S(1)}, u32[]{:S(2)}, u32[]{:S(2)}) %collective-permute-start.5) | collective-permute-done | bytes 110624 | tf_op jit(solution)/shard_map/ppermute | solution.py:351
  33.1 0.1 collective-permute-start.6
  33.1 4.9 %shard_map.114 = (bf16[64,64,128]{2,1,0:T(8,128)(2,1)}, bf16[48,128]{1,0:T(8,128)(2,1)S(1)}) custom-call(bf16[1536,128]{1,0:T(8,128)(2,1)S(1)} %get-tuple-element.37.refs_1_.refs_0_, f32[1,128]{1,0:T(1,128)S(1)} %get-tuple-element.38.refs_1_, bf16[32,4096]{1,0:T(8,128)(2,1)S(1)} %get-tuple-element.36.refs_6_.refs_2_, ...), custom_call_target="tpu_custom_call" | custom-call | flops 6000000000 | bytes 8000000 | tf_op jit(solution)/shard_map/pallas_call | solution.py:522
  38.1 0.4 collective-permute-done.6
  38.6 0.7 %collective-permute-start.7 = (bf16[432,128]{1,0:T(8,128)(2,1)S(1)}, bf16[432,128]{1,0:T(8,128)(2,1)S(1)}, u32[]{:S(2)}, u32[]{:S(2)}) collective-permute-start(bf16[432,128]{1,0:T(8,128)(2,1)S(1)} %pad_maximum_fusion.6), channel_id=1, source_target_pairs={{0,8},{4,12},{8,0},{12,4},{1,9},{5,13},{9,1},{13,5},{2,10},{6,14},... | collective-permute-start | bytes 331784 | tf_op jit(solution)/shard_map/ppermute | solution.py:351
  39.2 6.1 %shard_map.115 = (bf16[4,32,128]{2,1,0:T(8,128)(2,1)S(1)}, bf16[4,32,128]{2,1,0:T(8,128)(2,1)S(1)}, bf16[48,128]{1,0:T(8,128)(2,1)S(1)}) custom-call(bf16[64,64,128]{2,1,0:T(8,128)(2,1)S(1)} %get-tuple-element.39.refs_0_, bf16[1536,128]{1,0:T(8,128)(2,1)S(1)} %get-tuple-element.37.refs_1_.refs_0_, bf16[32,4096]{1,0:T(8,128)(2,1)S(1)} %get-tuple-element.36.refs_6_.refs_2_, ...), custom_call_target="tpu_custom_call" | custom-call | flops 6000000000 | bytes 8000000 | tf_op jit(solution)/shard_map/pallas_call | solution.py:534
  45.4 1.5 %collective-permute-done.7 = bf16[432,128]{1,0:T(8,128)(2,1)S(1)} collective-permute-done((bf16[432,128]{1,0:T(8,128)(2,1)S(1)}, bf16[432,128]{1,0:T(8,128)(2,1)S(1)}, u32[]{:S(2)}, u32[]{:S(2)}) %collective-permute-start.7) | collective-permute-done | bytes 110624 | tf_op jit(solution)/shard_map/ppermute | solution.py:351
  47.0 0.8 %collective-permute-start.8 = (bf16[496,128]{1,0:T(8,128)(2,1)S(1)}, bf16[496,128]{1,0:T(8,128)(2,1)S(1)}, u32[]{:S(2)}, u32[]{:S(2)}) collective-permute-start(bf16[496,128]{1,0:T(8,128)(2,1)S(1)} %pad_maximum_fusion.3), channel_id=1, source_target_pairs={{0,2},{1,3},{2,0},{3,1},{4,6},{5,7},{6,4},{7,5},{8,10},{9,11},{10,... | collective-permute-start | bytes 380936 | tf_op jit(solution)/shard_map/ppermute | solution.py:351
  47.8 4.2 %collective-permute-done.8 = bf16[496,128]{1,0:T(8,128)(2,1)S(1)} collective-permute-done((bf16[496,128]{1,0:T(8,128)(2,1)S(1)}, bf16[496,128]{1,0:T(8,128)(2,1)S(1)}, u32[]{:S(2)}, u32[]{:S(2)}) %collective-permute-start.8) | collective-permute-done | bytes 127008 | tf_op jit(solution)/shard_map/ppermute | solution.py:351
  52.1 0.1 collective-permute-start.9
  52.2 1.3 %collective-permute-done.9 = bf16[576,128]{1,0:T(8,128)(2,1)S(1)} collective-permute-done((bf16[576,128]{1,0:T(8,128)(2,1)S(1)}, bf16[576,128]{1,0:T(8,128)(2,1)S(1)}, u32[]{:S(2)}, u32[]{:S(2)}) %collective-permute-start.9) | collective-permute-done | bytes 147488 | tf_op jit(solution)/shard_map/ppermute | solution.py:351
  53.7 2.4 %shard_map.116 = (f32[256,64]{1,0:T(8,128)}, f32[64,64]{1,0:T(8,128)}, f32[1,128]{1,0:T(1,128)}, f32[32,32,128]{2,1,0:T(8,128)}) custom-call(bf16[32,256]{1,0:T(8,128)(2,1)S(1)} %bitcast.89, bf16[32,256]{1,0:T(8,128)(2,1)S(1)} %bitcast.90, bf16[16,512]{1,0:T(8,128)(2,1)S(1)} %bitcast.88, bf16[48,128]{1,0:T(8,128)(2,1)S(1)} %add_convert_fusion.2.refs_3_, ...), custom_call_target="tpu_custom_call" | custom-call | tf_op jit(solution)/shard_map/pallas_call | solution.py:582
  (44 shorter events, 0.6 us)
Async XLA Ops:
  0.6 1.0 %copy-start.4 = (bf16[16,16,64]{2,1,0:T(8,128)(2,1)S(1)}, bf16[16,16,64]{2,1,0:T(8,128)(2,1)}, u32[]{:S(2)}) copy-start(bf16[16,16,64]{2,1,0:T(8,128)(2,1)} %param.7) | copy-start | bytes 98308
  0.6 10.8 %copy-start = (bf16[64,64,128]{2,1,0:T(8,128)(2,1)S(1)}, bf16[64,64,128]{2,1,0:T(8,128)(2,1)}, u32[]{:S(2)}) copy-start(bf16[64,64,128]{2,1,0:T(8,128)(2,1)} %refs_0_.1) | copy-start | bytes 3145732
  2.3 1.4 %collective-permute-start = (bf16[272,128]{1,0:T(8,128)(2,1)S(1)}, bf16[272,128]{1,0:T(8,128)(2,1)S(1)}, u32[]{:S(2)}, u32[]{:S(2)}) collective-permute-start(bf16[272,128]{1,0:T(8,128)(2,1)S(1)} %pad_maximum_fusion.8), channel_id=1, source_target_pairs={{0,1},{1,0},{2,3},{3,2},{4,5},{5,4},{6,7},{7,6},{8,9},{9,8},{10,11... | collective-permute-start | bytes 208904 | tf_op jit(solution)/shard_map/ppermute | solution.py:351
  3.8 7.7 %copy-start.1 = (bf16[1024,128]{1,0:T(8,128)(2,1)S(1)}, bf16[1024,128]{1,0:T(8,128)(2,1)}, u32[]{:S(2)}) copy-start(bf16[1024,128]{1,0:T(8,128)(2,1)} %wide_ref.1) | copy-start | bytes 786436
  3.8 7.7 %collective-permute-start.1 = (bf16[2,144,128]{2,1,0:T(8,128)(2,1)S(1)}, bf16[2,144,128]{2,1,0:T(8,128)(2,1)S(1)}, u32[]{:S(2)}, u32[]{:S(2)}) collective-permute-start(bf16[2,144,128]{2,1,0:T(8,128)(2,1)S(1)} %get-tuple-element.60.refs_0_), channel_id=1, source_target_pairs={{0,2},{1,3},{2,0},{3,1},{4,6},{5,7},{6,4},{7,5},{8,10},{9,11},{10,... | collective-permute-start | bytes 221192 | tf_op jit(solution)/shard_map/ppermute | solution.py:425
  6.8 4.6 %copy-start.2 = (bf16[64,64]{1,0:T(8,128)(2,1)S(1)}, bf16[64,64]{1,0:T(8,128)(2,1)}, u32[]{:S(2)}) copy-start(bf16[64,64]{1,0:T(8,128)(2,1)} %w_ref.1) | copy-start | bytes 24580
  6.9 4.6 %copy-start.3 = (f32[128]{0:T(128)S(1)}, f32[128]{0:T(128)}, u32[]{:S(2)}) copy-start(f32[128]{0:T(128)} %param.12) | copy-start | bytes 1540
  6.9 5.4 %collective-permute-start.2 = (bf16[2,144,128]{2,1,0:T(8,128)(2,1)S(1)}, bf16[2,144,128]{2,1,0:T(8,128)(2,1)S(1)}, u32[]{:S(2)}, u32[]{:S(2)}) collective-permute-start(bf16[2,144,128]{2,1,0:T(8,128)(2,1)S(1)} %get-tuple-element.59), channel_id=1, source_target_pairs={{0,0},{1,4},{2,8},{3,12},{4,1},{5,5},{6,9},{7,13},{8,2},{9,6},{10,... | collective-permute-start | bytes 221192 | tf_op jit(solution)/shard_map/ppermute | solution.py:436
  7.5 8.5 %collective-permute-start.3 = (bf16[2,144,128]{2,1,0:T(8,128)(2,1)S(1)}, bf16[2,144,128]{2,1,0:T(8,128)(2,1)S(1)}, u32[]{:S(2)}, u32[]{:S(2)}) collective-permute-start(bf16[2,144,128]{2,1,0:T(8,128)(2,1)S(1)} %get-tuple-element.59), channel_id=1, source_target_pairs={{0,8},{1,12},{2,0},{3,4},{4,9},{5,13},{6,1},{7,5},{8,10},{9,14},{1... | collective-permute-start | bytes 221192 | tf_op jit(solution)/shard_map/ppermute | solution.py:436
  22.9 8.2 %collective-permute-start.4 = (bf16[512,128]{1,0:T(8,128)(2,1)S(1)}, bf16[512,128]{1,0:T(8,128)(2,1)S(1)}, u32[]{:S(2)}, u32[]{:S(2)}) collective-permute-start(bf16[512,128]{1,0:T(8,128)(2,1)S(1)} %bitcast.104), channel_id=1, source_target_pairs={{0,2},{1,3},{2,0},{3,1},{4,6},{5,7},{6,4},{7,5},{8,10},{9,11},{10,... | collective-permute-start | bytes 393224 | tf_op jit(solution)/shard_map/ppermute | solution.py:351
  31.2 1.8 %collective-permute-start.5 = (bf16[432,128]{1,0:T(8,128)(2,1)S(1)}, bf16[432,128]{1,0:T(8,128)(2,1)S(1)}, u32[]{:S(2)}, u32[]{:S(2)}) collective-permute-start(bf16[432,128]{1,0:T(8,128)(2,1)S(1)} %pad_maximum_fusion.4), channel_id=1, source_target_pairs={{0,1},{1,0},{2,3},{3,2},{4,5},{5,4},{6,7},{7,6},{8,9},{9,8},{10,11... | collective-permute-start | bytes 331784 | tf_op jit(solution)/shard_map/ppermute | solution.py:351
  33.1 5.4 %collective-permute-start.6 = (bf16[432,128]{1,0:T(8,128)(2,1)S(1)}, bf16[432,128]{1,0:T(8,128)(2,1)S(1)}, u32[]{:S(2)}, u32[]{:S(2)}) collective-permute-start(bf16[432,128]{1,0:T(8,128)(2,1)S(1)} %pad_maximum_fusion.5), channel_id=1, source_target_pairs={{0,4},{4,0},{8,12},{12,8},{1,5},{5,1},{9,13},{13,9},{2,6},{6,2},{1... | collective-permute-start | bytes 331784 | tf_op jit(solution)/shard_map/ppermute | solution.py:351
  38.6 8.3 %collective-permute-start.7 = (bf16[432,128]{1,0:T(8,128)(2,1)S(1)}, bf16[432,128]{1,0:T(8,128)(2,1)S(1)}, u32[]{:S(2)}, u32[]{:S(2)}) collective-permute-start(bf16[432,128]{1,0:T(8,128)(2,1)S(1)} %pad_maximum_fusion.6), channel_id=1, source_target_pairs={{0,8},{4,12},{8,0},{12,4},{1,9},{5,13},{9,1},{13,5},{2,10},{6,14},... | collective-permute-start | bytes 331784 | tf_op jit(solution)/shard_map/ppermute | solution.py:351
  47.0 5.0 %collective-permute-start.8 = (bf16[496,128]{1,0:T(8,128)(2,1)S(1)}, bf16[496,128]{1,0:T(8,128)(2,1)S(1)}, u32[]{:S(2)}, u32[]{:S(2)}) collective-permute-start(bf16[496,128]{1,0:T(8,128)(2,1)S(1)} %pad_maximum_fusion.3), channel_id=1, source_target_pairs={{0,2},{1,3},{2,0},{3,1},{4,6},{5,7},{6,4},{7,5},{8,10},{9,11},{10,... | collective-permute-start | bytes 380936 | tf_op jit(solution)/shard_map/ppermute | solution.py:351
  52.1 1.4 %collective-permute-start.9 = (bf16[576,128]{1,0:T(8,128)(2,1)S(1)}, bf16[576,128]{1,0:T(8,128)(2,1)S(1)}, u32[]{:S(2)}, u32[]{:S(2)}) collective-permute-start(bf16[576,128]{1,0:T(8,128)(2,1)S(1)} %pad_maximum_fusion.1), channel_id=1, source_target_pairs={{0,1},{1,0},{2,3},{3,2},{4,5},{5,4},{6,7},{7,6},{8,9},{9,8},{10,11... | collective-permute-start | bytes 442376 | tf_op jit(solution)/shard_map/ppermute | solution.py:351

commit v13 on v12

--- a/solution.py
+++ b/solution.py
@@ -106,7 +106,19 @@
     return jnp.concatenate([held_ref[at + k * block : at + (k + 1) * block, :] for k in range(tiles)], axis=1)
 
 
-def factor_kernel(own, pieces, w_ref, wide_ref, offset_ref, up_ref, *refs):
+def factor_kernel(own, depth, pieces, *refs):
+    g = pl.program_id(0)
+
+    @pl.when(g == 0)
+    def _():
+        factors(own, pieces, *refs[: 4 + pieces], *refs[5 + pieces :])
+
+    t_ref, _, wc_ref, _, _, a_ref = refs[4 + pieces : 10 + pieces]
+    span = t_ref.shape[0] * depth
+    fill_t(a_ref[pl.ds(pl.multiple_of(g * span, span), span), :], wc_ref, t_ref, depth)
+
+
+def factors(own, pieces, w_ref, wide_ref, offset_ref, up_ref, *refs):
     wt_ref, wc_ref, pass_ref, bias_ref, a_ref, at_ref, seen_ref, rows_ref, mi_ref = refs[pieces:]
     features, width = w_ref.shape[0], w_ref.shape[1] // 2
     pair = wide_ref.shape[1]
@@ -143,8 +155,8 @@
 
 
 def weight_kernel(depth, features, own, pieces, part_size, *refs):
-    up_ref, a_ref, at_ref, seen_i_ref, wt_ref, perm_ref, wc_ref = refs[:7]
-    j_refs, refs = refs[7 : 7 + pieces], refs[7 + pieces :]
+    up_ref, _, a_ref, at_ref, seen_i_ref, wt_ref, perm_ref, wc_ref = refs[:8]
+    j_refs, refs = refs[8 : 8 + pieces], refs[8 + pieces :]
     g_ref, held_ref, dw_ref, left_ref, mj_ref, seen_j_ref, bt_ref, inv_ref, v_ref, acc_ref, wide_ref = refs
     g, last = pl.program_id(0), pl.num_programs(0) - 1
     chunk, block, pair = up_ref.shape
@@ -248,8 +260,7 @@
 
 
 def token_kernel(depth, features, n, *refs):
-    g_ref, held_ref, wc_ref, mj_ref, perm_ref, bias_ref, left_ref = refs[:7]
-    small_ref, out_ref, t_ref, db_ref = refs[7:]
+    g_ref, t_ref, _, mj_ref, perm_ref, bias_ref, left_ref, small_ref, out_ref, db_ref = refs
     g, last = pl.program_id(0), pl.num_programs(0) - 1
     chunk, block = g_ref.shape[:2]
     width = left_ref.shape[0]
@@ -258,8 +269,6 @@
     def _():
         db_ref[...] = jnp.zeros_like(db_ref)
 
-    span = chunk * depth
-    fill_t(held_ref[pl.ds(pl.multiple_of(g * span, span), span), :width], wc_ref, t_ref, depth)
     t = jnp.concatenate([t_ref[i] for i in range(chunk)], axis=1)
     scaled = jnp.concatenate([g_ref[i] for i in range(chunk)], axis=1)
     db_ref[...] += dot_nt(t, scaled)
@@ -456,12 +465,13 @@
         sds((width + features, tokens), BF16),
         sds((block, LANES), BF16),
     ]
-    factors_t, pairing_wide, offset, bias, a, a_t, seen = call(
-        functools.partial(factor_kernel, own, len(a_pieces)),
-        (),
+    t_spec = pl.BlockSpec((chunk, wide, pair), lambda g: (g, 0, 0))
+    t, factors_t, pairing_wide, offset, bias, a, a_t, seen = call(
+        functools.partial(factor_kernel, own, depth, len(a_pieces)),
+        (steps,),
         [full(v.shape) for v in args],
-        [full(o.shape) for o in out_shapes],
-        out_shapes,
+        [t_spec] + [full(o.shape) for o in out_shapes],
+        [sds((block, wide, pair), BF16)] + out_shapes,
         [pltpu.VMEM((width * width, pair), F32), pltpu.VMEM((tokens, features), BF16)],
         cost(3e9, 4e6),
     )(*args)
@@ -478,7 +488,7 @@
     scaled, held, d_pairing, left, mj = call(
         functools.partial(weight_kernel, depth, features, own, len(j_pieces), chunk),
         (block // large,),
-        [large_spec] + [full(v.shape) for v in args],
+        [large_spec, pl.BlockSpec(memory_space=pl.ANY)] + [full(v.shape) for v in args],
         [large_spec] + [full(o.shape) for o in out_shapes],
         [sds(upstream_adjoint.shape, BF16)] + out_shapes,
         [
@@ -490,7 +500,7 @@
             pltpu.VMEM((features, width * pair), F32),
         ],
         cost(5e9, 8e6),
-    )(upstream_adjoint, *args)
+    )(upstream_adjoint, t, *args)
 
     d_pairing = d_pairing.reshape(n, -1, LANES)
     for bit in reversed(range(1, bits)):
@@ -501,13 +511,12 @@
     small, d_b = call(
         functools.partial(token_kernel, depth, features, n),
         (steps,),
-        [up_spec]
-        + [full(v.shape) for v in (held, pairing_wide, mj, perm, bias, left)],
+        [up_spec, t_spec] + [full(v.shape) for v in (held, mj, perm, bias, left)],
         [full(o.shape) for o in out_shapes],
         out_shapes,
-        [pltpu.VMEM((chunk, wide, pair), BF16), pltpu.VMEM((wide, block), F32)],
+        [pltpu.VMEM((wide, block), F32)],
         cost(8e9, 8e6),
-    )(scaled, held, pairing_wide, mj, perm, bias, left)
+    )(scaled, t, held, mj, perm, bias, left)
 
     dp_keep, dp_go = halves(d_pairing, "col", 0, 0)
     db_keep, db_go = halves(d_b.reshape((n // 2, 2) + d_b.shape[1:]), "col", 0, 1)
@@ -533,12 +542,12 @@
             out_shapes = [sds(half, BF16), sds(half, BF16), sds(small.shape, BF16)]
             *d_a, small = call(
                 functools.partial(left_kernel, depth, bits - 1),
-                (steps,),
-                [up_spec] + [full(v.shape) for v in (held, pairing_wide, small)],
+                (block // large,),
+                [large_spec] + [full(v.shape) for v in (held, pairing_wide, small)],
                 [full(o.shape) for o in out_shapes],
                 out_shapes,
                 [
-                    pltpu.VMEM((width, chunk * depth, pair), BF16),
+                    pltpu.VMEM((width, large * depth, pair), BF16),
                     pltpu.VMEM((width * pair, width), BF16),
                     pltpu.VMEM((tokens // LANES, width, LANES), BF16),
                     pltpu.VMEM((wide, block), BF16),

time: 56.3 us -> 62.1 us (1.10)
  waiting for transfers between devices: 13 us -> 8.17 us
  Pallas kernels: 27.2 us -> 31.1 us
  local copies, waits for them, and re-layouts: 0.28 us -> 3.8 us
  starting transfers between devices: 13 us -> 15.2 us
  other arithmetic: 1.56 us -> 2.4 us
    pallas_call x2, Pallas kernels: 6.93 us -> 13 us  [the longest x1 9.41 us: per_device(): call(functools.partial(left_kernel, depth, bits - 1), (block // large,),...]
    ppermute x2, waiting for transfers between devices: 3.71 us -> 0.01 us  [per_device(): held.append(lax.ppermute(message, axes, pairs))]
    unnamed x11, local copies, waits for them, and re-layouts: 0.03 us -> 3.56 us
    ppermute x7, starting transfers between devices: 5.56 us -> 7.78 us  [swap_parts(): message = lax.ppermute(message, axis, pairs)]
    pallas_call x1, Pallas kernels: 5.56 us -> 3.42 us  [per_device(): call(functools.partial(token_kernel, depth, features, n), (steps,), [up_s...]
    ppermute x7, waiting for transfers between devices: 9.27 us -> 8.16 us  [swap_parts(): message = lax.ppermute(message, axis, pairs)]
    concatenate x1, other arithmetic: 0.09 us -> 0.93 us  [per_device(): jnp.concatenate([alignment_embedding, mask], axis=2).reshape(rows, LANES)]
  transfers between devices with their start and end apart: 10 -> 10, of which waited for: 7 -> 5; matrix products, arithmetic and copies ran while one was open for 0% -> 0% of each run, Pallas kernels for 31% -> 34%
where the time goes in v13:
time: 62.1 us; the launch traced here: 61.8 us
  Pallas kernels  31.1 us (50%)
  starting transfers between devices  15.2 us (24%)
  waiting for transfers between devices  8.17 us (13%)
  local copies, waits for them, and re-layouts  3.8 us (6%)
  other arithmetic  2.4 us (4%)
  between operations  1.03 us (2%)
    pallas_call x1, Pallas kernels, per_device(): call(functools.partial(left_kernel, depth, bits - 1), (block // large,),...  9.41 us
    ppermute x7, waiting for transfers between devices, swap_parts(): message = lax.ppermute(message, axis, pairs)  8.16 us
    ppermute x7, starting transfers between devices, swap_parts(): message = lax.ppermute(message, axis, pairs)  7.78 us
    pallas_call x1, Pallas kernels, per_device(): call(functools.partial(weight_kernel, depth, features, own, len(j_pieces)...  6.83 us
    pallas_call x1, Pallas kernels, per_device(): call(functools.partial(update_kernel, depth), (steps,), [full(v.shape) fo...  4.89 us
    ppermute x2, starting transfers between devices, per_device(): held.append(lax.ppermute(message, axes, pairs))  4.56 us
    pallas_call x1, Pallas kernels, per_device(): call(functools.partial(factor_kernel, own, depth, len(a_pieces)), (steps,...  3.59 us
    unnamed x11, local copies, waits for them, and re-layouts  3.56 us
  transfers between devices with their start and end apart: 10, of which 5 were waited for; matrix products, arithmetic and copies ran while one was open for 0% of the time, Pallas kernels for 34%

profile of v13, /device:TPU:0, one launch (start us, length us, event | category | flops | bytes accessed | tf_op | source)
XLA Modules:
  0.0 61.8 jit_solution(8228902901408316256)
XLA Ops:
  0.6 0.0 copy-start.1
  0.6 0.9 %multiply_convert_fusion = bf16[16,16]{1,0:T(8,128)(2,1)S(1)} fusion(s32[16,16]{1,0:T(8,128)} %param.8, s32[16]{0:T(128)} %param.9), kind=kLoop, calls=%fused_computation.52 | loop fusion | flops 512 | bytes 1600 | tf_op jit(solution)/shard_map/convert_element_type | solution.py:417
  1.5 0.1 broadcast_in_dim.2
  1.6 0.9 %pad_maximum_fusion.9 = bf16[16,16,128]{2,1,0:T(8,128)(2,1)S(1)} fusion(bf16[16,16,64]{2,1,0:T(8,128)(2,1)S(1)} %broadcast_in_dim.2, bf16[16,16,64]{2,1,0:T(8,128)(2,1)} %param.7), kind=kLoop, calls=%fused_computation.28 | loop fusion | flops 131072 | bytes 131072 | tf_op jit(solution)/shard_map/concatenate | solution.py:419
  2.5 0.5 shard_map.110
  3.1 0.5 collective-permute-start
  3.6 0.9 %collective-permute-done = bf16[272,128]{1,0:T(8,128)(2,1)S(1)} collective-permute-done((bf16[272,128]{1,0:T(8,128)(2,1)S(1)}, bf16[272,128]{1,0:T(8,128)(2,1)S(1)}, u32[]{:S(2)}, u32[]{:S(2)}) %collective-permute-start) | collective-permute-done | bytes 69664 | tf_op jit(solution)/shard_map/ppermute | solution.py:360
  4.6 2.9 %collective-permute-start.1 = (bf16[2,144,128]{2,1,0:T(8,128)(2,1)S(1)}, bf16[2,144,128]{2,1,0:T(8,128)(2,1)S(1)}, u32[]{:S(2)}, u32[]{:S(2)}) collective-permute-start(bf16[2,144,128]{2,1,0:T(8,128)(2,1)S(1)} %get-tuple-element.62.refs_4_), channel_id=1, source_target_pairs={{0,2},{1,3},{2,0},{3,1},{4,6},{5,7},{6,4},{7,5},{8,10},{9,11},{10,... | collective-permute-start | bytes 221192 | tf_op jit(solution)/shard_map/ppermute | solution.py:434
  7.5 0.1 fusion.refs_6_.refs_4_.refs_7_
  7.7 0.7 %collective-permute-start.2 = (bf16[2,144,128]{2,1,0:T(8,128)(2,1)S(1)}, bf16[2,144,128]{2,1,0:T(8,128)(2,1)S(1)}, u32[]{:S(2)}, u32[]{:S(2)}) collective-permute-start(bf16[2,144,128]{2,1,0:T(8,128)(2,1)S(1)} %get-tuple-element.61), channel_id=1, source_target_pairs={{0,0},{1,4},{2,8},{3,12},{4,1},{5,5},{6,9},{7,13},{8,2},{9,6},{10,... | collective-permute-start | bytes 221192 | tf_op jit(solution)/shard_map/ppermute | solution.py:445
  8.3 3.9 %collective-permute-start.3 = (bf16[2,144,128]{2,1,0:T(8,128)(2,1)S(1)}, bf16[2,144,128]{2,1,0:T(8,128)(2,1)S(1)}, u32[]{:S(2)}, u32[]{:S(2)}) collective-permute-start(bf16[2,144,128]{2,1,0:T(8,128)(2,1)S(1)} %get-tuple-element.61), channel_id=1, source_target_pairs={{0,8},{1,12},{2,0},{3,4},{4,9},{5,13},{6,1},{7,5},{8,10},{9,14},{1... | collective-permute-start | bytes 221192 | tf_op jit(solution)/shard_map/ppermute | solution.py:445
  12.2 0.0 collective-permute-done.1.refs_5_
  12.2 0.0 copy-start
  12.2 1.2 %copy-done = bf16[64,64,128]{2,1,0:T(8,128)(2,1)S(1)} copy-done((bf16[64,64,128]{2,1,0:T(8,128)(2,1)S(1)}, bf16[64,64,128]{2,1,0:T(8,128)(2,1)}, u32[]{:S(2)}) %copy-start) | copy-done | bytes 1048600
  13.5 0.0 copy-start.2
  13.5 0.9 %copy-done.2 = bf16[1024,128]{1,0:T(8,128)(2,1)S(1)} copy-done((bf16[1024,128]{1,0:T(8,128)(2,1)S(1)}, bf16[1024,128]{1,0:T(8,128)(2,1)}, u32[]{:S(2)}) %copy-start.2) | copy-done | bytes 262168
  14.4 0.0 copy-start.3
  14.4 0.7 %copy-done.3 = bf16[64,64]{1,0:T(8,128)(2,1)S(1)} copy-done((bf16[64,64]{1,0:T(8,128)(2,1)S(1)}, bf16[64,64]{1,0:T(8,128)(2,1)}, u32[]{:S(2)}) %copy-start.3) | copy-done | bytes 8216
  15.1 0.0 copy-start.4
  15.1 0.7 %copy-done.4 = f32[128]{0:T(128)S(1)} copy-done((f32[128]{0:T(128)S(1)}, f32[128]{0:T(128)}, u32[]{:S(2)}) %copy-start.4) | copy-done | bytes 536
  15.8 3.6 %shard_map.111 = (bf16[64,512,128]{2,1,0:T(8,128)(2,1)S(1)}, bf16[64,64]{1,0:T(8,128)(2,1)S(1)}, bf16[32,4096]{1,0:T(8,128)(2,1)S(1)}, f32[1,128]{1,0:T(1,128)S(...) custom-call(bf16[64,64]{1,0:T(8,128)(2,1)S(1)} %copy-done.3, ...), custom_call_target="tpu_custom_call" | custom-call | flops 3000000000 | bytes 4000000 | tf_op jit(solution)/shard_map/pallas_call | solution.py:469
  19.4 0.0 collective-permute-done.2.refs_8_
  19.4 0.0 collective-permute-done.3.refs_9_
  19.4 0.0 copy-done.1
  19.4 6.8 %shard_map.112 = (bf16[64,64,128]{2,1,0:T(8,128)(2,1)S(1)}, bf16[1536,128]{1,0:T(8,128)(2,1)S(1)}, bf16[1024,128]{1,0:T(8,128)(2,1)S(1)}, f32[32,64]{1,0:T(8,128)S(1)}, bf16[16,64,64]{2,1,0:T(8,128)(2,1)S(1)}) custom-call(bf16[64,64,128]{2,1,0:T(8,128)(2,1)S(1)} %copy-done.1, bf16[64,512,128]{2,1,0:T(8,128)(2,1)S(1)} %get-tuple-element.33.refs_1_, ...), custom_call_target="tpu_custom_call" | custom-call | flops 5000000000 | bytes 8000000 | tf_op jit(solution)/shard_map/pallas_call | solution.py:488
  26.3 1.5 %collective-permute-start.4 = (bf16[512,128]{1,0:T(8,128)(2,1)S(1)}, bf16[512,128]{1,0:T(8,128)(2,1)S(1)}, u32[]{:S(2)}, u32[]{:S(2)}) collective-permute-start(bf16[512,128]{1,0:T(8,128)(2,1)S(1)} %bitcast.104), channel_id=1, source_target_pairs={{0,2},{1,3},{2,0},{3,1},{4,6},{5,7},{6,4},{7,5},{8,10},{9,11},{10,... | collective-permute-start | bytes 393224 | tf_op jit(solution)/shard_map/ppermute | solution.py:360
  27.8 3.4 %shard_map.113 = (bf16[48,128]{1,0:T(8,128)(2,1)S(1)}, bf16[4,64,128]{2,1,0:T(8,128)(2,1)S(1)}) custom-call(bf16[64,64,128]{2,1,0:T(8,128)(2,1)S(1)} %get-tuple-element.41.refs_0_, bf16[64,512,128]{2,1,0:T(8,128)(2,1)S(1)} %get-tuple-element.33.refs_1_, bf16[1536,128]{1,0:T(8,128)(2,1)S(1)} %get-tuple-element.39.refs_2_.refs_0_.refs_1_, ...), custom_call_target="tpu_custom_call" | custom-call | flops 8000000000 | bytes 8000000 | tf_op jit(solution)/shard_map/pallas_call | solution.py:511
  31.2 1.3 %collective-permute-done.4 = bf16[512,128]{1,0:T(8,128)(2,1)S(1)} collective-permute-done((bf16[512,128]{1,0:T(8,128)(2,1)S(1)}, bf16[512,128]{1,0:T(8,128)(2,1)S(1)}, u32[]{:S(2)}, u32[]{:S(2)}) %collective-permute-start.4) | collective-permute-done | bytes 131104 | tf_op jit(solution)/shard_map/ppermute | solution.py:360
  32.7 0.2 collective-permute-start.5
  32.8 1.2 %collective-permute-done.5 = bf16[432,128]{1,0:T(8,128)(2,1)S(1)} collective-permute-done((bf16[432,128]{1,0:T(8,128)(2,1)S(1)}, bf16[432,128]{1,0:T(8,128)(2,1)S(1)}, u32[]{:S(2)}, u32[]{:S(2)}) %collective-permute-start.5) | collective-permute-done | bytes 110624 | tf_op jit(solution)/shard_map/ppermute | solution.py:360
  34.2 0.4 collective-permute-start.6
  34.6 4.9 %shard_map.114 = (bf16[64,64,128]{2,1,0:T(8,128)(2,1)}, bf16[48,128]{1,0:T(8,128)(2,1)S(1)}) custom-call(bf16[1536,128]{1,0:T(8,128)(2,1)S(1)} %get-tuple-element.39.refs_2_.refs_0_.refs_1_, f32[1,128]{1,0:T(1,128)S(1)} %get-tuple-element.40.refs_1_, bf16[32,4096]{1,0:T(8,128)(2,1)S(1)} %get-tuple-element.38.refs_7_.refs_2_, ...), custom_call_target="tpu_custom_call" | custom-call | flops 6000000000 | bytes 8000000 | tf_op jit(solution)/shard_map/pallas_call | solution.py:531
  39.5 0.0 collective-permute-done.6
  39.6 3.5 %collective-permute-start.7 = (bf16[432,128]{1,0:T(8,128)(2,1)S(1)}, bf16[432,128]{1,0:T(8,128)(2,1)S(1)}, u32[]{:S(2)}, u32[]{:S(2)}) collective-permute-start(bf16[432,128]{1,0:T(8,128)(2,1)S(1)} %pad_maximum_fusion.6), channel_id=1, source_target_pairs={{0,8},{4,12},{8,0},{12,4},{1,9},{5,13},{9,1},{13,5},{2,10},{6,14},... | collective-permute-start | bytes 331784 | tf_op jit(solution)/shard_map/ppermute | solution.py:360
  43.1 9.4 %shard_map.115 = (bf16[4,32,128]{2,1,0:T(8,128)(2,1)S(1)}, bf16[4,32,128]{2,1,0:T(8,128)(2,1)S(1)}, bf16[48,128]{1,0:T(8,128)(2,1)S(1)}) custom-call(bf16[64,64,128]{2,1,0:T(8,128)(2,1)S(1)} %get-tuple-element.41.refs_0_, bf16[1536,128]{1,0:T(8,128)(2,1)S(1)} %get-tuple-element.39.refs_2_.refs_0_.refs_1_, ...), custom_call_target="tpu_custom_call" | custom-call | flops 6000000000 | bytes 8000000 | tf_op jit(solution)/shard_map/pallas_call | solution.py:543
  52.5 0.0 collective-permute-done.7
  52.6 1.6 %collective-permute-start.8 = (bf16[496,128]{1,0:T(8,128)(2,1)S(1)}, bf16[496,128]{1,0:T(8,128)(2,1)S(1)}, u32[]{:S(2)}, u32[]{:S(2)}) collective-permute-start(bf16[496,128]{1,0:T(8,128)(2,1)S(1)} %pad_maximum_fusion.3), channel_id=1, source_target_pairs={{0,2},{1,3},{2,0},{3,1},{4,6},{5,7},{6,4},{7,5},{8,10},{9,11},{10,... | collective-permute-start | bytes 380936 | tf_op jit(solution)/shard_map/ppermute | solution.py:360
  54.2 3.4 %collective-permute-done.8 = bf16[496,128]{1,0:T(8,128)(2,1)S(1)} collective-permute-done((bf16[496,128]{1,0:T(8,128)(2,1)S(1)}, bf16[496,128]{1,0:T(8,128)(2,1)S(1)}, u32[]{:S(2)}, u32[]{:S(2)}) %collective-permute-start.8) | collective-permute-done | bytes 127008 | tf_op jit(solution)/shard_map/ppermute | solution.py:360
  57.7 0.1 collective-permute-start.9
  57.9 1.3 %collective-permute-done.9 = bf16[576,128]{1,0:T(8,128)(2,1)S(1)} collective-permute-done((bf16[576,128]{1,0:T(8,128)(2,1)S(1)}, bf16[576,128]{1,0:T(8,128)(2,1)S(1)}, u32[]{:S(2)}, u32[]{:S(2)}) %collective-permute-start.9) | collective-permute-done | bytes 147488 | tf_op jit(solution)/shard_map/ppermute | solution.py:360
  59.3 2.4 %shard_map.116 = (f32[256,64]{1,0:T(8,128)}, f32[64,64]{1,0:T(8,128)}, f32[1,128]{1,0:T(1,128)}, f32[32,32,128]{2,1,0:T(8,128)}) custom-call(bf16[32,256]{1,0:T(8,128)(2,1)S(1)} %bitcast.89, bf16[32,256]{1,0:T(8,128)(2,1)S(1)} %bitcast.90, bf16[16,512]{1,0:T(8,128)(2,1)S(1)} %bitcast.88, bf16[48,128]{1,0:T(8,128)(2,1)S(1)} %add_convert_fusion.2.refs_3_, ...), custom_call_target="tpu_custom_call" | custom-call | tf_op jit(solution)/shard_map/pallas_call | solution.py:591
  (44 shorter events, 0.6 us)
Async XLA Ops:
  0.6 18.8 %copy-start.1 = (bf16[64,64,128]{2,1,0:T(8,128)(2,1)S(1)}, bf16[64,64,128]{2,1,0:T(8,128)(2,1)}, u32[]{:S(2)}) copy-start(bf16[64,64,128]{2,1,0:T(8,128)(2,1)} %refs_0_.3) | copy-start | bytes 3145732
  3.1 1.4 %collective-permute-start = (bf16[272,128]{1,0:T(8,128)(2,1)S(1)}, bf16[272,128]{1,0:T(8,128)(2,1)S(1)}, u32[]{:S(2)}, u32[]{:S(2)}) collective-permute-start(bf16[272,128]{1,0:T(8,128)(2,1)S(1)} %pad_maximum_fusion.8), channel_id=1, source_target_pairs={{0,1},{1,0},{2,3},{3,2},{4,5},{5,4},{6,7},{7,6},{8,9},{9,8},{10,11... | collective-permute-start | bytes 208904 | tf_op jit(solution)/shard_map/ppermute | solution.py:360
  4.6 7.6 %collective-permute-start.1 = (bf16[2,144,128]{2,1,0:T(8,128)(2,1)S(1)}, bf16[2,144,128]{2,1,0:T(8,128)(2,1)S(1)}, u32[]{:S(2)}, u32[]{:S(2)}) collective-permute-start(bf16[2,144,128]{2,1,0:T(8,128)(2,1)S(1)} %get-tuple-element.62.refs_4_), channel_id=1, source_target_pairs={{0,2},{1,3},{2,0},{3,1},{4,6},{5,7},{6,4},{7,5},{8,10},{9,11},{10,... | collective-permute-start | bytes 221192 | tf_op jit(solution)/shard_map/ppermute | solution.py:434
  7.7 11.7 %collective-permute-start.2 = (bf16[2,144,128]{2,1,0:T(8,128)(2,1)S(1)}, bf16[2,144,128]{2,1,0:T(8,128)(2,1)S(1)}, u32[]{:S(2)}, u32[]{:S(2)}) collective-permute-start(bf16[2,144,128]{2,1,0:T(8,128)(2,1)S(1)} %get-tuple-element.61), channel_id=1, source_target_pairs={{0,0},{1,4},{2,8},{3,12},{4,1},{5,5},{6,9},{7,13},{8,2},{9,6},{10,... | collective-permute-start | bytes 221192 | tf_op jit(solution)/shard_map/ppermute | solution.py:445
  8.3 11.1 %collective-permute-start.3 = (bf16[2,144,128]{2,1,0:T(8,128)(2,1)S(1)}, bf16[2,144,128]{2,1,0:T(8,128)(2,1)S(1)}, u32[]{:S(2)}, u32[]{:S(2)}) collective-permute-start(bf16[2,144,128]{2,1,0:T(8,128)(2,1)S(1)} %get-tuple-element.61), channel_id=1, source_target_pairs={{0,8},{1,12},{2,0},{3,4},{4,9},{5,13},{6,1},{7,5},{8,10},{9,14},{1... | collective-permute-start | bytes 221192 | tf_op jit(solution)/shard_map/ppermute | solution.py:445
  12.2 1.2 %copy-start = (bf16[64,64,128]{2,1,0:T(8,128)(2,1)S(1)}, bf16[64,64,128]{2,1,0:T(8,128)(2,1)}, u32[]{:S(2)}) copy-start(bf16[64,64,128]{2,1,0:T(8,128)(2,1)} %refs_0_.3) | copy-start | bytes 3145732
  13.5 0.9 %copy-start.2 = (bf16[1024,128]{1,0:T(8,128)(2,1)S(1)}, bf16[1024,128]{1,0:T(8,128)(2,1)}, u32[]{:S(2)}) copy-start(bf16[1024,128]{1,0:T(8,128)(2,1)} %refs_1_.1) | copy-start | bytes 786436
  14.4 0.7 %copy-start.3 = (bf16[64,64]{1,0:T(8,128)(2,1)S(1)}, bf16[64,64]{1,0:T(8,128)(2,1)}, u32[]{:S(2)}) copy-start(bf16[64,64]{1,0:T(8,128)(2,1)} %refs_0_.2) | copy-start | bytes 24580
  15.1 0.7 %copy-start.4 = (f32[128]{0:T(128)S(1)}, f32[128]{0:T(128)}, u32[]{:S(2)}) copy-start(f32[128]{0:T(128)} %param.12) | copy-start | bytes 1540
  26.3 6.3 %collective-permute-start.4 = (bf16[512,128]{1,0:T(8,128)(2,1)S(1)}, bf16[512,128]{1,0:T(8,128)(2,1)S(1)}, u32[]{:S(2)}, u32[]{:S(2)}) collective-permute-start(bf16[512,128]{1,0:T(8,128)(2,1)S(1)} %bitcast.104), channel_id=1, source_target_pairs={{0,2},{1,3},{2,0},{3,1},{4,6},{5,7},{6,4},{7,5},{8,10},{9,11},{10,... | collective-permute-start | bytes 393224 | tf_op jit(solution)/shard_map/ppermute | solution.py:360
  32.7 1.4 %collective-permute-start.5 = (bf16[432,128]{1,0:T(8,128)(2,1)S(1)}, bf16[432,128]{1,0:T(8,128)(2,1)S(1)}, u32[]{:S(2)}, u32[]{:S(2)}) collective-permute-start(bf16[432,128]{1,0:T(8,128)(2,1)S(1)} %pad_maximum_fusion.4), channel_id=1, source_target_pairs={{0,1},{1,0},{2,3},{3,2},{4,5},{5,4},{6,7},{7,6},{8,9},{9,8},{10,11... | collective-permute-start | bytes 331784 | tf_op jit(solution)/shard_map/ppermute | solution.py:360
  34.2 5.3 %collective-permute-start.6 = (bf16[432,128]{1,0:T(8,128)(2,1)S(1)}, bf16[432,128]{1,0:T(8,128)(2,1)S(1)}, u32[]{:S(2)}, u32[]{:S(2)}) collective-permute-start(bf16[432,128]{1,0:T(8,128)(2,1)S(1)} %pad_maximum_fusion.5), channel_id=1, source_target_pairs={{0,4},{4,0},{8,12},{12,8},{1,5},{5,1},{9,13},{13,9},{2,6},{6,2},{1... | collective-permute-start | bytes 331784 | tf_op jit(solution)/shard_map/ppermute | solution.py:360
  39.6 12.9 %collective-permute-start.7 = (bf16[432,128]{1,0:T(8,128)(2,1)S(1)}, bf16[432,128]{1,0:T(8,128)(2,1)S(1)}, u32[]{:S(2)}, u32[]{:S(2)}) collective-permute-start(bf16[432,128]{1,0:T(8,128)(2,1)S(1)} %pad_maximum_fusion.6), channel_id=1, source_target_pairs={{0,8},{4,12},{8,0},{12,4},{1,9},{5,13},{9,1},{13,5},{2,10},{6,14},... | collective-permute-start | bytes 331784 | tf_op jit(solution)/shard_map/ppermute | solution.py:360
  52.6 5.0 %collective-permute-start.8 = (bf16[496,128]{1,0:T(8,128)(2,1)S(1)}, bf16[496,128]{1,0:T(8,128)(2,1)S(1)}, u32[]{:S(2)}, u32[]{:S(2)}) collective-permute-start(bf16[496,128]{1,0:T(8,128)(2,1)S(1)} %pad_maximum_fusion.3), channel_id=1, source_target_pairs={{0,2},{1,3},{2,0},{3,1},{4,6},{5,7},{6,4},{7,5},{8,10},{9,11},{10,... | collective-permute-start | bytes 380936 | tf_op jit(solution)/shard_map/ppermute | solution.py:360
  57.7 1.4 %collective-permute-start.9 = (bf16[576,128]{1,0:T(8,128)(2,1)S(1)}, bf16[576,128]{1,0:T(8,128)(2,1)S(1)}, u32[]{:S(2)}, u32[]{:S(2)}) collective-permute-start(bf16[576,128]{1,0:T(8,128)(2,1)S(1)} %pad_maximum_fusion.1), channel_id=1, source_target_pairs={{0,1},{1,0},{2,3},{3,2},{4,5},{5,4},{6,7},{7,6},{8,9},{9,8},{10,11... | collective-permute-start | bytes 442376 | tf_op jit(solution)/shard_map/ppermute | solution.py:360

commit v14 on v12

--- a/solution.py
+++ b/solution.py
@@ -76,28 +76,28 @@
     by_token_ref[half:, :] = mask
 
 
-def two(ref, at):
-    return jnp.concatenate([ref[at], ref[at + 1]], axis=1)
-
-
 def fill_v(g_ref, bt, v_ref, depth):
-    chunk, _, pair = g_ref.shape
-    width = v_ref.shape[0]
-    for at in range(0, chunk, 2):
-        v = dot(bt, two(g_ref, at)).astype(BF16)
+    width = bt.shape[0] // depth
+    pair = v_ref.shape[1] // width
+    for at in range(0, v_ref.shape[0] // depth, 2):
+        v = dot(bt, g_ref[:, at * pair : (at + 2) * pair]).astype(BF16)
         for k in range(2):
-            part = v[:, k * pair : (k + 1) * pair].reshape(width, depth, pair)
-            v_ref[:, (at + k) * depth : (at + k + 1) * depth, :] = part
+            rows = slice((at + k) * depth, (at + k + 1) * depth)
+            for e in range(width):
+                part = v[e * depth : (e + 1) * depth, k * pair : (k + 1) * pair]
+                v_ref[rows, e * pair : (e + 1) * pair] = part
 
 
 def fill_t(a_chunk, wc_ref, t_ref, depth):
-    chunk, wide, pair = t_ref.shape
-    width = wide // depth
+    width = wc_ref.shape[0]
+    pair = wc_ref.shape[1] // width
     for e in range(0, width, 2):
         t = dot(a_chunk, wc_ref[:, e * pair : (e + 2) * pair]).astype(BF16)
         for k in range(2):
-            part = t[:, k * pair : (k + 1) * pair].reshape(chunk, depth, pair)
-            t_ref[:, (e + k) * depth : (e + k + 1) * depth, :] = part
+            rows = slice((e + k) * depth, (e + k + 1) * depth)
+            for i in range(a_chunk.shape[0] // depth):
+                part = t[i * depth : (i + 1) * depth, k * pair : (k + 1) * pair]
+                t_ref[rows, i * pair : (i + 1) * pair] = part
 
 
 def held_b(held_ref, block, width, depth):
@@ -190,12 +190,13 @@
         inv = inv_ref[g * (chunk // part_size) + k]
         for i in range(part_size):
             up = up_ref[k * part_size + i].astype(F32)
-            g_ref[k * part_size + i] = (up * inv[:, i : i + 1]).astype(BF16)
+            at = (k * part_size + i) * pair
+            g_ref[:, at : at + pair] = (up * inv[:, i : i + 1]).astype(BF16)
     fill_v(g_ref, bt_ref[...], v_ref, depth)
     span = chunk * depth
     a_t = at_ref[:, pl.ds(pl.multiple_of(g * span, span), span)]
     for e in range(0, width, 2):
-        part = dot(a_t, two(v_ref, e))
+        part = dot(a_t, v_ref[:, e * pair : (e + 2) * pair])
         for k in range(2):
             rows = slice((e + k) * width, (e + k + 1) * width)
             acc_ref[rows, :] += part[:width, k * pair : (k + 1) * pair]
@@ -214,9 +215,9 @@
 def left_kernel(depth, bit, *refs):
     g_ref, held_ref, wc_ref, small_ref, keep_ref, go_ref, pass_ref, v_ref, wd_ref, da_ref, bt_ref = refs
     g, last = pl.program_id(0), pl.num_programs(0) - 1
-    chunk, block, pair = g_ref.shape
-    width = wc_ref.shape[0]
-    span = chunk * depth
+    block, width = g_ref.shape[0], wc_ref.shape[0]
+    pair = wc_ref.shape[1] // width
+    span = v_ref.shape[0]
 
     @pl.when(g == 0)
     def _():
@@ -227,12 +228,10 @@
             wd_ref[at : at + 2 * pair, :] = dot_nt(same, wc_ref[:, at : at + 2 * pair]).astype(BF16)
 
     fill_v(g_ref, bt_ref[...], v_ref, depth)
-    d_a = []
-    each = width // 4
-    for e in range(0, width, each):
-        v = jnp.concatenate([v_ref[e + k] for k in range(each)], axis=1)
-        d_a.append(dot(v, wd_ref[e * pair : (e + each) * pair, :]))
-    d_a = (d_a[0] + d_a[1]) + (d_a[2] + d_a[3])
+    d_a = jnp.zeros((span, width), F32)
+    each = v_ref.shape[1] // 4
+    for at in range(0, 4 * each, each):
+        d_a = d_a + dot(v_ref[:, at : at + each], wd_ref[at : at + each, :])
     same = one_hot(iota((width, width), 0) == iota((width, width), 1))
     d_a = dot_nt(same, d_a.astype(BF16)).astype(BF16)
     tiles = span // LANES
@@ -251,8 +250,8 @@
     g_ref, held_ref, wc_ref, mj_ref, perm_ref, bias_ref, left_ref = refs[:7]
     small_ref, out_ref, t_ref, db_ref = refs[7:]
     g, last = pl.program_id(0), pl.num_programs(0) - 1
-    chunk, block = g_ref.shape[:2]
-    width = left_ref.shape[0]
+    block, width = g_ref.shape[0], left_ref.shape[0]
+    chunk = t_ref.shape[1] // (wc_ref.shape[1] // width)
 
     @pl.when(g == 0)
     def _():
@@ -260,9 +259,7 @@
 
     span = chunk * depth
     fill_t(held_ref[pl.ds(pl.multiple_of(g * span, span), span), :width], wc_ref, t_ref, depth)
-    t = jnp.concatenate([t_ref[i] for i in range(chunk)], axis=1)
-    scaled = jnp.concatenate([g_ref[i] for i in range(chunk)], axis=1)
-    db_ref[...] += dot_nt(t, scaled)
+    db_ref[...] += dot_nt(t_ref[...], g_ref[...])
 
     @pl.when(g == last)
     def _():
@@ -299,7 +296,7 @@
     b = held_b(held_ref, block, width, depth)
     offset = offset_ref[...]
     for at in range(0, chunk, 2):
-        part = dot(b, two(t_ref, at))
+        part = dot(b, t_ref[:, at * pair : (at + 2) * pair])
         for k in range(2):
             value = part[:, k * pair : (k + 1) * pair] * inv[:, at + k : at + k + 1] + offset
             out_ref[at + k] = value.astype(BF16)
@@ -463,7 +460,6 @@
         [full(o.shape) for o in out_shapes],
         out_shapes,
         [pltpu.VMEM((width * width, pair), F32), pltpu.VMEM((tokens, features), BF16)],
-        cost(3e9, 4e6),
     )(*args)
 
     out_shapes = [
@@ -474,18 +470,19 @@
     ]
     args = (a, a_t, seen, factors_t, perm, pairing_wide, *j_pieces)
     large = 2 * chunk
+    g_spec = pl.BlockSpec((block, chunk * pair), lambda g: (0, g))
     large_spec = pl.BlockSpec((large, block, pair), lambda g: (g, 0, 0))
     scaled, held, d_pairing, left, mj = call(
         functools.partial(weight_kernel, depth, features, own, len(j_pieces), chunk),
         (block // large,),
         [large_spec] + [full(v.shape) for v in args],
-        [large_spec] + [full(o.shape) for o in out_shapes],
-        [sds(upstream_adjoint.shape, BF16)] + out_shapes,
+        [pl.BlockSpec((block, large * pair), lambda g: (0, g))] + [full(o.shape) for o in out_shapes],
+        [sds((block, block * pair), BF16)] + out_shapes,
         [
             pltpu.VMEM((block, LANES), BF16),
             pltpu.VMEM((wide, block), BF16),
             pltpu.VMEM((steps, block, chunk), F32),
-            pltpu.VMEM((width, large * depth, pair), BF16),
+            pltpu.VMEM((large * depth, width * pair), BF16),
             pltpu.VMEM((width * width, pair), F32),
             pltpu.VMEM((features, width * pair), F32),
         ],
@@ -501,11 +498,10 @@
     small, d_b = call(
         functools.partial(token_kernel, depth, features, n),
         (steps,),
-        [up_spec]
-        + [full(v.shape) for v in (held, pairing_wide, mj, perm, bias, left)],
+        [g_spec] + [full(v.shape) for v in (held, pairing_wide, mj, perm, bias, left)],
         [full(o.shape) for o in out_shapes],
         out_shapes,
-        [pltpu.VMEM((chunk, wide, pair), BF16), pltpu.VMEM((wide, block), F32)],
+        [pltpu.VMEM((wide, chunk * pair), BF16), pltpu.VMEM((wide, block), F32)],
         cost(8e9, 8e6),
     )(scaled, held, pairing_wide, mj, perm, bias, left)
 
@@ -525,7 +521,7 @@
                 [full(v.shape) for v in args],
                 [up_spec, full(small.shape)],
                 [sds((block, block, pair), BF16), sds(small.shape, BF16)],
-                [pltpu.VMEM((chunk, wide, pair), BF16)],
+                [pltpu.VMEM((wide, chunk * pair), BF16)],
                 cost(6e9, 8e6),
             )(*args)
         if bit == 1:
@@ -534,11 +530,11 @@
             *d_a, small = call(
                 functools.partial(left_kernel, depth, bits - 1),
                 (steps,),
-                [up_spec] + [full(v.shape) for v in (held, pairing_wide, small)],
+                [g_spec] + [full(v.shape) for v in (held, pairing_wide, small)],
                 [full(o.shape) for o in out_shapes],
                 out_shapes,
                 [
-                    pltpu.VMEM((width, chunk * depth, pair), BF16),
+                    pltpu.VMEM((chunk * depth, width * pair), BF16),
                     pltpu.VMEM((width * pair, width), BF16),
                     pltpu.VMEM((tokens // LANES, width, LANES), BF16),
                     pltpu.VMEM((wide, block), BF16),

time: 56.3 us -> 56.6 us (level)
    ppermute x1, waiting for transfers between devices: 0.01 us -> 4.47 us  [per_device(): held.append(lax.ppermute(message, 'col', [(j, j ^ k) for j in range(n)]))]
    ppermute x2, waiting for transfers between devices: 3.71 us -> 0.01 us  [per_device(): held.append(lax.ppermute(message, axes, pairs))]
    ppermute x1, starting transfers between devices: 2.9 us -> 0.29 us  [per_device(): held.append(lax.ppermute(message, 'col', [(j, j ^ k) for j in range(n)]))]
    ppermute x2, starting transfers between devices: 4.56 us -> 7.16 us  [per_device(): held.append(lax.ppermute(message, axes, pairs))]
    ppermute x7, waiting for transfers between devices: 9.27 us -> 8.03 us  [swap_parts(): message = lax.ppermute(message, axis, pairs)]
  transfers between devices with their start and end apart: 10 -> 10, of which waited for: 7 -> 6; matrix products, arithmetic and copies ran while one was open for 0% -> 0% of each run, Pallas kernels for 31% -> 31%
where the time goes in v14:
time: 56.6 us; the launch traced here: 56.4 us
  Pallas kernels  27.5 us (49%)
  starting transfers between devices  13.5 us (24%)
  waiting for transfers between devices  12.5 us (22%)
  other arithmetic  1.56 us (3%)
  between operations  1.09 us (2%)
    ppermute x7, waiting for transfers between devices, swap_parts(): message = lax.ppermute(message, axis, pairs)  8.03 us
    ppermute x2, starting transfers between devices, per_device(): held.append(lax.ppermute(message, axes, pairs))  7.16 us
    pallas_call x1, Pallas kernels, per_device(): call(functools.partial(weight_kernel, depth, features, own, len(j_pieces)...  6.95 us
    pallas_call x1, Pallas kernels, per_device(): call(functools.partial(left_kernel, depth, bits - 1), (steps,), [g_spec]...  6.19 us
    ppermute x7, starting transfers between devices, swap_parts(): message = lax.ppermute(message, axis, pairs)  6.03 us
    pallas_call x1, Pallas kernels, per_device(): call(functools.partial(token_kernel, depth, features, n), (steps,), [g_sp...  5.67 us
    pallas_call x1, Pallas kernels, per_device(): call(functools.partial(update_kernel, depth), (steps,), [full(v.shape) fo...  4.87 us
    ppermute x1, waiting for transfers between devices, per_device(): held.append(lax.ppermute(message, 'col', [(j, j ^ k) for j in range(n)]))  4.47 us
  transfers between devices with their start and end apart: 10, of which 6 were waited for; matrix products, arithmetic and copies ran while one was open for 0% of the time, Pallas kernels for 31%

profile of v14, /device:TPU:0, one launch (start us, length us, event | category | flops | bytes accessed | tf_op | source)
XLA Modules:
  0.0 56.4 jit_solution(1312674569832302502)
XLA Ops:
  0.6 0.0 copy-start.4
  0.6 0.0 copy-start
  0.7 0.9 %multiply_convert_fusion = bf16[16,16]{1,0:T(8,128)(2,1)S(1)} fusion(s32[16,16]{1,0:T(8,128)} %param.8, s32[16]{0:T(128)} %param.9), kind=kLoop, calls=%fused_computation.52 | loop fusion | flops 512 | bytes 1600 | tf_op jit(solution)/shard_map/convert_element_type | solution.py:405
  1.5 0.1 broadcast_in_dim.2
  1.6 0.0 copy-done.4
  1.6 0.1 pad_maximum_fusion.9
  1.7 0.5 shard_map.110
  2.3 0.5 collective-permute-start
  2.8 0.9 %collective-permute-done = bf16[272,128]{1,0:T(8,128)(2,1)S(1)} collective-permute-done((bf16[272,128]{1,0:T(8,128)(2,1)S(1)}, bf16[272,128]{1,0:T(8,128)(2,1)S(1)}, u32[]{:S(2)}, u32[]{:S(2)}) %collective-permute-start) | collective-permute-done | bytes 69664 | tf_op jit(solution)/shard_map/ppermute | solution.py:348
  3.8 0.7 %collective-permute-start.2 = (bf16[2,144,128]{2,1,0:T(8,128)(2,1)S(1)}, bf16[2,144,128]{2,1,0:T(8,128)(2,1)S(1)}, u32[]{:S(2)}, u32[]{:S(2)}) collective-permute-start(bf16[2,144,128]{2,1,0:T(8,128)(2,1)S(1)} %get-tuple-element.59), channel_id=1, source_target_pairs={{0,0},{1,4},{2,8},{3,12},{4,1},{5,5},{6,9},{7,13},{8,2},{9,6},{10,... | collective-permute-start | bytes 221192 | tf_op jit(solution)/shard_map/ppermute | solution.py:433
  4.4 6.5 %collective-permute-start.3 = (bf16[2,144,128]{2,1,0:T(8,128)(2,1)S(1)}, bf16[2,144,128]{2,1,0:T(8,128)(2,1)S(1)}, u32[]{:S(2)}, u32[]{:S(2)}) collective-permute-start(bf16[2,144,128]{2,1,0:T(8,128)(2,1)S(1)} %get-tuple-element.59), channel_id=1, source_target_pairs={{0,8},{1,12},{2,0},{3,4},{4,9},{5,13},{6,1},{7,5},{8,10},{9,14},{1... | collective-permute-start | bytes 221192 | tf_op jit(solution)/shard_map/ppermute | solution.py:433
  10.9 0.0 copy-start.1
  10.9 0.3 collective-permute-start.1
  11.2 0.1 fusion.refs_5_.refs_4_.refs_7_
  11.4 0.0 copy-start.2
  11.4 0.0 copy-start.3
  11.4 4.5 %collective-permute-done.1.refs_1_ = bf16[2,144,128]{2,1,0:T(8,128)(2,1)S(1)} collective-permute-done((bf16[2,144,128]{2,1,0:T(8,128)(2,1)S(1)}, bf16[2,144,128]{2,1,0:T(8,128)(2,1)S(1)}, u32[]{:S(2)}, u32[]{:S(2)}) %collective-permute-start.1) | collective-permute-done | bytes 73760 | tf_op jit(solution)/shard_map/ppermute | solution.py:422
  15.9 0.0 copy-done
  15.9 0.0 copy-done.1
  15.9 0.0 copy-done.2
  15.9 0.0 copy-done.3
  15.9 0.8 %shard_map.111 = (bf16[64,64]{1,0:T(8,128)(2,1)S(1)}, bf16[32,4096]{1,0:T(8,128)(2,1)S(1)}, f32[1,128]{1,0:T(1,128)S(1)}, f32[8,128]{1,0:T(8,128)S(1)}, bf16[102...) custom-call(bf16[64,64]{1,0:T(8,128)(2,1)S(1)} %copy-done.2, ...), custom_call_target="tpu_custom_call" | custom-call | tf_op jit(solution)/shard_map/pallas_call | solution.py:456
  16.7 0.0 collective-permute-done.2.refs_7_
  16.7 0.0 collective-permute-done.3.refs_8_
  16.7 7.0 %shard_map.112 = (bf16[64,8192]{1,0:T(8,128)(2,1)S(1)}, bf16[1536,128]{1,0:T(8,128)(2,1)S(1)}, bf16[1024,128]{1,0:T(8,128)(2,1)S(1)}, f32[32,64]{1,0:T(8,128)S(1)}, bf16[16,64,64]{2,1,0:T(8,128)(2,1)S(1)}) custom-call(bf16[64,64,128]{2,1,0:T(8,128)(2,1)S(1)} %copy-done, bf16[1024,32]{1,0:T(8,128)(2,1)S(1)} %get-tuple-element.32.refs_1_, ...), custom_call_target="tpu_custom_call" | custom-call | flops 5000000000 | bytes 8000000 | tf_op jit(solution)/shard_map/pallas_call | solution.py:475
  23.7 1.7 %collective-permute-start.4 = (bf16[512,128]{1,0:T(8,128)(2,1)S(1)}, bf16[512,128]{1,0:T(8,128)(2,1)S(1)}, u32[]{:S(2)}, u32[]{:S(2)}) collective-permute-start(bf16[512,128]{1,0:T(8,128)(2,1)S(1)} %bitcast.104), channel_id=1, source_target_pairs={{0,2},{1,3},{2,0},{3,1},{4,6},{5,7},{6,4},{7,5},{8,10},{9,11},{10,... | collective-permute-start | bytes 393224 | tf_op jit(solution)/shard_map/ppermute | solution.py:348
  25.5 5.7 %shard_map.113 = (bf16[48,128]{1,0:T(8,128)(2,1)S(1)}, bf16[4,64,128]{2,1,0:T(8,128)(2,1)S(1)}) custom-call(bf16[64,8192]{1,0:T(8,128)(2,1)S(1)} %get-tuple-element.39.refs_0_, bf16[1536,128]{1,0:T(8,128)(2,1)S(1)} %get-tuple-element.37.refs_1_.refs_0_, bf16[32,4096]{1,0:T(8,128)(2,1)S(1)} %get-tuple-element.36.refs_6_.refs_2_, ...), custom_call_target="tpu_custom_call" | custom-call | flops 8000000000 | bytes 8000000 | tf_op jit(solution)/shard_map/pallas_call | solution.py:498
  31.1 0.0 collective-permute-done.4
  31.3 0.1 collective-permute-start.5
  31.3 1.3 %collective-permute-done.5 = bf16[432,128]{1,0:T(8,128)(2,1)S(1)} collective-permute-done((bf16[432,128]{1,0:T(8,128)(2,1)S(1)}, bf16[432,128]{1,0:T(8,128)(2,1)S(1)}, u32[]{:S(2)}, u32[]{:S(2)}) %collective-permute-start.5) | collective-permute-done | bytes 110624 | tf_op jit(solution)/shard_map/ppermute | solution.py:348
  32.8 0.1 collective-permute-start.6
  32.8 4.9 %shard_map.114 = (bf16[64,64,128]{2,1,0:T(8,128)(2,1)}, bf16[48,128]{1,0:T(8,128)(2,1)S(1)}) custom-call(bf16[1536,128]{1,0:T(8,128)(2,1)S(1)} %get-tuple-element.37.refs_1_.refs_0_, f32[1,128]{1,0:T(1,128)S(1)} %get-tuple-element.38.refs_1_, bf16[32,4096]{1,0:T(8,128)(2,1)S(1)} %get-tuple-element.36.refs_6_.refs_2_, ...), custom_call_target="tpu_custom_call" | custom-call | flops 6000000000 | bytes 8000000 | tf_op jit(solution)/shard_map/pallas_call | solution.py:518
  37.7 0.2 collective-permute-done.6
  38.1 2.9 %collective-permute-start.7 = (bf16[432,128]{1,0:T(8,128)(2,1)S(1)}, bf16[432,128]{1,0:T(8,128)(2,1)S(1)}, u32[]{:S(2)}, u32[]{:S(2)}) collective-permute-start(bf16[432,128]{1,0:T(8,128)(2,1)S(1)} %pad_maximum_fusion.6), channel_id=1, source_target_pairs={{0,8},{4,12},{8,0},{12,4},{1,9},{5,13},{9,1},{13,5},{2,10},{6,14},... | collective-permute-start | bytes 331784 | tf_op jit(solution)/shard_map/ppermute | solution.py:348
  40.9 6.2 %shard_map.115 = (bf16[4,32,128]{2,1,0:T(8,128)(2,1)S(1)}, bf16[4,32,128]{2,1,0:T(8,128)(2,1)S(1)}, bf16[48,128]{1,0:T(8,128)(2,1)S(1)}) custom-call(bf16[64,8192]{1,0:T(8,128)(2,1)S(1)} %get-tuple-element.39.refs_0_, bf16[1536,128]{1,0:T(8,128)(2,1)S(1)} %get-tuple-element.37.refs_1_.refs_0_, bf16[32,4096]{1,0:T(8,128)(2,1)S(1)} %get-tuple-element.36.refs_6_.refs_2_, ...), custom_call_target="tpu_custom_call" | custom-call | flops 6000000000 | bytes 8000000 | tf_op jit(solution)/shard_map/pallas_call | solution.py:530
  47.1 0.0 collective-permute-done.7
  47.2 0.7 %collective-permute-start.8 = (bf16[496,128]{1,0:T(8,128)(2,1)S(1)}, bf16[496,128]{1,0:T(8,128)(2,1)S(1)}, u32[]{:S(2)}, u32[]{:S(2)}) collective-permute-start(bf16[496,128]{1,0:T(8,128)(2,1)S(1)} %pad_maximum_fusion.3), channel_id=1, source_target_pairs={{0,2},{1,3},{2,0},{3,1},{4,6},{5,7},{6,4},{7,5},{8,10},{9,11},{10,... | collective-permute-start | bytes 380936 | tf_op jit(solution)/shard_map/ppermute | solution.py:348
  48.0 4.3 %collective-permute-done.8 = bf16[496,128]{1,0:T(8,128)(2,1)S(1)} collective-permute-done((bf16[496,128]{1,0:T(8,128)(2,1)S(1)}, bf16[496,128]{1,0:T(8,128)(2,1)S(1)}, u32[]{:S(2)}, u32[]{:S(2)}) %collective-permute-start.8) | collective-permute-done | bytes 127008 | tf_op jit(solution)/shard_map/ppermute | solution.py:348
  52.3 0.1 collective-permute-start.9
  52.5 1.3 %collective-permute-done.9 = bf16[576,128]{1,0:T(8,128)(2,1)S(1)} collective-permute-done((bf16[576,128]{1,0:T(8,128)(2,1)S(1)}, bf16[576,128]{1,0:T(8,128)(2,1)S(1)}, u32[]{:S(2)}, u32[]{:S(2)}) %collective-permute-start.9) | collective-permute-done | bytes 147488 | tf_op jit(solution)/shard_map/ppermute | solution.py:348
  53.9 2.4 %shard_map.116 = (f32[256,64]{1,0:T(8,128)}, f32[64,64]{1,0:T(8,128)}, f32[1,128]{1,0:T(1,128)}, f32[32,32,128]{2,1,0:T(8,128)}) custom-call(bf16[32,256]{1,0:T(8,128)(2,1)S(1)} %bitcast.89, bf16[32,256]{1,0:T(8,128)(2,1)S(1)} %bitcast.90, bf16[16,512]{1,0:T(8,128)(2,1)S(1)} %bitcast.88, bf16[48,128]{1,0:T(8,128)(2,1)S(1)} %add_convert_fusion.2.refs_3_, ...), custom_call_target="tpu_custom_call" | custom-call | tf_op jit(solution)/shard_map/pallas_call | solution.py:578
  (44 shorter events, 0.6 us)
Async XLA Ops:
  0.6 1.0 %copy-start.4 = (bf16[16,16,64]{2,1,0:T(8,128)(2,1)S(1)}, bf16[16,16,64]{2,1,0:T(8,128)(2,1)}, u32[]{:S(2)}) copy-start(bf16[16,16,64]{2,1,0:T(8,128)(2,1)} %param.7) | copy-start | bytes 98308
  0.6 15.2 %copy-start = (bf16[64,64,128]{2,1,0:T(8,128)(2,1)S(1)}, bf16[64,64,128]{2,1,0:T(8,128)(2,1)}, u32[]{:S(2)}) copy-start(bf16[64,64,128]{2,1,0:T(8,128)(2,1)} %refs_0_.1) | copy-start | bytes 3145732
  2.3 1.4 %collective-permute-start = (bf16[272,128]{1,0:T(8,128)(2,1)S(1)}, bf16[272,128]{1,0:T(8,128)(2,1)S(1)}, u32[]{:S(2)}, u32[]{:S(2)}) collective-permute-start(bf16[272,128]{1,0:T(8,128)(2,1)S(1)} %pad_maximum_fusion.8), channel_id=1, source_target_pairs={{0,1},{1,0},{2,3},{3,2},{4,5},{5,4},{6,7},{7,6},{8,9},{9,8},{10,11... | collective-permute-start | bytes 208904 | tf_op jit(solution)/shard_map/ppermute | solution.py:348
  3.8 13.0 %collective-permute-start.2 = (bf16[2,144,128]{2,1,0:T(8,128)(2,1)S(1)}, bf16[2,144,128]{2,1,0:T(8,128)(2,1)S(1)}, u32[]{:S(2)}, u32[]{:S(2)}) collective-permute-start(bf16[2,144,128]{2,1,0:T(8,128)(2,1)S(1)} %get-tuple-element.59), channel_id=1, source_target_pairs={{0,0},{1,4},{2,8},{3,12},{4,1},{5,5},{6,9},{7,13},{8,2},{9,6},{10,... | collective-permute-start | bytes 221192 | tf_op jit(solution)/shard_map/ppermute | solution.py:433
  4.4 12.3 %collective-permute-start.3 = (bf16[2,144,128]{2,1,0:T(8,128)(2,1)S(1)}, bf16[2,144,128]{2,1,0:T(8,128)(2,1)S(1)}, u32[]{:S(2)}, u32[]{:S(2)}) collective-permute-start(bf16[2,144,128]{2,1,0:T(8,128)(2,1)S(1)} %get-tuple-element.59), channel_id=1, source_target_pairs={{0,8},{1,12},{2,0},{3,4},{4,9},{5,13},{6,1},{7,5},{8,10},{9,14},{1... | collective-permute-start | bytes 221192 | tf_op jit(solution)/shard_map/ppermute | solution.py:433
  10.9 5.0 %copy-start.1 = (bf16[1024,128]{1,0:T(8,128)(2,1)S(1)}, bf16[1024,128]{1,0:T(8,128)(2,1)}, u32[]{:S(2)}) copy-start(bf16[1024,128]{1,0:T(8,128)(2,1)} %wide_ref.1) | copy-start | bytes 786436
  10.9 4.9 %collective-permute-start.1 = (bf16[2,144,128]{2,1,0:T(8,128)(2,1)S(1)}, bf16[2,144,128]{2,1,0:T(8,128)(2,1)S(1)}, u32[]{:S(2)}, u32[]{:S(2)}) collective-permute-start(bf16[2,144,128]{2,1,0:T(8,128)(2,1)S(1)} %get-tuple-element.60.refs_0_), channel_id=1, source_target_pairs={{0,2},{1,3},{2,0},{3,1},{4,6},{5,7},{6,4},{7,5},{8,10},{9,11},{10,... | collective-permute-start | bytes 221192 | tf_op jit(solution)/shard_map/ppermute | solution.py:422
  11.4 4.5 %copy-start.2 = (bf16[64,64]{1,0:T(8,128)(2,1)S(1)}, bf16[64,64]{1,0:T(8,128)(2,1)}, u32[]{:S(2)}) copy-start(bf16[64,64]{1,0:T(8,128)(2,1)} %w_ref.1) | copy-start | bytes 24580
  11.4 4.5 %copy-start.3 = (f32[128]{0:T(128)S(1)}, f32[128]{0:T(128)}, u32[]{:S(2)}) copy-start(f32[128]{0:T(128)} %param.12) | copy-start | bytes 1540
  23.7 7.4 %collective-permute-start.4 = (bf16[512,128]{1,0:T(8,128)(2,1)S(1)}, bf16[512,128]{1,0:T(8,128)(2,1)S(1)}, u32[]{:S(2)}, u32[]{:S(2)}) collective-permute-start(bf16[512,128]{1,0:T(8,128)(2,1)S(1)} %bitcast.104), channel_id=1, source_target_pairs={{0,2},{1,3},{2,0},{3,1},{4,6},{5,7},{6,4},{7,5},{8,10},{9,11},{10,... | collective-permute-start | bytes 393224 | tf_op jit(solution)/shard_map/ppermute | solution.py:348
  31.3 1.4 %collective-permute-start.5 = (bf16[432,128]{1,0:T(8,128)(2,1)S(1)}, bf16[432,128]{1,0:T(8,128)(2,1)S(1)}, u32[]{:S(2)}, u32[]{:S(2)}) collective-permute-start(bf16[432,128]{1,0:T(8,128)(2,1)S(1)} %pad_maximum_fusion.4), channel_id=1, source_target_pairs={{0,1},{1,0},{2,3},{3,2},{4,5},{5,4},{6,7},{7,6},{8,9},{9,8},{10,11... | collective-permute-start | bytes 331784 | tf_op jit(solution)/shard_map/ppermute | solution.py:348
  32.8 5.2 %collective-permute-start.6 = (bf16[432,128]{1,0:T(8,128)(2,1)S(1)}, bf16[432,128]{1,0:T(8,128)(2,1)S(1)}, u32[]{:S(2)}, u32[]{:S(2)}) collective-permute-start(bf16[432,128]{1,0:T(8,128)(2,1)S(1)} %pad_maximum_fusion.5), channel_id=1, source_target_pairs={{0,4},{4,0},{8,12},{12,8},{1,5},{5,1},{9,13},{13,9},{2,6},{6,2},{1... | collective-permute-start | bytes 331784 | tf_op jit(solution)/shard_map/ppermute | solution.py:348
  38.1 9.1 %collective-permute-start.7 = (bf16[432,128]{1,0:T(8,128)(2,1)S(1)}, bf16[432,128]{1,0:T(8,128)(2,1)S(1)}, u32[]{:S(2)}, u32[]{:S(2)}) collective-permute-start(bf16[432,128]{1,0:T(8,128)(2,1)S(1)} %pad_maximum_fusion.6), channel_id=1, source_target_pairs={{0,8},{4,12},{8,0},{12,4},{1,9},{5,13},{9,1},{13,5},{2,10},{6,14},... | collective-permute-start | bytes 331784 | tf_op jit(solution)/shard_map/ppermute | solution.py:348
  47.2 5.0 %collective-permute-start.8 = (bf16[496,128]{1,0:T(8,128)(2,1)S(1)}, bf16[496,128]{1,0:T(8,128)(2,1)S(1)}, u32[]{:S(2)}, u32[]{:S(2)}) collective-permute-start(bf16[496,128]{1,0:T(8,128)(2,1)S(1)} %pad_maximum_fusion.3), channel_id=1, source_target_pairs={{0,2},{1,3},{2,0},{3,1},{4,6},{5,7},{6,4},{7,5},{8,10},{9,11},{10,... | collective-permute-start | bytes 380936 | tf_op jit(solution)/shard_map/ppermute | solution.py:348
  52.3 1.4 %collective-permute-start.9 = (bf16[576,128]{1,0:T(8,128)(2,1)S(1)}, bf16[576,128]{1,0:T(8,128)(2,1)S(1)}, u32[]{:S(2)}, u32[]{:S(2)}) collective-permute-start(bf16[576,128]{1,0:T(8,128)(2,1)S(1)} %pad_maximum_fusion.1), channel_id=1, source_target_pairs={{0,1},{1,0},{2,3},{3,2},{4,5},{5,4},{6,7},{7,6},{8,9},{9,8},{10,11... | collective-permute-start | bytes 442376 | tf_op jit(solution)/shard_map/ppermute | solution.py:348

commit v15 on v14

--- a/solution.py
+++ b/solution.py
@@ -106,35 +106,16 @@
     return jnp.concatenate([held_ref[at + k * block : at + (k + 1) * block, :] for k in range(tiles)], axis=1)
 
 
-def factor_kernel(own, pieces, w_ref, wide_ref, offset_ref, up_ref, *refs):
-    wt_ref, wc_ref, pass_ref, bias_ref, a_ref, at_ref, seen_ref, rows_ref, mi_ref = refs[pieces:]
-    features, width = w_ref.shape[0], w_ref.shape[1] // 2
+def factor_kernel(w_ref, wide_ref, offset_ref, up_ref, wt_ref, wc_ref, pass_ref, bias_ref, rows_ref):
+    width = w_ref.shape[1] // 2
     pair = wide_ref.shape[1]
-    if own % 16 == 0:
-        half = refs[0].shape[1] - own
-        for k in range(pieces):
-            for core in range(2):
-                at = ((lax.axis_index("col") >> 1) ^ k) * 2 + core
-                for q in range(2):
-                    rows = pl.ds(pl.multiple_of((at * 2 + q) * half, half), half)
-                    mi_ref[rows, :] = refs[k][core, :half, q * features : (q + 1) * features]
-                rows = pl.ds(pl.multiple_of(at * own, own), own)
-                seen_ref[rows, :] = refs[k][core, half:, :]
-    else:
-        mi_ref[...] = refs[0][...]
-        seen_ref[...] = refs[1][...]
     pass_ref[...] = offset_ref[...]
     rows_ref[...] = wide_ref[...].astype(F32)
     for e in range(width):
         part = rows_ref[pl.ds(e, width, stride=width), :]
         wc_ref[:, e * pair : (e + 1) * pair] = part.astype(BF16)
     same = one_hot(iota((2 * width, 2 * width), 0) == iota((2 * width, 2 * width), 1))
-    wt = dot_nt(same, w_ref[...]).astype(BF16)
-    wt_ref[...] = wt
-    mi = mi_ref[...]
-    a_ref[...] = dot_nt(mi, wt[:width, :]).astype(BF16)
-    same = one_hot(iota((features, features), 0) == iota((features, features), 1))
-    at_ref[...] = dot_nt(jnp.concatenate([wt[:width, :], same], axis=0), mi).astype(BF16)
+    wt_ref[...] = dot_nt(same, w_ref[...]).astype(BF16)
     bias = [jnp.zeros(up_ref.shape[1:], F32)] * 2
     for i in range(up_ref.shape[0]):
         bias[i % 2] = bias[i % 2] + up_ref[i].astype(F32)
@@ -142,74 +123,84 @@
     bias_ref[...] = jnp.broadcast_to(bias, bias_ref.shape)
 
 
-def weight_kernel(depth, features, own, pieces, part_size, *refs):
-    up_ref, a_ref, at_ref, seen_i_ref, wt_ref, perm_ref, wc_ref = refs[:7]
-    j_refs, refs = refs[7 : 7 + pieces], refs[7 + pieces :]
-    g_ref, held_ref, dw_ref, left_ref, mj_ref, seen_j_ref, bt_ref, inv_ref, v_ref, acc_ref, wide_ref = refs
-    g, last = pl.program_id(0), pl.num_programs(0) - 1
-    chunk, block, pair = up_ref.shape
+def unpack(depth, own, features, a_refs, j_refs, mi_ref, mj_ref, seen_i_ref, seen_j_ref):
+    half = depth * own // 2
+    for k, ref in enumerate(a_refs):
+        for core in range(2):
+            at = ((lax.axis_index("col") >> 1) ^ k) * 2 + core
+            for q in range(2):
+                rows = pl.ds(pl.multiple_of((at * 2 + q) * half, half), half)
+                mi_ref[rows, :] = ref[core, :half, q * features : (q + 1) * features]
+            rows = pl.ds(pl.multiple_of(at * own, own), own)
+            seen_i_ref[rows, :] = ref[core, half:, :]
+    half = depth // 2
+    for k, ref in enumerate(j_refs):
+        for core in range(2):
+            at = ((lax.axis_index("row") >> 1) ^ k) * 2 + core
+            rows = pl.ds(pl.multiple_of(at * own, own), own)
+            seen_j_ref[rows, :] = ref[core, :own, :]
+            for s in range(depth):
+                lanes = slice(s // half * features, (s // half + 1) * features)
+                start = own + s % half * own
+                mj_ref[s, rows, :] = ref[core, start : start + own, lanes]
+
+
+def weight_kernel(depth, features, own, pieces, chunk, *refs):
+    up_ref, wt_ref, perm_ref, wc_ref = refs[:4]
+    a_refs, j_refs, refs = refs[4 : 4 + pieces], refs[4 + pieces : 4 + 2 * pieces], refs[4 + 2 * pieces :]
+    g_ref, held_ref, dw_ref, left_ref, mj_ref = refs[:5]
+    mi_ref, seen_i_ref, seen_j_ref, bt_ref, inv_ref, v_ref = refs[5:]
+    block, pair = up_ref.shape[1:]
     width = wt_ref.shape[0] // 2
-
-    @pl.when(g == 0)
-    def _():
-        if own % 16 == 0:
-            half = depth // 2
-            for k in range(pieces):
-                for core in range(2):
-                    at = ((lax.axis_index("row") >> 1) ^ k) * 2 + core
-                    rows = pl.ds(pl.multiple_of(at * own, own), own)
-                    seen_j_ref[rows, :] = j_refs[k][core, :own, :]
-                    for s in range(depth):
-                        lanes = slice(s // half * features, (s // half + 1) * features)
-                        start = own + s % half * own
-                        mj_ref[s, rows, :] = j_refs[k][core, start : start + own, lanes]
-        else:
-            mj_ref[...] = j_refs[0][...]
-            seen_j_ref[...] = j_refs[1][...]
-        wt = wt_ref[...]
-        b = jnp.zeros((block, width * depth), F32)
-        for s in range(depth):
-            part = dot_nt(mj_ref[s], wt[width:, :]).astype(BF16)
-            b = b + dot(part, perm_ref[s * width : (s + 1) * width, :])
-        bt_ref[...] = b.T.astype(BF16)
-        at = block * depth
-        held_ref[:at, :width] = a_ref[...]
-        for k in range(width * depth // LANES):
-            held_ref[at : at + block, :] = b[:, k * LANES : (k + 1) * LANES].astype(BF16)
-            at += block
-        for k in range(block // part_size):
-            rows = slice(k * part_size, (k + 1) * part_size)
-            count = dot_nt(seen_j_ref[...], seen_i_ref[rows, :])
-            inv_ref[k] = 1.0 / (count + 0.001)
-            held_ref[at : at + block, :part_size] = count.astype(BF16)
-            at += block
-        acc_ref[...] = jnp.zeros_like(acc_ref)
-        wide_ref[...] = jnp.zeros_like(wide_ref)
-
-    for k in range(chunk // part_size):
-        inv = inv_ref[g * (chunk // part_size) + k]
-        for i in range(part_size):
-            up = up_ref[k * part_size + i].astype(F32)
-            at = (k * part_size + i) * pair
-            g_ref[:, at : at + pair] = (up * inv[:, i : i + 1]).astype(BF16)
-    fill_v(g_ref, bt_ref[...], v_ref, depth)
-    span = chunk * depth
-    a_t = at_ref[:, pl.ds(pl.multiple_of(g * span, span), span)]
+    if own % 16 == 0:
+        unpack(depth, own, features, a_refs, j_refs, mi_ref, mj_ref, seen_i_ref, seen_j_ref)
+    else:
+        mi_ref[...], seen_i_ref[...] = a_refs[0][...], a_refs[1][...]
+        mj_ref[...], seen_j_ref[...] = j_refs[0][...], j_refs[1][...]
+    wt = wt_ref[...]
+    mi = mi_ref[...]
+    held_ref[: block * depth, :width] = dot_nt(mi, wt[:width, :]).astype(BF16)
+    same = one_hot(iota((features, features), 0) == iota((features, features), 1))
+    a_t = dot_nt(jnp.concatenate([wt[:width, :], same], axis=0), mi).astype(BF16)
+    b = jnp.zeros((block, width * depth), F32)
+    for s in range(depth):
+        part = dot_nt(mj_ref[s], wt[width:, :]).astype(BF16)
+        b = b + dot(part, perm_ref[s * width : (s + 1) * width, :])
+    bt_ref[...] = b.T.astype(BF16)
+    at = block * depth
+    for k in range(width * depth // LANES):
+        held_ref[at : at + block, :] = b[:, k * LANES : (k + 1) * LANES].astype(BF16)
+        at += block
+    for k in range(block // chunk):
+        count = dot_nt(seen_j_ref[...], seen_i_ref[k * chunk : (k + 1) * chunk, :])
+        inv_ref[k] = 1.0 / (count + 0.001)
+        held_ref[at : at + block, :chunk] = count.astype(BF16)
+        at += block
+
+    def fill(k, carry):
+        inv = inv_ref[k]
+        b_t = bt_ref[...]
+        for i in range(0, chunk, 2):
+            parts = [up_ref[k * chunk + i + q].astype(F32) * inv[:, i + q : i + q + 1] for q in range(2)]
+            scaled = jnp.concatenate(parts, axis=1).astype(BF16)
+            g_ref[:, pl.ds(pl.multiple_of((k * chunk + i) * pair, 2 * pair), 2 * pair)] = scaled
+            v = dot(b_t, scaled).astype(BF16)
+            for q in range(2):
+                rows = pl.ds(pl.multiple_of((k * chunk + i + q) * depth, depth), depth)
+                for e in range(width):
+                    part = v[e * depth : (e + 1) * depth, q * pair : (q + 1) * pair]
+                    v_ref[rows, e * pair : (e + 1) * pair] = part
+        return carry
+
+    lax.fori_loop(0, block // chunk, fill, 0)
+    left = jnp.zeros((width, features), F32)
     for e in range(0, width, 2):
-        part = dot(a_t, v_ref[:, e * pair : (e + 2) * pair])
+        lanes = slice(e * pair, (e + 2) * pair)
+        part = dot(a_t, v_ref[:, lanes]).astype(BF16)
         for k in range(2):
-            rows = slice((e + k) * width, (e + k + 1) * width)
-            acc_ref[rows, :] += part[:width, k * pair : (k + 1) * pair]
-        wide_ref[:, e * pair : (e + 2) * pair] += part[width:]
-
-    @pl.when(g == last)
-    def _():
-        dw_ref[...] = acc_ref[...].astype(BF16)
-        left = jnp.zeros((width, features), F32)
-        for e in range(0, width, 2):
-            lanes = slice(e * pair, (e + 2) * pair)
-            left = left + dot_nt(wc_ref[:, lanes], wide_ref[:, lanes].astype(BF16))
-        left_ref[...] = left
+            dw_ref[(e + k) * width : (e + k + 1) * width, :] = part[:width, k * pair : (k + 1) * pair]
+        left = left + dot_nt(wc_ref[:, lanes], part[width:])
+    left_ref[...] = left
 
 
 def left_kernel(depth, bit, *refs):
@@ -443,51 +434,48 @@
     source = jnp.arange(wide)
     perm = (jnp.arange(wide)[None, :] == (source % width * depth + source // width)[:, None]).astype(BF16)
     up_spec = pl.BlockSpec((chunk, block, pair), lambda g: (g, 0, 0))
-    args = (sitewise_factors, pairing_matrix, offset, upstream_adjoint, *a_pieces)
+    args = (sitewise_factors, pairing_matrix, offset, upstream_adjoint)
     out_shapes = [
         sds((2 * width, features), BF16),
         sds((width, width * pair), BF16),
         sds((1, pair), F32),
         sds((8, pair), F32),
-        sds((tokens, width), BF16),
-        sds((width + features, tokens), BF16),
-        sds((block, LANES), BF16),
     ]
-    factors_t, pairing_wide, offset, bias, a, a_t, seen = call(
-        functools.partial(factor_kernel, own, len(a_pieces)),
+    factors_t, pairing_wide, offset, bias = call(
+        factor_kernel,
         (),
         [full(v.shape) for v in args],
         [full(o.shape) for o in out_shapes],
         out_shapes,
-        [pltpu.VMEM((width * width, pair), F32), pltpu.VMEM((tokens, features), BF16)],
+        [pltpu.VMEM((width * width, pair), F32)],
     )(*args)
 
     out_shapes = [
+        sds((block, block * pair), BF16),
         sds((tokens + block * wide // LANES + block * steps, LANES), BF16),
         sds((width * width, pair), BF16),
         sds((width, features), F32),
         sds((depth, block, features), BF16),
     ]
-    args = (a, a_t, seen, factors_t, perm, pairing_wide, *j_pieces)
-    large = 2 * chunk
-    g_spec = pl.BlockSpec((block, chunk * pair), lambda g: (0, g))
-    large_spec = pl.BlockSpec((large, block, pair), lambda g: (g, 0, 0))
+    args = (upstream_adjoint, factors_t, perm, pairing_wide, *a_pieces, *j_pieces)
     scaled, held, d_pairing, left, mj = call(
-        functools.partial(weight_kernel, depth, features, own, len(j_pieces), chunk),
-        (block // large,),
-        [large_spec] + [full(v.shape) for v in args],
-        [pl.BlockSpec((block, large * pair), lambda g: (0, g))] + [full(o.shape) for o in out_shapes],
-        [sds((block, block * pair), BF16)] + out_shapes,
+        functools.partial(weight_kernel, depth, features, own, len(a_pieces), chunk),
+        (),
+        [full(v.shape) for v in args],
+        [full(o.shape) for o in out_shapes],
+        out_shapes,
         [
+            pltpu.VMEM((tokens, features), BF16),
+            pltpu.VMEM((block, LANES), BF16),
             pltpu.VMEM((block, LANES), BF16),
             pltpu.VMEM((wide, block), BF16),
             pltpu.VMEM((steps, block, chunk), F32),
-            pltpu.VMEM((large * depth, width * pair), BF16),
-            pltpu.VMEM((width * width, pair), F32),
-            pltpu.VMEM((features, width * pair), F32),
+            pltpu.VMEM((tokens, width * pair), BF16),
         ],
         cost(5e9, 8e6),
-    )(upstream_adjoint, *args)
+    )(*args)
+    large = 2 * chunk
+    g_spec = pl.BlockSpec((block, chunk * pair), lambda g: (0, g))
 
     d_pairing = d_pairing.reshape(n, -1, LANES)
     for bit in reversed(range(1, bits)):
@@ -497,11 +485,11 @@
     out_shapes = [sds((width + 16, LANES), BF16), sds((n, own * wide // LANES, LANES), BF16)]
     small, d_b = call(
         functools.partial(token_kernel, depth, features, n),
-        (steps,),
-        [g_spec] + [full(v.shape) for v in (held, pairing_wide, mj, perm, bias, left)],
+        (block // large,),
+        [pl.BlockSpec((block, large * pair), lambda g: (0, g))] + [full(v.shape) for v in (held, pairing_wide, mj, perm, bias, left)],
         [full(o.shape) for o in out_shapes],
         out_shapes,
-        [pltpu.VMEM((wide, chunk * pair), BF16), pltpu.VMEM((wide, block), F32)],
+        [pltpu.VMEM((wide, large * pair), BF16), pltpu.VMEM((wide, block), F32)],
         cost(8e9, 8e6),
     )(scaled, held, pairing_wide, mj, perm, bias, left)
 

time: 56.6 us -> 57.3 us (1.012)
  Pallas kernels: 27.5 us -> 28.8 us
  waiting for transfers between devices: 12.5 us -> 11.2 us
  local copies, waits for them, and re-layouts: 0.27 us -> 0.97 us
    ppermute x1, waiting for transfers between devices: 4.47 us -> 1.63 us  [per_device(): held.append(lax.ppermute(message, 'col', [(j, j ^ k) for j in range(n)]))]
    ppermute x2, waiting for transfers between devices: 0.01 us -> 1.63 us  [per_device(): held.append(lax.ppermute(message, axes, pairs))]
    pallas_call x3, Pallas kernels: 13.4 us -> 14.7 us  [the longest x1 8.86 us: per_device(): call(functools.partial(weight_kernel, depth, features, own, len(a_pieces)...]
    unnamed x11 -> x15, local copies, waits for them, and re-layouts: 0.03 us -> 0.73 us
  transfers between devices with their start and end apart: 10 -> 10, of which waited for: 6 -> 7; matrix products, arithmetic and copies ran while one was open for 0% -> 0% of each run, Pallas kernels for 31% -> 30%
where the time goes in v15:
time: 57.3 us; the launch traced here: 57.1 us
  Pallas kernels  28.8 us (50%)
  starting transfers between devices  13.5 us (24%)
  waiting for transfers between devices  11.2 us (20%)
  other arithmetic  1.56 us (3%)
  between operations  1.1 us (2%)
  local copies, waits for them, and re-layouts  0.97 us (2%)
    pallas_call x1, Pallas kernels, per_device(): call(functools.partial(weight_kernel, depth, features, own, len(a_pieces)...  8.86 us
    ppermute x7, waiting for transfers between devices, swap_parts(): message = lax.ppermute(message, axis, pairs)  7.97 us
    ppermute x2, starting transfers between devices, per_device(): held.append(lax.ppermute(message, axes, pairs))  7.16 us
    pallas_call x1, Pallas kernels, per_device(): call(functools.partial(left_kernel, depth, bits - 1), (steps,), [g_spec]...  6.18 us
    ppermute x7, starting transfers between devices, swap_parts(): message = lax.ppermute(message, axis, pairs)  6.05 us
    pallas_call x1, Pallas kernels, per_device(): call(functools.partial(token_kernel, depth, features, n), (block // large...  5.36 us
    pallas_call x1, Pallas kernels, per_device(): call(functools.partial(update_kernel, depth), (steps,), [full(v.shape) fo...  4.89 us
    pallas_call x1, Pallas kernels, per_device(): call(functools.partial(owner_kernel, depth, own, features), (), [full(v.s...  2.45 us
  transfers between devices with their start and end apart: 10, of which 7 were waited for; matrix products, arithmetic and copies ran while one was open for 0% of the time, Pallas kernels for 30%

profile of v15, /device:TPU:0, one launch (start us, length us, event | category | flops | bytes accessed | tf_op | source)
XLA Modules:
  0.0 57.1 jit_solution(4033056926797127188)
XLA Ops:
  0.6 0.0 copy-start.6
  0.6 0.0 copy-start
  0.7 0.9 %multiply_convert_fusion = bf16[16,16]{1,0:T(8,128)(2,1)S(1)} fusion(s32[16,16]{1,0:T(8,128)} %param.8, s32[16]{0:T(128)} %param.9), kind=kLoop, calls=%fused_computation.52 | loop fusion | flops 512 | bytes 1600 | tf_op jit(solution)/shard_map/convert_element_type | solution.py:396
  1.5 0.1 broadcast_in_dim.2
  1.6 0.0 copy-done.6
  1.6 0.1 pad_maximum_fusion.9
  1.7 0.5 shard_map.111
  2.3 0.5 collective-permute-start
  2.8 0.9 %collective-permute-done = bf16[272,128]{1,0:T(8,128)(2,1)S(1)} collective-permute-done((bf16[272,128]{1,0:T(8,128)(2,1)S(1)}, bf16[272,128]{1,0:T(8,128)(2,1)S(1)}, u32[]{:S(2)}, u32[]{:S(2)}) %collective-permute-start) | collective-permute-done | bytes 69664 | tf_op jit(solution)/shard_map/ppermute | solution.py:339
  3.8 0.7 %collective-permute-start.2 = (bf16[2,144,128]{2,1,0:T(8,128)(2,1)S(1)}, bf16[2,144,128]{2,1,0:T(8,128)(2,1)S(1)}, u32[]{:S(2)}, u32[]{:S(2)}) collective-permute-start(bf16[2,144,128]{2,1,0:T(8,128)(2,1)S(1)} %get-tuple-element.53), channel_id=1, source_target_pairs={{0,0},{1,4},{2,8},{3,12},{4,1},{5,5},{6,9},{7,13},{8,2},{9,6},{10,... | collective-permute-start | bytes 221192 | tf_op jit(solution)/shard_map/ppermute | solution.py:424
  4.4 6.5 %collective-permute-start.3 = (bf16[2,144,128]{2,1,0:T(8,128)(2,1)S(1)}, bf16[2,144,128]{2,1,0:T(8,128)(2,1)S(1)}, u32[]{:S(2)}, u32[]{:S(2)}) collective-permute-start(bf16[2,144,128]{2,1,0:T(8,128)(2,1)S(1)} %get-tuple-element.53), channel_id=1, source_target_pairs={{0,8},{1,12},{2,0},{3,4},{4,9},{5,13},{6,1},{7,5},{8,10},{9,14},{1... | collective-permute-start | bytes 221192 | tf_op jit(solution)/shard_map/ppermute | solution.py:424
  10.9 0.0 copy-start.1
  10.9 0.3 collective-permute-start.1
  11.2 0.1 fusion.refs_2_.refs_4_.refs_7_
  11.4 0.0 copy-start.2
  11.4 0.0 copy-start.3
  11.4 0.0 copy-done
  11.4 0.5 copy-done.1
  11.9 0.2 copy-done.2
  12.1 0.0 copy-done.3
  12.1 0.5 shard_map.110
  12.6 0.0 collective-permute-done.2.refs_6_
  12.6 1.6 %collective-permute-done.3.refs_7_ = bf16[2,144,128]{2,1,0:T(8,128)(2,1)S(1)} collective-permute-done((bf16[2,144,128]{2,1,0:T(8,128)(2,1)S(1)}, bf16[2,144,128]{2,1,0:T(8,128)(2,1)S(1)}, u32[]{:S(2)}, u32[]{:S(2)}) %collective-permute-start.3) | collective-permute-done | bytes 73760 | tf_op jit(solution)/shard_map/ppermute | solution.py:424
  14.2 1.6 %collective-permute-done.1.refs_5_ = bf16[2,144,128]{2,1,0:T(8,128)(2,1)S(1)} collective-permute-done((bf16[2,144,128]{2,1,0:T(8,128)(2,1)S(1)}, bf16[2,144,128]{2,1,0:T(8,128)(2,1)S(1)}, u32[]{:S(2)}, u32[]{:S(2)}) %collective-permute-start.1) | collective-permute-done | bytes 73760 | tf_op jit(solution)/shard_map/ppermute | solution.py:413
  15.9 8.9 %shard_map.112 = (bf16[64,8192]{1,0:T(8,128)(2,1)S(1)}, bf16[1536,128]{1,0:T(8,128)(2,1)S(1)}, bf16[1024,128]{1,0:T(8,128)(2,1)S(1)}, f32[32,64]{1,0:T(8,128)S(1)}, bf16[16,64,64]{2,1,0:T(8,128)(2,1)S(1)}) custom-call(bf16[64,64,128]{2,1,0:T(8,128)(2,1)S(1)} %copy-done, bf16[64,64]{1,0:T(8,128)(2,1)S(1)} %get-tuple-element.27.refs_1_.refs_6_, ...), custom_call_target="tpu_custom_call" | custom-call | flops 5000000000 | bytes 8000000 | tf_op jit(solution)/shard_map/pallas_call | solution.py:461
  24.7 0.0 copy-start.4
  24.8 1.7 %collective-permute-start.4 = (bf16[512,128]{1,0:T(8,128)(2,1)S(1)}, bf16[512,128]{1,0:T(8,128)(2,1)S(1)}, u32[]{:S(2)}, u32[]{:S(2)}) collective-permute-start(bf16[512,128]{1,0:T(8,128)(2,1)S(1)} %bitcast.104), channel_id=1, source_target_pairs={{0,2},{1,3},{2,0},{3,1},{4,6},{5,7},{6,4},{7,5},{8,10},{9,11},{10,... | collective-permute-start | bytes 393224 | tf_op jit(solution)/shard_map/ppermute | solution.py:339
  26.5 5.4 %shard_map.113 = (bf16[48,128]{1,0:T(8,128)(2,1)S(1)}, bf16[4,64,128]{2,1,0:T(8,128)(2,1)S(1)}) custom-call(bf16[64,8192]{1,0:T(8,128)(2,1)S(1)} %get-tuple-element.33.refs_0_, bf16[1536,128]{1,0:T(8,128)(2,1)S(1)} %get-tuple-element.31.refs_1_.refs_0_, bf16[32,4096]{1,0:T(8,128)(2,1)S(1)} %get-tuple-element.28.refs_3_.refs_2_, ...), custom_call_target="tpu_custom_call" | custom-call | flops 8000000000 | bytes 8000000 | tf_op jit(solution)/shard_map/pallas_call | solution.py:486
  31.9 0.0 copy-done.4
  31.9 0.0 collective-permute-done.4
  32.0 0.1 collective-permute-start.5
  32.1 0.0 copy-start.5
  32.1 1.3 %collective-permute-done.5 = bf16[432,128]{1,0:T(8,128)(2,1)S(1)} collective-permute-done((bf16[432,128]{1,0:T(8,128)(2,1)S(1)}, bf16[432,128]{1,0:T(8,128)(2,1)S(1)}, u32[]{:S(2)}, u32[]{:S(2)}) %collective-permute-start.5) | collective-permute-done | bytes 110624 | tf_op jit(solution)/shard_map/ppermute | solution.py:339
  33.5 0.1 collective-permute-start.6
  33.6 0.0 copy-done.5
  33.6 4.9 %shard_map.114 = (bf16[64,64,128]{2,1,0:T(8,128)(2,1)}, bf16[48,128]{1,0:T(8,128)(2,1)S(1)}) custom-call(bf16[1536,128]{1,0:T(8,128)(2,1)S(1)} %copy-done.5, f32[1,128]{1,0:T(1,128)S(1)} %get-tuple-element.32.refs_1_, bf16[32,4096]{1,0:T(8,128)(2,1)S(1)} %get-tuple-element.28.refs_3_.refs_2_, bf16[48,128]{1,0:T(8,128)(2,1)S(1)} %add_convert_fusion.4.refs_3_), custom_call_target="tpu_custom_call" | custom-call | flops 6000000000 | bytes 8000000 | tf_op jit(solution)/shard_map/pallas_call | solution.py:506
  38.5 0.2 collective-permute-done.6
  38.8 2.9 %collective-permute-start.7 = (bf16[432,128]{1,0:T(8,128)(2,1)S(1)}, bf16[432,128]{1,0:T(8,128)(2,1)S(1)}, u32[]{:S(2)}, u32[]{:S(2)}) collective-permute-start(bf16[432,128]{1,0:T(8,128)(2,1)S(1)} %pad_maximum_fusion.6), channel_id=1, source_target_pairs={{0,8},{4,12},{8,0},{12,4},{1,9},{5,13},{9,1},{13,5},{2,10},{6,14},... | collective-permute-start | bytes 331784 | tf_op jit(solution)/shard_map/ppermute | solution.py:339
  41.7 6.2 %shard_map.115 = (bf16[4,32,128]{2,1,0:T(8,128)(2,1)S(1)}, bf16[4,32,128]{2,1,0:T(8,128)(2,1)S(1)}, bf16[48,128]{1,0:T(8,128)(2,1)S(1)}) custom-call(bf16[64,8192]{1,0:T(8,128)(2,1)S(1)} %get-tuple-element.33.refs_0_, bf16[1536,128]{1,0:T(8,128)(2,1)S(1)} %copy-done.5, bf16[32,4096]{1,0:T(8,128)(2,1)S(1)} %get-tuple-element.28.refs_3_.refs_2_, ...), custom_call_target="tpu_custom_call" | custom-call | flops 6000000000 | bytes 8000000 | tf_op jit(solution)/shard_map/pallas_call | solution.py:518
  47.8 0.0 collective-permute-done.7
  48.0 0.7 %collective-permute-start.8 = (bf16[496,128]{1,0:T(8,128)(2,1)S(1)}, bf16[496,128]{1,0:T(8,128)(2,1)S(1)}, u32[]{:S(2)}, u32[]{:S(2)}) collective-permute-start(bf16[496,128]{1,0:T(8,128)(2,1)S(1)} %pad_maximum_fusion.3), channel_id=1, source_target_pairs={{0,2},{1,3},{2,0},{3,1},{4,6},{5,7},{6,4},{7,5},{8,10},{9,11},{10,... | collective-permute-start | bytes 380936 | tf_op jit(solution)/shard_map/ppermute | solution.py:339
  48.7 4.3 %collective-permute-done.8 = bf16[496,128]{1,0:T(8,128)(2,1)S(1)} collective-permute-done((bf16[496,128]{1,0:T(8,128)(2,1)S(1)}, bf16[496,128]{1,0:T(8,128)(2,1)S(1)}, u32[]{:S(2)}, u32[]{:S(2)}) %collective-permute-start.8) | collective-permute-done | bytes 127008 | tf_op jit(solution)/shard_map/ppermute | solution.py:339
  53.1 0.1 collective-permute-start.9
  53.2 1.3 %collective-permute-done.9 = bf16[576,128]{1,0:T(8,128)(2,1)S(1)} collective-permute-done((bf16[576,128]{1,0:T(8,128)(2,1)S(1)}, bf16[576,128]{1,0:T(8,128)(2,1)S(1)}, u32[]{:S(2)}, u32[]{:S(2)}) %collective-permute-start.9) | collective-permute-done | bytes 147488 | tf_op jit(solution)/shard_map/ppermute | solution.py:339
  54.7 2.4 %shard_map.116 = (f32[256,64]{1,0:T(8,128)}, f32[64,64]{1,0:T(8,128)}, f32[1,128]{1,0:T(1,128)}, f32[32,32,128]{2,1,0:T(8,128)}) custom-call(bf16[32,256]{1,0:T(8,128)(2,1)S(1)} %bitcast.89, bf16[32,256]{1,0:T(8,128)(2,1)S(1)} %bitcast.90, bf16[16,512]{1,0:T(8,128)(2,1)S(1)} %bitcast.88, bf16[48,128]{1,0:T(8,128)(2,1)S(1)} %add_convert_fusion.2.refs_3_, ...), custom_call_target="tpu_custom_call" | custom-call | tf_op jit(solution)/shard_map/pallas_call | solution.py:566
  (44 shorter events, 0.6 us)
Async XLA Ops:
  0.6 1.0 %copy-start.6 = (bf16[16,16,64]{2,1,0:T(8,128)(2,1)S(1)}, bf16[16,16,64]{2,1,0:T(8,128)(2,1)}, u32[]{:S(2)}) copy-start(bf16[16,16,64]{2,1,0:T(8,128)(2,1)} %param.7) | copy-start | bytes 98308
  0.6 10.8 %copy-start = (bf16[64,64,128]{2,1,0:T(8,128)(2,1)S(1)}, bf16[64,64,128]{2,1,0:T(8,128)(2,1)}, u32[]{:S(2)}) copy-start(bf16[64,64,128]{2,1,0:T(8,128)(2,1)} %refs_0_.1) | copy-start | bytes 3145732
  2.3 1.4 %collective-permute-start = (bf16[272,128]{1,0:T(8,128)(2,1)S(1)}, bf16[272,128]{1,0:T(8,128)(2,1)S(1)}, u32[]{:S(2)}, u32[]{:S(2)}) collective-permute-start(bf16[272,128]{1,0:T(8,128)(2,1)S(1)} %pad_maximum_fusion.8), channel_id=1, source_target_pairs={{0,1},{1,0},{2,3},{3,2},{4,5},{5,4},{6,7},{7,6},{8,9},{9,8},{10,11... | collective-permute-start | bytes 208904 | tf_op jit(solution)/shard_map/ppermute | solution.py:339
  3.8 8.9 %collective-permute-start.2 = (bf16[2,144,128]{2,1,0:T(8,128)(2,1)S(1)}, bf16[2,144,128]{2,1,0:T(8,128)(2,1)S(1)}, u32[]{:S(2)}, u32[]{:S(2)}) collective-permute-start(bf16[2,144,128]{2,1,0:T(8,128)(2,1)S(1)} %get-tuple-element.53), channel_id=1, source_target_pairs={{0,0},{1,4},{2,8},{3,12},{4,1},{5,5},{6,9},{7,13},{8,2},{9,6},{10,... | collective-permute-start | bytes 221192 | tf_op jit(solution)/shard_map/ppermute | solution.py:424
  4.4 9.8 %collective-permute-start.3 = (bf16[2,144,128]{2,1,0:T(8,128)(2,1)S(1)}, bf16[2,144,128]{2,1,0:T(8,128)(2,1)S(1)}, u32[]{:S(2)}, u32[]{:S(2)}) collective-permute-start(bf16[2,144,128]{2,1,0:T(8,128)(2,1)S(1)} %get-tuple-element.53), channel_id=1, source_target_pairs={{0,8},{1,12},{2,0},{3,4},{4,9},{5,13},{6,1},{7,5},{8,10},{9,14},{1... | collective-permute-start | bytes 221192 | tf_op jit(solution)/shard_map/ppermute | solution.py:424
  10.9 0.9 %copy-start.1 = (bf16[1024,128]{1,0:T(8,128)(2,1)S(1)}, bf16[1024,128]{1,0:T(8,128)(2,1)}, u32[]{:S(2)}) copy-start(bf16[1024,128]{1,0:T(8,128)(2,1)} %wide_ref.1) | copy-start | bytes 786436
  10.9 4.9 %collective-permute-start.1 = (bf16[2,144,128]{2,1,0:T(8,128)(2,1)S(1)}, bf16[2,144,128]{2,1,0:T(8,128)(2,1)S(1)}, u32[]{:S(2)}, u32[]{:S(2)}) collective-permute-start(bf16[2,144,128]{2,1,0:T(8,128)(2,1)S(1)} %get-tuple-element.54.refs_4_), channel_id=1, source_target_pairs={{0,2},{1,3},{2,0},{3,1},{4,6},{5,7},{6,4},{7,5},{8,10},{9,11},{10,... | collective-permute-start | bytes 221192 | tf_op jit(solution)/shard_map/ppermute | solution.py:413
  11.4 0.7 %copy-start.2 = (bf16[64,64]{1,0:T(8,128)(2,1)S(1)}, bf16[64,64]{1,0:T(8,128)(2,1)}, u32[]{:S(2)}) copy-start(bf16[64,64]{1,0:T(8,128)(2,1)} %w_ref.1) | copy-start | bytes 24580
  11.4 0.7 %copy-start.3 = (f32[128]{0:T(128)S(1)}, f32[128]{0:T(128)}, u32[]{:S(2)}) copy-start(f32[128]{0:T(128)} %param.12) | copy-start | bytes 1540
  24.7 7.1 %copy-start.4 = (bf16[1536,128]{1,0:T(8,128)(2,1)}, bf16[1536,128]{1,0:T(8,128)(2,1)S(1)}, u32[]{:S(2)}) copy-start(bf16[1536,128]{1,0:T(8,128)(2,1)S(1)} %get-tuple-element.31.refs_1_.refs_0_) | copy-start | bytes 1179652
  24.8 7.1 %collective-permute-start.4 = (bf16[512,128]{1,0:T(8,128)(2,1)S(1)}, bf16[512,128]{1,0:T(8,128)(2,1)S(1)}, u32[]{:S(2)}, u32[]{:S(2)}) collective-permute-start(bf16[512,128]{1,0:T(8,128)(2,1)S(1)} %bitcast.104), channel_id=1, source_target_pairs={{0,2},{1,3},{2,0},{3,1},{4,6},{5,7},{6,4},{7,5},{8,10},{9,11},{10,... | collective-permute-start | bytes 393224 | tf_op jit(solution)/shard_map/ppermute | solution.py:339
  32.0 1.4 %collective-permute-start.5 = (bf16[432,128]{1,0:T(8,128)(2,1)S(1)}, bf16[432,128]{1,0:T(8,128)(2,1)S(1)}, u32[]{:S(2)}, u32[]{:S(2)}) collective-permute-start(bf16[432,128]{1,0:T(8,128)(2,1)S(1)} %pad_maximum_fusion.4), channel_id=1, source_target_pairs={{0,1},{1,0},{2,3},{3,2},{4,5},{5,4},{6,7},{7,6},{8,9},{9,8},{10,11... | collective-permute-start | bytes 331784 | tf_op jit(solution)/shard_map/ppermute | solution.py:339
  32.1 1.5 %copy-start.5 = (bf16[1536,128]{1,0:T(8,128)(2,1)S(1)}, bf16[1536,128]{1,0:T(8,128)(2,1)}, u32[]{:S(2)}) copy-start(bf16[1536,128]{1,0:T(8,128)(2,1)} %copy-done.4) | copy-start | bytes 1179652
  33.5 5.2 %collective-permute-start.6 = (bf16[432,128]{1,0:T(8,128)(2,1)S(1)}, bf16[432,128]{1,0:T(8,128)(2,1)S(1)}, u32[]{:S(2)}, u32[]{:S(2)}) collective-permute-start(bf16[432,128]{1,0:T(8,128)(2,1)S(1)} %pad_maximum_fusion.5), channel_id=1, source_target_pairs={{0,4},{4,0},{8,12},{12,8},{1,5},{5,1},{9,13},{13,9},{2,6},{6,2},{1... | collective-permute-start | bytes 331784 | tf_op jit(solution)/shard_map/ppermute | solution.py:339
  38.8 9.0 %collective-permute-start.7 = (bf16[432,128]{1,0:T(8,128)(2,1)S(1)}, bf16[432,128]{1,0:T(8,128)(2,1)S(1)}, u32[]{:S(2)}, u32[]{:S(2)}) collective-permute-start(bf16[432,128]{1,0:T(8,128)(2,1)S(1)} %pad_maximum_fusion.6), channel_id=1, source_target_pairs={{0,8},{4,12},{8,0},{12,4},{1,9},{5,13},{9,1},{13,5},{2,10},{6,14},... | collective-permute-start | bytes 331784 | tf_op jit(solution)/shard_map/ppermute | solution.py:339
  48.0 5.0 %collective-permute-start.8 = (bf16[496,128]{1,0:T(8,128)(2,1)S(1)}, bf16[496,128]{1,0:T(8,128)(2,1)S(1)}, u32[]{:S(2)}, u32[]{:S(2)}) collective-permute-start(bf16[496,128]{1,0:T(8,128)(2,1)S(1)} %pad_maximum_fusion.3), channel_id=1, source_target_pairs={{0,2},{1,3},{2,0},{3,1},{4,6},{5,7},{6,4},{7,5},{8,10},{9,11},{10,... | collective-permute-start | bytes 380936 | tf_op jit(solution)/shard_map/ppermute | solution.py:339
  53.1 1.4 %collective-permute-start.9 = (bf16[576,128]{1,0:T(8,128)(2,1)S(1)}, bf16[576,128]{1,0:T(8,128)(2,1)S(1)}, u32[]{:S(2)}, u32[]{:S(2)}) collective-permute-start(bf16[576,128]{1,0:T(8,128)(2,1)S(1)} %pad_maximum_fusion.1), channel_id=1, source_target_pairs={{0,1},{1,0},{2,3},{3,2},{4,5},{5,4},{6,7},{7,6},{8,9},{9,8},{10,11... | collective-permute-start | bytes 442376 | tf_op jit(solution)/shard_map/ppermute | solution.py:339

commit v16 on v14

--- a/solution.py
+++ b/solution.py
@@ -106,35 +106,16 @@
     return jnp.concatenate([held_ref[at + k * block : at + (k + 1) * block, :] for k in range(tiles)], axis=1)
 
 
-def factor_kernel(own, pieces, w_ref, wide_ref, offset_ref, up_ref, *refs):
-    wt_ref, wc_ref, pass_ref, bias_ref, a_ref, at_ref, seen_ref, rows_ref, mi_ref = refs[pieces:]
-    features, width = w_ref.shape[0], w_ref.shape[1] // 2
+def factor_kernel(w_ref, wide_ref, offset_ref, up_ref, wt_ref, wc_ref, pass_ref, bias_ref, rows_ref):
+    width = w_ref.shape[1] // 2
     pair = wide_ref.shape[1]
-    if own % 16 == 0:
-        half = refs[0].shape[1] - own
-        for k in range(pieces):
-            for core in range(2):
-                at = ((lax.axis_index("col") >> 1) ^ k) * 2 + core
-                for q in range(2):
-                    rows = pl.ds(pl.multiple_of((at * 2 + q) * half, half), half)
-                    mi_ref[rows, :] = refs[k][core, :half, q * features : (q + 1) * features]
-                rows = pl.ds(pl.multiple_of(at * own, own), own)
-                seen_ref[rows, :] = refs[k][core, half:, :]
-    else:
-        mi_ref[...] = refs[0][...]
-        seen_ref[...] = refs[1][...]
     pass_ref[...] = offset_ref[...]
     rows_ref[...] = wide_ref[...].astype(F32)
     for e in range(width):
         part = rows_ref[pl.ds(e, width, stride=width), :]
         wc_ref[:, e * pair : (e + 1) * pair] = part.astype(BF16)
     same = one_hot(iota((2 * width, 2 * width), 0) == iota((2 * width, 2 * width), 1))
-    wt = dot_nt(same, w_ref[...]).astype(BF16)
-    wt_ref[...] = wt
-    mi = mi_ref[...]
-    a_ref[...] = dot_nt(mi, wt[:width, :]).astype(BF16)
-    same = one_hot(iota((features, features), 0) == iota((features, features), 1))
-    at_ref[...] = dot_nt(jnp.concatenate([wt[:width, :], same], axis=0), mi).astype(BF16)
+    wt_ref[...] = dot_nt(same, w_ref[...]).astype(BF16)
     bias = [jnp.zeros(up_ref.shape[1:], F32)] * 2
     for i in range(up_ref.shape[0]):
         bias[i % 2] = bias[i % 2] + up_ref[i].astype(F32)
@@ -142,10 +123,33 @@
     bias_ref[...] = jnp.broadcast_to(bias, bias_ref.shape)
 
 
+def unpack(depth, own, features, a_refs, j_refs, mi_ref, mj_ref, seen_i_ref, seen_j_ref):
+    half = depth * own // 2
+    for k, ref in enumerate(a_refs):
+        for core in range(2):
+            at = ((lax.axis_index("col") >> 1) ^ k) * 2 + core
+            for q in range(2):
+                rows = pl.ds(pl.multiple_of((at * 2 + q) * half, half), half)
+                mi_ref[rows, :] = ref[core, :half, q * features : (q + 1) * features]
+            rows = pl.ds(pl.multiple_of(at * own, own), own)
+            seen_i_ref[rows, :] = ref[core, half:, :]
+    half = depth // 2
+    for k, ref in enumerate(j_refs):
+        for core in range(2):
+            at = ((lax.axis_index("row") & (len(j_refs) - 1)) ^ k) * 2 + core
+            rows = pl.ds(pl.multiple_of(at * own, own), own)
+            seen_j_ref[rows, :] = ref[core, :own, :]
+            for s in range(depth):
+                lanes = slice(s // half * features, (s // half + 1) * features)
+                start = own + s % half * own
+                mj_ref[s, rows, :] = ref[core, start : start + own, lanes]
+
+
 def weight_kernel(depth, features, own, pieces, part_size, *refs):
-    up_ref, a_ref, at_ref, seen_i_ref, wt_ref, perm_ref, wc_ref = refs[:7]
-    j_refs, refs = refs[7 : 7 + pieces], refs[7 + pieces :]
-    g_ref, held_ref, dw_ref, left_ref, mj_ref, seen_j_ref, bt_ref, inv_ref, v_ref, acc_ref, wide_ref = refs
+    up_ref, wt_ref, perm_ref, wc_ref = refs[:4]
+    a_refs, j_refs, refs = refs[4 : 4 + pieces], refs[4 + pieces : 4 + 2 * pieces], refs[4 + 2 * pieces :]
+    g_ref, held_ref, dw_ref, left_ref, mj_ref = refs[:5]
+    mi_ref, seen_i_ref, seen_j_ref, at_ref, bt_ref, inv_ref, v_ref, acc_ref, wide_ref = refs[5:]
     g, last = pl.program_id(0), pl.num_programs(0) - 1
     chunk, block, pair = up_ref.shape
     width = wt_ref.shape[0] // 2
@@ -153,27 +157,21 @@
     @pl.when(g == 0)
     def _():
         if own % 16 == 0:
-            half = depth // 2
-            for k in range(pieces):
-                for core in range(2):
-                    at = ((lax.axis_index("row") >> 1) ^ k) * 2 + core
-                    rows = pl.ds(pl.multiple_of(at * own, own), own)
-                    seen_j_ref[rows, :] = j_refs[k][core, :own, :]
-                    for s in range(depth):
-                        lanes = slice(s // half * features, (s // half + 1) * features)
-                        start = own + s % half * own
-                        mj_ref[s, rows, :] = j_refs[k][core, start : start + own, lanes]
+            unpack(depth, own, features, a_refs, j_refs, mi_ref, mj_ref, seen_i_ref, seen_j_ref)
         else:
-            mj_ref[...] = j_refs[0][...]
-            seen_j_ref[...] = j_refs[1][...]
+            mi_ref[...], seen_i_ref[...] = a_refs[0][...], a_refs[1][...]
+            mj_ref[...], seen_j_ref[...] = j_refs[0][...], j_refs[1][...]
         wt = wt_ref[...]
+        mi = mi_ref[...]
+        held_ref[: block * depth, :width] = dot_nt(mi, wt[:width, :]).astype(BF16)
+        same = one_hot(iota((features, features), 0) == iota((features, features), 1))
+        at_ref[...] = dot_nt(jnp.concatenate([wt[:width, :], same], axis=0), mi).astype(BF16)
         b = jnp.zeros((block, width * depth), F32)
         for s in range(depth):
             part = dot_nt(mj_ref[s], wt[width:, :]).astype(BF16)
             b = b + dot(part, perm_ref[s * width : (s + 1) * width, :])
         bt_ref[...] = b.T.astype(BF16)
         at = block * depth
-        held_ref[:at, :width] = a_ref[...]
         for k in range(width * depth // LANES):
             held_ref[at : at + block, :] = b[:, k * LANES : (k + 1) * LANES].astype(BF16)
             at += block
@@ -369,11 +367,11 @@
     return jnp.stack([low, jnp.where(first, other, mine)], axis=at)
 
 
-def unswap(x, axis):
+def unswap(x, axis, first):
     n = x.shape[0]
     for bit in range(n.bit_length() - 1):
         y = x.reshape((n >> (bit + 1), 2, 1 << bit) + x.shape[1:])
-        x = jnp.where(bit_of(axis, bit + 1) == 0, y, y[:, ::-1]).reshape(x.shape)
+        x = jnp.where(bit_of(axis, bit + first) == 0, y, y[:, ::-1]).reshape(x.shape)
     return x
 
 
@@ -422,18 +420,20 @@
         held.append(lax.ppermute(message, "col", [(j, j ^ k) for j in range(n)]))
     a_pieces = held
     if own % 16:
-        held = unswap(jnp.stack(held), "col").reshape((n,) + message.shape[1:])
+        held = unswap(jnp.stack(held), "col", 1).reshape((n,) + message.shape[1:])
         parts = held[:, : rows // 2].reshape(n, rows // 2, 2, features)
         mi = parts.transpose(0, 2, 1, 3).reshape(block * depth, features)
         a_pieces = [mi, held[:, rows // 2 :].reshape(block, LANES)]
     message = both[:, rows // 2 :]
     held = []
-    for k in range(0, n, 2):
-        pairs = [(i * n + j, (j ^ k) * n + i) for i in range(n) for j in range(n)]
+    half = n // 2
+    for k in range(half):
+        target = [((j >> 1) | (j & 1) * half) ^ half ^ k for j in range(n)]
+        pairs = [(i * n + j, target[j] * n + i) for i in range(n) for j in range(n)]
         held.append(lax.ppermute(message, axes, pairs))
     j_pieces = held
     if own % 16:
-        held = unswap(jnp.stack(held), "row").reshape((n,) + message.shape[1:])
+        held = unswap(jnp.stack(held), "row", 0).reshape((n,) + message.shape[1:])
         parts = held[:, own:].reshape(n, depth // 2, own, 2, features)
         mj = parts.transpose(3, 1, 0, 2, 4).reshape(depth, block, features)
         j_pieces = [mj, held[:, :own].reshape(block, LANES)]
@@ -443,43 +443,44 @@
     source = jnp.arange(wide)
     perm = (jnp.arange(wide)[None, :] == (source % width * depth + source // width)[:, None]).astype(BF16)
     up_spec = pl.BlockSpec((chunk, block, pair), lambda g: (g, 0, 0))
-    args = (sitewise_factors, pairing_matrix, offset, upstream_adjoint, *a_pieces)
+    args = (sitewise_factors, pairing_matrix, offset, upstream_adjoint)
     out_shapes = [
         sds((2 * width, features), BF16),
         sds((width, width * pair), BF16),
         sds((1, pair), F32),
         sds((8, pair), F32),
-        sds((tokens, width), BF16),
-        sds((width + features, tokens), BF16),
-        sds((block, LANES), BF16),
     ]
-    factors_t, pairing_wide, offset, bias, a, a_t, seen = call(
-        functools.partial(factor_kernel, own, len(a_pieces)),
+    factors_t, pairing_wide, offset, bias = call(
+        factor_kernel,
         (),
         [full(v.shape) for v in args],
         [full(o.shape) for o in out_shapes],
         out_shapes,
-        [pltpu.VMEM((width * width, pair), F32), pltpu.VMEM((tokens, features), BF16)],
+        [pltpu.VMEM((width * width, pair), F32)],
     )(*args)
 
     out_shapes = [
+        sds((block, block * pair), BF16),
         sds((tokens + block * wide // LANES + block * steps, LANES), BF16),
         sds((width * width, pair), BF16),
         sds((width, features), F32),
         sds((depth, block, features), BF16),
     ]
-    args = (a, a_t, seen, factors_t, perm, pairing_wide, *j_pieces)
+    args = (upstream_adjoint, factors_t, perm, pairing_wide, *a_pieces, *j_pieces)
     large = 2 * chunk
     g_spec = pl.BlockSpec((block, chunk * pair), lambda g: (0, g))
-    large_spec = pl.BlockSpec((large, block, pair), lambda g: (g, 0, 0))
+    large_spec = pl.BlockSpec((block, large * pair), lambda g: (0, g))
     scaled, held, d_pairing, left, mj = call(
-        functools.partial(weight_kernel, depth, features, own, len(j_pieces), chunk),
+        functools.partial(weight_kernel, depth, features, own, len(a_pieces), chunk),
         (block // large,),
-        [large_spec] + [full(v.shape) for v in args],
-        [pl.BlockSpec((block, large * pair), lambda g: (0, g))] + [full(o.shape) for o in out_shapes],
-        [sds((block, block * pair), BF16)] + out_shapes,
+        [pl.BlockSpec((large, block, pair), lambda g: (g, 0, 0))] + [full(v.shape) for v in args[1:]],
+        [large_spec] + [full(o.shape) for o in out_shapes[1:]],
+        out_shapes,
         [
+            pltpu.VMEM((tokens, features), BF16),
             pltpu.VMEM((block, LANES), BF16),
+            pltpu.VMEM((block, LANES), BF16),
+            pltpu.VMEM((width + features, tokens), BF16),
             pltpu.VMEM((wide, block), BF16),
             pltpu.VMEM((steps, block, chunk), F32),
             pltpu.VMEM((large * depth, width * pair), BF16),
@@ -487,7 +488,7 @@
             pltpu.VMEM((features, width * pair), F32),
         ],
         cost(5e9, 8e6),
-    )(upstream_adjoint, *args)
+    )(*args)
 
     d_pairing = d_pairing.reshape(n, -1, LANES)
     for bit in reversed(range(1, bits)):
@@ -497,11 +498,11 @@
     out_shapes = [sds((width + 16, LANES), BF16), sds((n, own * wide // LANES, LANES), BF16)]
     small, d_b = call(
         functools.partial(token_kernel, depth, features, n),
-        (steps,),
-        [g_spec] + [full(v.shape) for v in (held, pairing_wide, mj, perm, bias, left)],
+        (block // large,),
+        [large_spec] + [full(v.shape) for v in (held, pairing_wide, mj, perm, bias, left)],
         [full(o.shape) for o in out_shapes],
         out_shapes,
-        [pltpu.VMEM((wide, chunk * pair), BF16), pltpu.VMEM((wide, block), F32)],
+        [pltpu.VMEM((wide, large * pair), BF16), pltpu.VMEM((wide, block), F32)],
         cost(8e9, 8e6),
     )(scaled, held, pairing_wide, mj, perm, bias, left)
 

time: 56.6 us -> 54.8 us (0.968)
  waiting for transfers between devices: 12.5 us -> 10.3 us
  local copies, waits for them, and re-layouts: 0.27 us -> 0.95 us
    ppermute x1, waiting for transfers between devices: 4.47 us -> 2.15 us  [per_device(): held.append(lax.ppermute(message, 'col', [(j, j ^ k) for j in range(n)]))]
    ppermute x7, starting transfers between devices: 6.03 us -> 4.77 us  [swap_parts(): message = lax.ppermute(message, axis, pairs)]
    ppermute x2, starting transfers between devices: 7.16 us -> 8.04 us  [per_device(): held.append(lax.ppermute(message, axes, pairs))]
    unnamed x11 -> x15, local copies, waits for them, and re-layouts: 0.03 us -> 0.71 us
    ppermute x1, starting transfers between devices: 0.29 us -> 0.87 us  [per_device(): held.append(lax.ppermute(message, 'col', [(j, j ^ k) for j in range(n)]))]
where the time goes in v16:
time: 54.8 us; the launch traced here: 54.6 us
  Pallas kernels  27 us (49%)
  starting transfers between devices  13.7 us (25%)
  waiting for transfers between devices  10.3 us (19%)
  other arithmetic  1.55 us (3%)
  between operations  1.1 us (2%)
  local copies, waits for them, and re-layouts  0.95 us (2%)
    ppermute x7, waiting for transfers between devices, swap_parts(): message = lax.ppermute(message, axis, pairs)  8.14 us
    ppermute x2, starting transfers between devices, per_device(): held.append(lax.ppermute(message, axes, pairs))  8.04 us
    pallas_call x1, Pallas kernels, per_device(): call(functools.partial(weight_kernel, depth, features, own, len(a_pieces)...  7.18 us
    pallas_call x1, Pallas kernels, per_device(): call(functools.partial(left_kernel, depth, bits - 1), (steps,), [g_spec]...  6.18 us
    pallas_call x1, Pallas kernels, per_device(): call(functools.partial(token_kernel, depth, features, n), (block // large...  5.34 us
    pallas_call x1, Pallas kernels, per_device(): call(functools.partial(update_kernel, depth), (steps,), [full(v.shape) fo...  4.86 us
    ppermute x7, starting transfers between devices, swap_parts(): message = lax.ppermute(message, axis, pairs)  4.77 us
    pallas_call x1, Pallas kernels, per_device(): call(functools.partial(owner_kernel, depth, own, features), (), [full(v.s...  2.45 us
  transfers between devices with their start and end apart: 10, of which 6 were waited for; matrix products, arithmetic and copies ran while one was open for 0% of the time, Pallas kernels for 31%

profile of v16, /device:TPU:0, one launch (start us, length us, event | category | flops | bytes accessed | tf_op | source)
XLA Modules:
  0.0 54.6 jit_solution(18102488658645666476)
XLA Ops:
  0.6 0.0 copy-start.6
  0.6 0.0 copy-start
  0.7 0.9 %multiply_convert_fusion = bf16[16,16]{1,0:T(8,128)(2,1)S(1)} fusion(s32[16,16]{1,0:T(8,128)} %param.8, s32[16]{0:T(128)} %param.9), kind=kLoop, calls=%fused_computation.52 | loop fusion | flops 512 | bytes 1600 | tf_op jit(solution)/shard_map/convert_element_type | solution.py:403
  1.5 0.1 broadcast_in_dim.2
  1.6 0.0 copy-done.6
  1.6 0.1 pad_maximum_fusion.9
  1.7 0.5 shard_map.111
  2.3 0.5 collective-permute-start
  2.8 0.9 %collective-permute-done = bf16[272,128]{1,0:T(8,128)(2,1)S(1)} collective-permute-done((bf16[272,128]{1,0:T(8,128)(2,1)S(1)}, bf16[272,128]{1,0:T(8,128)(2,1)S(1)}, u32[]{:S(2)}, u32[]{:S(2)}) %collective-permute-start) | collective-permute-done | bytes 69664 | tf_op jit(solution)/shard_map/ppermute | solution.py:346
  3.8 4.0 %collective-permute-start.2 = (bf16[2,144,128]{2,1,0:T(8,128)(2,1)S(1)}, bf16[2,144,128]{2,1,0:T(8,128)(2,1)S(1)}, u32[]{:S(2)}, u32[]{:S(2)}) collective-permute-start(bf16[2,144,128]{2,1,0:T(8,128)(2,1)S(1)} %get-tuple-element.53), channel_id=1, source_target_pairs={{0,8},{1,0},{2,12},{3,4},{4,9},{5,1},{6,13},{7,5},{8,10},{9,2},{10... | collective-permute-start | bytes 221192 | tf_op jit(solution)/shard_map/ppermute | solution.py:433
  7.8 4.0 %collective-permute-start.3 = (bf16[2,144,128]{2,1,0:T(8,128)(2,1)S(1)}, bf16[2,144,128]{2,1,0:T(8,128)(2,1)S(1)}, u32[]{:S(2)}, u32[]{:S(2)}) collective-permute-start(bf16[2,144,128]{2,1,0:T(8,128)(2,1)S(1)} %get-tuple-element.53), channel_id=1, source_target_pairs={{0,12},{1,4},{2,8},{3,0},{4,13},{5,5},{6,9},{7,1},{8,14},{9,6},{10... | collective-permute-start | bytes 221192 | tf_op jit(solution)/shard_map/ppermute | solution.py:433
  11.8 0.0 copy-start.1
  11.8 0.9 %collective-permute-start.1 = (bf16[2,144,128]{2,1,0:T(8,128)(2,1)S(1)}, bf16[2,144,128]{2,1,0:T(8,128)(2,1)S(1)}, u32[]{:S(2)}, u32[]{:S(2)}) collective-permute-start(bf16[2,144,128]{2,1,0:T(8,128)(2,1)S(1)} %get-tuple-element.54.refs_4_), channel_id=1, source_target_pairs={{0,2},{1,3},{2,0},{3,1},{4,6},{5,7},{6,4},{7,5},{8,10},{9,11},{10,... | collective-permute-start | bytes 221192 | tf_op jit(solution)/shard_map/ppermute | solution.py:420
  12.7 0.1 fusion.refs_2_.refs_4_.refs_7_
  12.8 0.0 copy-start.2
  12.9 0.0 copy-start.3
  12.9 0.0 copy-done
  12.9 0.0 copy-done.1
  12.9 0.7 %copy-done.2 = bf16[64,64]{1,0:T(8,128)(2,1)S(1)} copy-done((bf16[64,64]{1,0:T(8,128)(2,1)S(1)}, bf16[64,64]{1,0:T(8,128)(2,1)}, u32[]{:S(2)}) %copy-start.2) | copy-done | bytes 8216
  13.6 0.0 copy-done.3
  13.6 0.5 shard_map.110
  14.1 0.0 collective-permute-done.2.refs_6_
  14.1 0.0 collective-permute-done.3.refs_7_
  14.1 2.2 %collective-permute-done.1.refs_5_ = bf16[2,144,128]{2,1,0:T(8,128)(2,1)S(1)} collective-permute-done((bf16[2,144,128]{2,1,0:T(8,128)(2,1)S(1)}, bf16[2,144,128]{2,1,0:T(8,128)(2,1)S(1)}, u32[]{:S(2)}, u32[]{:S(2)}) %collective-permute-start.1) | collective-permute-done | bytes 73760 | tf_op jit(solution)/shard_map/ppermute | solution.py:420
  16.2 7.2 %shard_map.112 = (bf16[64,8192]{1,0:T(8,128)(2,1)S(1)}, bf16[1536,128]{1,0:T(8,128)(2,1)S(1)}, bf16[1024,128]{1,0:T(8,128)(2,1)S(1)}, f32[32,64]{1,0:T(8,128)S(1)}, bf16[16,64,64]{2,1,0:T(8,128)(2,1)S(1)}) custom-call(bf16[64,64,128]{2,1,0:T(8,128)(2,1)S(1)} %copy-done, bf16[64,64]{1,0:T(8,128)(2,1)S(1)} %get-tuple-element.27.refs_1_.refs_6_, ...), custom_call_target="tpu_custom_call" | custom-call | flops 5000000000 | bytes 8000000 | tf_op jit(solution)/shard_map/pallas_call | solution.py:473
  23.4 0.0 copy-start.4
  23.5 0.9 %collective-permute-start.4 = (bf16[512,128]{1,0:T(8,128)(2,1)S(1)}, bf16[512,128]{1,0:T(8,128)(2,1)S(1)}, u32[]{:S(2)}, u32[]{:S(2)}) collective-permute-start(bf16[512,128]{1,0:T(8,128)(2,1)S(1)} %bitcast.104), channel_id=1, source_target_pairs={{0,2},{1,3},{2,0},{3,1},{4,6},{5,7},{6,4},{7,5},{8,10},{9,11},{10,... | collective-permute-start | bytes 393224 | tf_op jit(solution)/shard_map/ppermute | solution.py:346
  24.3 5.3 %shard_map.113 = (bf16[48,128]{1,0:T(8,128)(2,1)S(1)}, bf16[4,64,128]{2,1,0:T(8,128)(2,1)S(1)}) custom-call(bf16[64,8192]{1,0:T(8,128)(2,1)S(1)} %get-tuple-element.33.refs_0_, bf16[1536,128]{1,0:T(8,128)(2,1)S(1)} %get-tuple-element.31.refs_1_.refs_0_, bf16[32,4096]{1,0:T(8,128)(2,1)S(1)} %get-tuple-element.28.refs_3_.refs_2_, ...), custom_call_target="tpu_custom_call" | custom-call | flops 8000000000 | bytes 8000000 | tf_op jit(solution)/shard_map/pallas_call | solution.py:499
  29.7 0.0 copy-done.4
  29.7 0.0 collective-permute-done.4
  29.8 0.1 collective-permute-start.5
  29.9 0.0 copy-start.5
  29.9 1.3 %collective-permute-done.5 = bf16[432,128]{1,0:T(8,128)(2,1)S(1)} collective-permute-done((bf16[432,128]{1,0:T(8,128)(2,1)S(1)}, bf16[432,128]{1,0:T(8,128)(2,1)S(1)}, u32[]{:S(2)}, u32[]{:S(2)}) %collective-permute-start.5) | collective-permute-done | bytes 110624 | tf_op jit(solution)/shard_map/ppermute | solution.py:346
  31.3 0.9 %collective-permute-start.6 = (bf16[432,128]{1,0:T(8,128)(2,1)S(1)}, bf16[432,128]{1,0:T(8,128)(2,1)S(1)}, u32[]{:S(2)}, u32[]{:S(2)}) collective-permute-start(bf16[432,128]{1,0:T(8,128)(2,1)S(1)} %pad_maximum_fusion.5), channel_id=1, source_target_pairs={{0,4},{4,0},{8,12},{12,8},{1,5},{5,1},{9,13},{13,9},{2,6},{6,2},{1... | collective-permute-start | bytes 331784 | tf_op jit(solution)/shard_map/ppermute | solution.py:346
  32.2 0.0 copy-done.5
  32.2 4.9 %shard_map.114 = (bf16[64,64,128]{2,1,0:T(8,128)(2,1)}, bf16[48,128]{1,0:T(8,128)(2,1)S(1)}) custom-call(bf16[1536,128]{1,0:T(8,128)(2,1)S(1)} %copy-done.5, f32[1,128]{1,0:T(1,128)S(1)} %get-tuple-element.32.refs_1_, bf16[32,4096]{1,0:T(8,128)(2,1)S(1)} %get-tuple-element.28.refs_3_.refs_2_, bf16[48,128]{1,0:T(8,128)(2,1)S(1)} %add_convert_fusion.4.refs_3_), custom_call_target="tpu_custom_call" | custom-call | flops 6000000000 | bytes 8000000 | tf_op jit(solution)/shard_map/pallas_call | solution.py:519
  37.1 0.0 collective-permute-done.6
  37.2 1.5 %collective-permute-start.7 = (bf16[432,128]{1,0:T(8,128)(2,1)S(1)}, bf16[432,128]{1,0:T(8,128)(2,1)S(1)}, u32[]{:S(2)}, u32[]{:S(2)}) collective-permute-start(bf16[432,128]{1,0:T(8,128)(2,1)S(1)} %pad_maximum_fusion.6), channel_id=1, source_target_pairs={{0,8},{4,12},{8,0},{12,4},{1,9},{5,13},{9,1},{13,5},{2,10},{6,14},... | collective-permute-start | bytes 331784 | tf_op jit(solution)/shard_map/ppermute | solution.py:346
  38.7 6.2 %shard_map.115 = (bf16[4,32,128]{2,1,0:T(8,128)(2,1)S(1)}, bf16[4,32,128]{2,1,0:T(8,128)(2,1)S(1)}, bf16[48,128]{1,0:T(8,128)(2,1)S(1)}) custom-call(bf16[64,8192]{1,0:T(8,128)(2,1)S(1)} %get-tuple-element.33.refs_0_, bf16[1536,128]{1,0:T(8,128)(2,1)S(1)} %copy-done.5, bf16[32,4096]{1,0:T(8,128)(2,1)S(1)} %get-tuple-element.28.refs_3_.refs_2_, ...), custom_call_target="tpu_custom_call" | custom-call | flops 6000000000 | bytes 8000000 | tf_op jit(solution)/shard_map/pallas_call | solution.py:531
  44.9 0.5 collective-permute-done.7
  45.5 0.8 %collective-permute-start.8 = (bf16[496,128]{1,0:T(8,128)(2,1)S(1)}, bf16[496,128]{1,0:T(8,128)(2,1)S(1)}, u32[]{:S(2)}, u32[]{:S(2)}) collective-permute-start(bf16[496,128]{1,0:T(8,128)(2,1)S(1)} %pad_maximum_fusion.3), channel_id=1, source_target_pairs={{0,2},{1,3},{2,0},{3,1},{4,6},{5,7},{6,4},{7,5},{8,10},{9,11},{10,... | collective-permute-start | bytes 380936 | tf_op jit(solution)/shard_map/ppermute | solution.py:346
  46.3 4.2 %collective-permute-done.8 = bf16[496,128]{1,0:T(8,128)(2,1)S(1)} collective-permute-done((bf16[496,128]{1,0:T(8,128)(2,1)S(1)}, bf16[496,128]{1,0:T(8,128)(2,1)S(1)}, u32[]{:S(2)}, u32[]{:S(2)}) %collective-permute-start.8) | collective-permute-done | bytes 127008 | tf_op jit(solution)/shard_map/ppermute | solution.py:346
  50.6 0.1 collective-permute-start.9
  50.7 1.3 %collective-permute-done.9 = bf16[576,128]{1,0:T(8,128)(2,1)S(1)} collective-permute-done((bf16[576,128]{1,0:T(8,128)(2,1)S(1)}, bf16[576,128]{1,0:T(8,128)(2,1)S(1)}, u32[]{:S(2)}, u32[]{:S(2)}) %collective-permute-start.9) | collective-permute-done | bytes 147488 | tf_op jit(solution)/shard_map/ppermute | solution.py:346
  52.2 2.4 %shard_map.116 = (f32[256,64]{1,0:T(8,128)}, f32[64,64]{1,0:T(8,128)}, f32[1,128]{1,0:T(1,128)}, f32[32,32,128]{2,1,0:T(8,128)}) custom-call(bf16[32,256]{1,0:T(8,128)(2,1)S(1)} %bitcast.89, bf16[32,256]{1,0:T(8,128)(2,1)S(1)} %bitcast.90, bf16[16,512]{1,0:T(8,128)(2,1)S(1)} %bitcast.88, bf16[48,128]{1,0:T(8,128)(2,1)S(1)} %add_convert_fusion.2.refs_3_, ...), custom_call_target="tpu_custom_call" | custom-call | tf_op jit(solution)/shard_map/pallas_call | solution.py:579
  (44 shorter events, 0.6 us)
Async XLA Ops:
  0.6 1.0 %copy-start.6 = (bf16[16,16,64]{2,1,0:T(8,128)(2,1)S(1)}, bf16[16,16,64]{2,1,0:T(8,128)(2,1)}, u32[]{:S(2)}) copy-start(bf16[16,16,64]{2,1,0:T(8,128)(2,1)} %param.7) | copy-start | bytes 98308
  0.6 12.2 %copy-start = (bf16[64,64,128]{2,1,0:T(8,128)(2,1)S(1)}, bf16[64,64,128]{2,1,0:T(8,128)(2,1)}, u32[]{:S(2)}) copy-start(bf16[64,64,128]{2,1,0:T(8,128)(2,1)} %refs_0_.1) | copy-start | bytes 3145732
  2.3 1.4 %collective-permute-start = (bf16[272,128]{1,0:T(8,128)(2,1)S(1)}, bf16[272,128]{1,0:T(8,128)(2,1)S(1)}, u32[]{:S(2)}, u32[]{:S(2)}) collective-permute-start(bf16[272,128]{1,0:T(8,128)(2,1)S(1)} %pad_maximum_fusion.8), channel_id=1, source_target_pairs={{0,1},{1,0},{2,3},{3,2},{4,5},{5,4},{6,7},{7,6},{8,9},{9,8},{10,11... | collective-permute-start | bytes 208904 | tf_op jit(solution)/shard_map/ppermute | solution.py:346
  3.8 10.3 %collective-permute-start.2 = (bf16[2,144,128]{2,1,0:T(8,128)(2,1)S(1)}, bf16[2,144,128]{2,1,0:T(8,128)(2,1)S(1)}, u32[]{:S(2)}, u32[]{:S(2)}) collective-permute-start(bf16[2,144,128]{2,1,0:T(8,128)(2,1)S(1)} %get-tuple-element.53), channel_id=1, source_target_pairs={{0,8},{1,0},{2,12},{3,4},{4,9},{5,1},{6,13},{7,5},{8,10},{9,2},{10... | collective-permute-start | bytes 221192 | tf_op jit(solution)/shard_map/ppermute | solution.py:433
  7.8 6.3 %collective-permute-start.3 = (bf16[2,144,128]{2,1,0:T(8,128)(2,1)S(1)}, bf16[2,144,128]{2,1,0:T(8,128)(2,1)S(1)}, u32[]{:S(2)}, u32[]{:S(2)}) collective-permute-start(bf16[2,144,128]{2,1,0:T(8,128)(2,1)S(1)} %get-tuple-element.53), channel_id=1, source_target_pairs={{0,12},{1,4},{2,8},{3,0},{4,13},{5,5},{6,9},{7,1},{8,14},{9,6},{10... | collective-permute-start | bytes 221192 | tf_op jit(solution)/shard_map/ppermute | solution.py:433
  11.8 1.1 %copy-start.1 = (bf16[1024,128]{1,0:T(8,128)(2,1)S(1)}, bf16[1024,128]{1,0:T(8,128)(2,1)}, u32[]{:S(2)}) copy-start(bf16[1024,128]{1,0:T(8,128)(2,1)} %wide_ref.1) | copy-start | bytes 786436
  11.8 4.4 %collective-permute-start.1 = (bf16[2,144,128]{2,1,0:T(8,128)(2,1)S(1)}, bf16[2,144,128]{2,1,0:T(8,128)(2,1)S(1)}, u32[]{:S(2)}, u32[]{:S(2)}) collective-permute-start(bf16[2,144,128]{2,1,0:T(8,128)(2,1)S(1)} %get-tuple-element.54.refs_4_), channel_id=1, source_target_pairs={{0,2},{1,3},{2,0},{3,1},{4,6},{5,7},{6,4},{7,5},{8,10},{9,11},{10,... | collective-permute-start | bytes 221192 | tf_op jit(solution)/shard_map/ppermute | solution.py:420
  12.8 0.7 %copy-start.2 = (bf16[64,64]{1,0:T(8,128)(2,1)S(1)}, bf16[64,64]{1,0:T(8,128)(2,1)}, u32[]{:S(2)}) copy-start(bf16[64,64]{1,0:T(8,128)(2,1)} %w_ref.1) | copy-start | bytes 24580
  12.9 0.7 %copy-start.3 = (f32[128]{0:T(128)S(1)}, f32[128]{0:T(128)}, u32[]{:S(2)}) copy-start(f32[128]{0:T(128)} %param.12) | copy-start | bytes 1540
  23.4 6.3 %copy-start.4 = (bf16[1536,128]{1,0:T(8,128)(2,1)}, bf16[1536,128]{1,0:T(8,128)(2,1)S(1)}, u32[]{:S(2)}) copy-start(bf16[1536,128]{1,0:T(8,128)(2,1)S(1)} %get-tuple-element.31.refs_1_.refs_0_) | copy-start | bytes 1179652
  23.5 6.2 %collective-permute-start.4 = (bf16[512,128]{1,0:T(8,128)(2,1)S(1)}, bf16[512,128]{1,0:T(8,128)(2,1)S(1)}, u32[]{:S(2)}, u32[]{:S(2)}) collective-permute-start(bf16[512,128]{1,0:T(8,128)(2,1)S(1)} %bitcast.104), channel_id=1, source_target_pairs={{0,2},{1,3},{2,0},{3,1},{4,6},{5,7},{6,4},{7,5},{8,10},{9,11},{10,... | collective-permute-start | bytes 393224 | tf_op jit(solution)/shard_map/ppermute | solution.py:346
  29.8 1.4 %collective-permute-start.5 = (bf16[432,128]{1,0:T(8,128)(2,1)S(1)}, bf16[432,128]{1,0:T(8,128)(2,1)S(1)}, u32[]{:S(2)}, u32[]{:S(2)}) collective-permute-start(bf16[432,128]{1,0:T(8,128)(2,1)S(1)} %pad_maximum_fusion.4), channel_id=1, source_target_pairs={{0,1},{1,0},{2,3},{3,2},{4,5},{5,4},{6,7},{7,6},{8,9},{9,8},{10,11... | collective-permute-start | bytes 331784 | tf_op jit(solution)/shard_map/ppermute | solution.py:346
  29.9 2.3 %copy-start.5 = (bf16[1536,128]{1,0:T(8,128)(2,1)S(1)}, bf16[1536,128]{1,0:T(8,128)(2,1)}, u32[]{:S(2)}) copy-start(bf16[1536,128]{1,0:T(8,128)(2,1)} %copy-done.4) | copy-start | bytes 1179652
  31.3 5.8 %collective-permute-start.6 = (bf16[432,128]{1,0:T(8,128)(2,1)S(1)}, bf16[432,128]{1,0:T(8,128)(2,1)S(1)}, u32[]{:S(2)}, u32[]{:S(2)}) collective-permute-start(bf16[432,128]{1,0:T(8,128)(2,1)S(1)} %pad_maximum_fusion.5), channel_id=1, source_target_pairs={{0,4},{4,0},{8,12},{12,8},{1,5},{5,1},{9,13},{13,9},{2,6},{6,2},{1... | collective-permute-start | bytes 331784 | tf_op jit(solution)/shard_map/ppermute | solution.py:346
  37.2 8.2 %collective-permute-start.7 = (bf16[432,128]{1,0:T(8,128)(2,1)S(1)}, bf16[432,128]{1,0:T(8,128)(2,1)S(1)}, u32[]{:S(2)}, u32[]{:S(2)}) collective-permute-start(bf16[432,128]{1,0:T(8,128)(2,1)S(1)} %pad_maximum_fusion.6), channel_id=1, source_target_pairs={{0,8},{4,12},{8,0},{12,4},{1,9},{5,13},{9,1},{13,5},{2,10},{6,14},... | collective-permute-start | bytes 331784 | tf_op jit(solution)/shard_map/ppermute | solution.py:346
  45.5 5.0 %collective-permute-start.8 = (bf16[496,128]{1,0:T(8,128)(2,1)S(1)}, bf16[496,128]{1,0:T(8,128)(2,1)S(1)}, u32[]{:S(2)}, u32[]{:S(2)}) collective-permute-start(bf16[496,128]{1,0:T(8,128)(2,1)S(1)} %pad_maximum_fusion.3), channel_id=1, source_target_pairs={{0,2},{1,3},{2,0},{3,1},{4,6},{5,7},{6,4},{7,5},{8,10},{9,11},{10,... | collective-permute-start | bytes 380936 | tf_op jit(solution)/shard_map/ppermute | solution.py:346
  50.6 1.4 %collective-permute-start.9 = (bf16[576,128]{1,0:T(8,128)(2,1)S(1)}, bf16[576,128]{1,0:T(8,128)(2,1)S(1)}, u32[]{:S(2)}, u32[]{:S(2)}) collective-permute-start(bf16[576,128]{1,0:T(8,128)(2,1)S(1)} %pad_maximum_fusion.1), channel_id=1, source_target_pairs={{0,1},{1,0},{2,3},{3,2},{4,5},{5,4},{6,7},{7,6},{8,9},{9,8},{10,11... | collective-permute-start | bytes 442376 | tf_op jit(solution)/shard_map/ppermute | solution.py:346

commit v17 on v16

--- a/solution.py
+++ b/solution.py
@@ -10,7 +10,7 @@
 F32 = jnp.float32
 BF16 = jnp.bfloat16
 LANES = 128
-VMEM_LIMIT = 24 * 1024 * 1024
+VMEM_LIMIT = 16 * 1024 * 1024
 NT = (((1,), (1,)), ((), ()))
 
 
@@ -106,21 +106,35 @@
     return jnp.concatenate([held_ref[at + k * block : at + (k + 1) * block, :] for k in range(tiles)], axis=1)
 
 
-def factor_kernel(w_ref, wide_ref, offset_ref, up_ref, wt_ref, wc_ref, pass_ref, bias_ref, rows_ref):
+def factor_kernel(own, depth, features, pieces, *refs):
+    w_ref, wide_ref, offset_ref = refs[:3]
+    a_refs, refs = refs[3 : 3 + pieces], refs[3 + pieces :]
+    t_ref, wt_ref, wc_ref, pass_ref, a_ref, at_ref, seen_ref, rows_ref, mi_ref = refs
+    g = pl.program_id(0)
     width = w_ref.shape[1] // 2
     pair = wide_ref.shape[1]
-    pass_ref[...] = offset_ref[...]
-    rows_ref[...] = wide_ref[...].astype(F32)
-    for e in range(width):
-        part = rows_ref[pl.ds(e, width, stride=width), :]
-        wc_ref[:, e * pair : (e + 1) * pair] = part.astype(BF16)
-    same = one_hot(iota((2 * width, 2 * width), 0) == iota((2 * width, 2 * width), 1))
-    wt_ref[...] = dot_nt(same, w_ref[...]).astype(BF16)
-    bias = [jnp.zeros(up_ref.shape[1:], F32)] * 2
-    for i in range(up_ref.shape[0]):
-        bias[i % 2] = bias[i % 2] + up_ref[i].astype(F32)
-    bias = jnp.sum(bias[0] + bias[1], axis=0, keepdims=True)
-    bias_ref[...] = jnp.broadcast_to(bias, bias_ref.shape)
+
+    @pl.when(g == 0)
+    def _():
+        pass_ref[...] = offset_ref[...]
+        rows_ref[...] = wide_ref[...].astype(F32)
+        for e in range(width):
+            part = rows_ref[pl.ds(e, width, stride=width), :]
+            wc_ref[:, e * pair : (e + 1) * pair] = part.astype(BF16)
+        if own % 16 == 0:
+            unpack(depth, own, features, a_refs, (), mi_ref, None, seen_ref, None)
+        else:
+            mi_ref[...], seen_ref[...] = a_refs[0][...], a_refs[1][...]
+        same = one_hot(iota((2 * width, 2 * width), 0) == iota((2 * width, 2 * width), 1))
+        wt = dot_nt(same, w_ref[...]).astype(BF16)
+        wt_ref[...] = wt
+        mi = mi_ref[...]
+        a_ref[...] = dot_nt(mi, wt[:width, :]).astype(BF16)
+        same = one_hot(iota((features, features), 0) == iota((features, features), 1))
+        at_ref[...] = dot_nt(jnp.concatenate([wt[:width, :], same], axis=0), mi).astype(BF16)
+
+    span = t_ref.shape[1] // pair * depth
+    fill_t(a_ref[pl.ds(pl.multiple_of(g * span, span), span), :], wc_ref, t_ref, depth)
 
 
 def unpack(depth, own, features, a_refs, j_refs, mi_ref, mj_ref, seen_i_ref, seen_j_ref):
@@ -146,10 +160,10 @@
 
 
 def weight_kernel(depth, features, own, pieces, part_size, *refs):
-    up_ref, wt_ref, perm_ref, wc_ref = refs[:4]
-    a_refs, j_refs, refs = refs[4 : 4 + pieces], refs[4 + pieces : 4 + 2 * pieces], refs[4 + 2 * pieces :]
-    g_ref, held_ref, dw_ref, left_ref, mj_ref = refs[:5]
-    mi_ref, seen_i_ref, seen_j_ref, at_ref, bt_ref, inv_ref, v_ref, acc_ref, wide_ref = refs[5:]
+    up_ref, _, wt_ref, perm_ref, wc_ref, a_ref, at_ref, seen_i_ref = refs[:8]
+    j_refs, refs = refs[8 : 8 + pieces], refs[8 + pieces :]
+    g_ref, held_ref, dw_ref, left_ref, mj_ref, bias_ref = refs[:6]
+    seen_j_ref, bt_ref, inv_ref, v_ref, acc_ref, wide_ref = refs[6:]
     g, last = pl.program_id(0), pl.num_programs(0) - 1
     chunk, block, pair = up_ref.shape
     width = wt_ref.shape[0] // 2
@@ -157,15 +171,12 @@
     @pl.when(g == 0)
     def _():
         if own % 16 == 0:
-            unpack(depth, own, features, a_refs, j_refs, mi_ref, mj_ref, seen_i_ref, seen_j_ref)
+            unpack(depth, own, features, (), j_refs, None, mj_ref, None, seen_j_ref)
         else:
-            mi_ref[...], seen_i_ref[...] = a_refs[0][...], a_refs[1][...]
             mj_ref[...], seen_j_ref[...] = j_refs[0][...], j_refs[1][...]
         wt = wt_ref[...]
-        mi = mi_ref[...]
-        held_ref[: block * depth, :width] = dot_nt(mi, wt[:width, :]).astype(BF16)
-        same = one_hot(iota((features, features), 0) == iota((features, features), 1))
-        at_ref[...] = dot_nt(jnp.concatenate([wt[:width, :], same], axis=0), mi).astype(BF16)
+        held_ref[: block * depth, :width] = a_ref[...]
+        bias_ref[...] = jnp.zeros_like(bias_ref)
         b = jnp.zeros((block, width * depth), F32)
         for s in range(depth):
             part = dot_nt(mj_ref[s], wt[width:, :]).astype(BF16)
@@ -184,12 +195,15 @@
         acc_ref[...] = jnp.zeros_like(acc_ref)
         wide_ref[...] = jnp.zeros_like(wide_ref)
 
+    bias = jnp.zeros((block, pair), F32)
     for k in range(chunk // part_size):
         inv = inv_ref[g * (chunk // part_size) + k]
         for i in range(part_size):
             up = up_ref[k * part_size + i].astype(F32)
+            bias = bias + up
             at = (k * part_size + i) * pair
             g_ref[:, at : at + pair] = (up * inv[:, i : i + 1]).astype(BF16)
+    bias_ref[0:1, :] += jnp.sum(bias, axis=0, keepdims=True)
     fill_v(g_ref, bt_ref[...], v_ref, depth)
     span = chunk * depth
     a_t = at_ref[:, pl.ds(pl.multiple_of(g * span, span), span)]
@@ -245,18 +259,14 @@
 
 
 def token_kernel(depth, features, n, *refs):
-    g_ref, held_ref, wc_ref, mj_ref, perm_ref, bias_ref, left_ref = refs[:7]
-    small_ref, out_ref, t_ref, db_ref = refs[7:]
+    g_ref, t_ref, _, mj_ref, perm_ref, bias_ref, left_ref, small_ref, out_ref, db_ref = refs
     g, last = pl.program_id(0), pl.num_programs(0) - 1
     block, width = g_ref.shape[0], left_ref.shape[0]
-    chunk = t_ref.shape[1] // (wc_ref.shape[1] // width)
 
     @pl.when(g == 0)
     def _():
         db_ref[...] = jnp.zeros_like(db_ref)
 
-    span = chunk * depth
-    fill_t(held_ref[pl.ds(pl.multiple_of(g * span, span), span), :width], wc_ref, t_ref, depth)
     db_ref[...] += dot_nt(t_ref[...], g_ref[...])
 
     @pl.when(g == last)
@@ -443,20 +453,24 @@
     source = jnp.arange(wide)
     perm = (jnp.arange(wide)[None, :] == (source % width * depth + source // width)[:, None]).astype(BF16)
     up_spec = pl.BlockSpec((chunk, block, pair), lambda g: (g, 0, 0))
-    args = (sitewise_factors, pairing_matrix, offset, upstream_adjoint)
+    args = (sitewise_factors, pairing_matrix, offset, *a_pieces)
     out_shapes = [
+        sds((wide, block * pair), BF16),
         sds((2 * width, features), BF16),
         sds((width, width * pair), BF16),
         sds((1, pair), F32),
-        sds((8, pair), F32),
+        sds((tokens, width), BF16),
+        sds((width + features, tokens), BF16),
+        sds((block, LANES), BF16),
     ]
-    factors_t, pairing_wide, offset, bias = call(
-        factor_kernel,
-        (),
+    t, factors_t, pairing_wide, offset, a, a_t, seen = call(
+        functools.partial(factor_kernel, own, depth, features, len(a_pieces)),
+        (steps,),
         [full(v.shape) for v in args],
-        [full(o.shape) for o in out_shapes],
+        [pl.BlockSpec((wide, chunk * pair), lambda g: (0, g))] + [full(o.shape) for o in out_shapes[1:]],
         out_shapes,
-        [pltpu.VMEM((width * width, pair), F32)],
+        [pltpu.VMEM((width * width, pair), F32), pltpu.VMEM((tokens, features), BF16)],
+        cost(3e9, 8e6),
     )(*args)
 
     out_shapes = [
@@ -465,22 +479,21 @@
         sds((width * width, pair), BF16),
         sds((width, features), F32),
         sds((depth, block, features), BF16),
+        sds((8, pair), F32),
     ]
-    args = (upstream_adjoint, factors_t, perm, pairing_wide, *a_pieces, *j_pieces)
+    args = (upstream_adjoint, t, factors_t, perm, pairing_wide, a, a_t, seen, *j_pieces)
     large = 2 * chunk
     g_spec = pl.BlockSpec((block, chunk * pair), lambda g: (0, g))
     large_spec = pl.BlockSpec((block, large * pair), lambda g: (0, g))
-    scaled, held, d_pairing, left, mj = call(
-        functools.partial(weight_kernel, depth, features, own, len(a_pieces), chunk),
+    scaled, held, d_pairing, left, mj, bias = call(
+        functools.partial(weight_kernel, depth, features, own, len(j_pieces), chunk),
         (block // large,),
-        [pl.BlockSpec((large, block, pair), lambda g: (g, 0, 0))] + [full(v.shape) for v in args[1:]],
+        [pl.BlockSpec((large, block, pair), lambda g: (g, 0, 0)), pl.BlockSpec(memory_space=pl.ANY)]
+        + [full(v.shape) for v in args[2:]],
         [large_spec] + [full(o.shape) for o in out_shapes[1:]],
         out_shapes,
         [
-            pltpu.VMEM((tokens, features), BF16),
             pltpu.VMEM((block, LANES), BF16),
-            pltpu.VMEM((block, LANES), BF16),
-            pltpu.VMEM((width + features, tokens), BF16),
             pltpu.VMEM((wide, block), BF16),
             pltpu.VMEM((steps, block, chunk), F32),
             pltpu.VMEM((large * depth, width * pair), BF16),
@@ -499,12 +512,13 @@
     small, d_b = call(
         functools.partial(token_kernel, depth, features, n),
         (block // large,),
-        [large_spec] + [full(v.shape) for v in (held, pairing_wide, mj, perm, bias, left)],
+        [large_spec, pl.BlockSpec((wide, large * pair), lambda g: (0, g))]
+        + [full(v.shape) for v in (held, mj, perm, bias, left)],
         [full(o.shape) for o in out_shapes],
         out_shapes,
-        [pltpu.VMEM((wide, large * pair), BF16), pltpu.VMEM((wide, block), F32)],
+        [pltpu.VMEM((wide, block), F32)],
         cost(8e9, 8e6),
-    )(scaled, held, pairing_wide, mj, perm, bias, left)
+    )(scaled, t, held, mj, perm, bias, left)
 
     dp_keep, dp_go = halves(d_pairing, "col", 0, 0)
     db_keep, db_go = halves(d_b.reshape((n // 2, 2) + d_b.shape[1:]), "col", 0, 1)

time: 54.8 us -> 57.3 us (1.046)
  waiting for transfers between devices: 10.3 us -> 7.73 us
  Pallas kernels: 27 us -> 28.8 us
  local copies, waits for them, and re-layouts: 0.95 us -> 2.56 us
  other arithmetic: 1.55 us -> 2.4 us
  starting transfers between devices: 13.7 us -> 14.5 us
    pallas_call x2, Pallas kernels: 7.68 us -> 11 us  [the longest x1 7.03 us: per_device(): call(functools.partial(weight_kernel, depth, features, own, len(j_pieces)...]
    ppermute x2, starting transfers between devices: 8.04 us -> 5.58 us  [per_device(): held.append(lax.ppermute(message, axes, pairs))]
    ppermute x1, waiting for transfers between devices: 2.15 us -> 0.01 us  [per_device(): held.append(lax.ppermute(message, 'col', [(j, j ^ k) for j in range(n)]))]
    ppermute x1, starting transfers between devices: 0.87 us -> 2.9 us  [per_device(): held.append(lax.ppermute(message, 'col', [(j, j ^ k) for j in range(n)]))]
    unnamed x15 -> x9, local copies, waits for them, and re-layouts: 0.71 us -> 2.33 us
    pallas_call x1, Pallas kernels: 5.34 us -> 3.74 us  [per_device(): call(functools.partial(token_kernel, depth, features, n), (block // large...]
    ppermute x7, starting transfers between devices: 4.77 us -> 6 us  [swap_parts(): message = lax.ppermute(message, axis, pairs)]
    concatenate x1, other arithmetic: 0.09 us -> 0.93 us  [per_device(): jnp.concatenate([alignment_embedding, mask], axis=2).reshape(rows, LANES)]
  transfers between devices with their start and end apart: 10 -> 10, of which waited for: 6 -> 5; matrix products, arithmetic and copies ran while one was open for 0% -> 0% of each run, Pallas kernels for 31% -> 33%
where the time goes in v17:
time: 57.3 us; the launch traced here: 57 us
  Pallas kernels  28.8 us (50%)
  starting transfers between devices  14.5 us (25%)
  waiting for transfers between devices  7.73 us (13%)
  local copies, waits for them, and re-layouts  2.56 us (4%)
  other arithmetic  2.4 us (4%)
  between operations  1.07 us (2%)
    ppermute x7, waiting for transfers between devices, swap_parts(): message = lax.ppermute(message, axis, pairs)  7.72 us
    pallas_call x1, Pallas kernels, per_device(): call(functools.partial(weight_kernel, depth, features, own, len(j_pieces)...  7.03 us
    pallas_call x1, Pallas kernels, per_device(): call(functools.partial(left_kernel, depth, bits - 1), (steps,), [g_spec]...  6.18 us
    ppermute x7, starting transfers between devices, swap_parts(): message = lax.ppermute(message, axis, pairs)  6 us
    ppermute x2, starting transfers between devices, per_device(): held.append(lax.ppermute(message, axes, pairs))  5.58 us
    pallas_call x1, Pallas kernels, per_device(): call(functools.partial(update_kernel, depth), (steps,), [full(v.shape) fo...  4.85 us
    pallas_call x1, Pallas kernels, per_device(): call(functools.partial(factor_kernel, own, depth, features, len(a_pieces)...  4.01 us
    pallas_call x1, Pallas kernels, per_device(): call(functools.partial(token_kernel, depth, features, n), (block // large...  3.74 us
  transfers between devices with their start and end apart: 10, of which 5 were waited for; matrix products, arithmetic and copies ran while one was open for 0% of the time, Pallas kernels for 33%

profile of v17, /device:TPU:0, one launch (start us, length us, event | category | flops | bytes accessed | tf_op | source)
XLA Modules:
  0.0 57.0 jit_solution(16474316656906231411)
XLA Ops:
  0.6 0.0 copy-start
  0.6 0.9 %multiply_convert_fusion = bf16[16,16]{1,0:T(8,128)(2,1)S(1)} fusion(s32[16,16]{1,0:T(8,128)} %param.8, s32[16]{0:T(128)} %param.9), kind=kLoop, calls=%fused_computation.52 | loop fusion | flops 512 | bytes 1600 | tf_op jit(solution)/shard_map/convert_element_type | solution.py:413
  1.5 0.1 broadcast_in_dim.2
  1.6 0.9 %pad_maximum_fusion.9 = bf16[16,16,128]{2,1,0:T(8,128)(2,1)S(1)} fusion(bf16[16,16,64]{2,1,0:T(8,128)(2,1)S(1)} %broadcast_in_dim.2, bf16[16,16,64]{2,1,0:T(8,128)(2,1)} %param.7), kind=kLoop, calls=%fused_computation.28 | loop fusion | flops 131072 | bytes 131072 | tf_op jit(solution)/shard_map/concatenate | solution.py:415
  2.5 0.5 shard_map.110
  3.1 0.5 collective-permute-start
  3.6 0.9 %collective-permute-done = bf16[272,128]{1,0:T(8,128)(2,1)S(1)} collective-permute-done((bf16[272,128]{1,0:T(8,128)(2,1)S(1)}, bf16[272,128]{1,0:T(8,128)(2,1)S(1)}, u32[]{:S(2)}, u32[]{:S(2)}) %collective-permute-start) | collective-permute-done | bytes 69664 | tf_op jit(solution)/shard_map/ppermute | solution.py:356
  4.6 2.9 %collective-permute-start.1 = (bf16[2,144,128]{2,1,0:T(8,128)(2,1)S(1)}, bf16[2,144,128]{2,1,0:T(8,128)(2,1)S(1)}, u32[]{:S(2)}, u32[]{:S(2)}) collective-permute-start(bf16[2,144,128]{2,1,0:T(8,128)(2,1)S(1)} %get-tuple-element.62.refs_3_), channel_id=1, source_target_pairs={{0,2},{1,3},{2,0},{3,1},{4,6},{5,7},{6,4},{7,5},{8,10},{9,11},{10,... | collective-permute-start | bytes 221192 | tf_op jit(solution)/shard_map/ppermute | solution.py:430
  7.5 0.1 fusion.refs_3_.refs_4_.refs_7_
  7.7 2.6 %collective-permute-start.2 = (bf16[2,144,128]{2,1,0:T(8,128)(2,1)S(1)}, bf16[2,144,128]{2,1,0:T(8,128)(2,1)S(1)}, u32[]{:S(2)}, u32[]{:S(2)}) collective-permute-start(bf16[2,144,128]{2,1,0:T(8,128)(2,1)S(1)} %get-tuple-element.61), channel_id=1, source_target_pairs={{0,8},{1,0},{2,12},{3,4},{4,9},{5,1},{6,13},{7,5},{8,10},{9,2},{10... | collective-permute-start | bytes 221192 | tf_op jit(solution)/shard_map/ppermute | solution.py:443
  10.3 2.9 %collective-permute-start.3 = (bf16[2,144,128]{2,1,0:T(8,128)(2,1)S(1)}, bf16[2,144,128]{2,1,0:T(8,128)(2,1)S(1)}, u32[]{:S(2)}, u32[]{:S(2)}) collective-permute-start(bf16[2,144,128]{2,1,0:T(8,128)(2,1)S(1)} %get-tuple-element.61), channel_id=1, source_target_pairs={{0,12},{1,4},{2,8},{3,0},{4,13},{5,5},{6,9},{7,1},{8,14},{9,6},{10... | collective-permute-start | bytes 221192 | tf_op jit(solution)/shard_map/ppermute | solution.py:443
  13.2 0.0 collective-permute-done.1.refs_4_
  13.3 0.0 copy-start.1
  13.3 0.9 %copy-done.1 = bf16[1024,128]{1,0:T(8,128)(2,1)S(1)} copy-done((bf16[1024,128]{1,0:T(8,128)(2,1)S(1)}, bf16[1024,128]{1,0:T(8,128)(2,1)}, u32[]{:S(2)}) %copy-start.1) | copy-done | bytes 262168
  14.2 0.0 copy-start.2
  14.2 0.7 %copy-done.2 = bf16[64,64]{1,0:T(8,128)(2,1)S(1)} copy-done((bf16[64,64]{1,0:T(8,128)(2,1)S(1)}, bf16[64,64]{1,0:T(8,128)(2,1)}, u32[]{:S(2)}) %copy-start.2) | copy-done | bytes 8216
  14.9 0.0 copy-start.3
  14.9 0.7 %copy-done.3 = f32[128]{0:T(128)S(1)} copy-done((f32[128]{0:T(128)S(1)}, f32[128]{0:T(128)}, u32[]{:S(2)}) %copy-start.3) | copy-done | bytes 536
  15.6 4.0 %shard_map.111 = (bf16[512,8192]{1,0:T(8,128)(2,1)S(1)}, bf16[64,64]{1,0:T(8,128)(2,1)S(1)}, bf16[32,4096]{1,0:T(8,128)(2,1)S(1)}, f32[1,128]{1,0:T(1,128)S(1)},...) custom-call(bf16[64,64]{1,0:T(8,128)(2,1)S(1)} %copy-done.2, ...), custom_call_target="tpu_custom_call" | custom-call | flops 3000000000 | bytes 8000000 | tf_op jit(solution)/shard_map/pallas_call | solution.py:466
  19.6 0.0 collective-permute-done.2.refs_8_
  19.6 0.0 collective-permute-done.3.refs_9_
  19.6 0.0 copy-done
  19.6 7.0 %shard_map.112 = (bf16[64,8192]{1,0:T(8,128)(2,1)S(1)}, bf16[1536,128]{1,0:T(8,128)(2,1)S(1)}, bf16[1024,128]{1,0:T(8,128)(2,1)S(1)}, f32[32,64]{1,0:T(8,128)S(1...) custom-call(bf16[64,64,128]{2,1,0:T(8,128)(2,1)S(1)} %copy-done, ...), custom_call_target="tpu_custom_call" | custom-call | flops 5000000000 | bytes 8000000 | tf_op jit(solution)/shard_map/pallas_call | solution.py:488
  26.7 1.5 %collective-permute-start.4 = (bf16[512,128]{1,0:T(8,128)(2,1)S(1)}, bf16[512,128]{1,0:T(8,128)(2,1)S(1)}, u32[]{:S(2)}, u32[]{:S(2)}) collective-permute-start(bf16[512,128]{1,0:T(8,128)(2,1)S(1)} %bitcast.104), channel_id=1, source_target_pairs={{0,2},{1,3},{2,0},{3,1},{4,6},{5,7},{6,4},{7,5},{8,10},{9,11},{10,... | collective-permute-start | bytes 393224 | tf_op jit(solution)/shard_map/ppermute | solution.py:356
  28.2 3.7 %shard_map.113 = (bf16[48,128]{1,0:T(8,128)(2,1)S(1)}, bf16[4,64,128]{2,1,0:T(8,128)(2,1)S(1)}) custom-call(bf16[64,8192]{1,0:T(8,128)(2,1)S(1)} %get-tuple-element.41.refs_0_, bf16[512,8192]{1,0:T(8,128)(2,1)S(1)} %get-tuple-element.33.refs_1_, bf16[1536,128]{1,0:T(8,128)(2,1)S(1)} %get-tuple-element.39.refs_2_.refs_0_.refs_1_, ...), custom_call_target="tpu_custom_call" | custom-call | flops 8000000000 | bytes 8000000 | tf_op jit(solution)/shard_map/pallas_call | solution.py:512
  32.0 0.0 collective-permute-done.4
  32.1 0.1 collective-permute-start.5
  32.1 1.3 %collective-permute-done.5 = bf16[432,128]{1,0:T(8,128)(2,1)S(1)} collective-permute-done((bf16[432,128]{1,0:T(8,128)(2,1)S(1)}, bf16[432,128]{1,0:T(8,128)(2,1)S(1)}, u32[]{:S(2)}, u32[]{:S(2)}) %collective-permute-start.5) | collective-permute-done | bytes 110624 | tf_op jit(solution)/shard_map/ppermute | solution.py:356
  33.6 0.1 collective-permute-start.6
  33.7 4.9 %shard_map.114 = (bf16[64,64,128]{2,1,0:T(8,128)(2,1)}, bf16[48,128]{1,0:T(8,128)(2,1)S(1)}) custom-call(bf16[1536,128]{1,0:T(8,128)(2,1)S(1)} %get-tuple-element.39.refs_2_.refs_0_.refs_1_, f32[1,128]{1,0:T(1,128)S(1)} %get-tuple-element.40.refs_1_, bf16[32,4096]{1,0:T(8,128)(2,1)S(1)} %get-tuple-element.35.refs_4_.refs_2_, ...), custom_call_target="tpu_custom_call" | custom-call | flops 6000000000 | bytes 8000000 | tf_op jit(solution)/shard_map/pallas_call | solution.py:533
  38.5 0.2 collective-permute-done.6
  38.9 2.7 %collective-permute-start.7 = (bf16[432,128]{1,0:T(8,128)(2,1)S(1)}, bf16[432,128]{1,0:T(8,128)(2,1)S(1)}, u32[]{:S(2)}, u32[]{:S(2)}) collective-permute-start(bf16[432,128]{1,0:T(8,128)(2,1)S(1)} %pad_maximum_fusion.6), channel_id=1, source_target_pairs={{0,8},{4,12},{8,0},{12,4},{1,9},{5,13},{9,1},{13,5},{2,10},{6,14},... | collective-permute-start | bytes 331784 | tf_op jit(solution)/shard_map/ppermute | solution.py:356
  41.5 6.2 %shard_map.115 = (bf16[4,32,128]{2,1,0:T(8,128)(2,1)S(1)}, bf16[4,32,128]{2,1,0:T(8,128)(2,1)S(1)}, bf16[48,128]{1,0:T(8,128)(2,1)S(1)}) custom-call(bf16[64,8192]{1,0:T(8,128)(2,1)S(1)} %get-tuple-element.41.refs_0_, bf16[1536,128]{1,0:T(8,128)(2,1)S(1)} %get-tuple-element.39.refs_2_.refs_0_.refs_1_, ...), custom_call_target="tpu_custom_call" | custom-call | flops 6000000000 | bytes 8000000 | tf_op jit(solution)/shard_map/pallas_call | solution.py:545
  47.7 0.0 collective-permute-done.7
  47.9 1.0 %collective-permute-start.8 = (bf16[496,128]{1,0:T(8,128)(2,1)S(1)}, bf16[496,128]{1,0:T(8,128)(2,1)S(1)}, u32[]{:S(2)}, u32[]{:S(2)}) collective-permute-start(bf16[496,128]{1,0:T(8,128)(2,1)S(1)} %pad_maximum_fusion.3), channel_id=1, source_target_pairs={{0,2},{1,3},{2,0},{3,1},{4,6},{5,7},{6,4},{7,5},{8,10},{9,11},{10,... | collective-permute-start | bytes 380936 | tf_op jit(solution)/shard_map/ppermute | solution.py:356
  48.9 4.0 %collective-permute-done.8 = bf16[496,128]{1,0:T(8,128)(2,1)S(1)} collective-permute-done((bf16[496,128]{1,0:T(8,128)(2,1)S(1)}, bf16[496,128]{1,0:T(8,128)(2,1)S(1)}, u32[]{:S(2)}, u32[]{:S(2)}) %collective-permute-start.8) | collective-permute-done | bytes 127008 | tf_op jit(solution)/shard_map/ppermute | solution.py:356
  53.0 0.1 collective-permute-start.9
  53.1 1.3 %collective-permute-done.9 = bf16[576,128]{1,0:T(8,128)(2,1)S(1)} collective-permute-done((bf16[576,128]{1,0:T(8,128)(2,1)S(1)}, bf16[576,128]{1,0:T(8,128)(2,1)S(1)}, u32[]{:S(2)}, u32[]{:S(2)}) %collective-permute-start.9) | collective-permute-done | bytes 147488 | tf_op jit(solution)/shard_map/ppermute | solution.py:356
  54.6 2.4 %shard_map.116 = (f32[256,64]{1,0:T(8,128)}, f32[64,64]{1,0:T(8,128)}, f32[1,128]{1,0:T(1,128)}, f32[32,32,128]{2,1,0:T(8,128)}) custom-call(bf16[32,256]{1,0:T(8,128)(2,1)S(1)} %bitcast.89, bf16[32,256]{1,0:T(8,128)(2,1)S(1)} %bitcast.90, bf16[16,512]{1,0:T(8,128)(2,1)S(1)} %bitcast.88, bf16[48,128]{1,0:T(8,128)(2,1)S(1)} %add_convert_fusion.2.refs_3_, ...), custom_call_target="tpu_custom_call" | custom-call | tf_op jit(solution)/shard_map/pallas_call | solution.py:593
  (44 shorter events, 0.6 us)
Async XLA Ops:
  0.6 19.0 %copy-start = (bf16[64,64,128]{2,1,0:T(8,128)(2,1)S(1)}, bf16[64,64,128]{2,1,0:T(8,128)(2,1)}, u32[]{:S(2)}) copy-start(bf16[64,64,128]{2,1,0:T(8,128)(2,1)} %refs_0_.3) | copy-start | bytes 3145732
  3.1 1.4 %collective-permute-start = (bf16[272,128]{1,0:T(8,128)(2,1)S(1)}, bf16[272,128]{1,0:T(8,128)(2,1)S(1)}, u32[]{:S(2)}, u32[]{:S(2)}) collective-permute-start(bf16[272,128]{1,0:T(8,128)(2,1)S(1)} %pad_maximum_fusion.8), channel_id=1, source_target_pairs={{0,1},{1,0},{2,3},{3,2},{4,5},{5,4},{6,7},{7,6},{8,9},{9,8},{10,11... | collective-permute-start | bytes 208904 | tf_op jit(solution)/shard_map/ppermute | solution.py:356
  4.6 8.7 %collective-permute-start.1 = (bf16[2,144,128]{2,1,0:T(8,128)(2,1)S(1)}, bf16[2,144,128]{2,1,0:T(8,128)(2,1)S(1)}, u32[]{:S(2)}, u32[]{:S(2)}) collective-permute-start(bf16[2,144,128]{2,1,0:T(8,128)(2,1)S(1)} %get-tuple-element.62.refs_3_), channel_id=1, source_target_pairs={{0,2},{1,3},{2,0},{3,1},{4,6},{5,7},{6,4},{7,5},{8,10},{9,11},{10,... | collective-permute-start | bytes 221192 | tf_op jit(solution)/shard_map/ppermute | solution.py:430
  7.7 11.9 %collective-permute-start.2 = (bf16[2,144,128]{2,1,0:T(8,128)(2,1)S(1)}, bf16[2,144,128]{2,1,0:T(8,128)(2,1)S(1)}, u32[]{:S(2)}, u32[]{:S(2)}) collective-permute-start(bf16[2,144,128]{2,1,0:T(8,128)(2,1)S(1)} %get-tuple-element.61), channel_id=1, source_target_pairs={{0,8},{1,0},{2,12},{3,4},{4,9},{5,1},{6,13},{7,5},{8,10},{9,2},{10... | collective-permute-start | bytes 221192 | tf_op jit(solution)/shard_map/ppermute | solution.py:443
  10.3 9.3 %collective-permute-start.3 = (bf16[2,144,128]{2,1,0:T(8,128)(2,1)S(1)}, bf16[2,144,128]{2,1,0:T(8,128)(2,1)S(1)}, u32[]{:S(2)}, u32[]{:S(2)}) collective-permute-start(bf16[2,144,128]{2,1,0:T(8,128)(2,1)S(1)} %get-tuple-element.61), channel_id=1, source_target_pairs={{0,12},{1,4},{2,8},{3,0},{4,13},{5,5},{6,9},{7,1},{8,14},{9,6},{10... | collective-permute-start | bytes 221192 | tf_op jit(solution)/shard_map/ppermute | solution.py:443
  13.3 1.0 %copy-start.1 = (bf16[1024,128]{1,0:T(8,128)(2,1)S(1)}, bf16[1024,128]{1,0:T(8,128)(2,1)}, u32[]{:S(2)}) copy-start(bf16[1024,128]{1,0:T(8,128)(2,1)} %refs_1_.1) | copy-start | bytes 786436
  14.2 0.7 %copy-start.2 = (bf16[64,64]{1,0:T(8,128)(2,1)S(1)}, bf16[64,64]{1,0:T(8,128)(2,1)}, u32[]{:S(2)}) copy-start(bf16[64,64]{1,0:T(8,128)(2,1)} %refs_0_.2) | copy-start | bytes 24580
  14.9 0.7 %copy-start.3 = (f32[128]{0:T(128)S(1)}, f32[128]{0:T(128)}, u32[]{:S(2)}) copy-start(f32[128]{0:T(128)} %param.12) | copy-start | bytes 1540
  26.7 5.3 %collective-permute-start.4 = (bf16[512,128]{1,0:T(8,128)(2,1)S(1)}, bf16[512,128]{1,0:T(8,128)(2,1)S(1)}, u32[]{:S(2)}, u32[]{:S(2)}) collective-permute-start(bf16[512,128]{1,0:T(8,128)(2,1)S(1)} %bitcast.104), channel_id=1, source_target_pairs={{0,2},{1,3},{2,0},{3,1},{4,6},{5,7},{6,4},{7,5},{8,10},{9,11},{10,... | collective-permute-start | bytes 393224 | tf_op jit(solution)/shard_map/ppermute | solution.py:356
  32.1 1.4 %collective-permute-start.5 = (bf16[432,128]{1,0:T(8,128)(2,1)S(1)}, bf16[432,128]{1,0:T(8,128)(2,1)S(1)}, u32[]{:S(2)}, u32[]{:S(2)}) collective-permute-start(bf16[432,128]{1,0:T(8,128)(2,1)S(1)} %pad_maximum_fusion.4), channel_id=1, source_target_pairs={{0,1},{1,0},{2,3},{3,2},{4,5},{5,4},{6,7},{7,6},{8,9},{9,8},{10,11... | collective-permute-start | bytes 331784 | tf_op jit(solution)/shard_map/ppermute | solution.py:356
  33.6 5.2 %collective-permute-start.6 = (bf16[432,128]{1,0:T(8,128)(2,1)S(1)}, bf16[432,128]{1,0:T(8,128)(2,1)S(1)}, u32[]{:S(2)}, u32[]{:S(2)}) collective-permute-start(bf16[432,128]{1,0:T(8,128)(2,1)S(1)} %pad_maximum_fusion.5), channel_id=1, source_target_pairs={{0,4},{4,0},{8,12},{12,8},{1,5},{5,1},{9,13},{13,9},{2,6},{6,2},{1... | collective-permute-start | bytes 331784 | tf_op jit(solution)/shard_map/ppermute | solution.py:356
  38.9 8.9 %collective-permute-start.7 = (bf16[432,128]{1,0:T(8,128)(2,1)S(1)}, bf16[432,128]{1,0:T(8,128)(2,1)S(1)}, u32[]{:S(2)}, u32[]{:S(2)}) collective-permute-start(bf16[432,128]{1,0:T(8,128)(2,1)S(1)} %pad_maximum_fusion.6), channel_id=1, source_target_pairs={{0,8},{4,12},{8,0},{12,4},{1,9},{5,13},{9,1},{13,5},{2,10},{6,14},... | collective-permute-start | bytes 331784 | tf_op jit(solution)/shard_map/ppermute | solution.py:356
  47.9 5.0 %collective-permute-start.8 = (bf16[496,128]{1,0:T(8,128)(2,1)S(1)}, bf16[496,128]{1,0:T(8,128)(2,1)S(1)}, u32[]{:S(2)}, u32[]{:S(2)}) collective-permute-start(bf16[496,128]{1,0:T(8,128)(2,1)S(1)} %pad_maximum_fusion.3), channel_id=1, source_target_pairs={{0,2},{1,3},{2,0},{3,1},{4,6},{5,7},{6,4},{7,5},{8,10},{9,11},{10,... | collective-permute-start | bytes 380936 | tf_op jit(solution)/shard_map/ppermute | solution.py:356
  53.0 1.4 %collective-permute-start.9 = (bf16[576,128]{1,0:T(8,128)(2,1)S(1)}, bf16[576,128]{1,0:T(8,128)(2,1)S(1)}, u32[]{:S(2)}, u32[]{:S(2)}) collective-permute-start(bf16[576,128]{1,0:T(8,128)(2,1)S(1)} %pad_maximum_fusion.1), channel_id=1, source_target_pairs={{0,1},{1,0},{2,3},{3,2},{4,5},{5,4},{6,7},{7,6},{8,9},{9,8},{10,11... | collective-permute-start | bytes 442376 | tf_op jit(solution)/shard_map/ppermute | solution.py:356
